TPU v7x, 32 devices: a whole 2x2x4 slice. The times are simulated.
32 devices in a mesh: section: 2 (over core), wide: 16 (over z, y, x).
Axes of the slice: x: 2, y: 2, z: 4, core: 2. Of those that a mesh axis runs over, the one named last changes fastest.
Arguments:
- frames: bfloat16 [1024, 48, 1024], P(('section', 'wide')), may hold values from -6 to 6
- qkv_weight: bfloat16 [1024, 3072], replicated, may hold values from -0.1875 to 0.1875
- out_weight: bfloat16 [1024, 1024], replicated, may hold values from -0.1875 to 0.1875
- proj_weight: bfloat16 [1024, 512], replicated, may hold values from -0.1875 to 0.1875
- mlp_weight: bfloat16 [1536, 1024], replicated, may hold values from -0.15625 to 0.15625
- logit_weight: bfloat16 [1024], replicated, may hold values from -0.1875 to 0.1875
- history: bfloat16 [128, 2048, 512], P(('section', 'wide')), may hold values from -6 to 6
- hist_len: int32 [128], P(('section', 'wide')), may hold values from 1 to 2048, as said below
- hist_mask: int32 [128, 2048], P(('section', 'wide')), may hold values 0 or 1
- req_owner: int32 [24576, 1], P(('section', 'wide')), may hold values from 0 to 31; in each aligned block of 768 rows (0 to 767, 768 to 1535, ...) at most 48 rows name the same one
- req_local: int32 [24576], P(('section', 'wide')), may hold values from 0 to 31
- labels: int32 [24576], P(('section', 'wide')), may hold values 0 or 1
Outputs:
- logits: float32 [24576], P(('section', 'wide'))
- grad_proj: float32 [1024, 512], P(('section', 'wide'))
Inputs may be any that keep to these rules, and one draw needn't show every extreme that they name: `hist_len`: some user has 2048 events and some user has 1. `req_owner`: among the 768 requests of one device at most 48 name the same device, and exactly 48 do on some device.
All inputs are finite; a program needn't handle non-finite values. No bound on the sum of `hist_mask` or of `labels` on one device may be relied on, other than what follows from the above.
Results may differ from a plain program's by a relative error of at most 0.01.
Values may be sent and summed in bfloat16 or wider, within the bound.
No kernel may reach another device: no remote copies, remote signals or barrier semaphores. Data moves between devices by JAX's collectives and lax.ppermute only.
A program may use at most 128 MiB of HBM per device.

v0:
```python
import functools
import math

import jax
import jax.numpy as jnp
from jax import lax
from jax.experimental import pallas as pl
from jax.experimental.pallas import tpu as pltpu
from jax.sharding import PartitionSpec as P

HEADS = 16
FRAMES = 3


EPSILON = 1e-06
MIB = 1024 * 1024


def layer_norm(values):
    center = values - jnp.mean(values, axis=-1, keepdims=True)
    spread = jnp.mean(jnp.square(center), axis=-1, keepdims=True)
    return center * lax.rsqrt(spread + EPSILON)


def dot(left, right):
    return jnp.dot(left, right, preferred_element_type=jnp.float32)


def dot_rows(left, right):
    return lax.dot_general(left, right, (((1,), (1,)), ((), ())), preferred_element_type=jnp.float32)


def dot_columns(left, right):
    return lax.dot_general(left, right, (((0,), (0,)), ((), ())), preferred_element_type=jnp.float32)


def split_rows(values):
    high = values.astype(jnp.bfloat16)
    low = (values - high.astype(jnp.float32)).astype(jnp.bfloat16)
    return jnp.concatenate([high, low], axis=0)


def dot_split(values, right):
    both = dot(split_rows(values), right)
    rows = values.shape[0]
    return both[:rows] + both[rows:]


def encode_kernel(
    tokens,
    core_ref,
    first_ref,
    next_ref,
    qkv_hbm,
    out_hbm,
    proj_hbm,
    history_hbm,
    keep_ref,
    send_ref,
    embedded_ref,
    history_ref,
    qkv_ref,
    out_ref,
    proj_ref,
    sems,
    normed_ref,
    packed_ref,
    scores_ref,
    mixed_rows_ref,
    sums_ref,
):
    group = pl.program_id(0)
    rows, width = next_ref.shape
    head_dim = width // HEADS
    patches = tokens // FRAMES
    cands = rows // tokens
    lanes = 2 * head_dim
    parts = 3
    copies = [
        pltpu.make_async_copy(
            qkv_hbm.at[:, pl.ds(part * width, width)],
            qkv_ref.at[:, pl.ds(part * width, width)],
            sems.at[part],
        )
        for part in range(parts)
    ]
    copies.append(pltpu.make_async_copy(out_hbm, out_ref, sems.at[parts]))
    copies.append(pltpu.make_async_copy(proj_hbm, proj_ref, sems.at[parts + 1]))
    copies.append(pltpu.make_async_copy(history_hbm, history_ref, sems.at[parts + 2]))

    @pl.when(group == 0)
    def _():
        for copy in copies:
            copy.start()

    def norm_cand(source_ref, half, cand_group, cand):
        at = cand * tokens
        inputs = source_ref[at : at + tokens, :].astype(jnp.float32)
        start = pl.multiple_of(half * rows, rows) + at
        normed_ref[pl.ds(pl.multiple_of(start, tokens), tokens), :] = layer_norm(inputs).astype(
            jnp.bfloat16
        )
        sums_ref[cand_group * cands + cand] = jnp.sum(inputs, axis=0, keepdims=True)

    @pl.when(group == 0)
    def _():
        for cand in range(cands):
            norm_cand(first_ref, 0, 0, cand)
        copies[0].wait()
        copies[1].wait()

    place = pl.multiple_of((group % 2) * rows, rows)
    following = jnp.minimum(group + 1, pl.num_programs(0) - 1)
    exponent = math.log2(math.e) / math.sqrt(head_dim)
    blocks = rows // lanes
    pairs = HEADS // 2
    quad = 4
    span = quad * head_dim
    frame_at = (lax.broadcasted_iota(jnp.int32, (patches, quad * lanes), 1) % lanes) // patches
    nothing = jnp.zeros((head_dim, lanes), jnp.bfloat16)
    for part in range(2):
        packed_ref[:, part * width : (part + 1) * width] = dot(
            normed_ref[pl.ds(place, rows), :], qkv_ref[:, part * width : (part + 1) * width]
        ).astype(jnp.bfloat16)
    for group_heads in range(HEADS // quad):
        start = group_heads * span
        for block in range(blocks):
            block_rows = slice(block * lanes, (block + 1) * lanes)
            query = packed_ref[block_rows, start : start + span]
            keys = packed_ref[block_rows, width + start : width + start + span].T
            keys = jnp.concatenate(
                [
                    jnp.concatenate(
                        [nothing] * head
                        + [keys[head * head_dim : (head + 1) * head_dim]]
                        + [nothing] * (quad - 1 - head),
                        axis=1,
                    )
                    for head in range(quad)
                ],
                axis=0,
            )
            scores = dot(query, keys)
            own_scores = scores[:patches]
            for frame in range(1, lanes // patches):
                own_scores = jnp.where(
                    frame_at == frame, scores[frame * patches : (frame + 1) * patches], own_scores
                )
            for side in range(quad // 2):
                scores_ref[block, group_heads * (quad // 2) + side] = own_scores[
                    :, side * 2 * lanes : (side + 1) * 2 * lanes
                ]
        for cand in range(group_heads * cands * quad // HEADS, (group_heads + 1) * cands * quad // HEADS):
            norm_cand(next_ref, 1 - group % 2, following, cand)

    ones_row = lax.broadcasted_iota(jnp.int32, (2 * lanes, 2 * lanes), 0) // patches
    ones_column = lax.broadcasted_iota(jnp.int32, (2 * lanes, 2 * lanes), 1) // patches
    frame_ones = (ones_row == ones_column).astype(jnp.bfloat16)
    exp_scores = jnp.exp2(
        scores_ref[...].reshape(blocks * pairs * patches, 2 * lanes) * exponent
    )
    totals = dot(exp_scores.astype(jnp.bfloat16), frame_ones)
    probs = (exp_scores / totals).reshape(blocks * pairs, patches, 2 * lanes)
    sums = jnp.sum(probs, axis=1)
    key_sums = [
        jnp.concatenate(
            [
                sums[block * pairs : (block + 1) * pairs, side * lanes : (side + 1) * lanes]
                for block in range(blocks)
            ],
            axis=1,
        )
        for side in range(2)
    ]
    own = lax.broadcasted_iota(jnp.int32, (cands, rows), 1) // tokens == lax.broadcasted_iota(
        jnp.int32, (cands, rows), 0
    )
    spread = jnp.concatenate(
        [jnp.where(own, key_sums[head % 2][head // 2 : head // 2 + 1], 0.0) for head in range(HEADS)], axis=0
    ).astype(jnp.bfloat16)
    mixed_rows = dot(spread, normed_ref[pl.ds(place, rows), :])
    for head in range(HEADS):
        mixed_rows_ref[head, pl.ds(pl.multiple_of(group * cands, cands), cands), :] = mixed_rows[
            head * cands : (head + 1) * cands
        ]

    @pl.when(group == pl.num_programs(0) - 1)
    def _():
        for copy in copies[2:]:
            copy.wait()
        total = embedded_ref.shape[0]
        pieces = []
        for part in range(HEADS // quad):
            left = mixed_rows_ref[pl.ds(part * quad, quad)].reshape(quad * total, width)
            both = dot_split(left, qkv_ref[:, pl.ds(2 * width + part * span, span)])
            head_at = lax.broadcasted_iota(jnp.int32, (total, span), 1) // head_dim
            piece = jnp.zeros((total, span), jnp.float32)
            for head in range(quad):
                piece = jnp.where(head_at == head, both[head * total : (head + 1) * total], piece)
            pieces.append(piece)
        mixed_mean = jnp.concatenate(pieces, axis=1) * (1.0 / tokens)
        hidden = sums_ref[...].reshape(total, width) * (1.0 / tokens) + dot_split(mixed_mean, out_ref[...])
        pooled = layer_norm(hidden).astype(jnp.bfloat16)
        first, second = pooled[:, : width // 2], pooled[:, width // 2 :]
        keep_ref[...] = jnp.where(core_ref[0] == 0, first, second)
        send_ref[...] = jnp.where(core_ref[0] == 0, second, first)
        embedded_ref[...] = dot(pooled, proj_ref[...]).astype(jnp.bfloat16)


def in_hbm(*arrays):
    return [pltpu.with_memory_space_constraint(array, pltpu.HBM) for array in arrays]


def encode_block(core, frames, qkv_weight, out_weight, proj_weight, history):
    cand_count, tokens, width = frames.shape
    key_width = proj_weight.shape[1]
    cands = 8
    rows = cands * tokens
    last = cand_count // cands - 1
    rows_in = in_hbm(frames.reshape(cand_count * tokens, width))[0]
    lanes = 2 * width // HEADS
    patches = tokens // FRAMES
    return pl.pallas_call(
        functools.partial(encode_kernel, tokens),
        grid=(cand_count // cands,),
        in_specs=[
            pl.BlockSpec(memory_space=pltpu.SMEM),
            pl.BlockSpec((rows, width), lambda group: (0, 0)),
            pl.BlockSpec((rows, width), lambda group: (jnp.minimum(group + 1, last), 0)),
            pl.BlockSpec(memory_space=pltpu.HBM),
            pl.BlockSpec(memory_space=pltpu.HBM),
            pl.BlockSpec(memory_space=pltpu.HBM),
            pl.BlockSpec(memory_space=pltpu.HBM),
        ],
        out_specs=[
            pl.BlockSpec((cand_count, width // 2), lambda group: (0, 0)),
            pl.BlockSpec((cand_count, width // 2), lambda group: (0, 0)),
            pl.BlockSpec((cand_count, key_width), lambda group: (0, 0)),
            pl.BlockSpec(memory_space=pltpu.VMEM),
        ],
        out_shape=[
            jax.ShapeDtypeStruct((cand_count, width // 2), jnp.bfloat16),
            jax.ShapeDtypeStruct((cand_count, width // 2), jnp.bfloat16),
            jax.ShapeDtypeStruct((cand_count, key_width), jnp.bfloat16),
            pltpu.VMEM(history.shape, history.dtype),
        ],
        scratch_shapes=[
            pltpu.VMEM(qkv_weight.shape, jnp.bfloat16),
            pltpu.VMEM(out_weight.shape, jnp.bfloat16),
            pltpu.VMEM(proj_weight.shape, jnp.bfloat16),
            pltpu.SemaphoreType.DMA((6,)),
            pltpu.VMEM((2 * rows, width), jnp.bfloat16),
            pltpu.VMEM((rows, 2 * width), jnp.bfloat16),
            pltpu.VMEM((rows * FRAMES // tokens * patches // lanes, HEADS // 2, patches, 2 * lanes), jnp.float32),
            pltpu.VMEM((HEADS, cand_count, width), jnp.float32),
            pltpu.VMEM((cand_count, 1, width), jnp.float32),
        ],
        compiler_params=pltpu.CompilerParams(vmem_limit_bytes=40 * MIB),
        cost_estimate=pl.CostEstimate(
            flops=5 * cand_count * tokens * width * width, bytes_accessed=1 << 24, transcendentals=0
        ),
        name="encode",
    )(core, rows_in, rows_in, *in_hbm(qkv_weight, out_weight, proj_weight, history))


def attend_kernel(
    inv_ref,
    slots_ref,
    near_ref,
    far_ref,
    history_ref,
    usable_ref,
    queries_ref,
    attended_ref,
    slope_ref,
):
    slots = slots_ref[...]
    half, key_width = near_ref.shape
    places = lax.broadcasted_iota(jnp.int32, (slots.shape[0], half), 1)
    queries = dot((slots == places).astype(jnp.bfloat16), near_ref[...])
    queries += dot((slots == places + half).astype(jnp.bfloat16), far_ref[...])
    queries_ref[...] = queries.astype(jnp.bfloat16)
    users, events, _ = history_ref.shape
    per_user = slots.shape[0] // users
    chunk = math.gcd(events, 1024)
    for user in range(users):
        rows = slice(user * per_user, (user + 1) * per_user)
        attended = jnp.zeros((per_user, key_width), jnp.float32)
        for at in range(0, events, chunk):
            keys = history_ref[user, at : at + chunk, :]
            usable = usable_ref[user, :, at : at + chunk]
            scores = dot_rows(queries_ref[rows, :], keys)
            half_gate = 0.5 * jnp.tanh(scores * (0.5 / math.sqrt(key_width)))
            weights = (0.5 + half_gate) * usable
            slope_ref[rows, at : at + chunk] = (weights * (0.5 - half_gate)).astype(jnp.bfloat16)
            attended += dot(weights.astype(jnp.bfloat16), keys)
        attended_ref[rows, :] = attended * inv_ref[user]


def attend(inv_count, slots, near, far, history, usable):
    users, events, key_width = history.shape
    requests = slots.shape[0]
    whole = pl.BlockSpec(memory_space=pltpu.VMEM)
    return pl.pallas_call(
        attend_kernel,
        in_specs=[pl.BlockSpec(memory_space=pltpu.SMEM)] + [whole] * 5,
        out_specs=[whole] * 3,
        out_shape=[
            jax.ShapeDtypeStruct((requests, key_width), jnp.bfloat16),
            jax.ShapeDtypeStruct((requests, key_width), jnp.float32),
            jax.ShapeDtypeStruct((requests, events), jnp.bfloat16),
        ],
        compiler_params=pltpu.CompilerParams(vmem_limit_bytes=28 * MIB),
        cost_estimate=pl.CostEstimate(
            flops=4 * requests * events * key_width, bytes_accessed=1 << 24, transcendentals=0
        ),
        name="attend",
    )(inv_count, slots, near, far, history, usable)


def score_kernel(
    inv_ref,
    queries_ref,
    attended_ref,
    labels_ref,
    mlp_ref,
    logit_weight_ref,
    logits_ref,
    grad_att_ref,
    direct_ref,
):
    step_users = inv_ref.shape[0] // pl.num_programs(0)
    per_user = queries_ref.shape[0] // step_users
    query_b = queries_ref[...]
    query_f = query_b.astype(jnp.float32)
    attended = attended_ref[...]
    key_width = query_f.shape[1]
    joined = jnp.concatenate(
        [query_b, attended.astype(jnp.bfloat16), (query_f * attended).astype(jnp.bfloat16)], axis=1
    )
    pre_act = dot(joined, mlp_ref[...])
    act_sig = 0.5 * jnp.tanh(0.5 * pre_act) + 0.5
    hidden_units = (pre_act * act_sig).astype(jnp.bfloat16)
    weight = logit_weight_ref[...].astype(jnp.float32)
    logits = jnp.sum(hidden_units.astype(jnp.float32) * weight, axis=1, keepdims=True)
    logits_ref[...] = logits
    dlogit = (0.5 * jnp.tanh(0.5 * logits) + 0.5) - labels_ref[...].astype(jnp.float32)
    grad_pre = (dlogit * weight * (act_sig * (1.0 + pre_act * (1.0 - act_sig)))).astype(jnp.bfloat16)
    djoined = dot_rows(grad_pre, mlp_ref[...])
    part_query = djoined[:, :key_width]
    part_att = djoined[:, key_width : 2 * key_width]
    part_prod = djoined[:, 2 * key_width :]
    grad_att = part_att + part_prod * query_f
    for user in range(step_users):
        rows = slice(user * per_user, (user + 1) * per_user)
        inv_count = inv_ref[pl.program_id(0) * step_users + user]
        grad_att_ref[rows, :] = (grad_att[rows] * inv_count).astype(jnp.bfloat16)
    direct_ref[...] = part_query + part_prod * attended


def score(inv_count, queries, attended, labels, mlp_weight, logit_weight):
    users = inv_count.shape[0]
    requests, key_width = queries.shape
    steps = math.gcd(users, 2)
    step_rows = requests // steps
    block = pl.BlockSpec((step_rows, key_width), lambda step: (step, 0))
    column = pl.BlockSpec((step_rows, 1), lambda step: (step, 0))
    return pl.pallas_call(
        score_kernel,
        grid=(steps,),
        in_specs=[
            pl.BlockSpec(memory_space=pltpu.SMEM),
            block,
            block,
            column,
            pl.BlockSpec(mlp_weight.shape, lambda step: (0, 0)),
            pl.BlockSpec(logit_weight.shape, lambda step: (0, 0)),
        ],
        out_specs=[column, block, block],
        out_shape=[
            jax.ShapeDtypeStruct((requests, 1), jnp.float32),
            jax.ShapeDtypeStruct((requests, key_width), jnp.bfloat16),
            jax.ShapeDtypeStruct((requests, key_width), jnp.float32),
        ],
        compiler_params=pltpu.CompilerParams(vmem_limit_bytes=32 * MIB),
        cost_estimate=pl.CostEstimate(
            flops=4 * requests * mlp_weight.shape[0] * mlp_weight.shape[1],
            bytes_accessed=1 << 23,
            transcendentals=0,
        ),
        name="score",
    )(inv_count, queries, attended, labels, mlp_weight, logit_weight)


def attend_back_kernel(first, grad_att_ref, direct_ref, slope_ref, history_ref, grad_rows_ref):
    users, events, key_width = history_ref.shape
    per_user = grad_att_ref.shape[0] // users
    chunk = math.gcd(events, 1024)
    for user in range(grad_rows_ref.shape[0] // per_user):
        rows = slice((first + user) * per_user, (first + user + 1) * per_user)
        back = jnp.zeros((per_user, key_width), jnp.float32)
        for at in range(0, events, chunk):
            keys = history_ref[first + user, at : at + chunk, :]
            slope = slope_ref[rows, at : at + chunk].astype(jnp.float32)
            grad_sig = (dot_rows(grad_att_ref[rows, :], keys) * slope).astype(jnp.bfloat16)
            back += dot(grad_sig, keys)
        grad_rows = direct_ref[rows, :] + back * (1.0 / math.sqrt(key_width))
        grad_rows_ref[user * per_user : (user + 1) * per_user, :] = grad_rows.astype(jnp.bfloat16)


def attend_back(first, count, grad_att, direct, slope, history):
    users, events, key_width = history.shape
    per_user = grad_att.shape[0] // users
    whole = pl.BlockSpec(memory_space=pltpu.VMEM)
    return pl.pallas_call(
        functools.partial(attend_back_kernel, first),
        in_specs=[whole] * 4,
        out_specs=whole,
        out_shape=jax.ShapeDtypeStruct((count * per_user, key_width), jnp.bfloat16),
        compiler_params=pltpu.CompilerParams(vmem_limit_bytes=20 * MIB),
        cost_estimate=pl.CostEstimate(
            flops=4 * count * per_user * events * key_width,
            bytes_accessed=1 << 23,
            transcendentals=0,
        ),
        name="attend_back",
    )(grad_att, direct, slope, history)


def terms_kernel(origins, wide_ref, slots_ref, *refs):
    grad_refs = refs[:-4]
    pooled_ref, out_ref, grad_rows_ref, terms_ref = refs[-4:]
    at = 0
    for grad_ref in grad_refs:
        grad_rows_ref[at : at + grad_ref.shape[0], :] = grad_ref[...]
        at += grad_ref.shape[0]
    cands = pooled_ref.shape[0]
    requests = slots_ref.shape[1]
    chunk = math.gcd(cands, 512)
    for at in range(0, cands, chunk):
        places = lax.broadcasted_iota(jnp.int32, (chunk, requests), 0) + at
        row_hot = (places == slots_ref[...]).astype(jnp.bfloat16)
        cand_grad = dot(row_hot, grad_rows_ref[...]).astype(jnp.bfloat16)
        term = dot_columns(pooled_ref[at : at + chunk, :], cand_grad)
        if at == 0:
            terms_ref[...] = term
        else:
            terms_ref[...] += term
    rows = terms_ref.shape[0] // len(origins)
    wide = wide_ref[0]
    batch = max(1, 32 // rows)
    for slot in range(0, len(origins), batch):
        found = [
            terms_ref[pl.ds(pl.multiple_of((wide ^ origins[slot + i]) * rows, rows), rows), :]
            for i in range(batch)
        ]
        found = found[0] if batch == 1 else jnp.concatenate(found, axis=0)
        out_ref[slot * rows : (slot + batch) * rows, :] = found.astype(jnp.bfloat16)


def chip_terms(origins, wide, slots, grad_parts, pooled):
    cands, width = pooled.shape
    requests = slots.shape[1]
    key_width = grad_parts[0].shape[1]
    whole = pl.BlockSpec(memory_space=pltpu.VMEM)
    return pl.pallas_call(
        functools.partial(terms_kernel, origins),
        in_specs=[pl.BlockSpec(memory_space=pltpu.SMEM)] + [whole] * (len(grad_parts) + 2),
        out_specs=whole,
        out_shape=jax.ShapeDtypeStruct((width, key_width), jnp.bfloat16),
        scratch_shapes=[
            pltpu.VMEM((requests, key_width), jnp.bfloat16),
            pltpu.VMEM((width, key_width), jnp.float32),
        ],
        compiler_params=pltpu.CompilerParams(vmem_limit_bytes=20 * MIB),
        cost_estimate=pl.CostEstimate(
            flops=2 * cands * key_width * (width + requests),
            bytes_accessed=1 << 22,
            transcendentals=0,
        ),
        name="chip_terms",
    )(wide, slots, *grad_parts, pooled)


def bit_groups(size):
    groups = []
    bit = 0
    while (1 << bit) < size:
        values = min(4, size >> bit)
        groups.append((bit, values))
        bit += values.bit_length() - 1
    return groups


def exchange(values, axis_name, size, distance):
    return lax.ppermute(values, axis_name, [(i, i ^ distance) for i in range(size)])


def send_stage(rows, wides, bit, values):
    return [exchange(rows, "wide", wides, step << bit) for step in range(1, values)]


def after(values, *others):
    return lax.optimization_barrier((tuple(values),) + others)[0]


def slot_of(distance, wides):
    slot = 0
    for bit, values in bit_groups(wides):
        slot = slot * values + ((distance >> bit) & (values - 1))
    return slot


def sum_blocks(blocks, wides):
    total = blocks
    for bit, values in bit_groups(wides):
        parts = total.astype(jnp.bfloat16).reshape((values, -1) + blocks.shape[1:])
        found = [
            exchange(parts[step], "wide", wides, step << bit).astype(jnp.float32)
            for step in range(1, values)
        ]
        total = sum(found, parts[0].astype(jnp.float32))
    return total


def body(
    frames,
    qkv_weight,
    out_weight,
    proj_weight,
    mlp_weight,
    logit_weight,
    history,
    hist_len,
    hist_mask,
    req_owner,
    req_local,
    labels,
):
    wides = lax.axis_size("wide")
    core, wide = lax.axis_index("section"), lax.axis_index("wide")
    cand_count = frames.shape[0]
    requests = req_local.shape[0]
    users, events, _ = history.shape
    keep, send, embedded, history = encode_block(
        core.reshape(1), frames, qkv_weight, out_weight, proj_weight, history
    )
    positions = jnp.arange(events, dtype=jnp.int32)[None, :]
    usable = (
        (positions < hist_len[:, None]) & ((hist_mask == 1) | (positions == 0))
    ).astype(jnp.float32)
    inv_count = lax.rsqrt(jnp.sum(usable, axis=1))
    usable = usable.reshape(users, 1, events)
    owner_core = req_owner[:, 0] // wides
    owner_slot = slot_of((req_owner[:, 0] % wides) ^ wide, wides)
    slots = ((owner_core ^ core) * wides + owner_slot) * cand_count + req_local
    pooled_slots = (owner_slot * 2 + owner_core) * cand_count + req_local
    stages = list(reversed(bit_groups(wides)))
    near = embedded
    for bit, values in stages:
        near = jnp.concatenate([near] + send_stage(near, wides, bit, values), axis=0)
        if bit == stages[0][0]:
            keep, send = after((keep, send), near)
    far = exchange(near, "section", 2, 1)
    far_slots = exchange(pooled_slots, "section", 2, 1)
    got = exchange(send, "section", 2, 1)
    pooled = jnp.where(
        core == 0, jnp.concatenate([keep, got], axis=0), jnp.concatenate([got, keep], axis=0)
    )
    found = send_stage(pooled, wides, *stages[0])
    queries, attended, slope = attend(
        inv_count, slots.reshape(requests, 1), near, far, history, usable
    )
    for stage in stages[1:]:
        pooled = jnp.concatenate(after([pooled] + found, attended), axis=0)
        found = send_stage(pooled, wides, *stage)
    logits, grad_att, direct = score(
        inv_count,
        queries,
        attended,
        labels.reshape(requests, 1),
        mlp_weight,
        logit_weight.reshape(1, -1),
    )
    half = users // 2
    grad_parts = [
        attend_back(0, half, grad_att, direct, slope, history),
        attend_back(half, users - half, grad_att, direct, slope, history),
    ]
    far_parts = [exchange(part, "section", 2, 1) for part in grad_parts]
    pooled = jnp.concatenate(after([pooled] + found, grad_parts[1]), axis=0)
    origins = [0] * wides
    for distance in range(wides):
        origins[slot_of(distance, wides)] = distance
    terms = chip_terms(
        origins,
        wide.reshape(1),
        jnp.concatenate([pooled_slots, far_slots]).reshape(1, 2 * requests),
        grad_parts + far_parts,
        pooled,
    )
    grad_proj = sum_blocks(terms, wides)
    return (logits.reshape(requests), grad_proj)


def solution(mesh):
    in_specs = (
        P(("section", "wide"), None, None),
        P(),
        P(),
        P(),
        P(),
        P(),
        P(("section", "wide"), None, None),
        P(("section", "wide")),
        P(("section", "wide"), None),
        P(("section", "wide"), None),
        P(("section", "wide")),
        P(("section", "wide")),
    )
    out_specs = (P(("section", "wide")), P(("section", "wide"), None))
    return jax.shard_map(body, mesh=mesh, in_specs=in_specs, out_specs=out_specs, check_vma=False)
```

profile of v0, /device:TPU:0, one launch (start us, length us, event | category | flops | bytes accessed | tf_op | source)
XLA Modules:
  0.0 94.5 jit_solution(7315903047411323932)
XLA Ops:
  0.7 17.4 %encode.1 = (bf16[32,512]{1,0:T(8,128)(2,1)S(1)}, bf16[32,512]{1,0:T(8,128)(2,1)S(1)}, bf16[32,512]{1,0:T(8,128)(2,1)S(1)}, bf16[4,2048,512]{2,1,0:T(8,128)(2,1)S(1)}) custom-call(s32[1]{0:T(128)} %bitcast.core_ref, bf16[1536,1024]{1,0:T(8,128)(2,1)} %bitcast.5, bf16[1536,1024]{1,0:T(8,128)(2,1)} %bitcast.6, bf16[1024,3072]{1,0:T(8,128)(2,1)} %qkv_hbm.1, ...), custom_call_target="tpu_custom_call" | custom-call | flops 8053063680 | bytes 16777216 | tf_op jit(solution)/shard_map/encode/pallas_call | solution.py:223
  18.1 3.3 %copy-done = bf16[4,2048,512]{2,1,0:T(8,128)(2,1)} copy-done((bf16[4,2048,512]{2,1,0:T(8,128)(2,1)}, bf16[4,2048,512]{2,1,0:T(8,128)(2,1)S(1)}, u32[]{:S(2)}) %copy-start) | copy-done | bytes 8388632
  21.4 3.0 %collective-permute-start = (bf16[32,512]{1,0:T(8,128)(2,1)S(1)}, bf16[32,512]{1,0:T(8,128)(2,1)S(1)}, u32[]{:S(2)}, u32[]{:S(2)}) collective-permute-start(bf16[32,512]{1,0:T(8,128)(2,1)S(1)} %get-tuple-element.22), channel_id=1, source_target_pairs={{0,4},{1,5},{2,6},{3,7},{4,0},{5,1},{6,2},{7,3},{8,12},{9,13},{10,... | collective-permute-start | bytes 98312 | tf_op jit(solution)/shard_map/ppermute | solution.py:496
  24.4 2.6 %collective-permute-start.1 = (bf16[32,512]{1,0:T(8,128)(2,1)S(1)}, bf16[32,512]{1,0:T(8,128)(2,1)S(1)}, u32[]{:S(2)}, u32[]{:S(2)}) collective-permute-start(bf16[32,512]{1,0:T(8,128)(2,1)S(1)} %get-tuple-element.22), channel_id=1, source_target_pairs={{0,8},{1,9},{2,10},{3,11},{4,12},{5,13},{6,14},{7,15},{8,0},{9,1},... | collective-permute-start | bytes 98312 | tf_op jit(solution)/shard_map/ppermute | solution.py:496
  27.0 2.8 %collective-permute-done.1 = bf16[32,512]{1,0:T(8,128)(2,1)S(1)} collective-permute-done((bf16[32,512]{1,0:T(8,128)(2,1)S(1)}, bf16[32,512]{1,0:T(8,128)(2,1)S(1)}, u32[]{:S(2)}, u32[]{:S(2)}) %collective-permute-start.1) | collective-permute-done | bytes 32800 | tf_op jit(solution)/shard_map/ppermute | solution.py:496
  29.8 2.9 %collective-permute-done.2 = bf16[32,512]{1,0:T(8,128)(2,1)S(1)} collective-permute-done((bf16[32,512]{1,0:T(8,128)(2,1)S(1)}, bf16[32,512]{1,0:T(8,128)(2,1)S(1)}, u32[]{:S(2)}, u32[]{:S(2)}) %collective-permute-start.2) | collective-permute-done | bytes 32800 | tf_op jit(solution)/shard_map/ppermute | solution.py:496
  32.7 1.5 %collective-permute-start.3 = (bf16[128,512]{1,0:T(8,128)(2,1)S(1)}, bf16[128,512]{1,0:T(8,128)(2,1)S(1)}, u32[]{:S(2)}, u32[]{:S(2)}) collective-permute-start(bf16[128,512]{1,0:T(8,128)(2,1)S(1)} %get-tuple-element.50), channel_id=1, source_target_pairs={{0,1},{1,0},{2,3},{3,2},{4,5},{5,4},{6,7},{7,6},{8,9},{9,8},{10,11... | collective-permute-start | bytes 393224 | tf_op jit(solution)/shard_map/ppermute | solution.py:496
  34.2 1.5 %collective-permute-start.4 = (bf16[128,512]{1,0:T(8,128)(2,1)S(1)}, bf16[128,512]{1,0:T(8,128)(2,1)S(1)}, u32[]{:S(2)}, u32[]{:S(2)}) collective-permute-start(bf16[128,512]{1,0:T(8,128)(2,1)S(1)} %get-tuple-element.50), channel_id=1, source_target_pairs={{0,2},{1,3},{2,0},{3,1},{4,6},{5,7},{6,4},{7,5},{8,10},{9,11},{10,... | collective-permute-start | bytes 393224 | tf_op jit(solution)/shard_map/ppermute | solution.py:496
  36.3 2.5 %collective-permute-done.3 = bf16[128,512]{1,0:T(8,128)(2,1)S(1)} collective-permute-done((bf16[128,512]{1,0:T(8,128)(2,1)S(1)}, bf16[128,512]{1,0:T(8,128)(2,1)S(1)}, u32[]{:S(2)}, u32[]{:S(2)}) %collective-permute-start.3) | collective-permute-done | bytes 131104 | tf_op jit(solution)/shard_map/ppermute | solution.py:496
  38.8 1.2 %collective-permute-done.4 = bf16[128,512]{1,0:T(8,128)(2,1)S(1)} collective-permute-done((bf16[128,512]{1,0:T(8,128)(2,1)S(1)}, bf16[128,512]{1,0:T(8,128)(2,1)S(1)}, u32[]{:S(2)}, u32[]{:S(2)}) %collective-permute-start.4) | collective-permute-done | bytes 131104 | tf_op jit(solution)/shard_map/ppermute | solution.py:496
  40.1 1.6 %collective-permute-done.5 = bf16[128,512]{1,0:T(8,128)(2,1)S(1)} collective-permute-done((bf16[128,512]{1,0:T(8,128)(2,1)S(1)}, bf16[128,512]{1,0:T(8,128)(2,1)S(1)}, u32[]{:S(2)}, u32[]{:S(2)}) %collective-permute-start.5) | collective-permute-done | bytes 131104 | tf_op jit(solution)/shard_map/ppermute | solution.py:496
  44.7 3.5 %collective-permute-start.13 = (bf16[64,512]{1,0:T(8,128)(2,1)S(1)}, bf16[64,512]{1,0:T(8,128)(2,1)S(1)}, u32[]{:S(2)}, u32[]{:S(2)}) collective-permute-start(bf16[64,512]{1,0:T(8,128)(2,1)S(1)} %maximum_select_fusion), channel_id=1, source_target_pairs={{0,12},{1,13},{2,14},{3,15},{4,8},{5,9},{6,10},{7,11},{8,4},{9,5},... | collective-permute-start | bytes 196616 | tf_op jit(solution)/shard_map/ppermute | solution.py:496
  48.2 3.4 %copy-done.1 = bf16[4,2048,512]{2,1,0:T(8,128)(2,1)S(1)} copy-done((bf16[4,2048,512]{2,1,0:T(8,128)(2,1)S(1)}, bf16[4,2048,512]{2,1,0:T(8,128)(2,1)}, u32[]{:S(2)}) %copy-start.1) | copy-done | bytes 8388632
  51.6 6.3 %attend.1 = (bf16[768,512]{1,0:T(8,128)(2,1)S(1)}, f32[768,512]{1,0:T(8,128)S(1)}, bf16[768,2048]{1,0:T(8,128)(2,1)S(1)}) custom-call(f32[4]{0:T(128)S(1)} %rsqrt.3.inv_ref, s32[768,1]{1,0:T(8,128)S(1)} %reshape.64.slots_ref, bf16[512,512]{1,0:T(8,128)(2,1)S(1)} %constant_dynamic-update-slice_fusion.4.near_ref, ...), custom_call_target="tpu_custom_call" | custom-call | flops 3221225472 | bytes 16777216 | tf_op jit(solution)/shard_map/attend/pallas_call | solution.py:304
  59.1 2.4 %collective-permute-start.16 = (bf16[256,512]{1,0:T(8,128)(2,1)S(1)}, bf16[256,512]{1,0:T(8,128)(2,1)S(1)}, u32[]{:S(2)}, u32[]{:S(2)}) collective-permute-start(bf16[256,512]{1,0:T(8,128)(2,1)S(1)} %constant_dynamic-update-slice_fusion.11), channel_id=1, source_target_pairs={{0,3},{1,2},{2,1},{3,0},{4,7},{5,6},{6,5},{7,4},{8,11},{9,10},{10,... | collective-permute-start | bytes 786440 | tf_op jit(solution)/shard_map/ppermute | solution.py:496
  61.6 7.5 %score.1 = (f32[768,1]{1,0:T(8,128)S(1)}, bf16[768,512]{1,0:T(8,128)(2,1)S(1)}, f32[768,512]{1,0:T(8,128)S(1)}) custom-call(f32[4]{0:T(128)S(1)} %rsqrt.3.inv_ref, bf16[768,512]{1,0:T(8,128)(2,1)S(1)} %get-tuple-element.24.queries_ref, f32[768,512]{1,0:T(8,128)S(1)} %get-tuple-element.25.attended_ref, s32[768,1]{1,0:T(8,128)S(1)} %reshape.65.labels_ref, ...), custom_call_target="tpu_custom_call" | custom-call | flops 4831838208 | bytes 8388608 | tf_op jit(solution)/shard_map/score/pallas_call | solution.py:368
  69.1 2.3 %attend_back.2.refs_0_ = bf16[384,512]{1,0:T(8,128)(2,1)S(1)} custom-call(bf16[768,512]{1,0:T(8,128)(2,1)S(1)} %get-tuple-element.27.grad_att_ref, f32[768,512]{1,0:T(8,128)S(1)} %get-tuple-element.28.direct_ref, bf16[768,2048]{1,0:T(8,128)(2,1)S(1)} %get-tuple-element.29.slope_ref, bf16[4,2048,512]{2,1,0:T(8,128)(2,1)S(1)} %bitcast.4), custom_call_target="tpu_custom_call" | custom-call | flops 1610612736 | bytes 8388608 | tf_op jit(solution)/shard_map/attend_back/pallas_call | solution.py:415
  71.4 2.3 %attend_back.3.refs_1_ = bf16[384,512]{1,0:T(8,128)(2,1)S(1)} custom-call(bf16[768,512]{1,0:T(8,128)(2,1)S(1)} %get-tuple-element.27.grad_att_ref, f32[768,512]{1,0:T(8,128)S(1)} %get-tuple-element.28.direct_ref, bf16[768,2048]{1,0:T(8,128)(2,1)S(1)} %get-tuple-element.29.slope_ref, bf16[4,2048,512]{2,1,0:T(8,128)(2,1)S(1)} %bitcast.4), custom_call_target="tpu_custom_call" | custom-call | flops 1610612736 | bytes 8388608 | tf_op jit(solution)/shard_map/attend_back/pallas_call | solution.py:415
  76.1 2.5 %chip_terms.1 = bf16[512,512]{1,0:T(8,128)(2,1)S(1)} custom-call(s32[1]{0:T(128)} %bitcast.2.wide_ref, s32[1,1536]{1,0:T(1,128)S(1)} %reshape.63.slots_ref, bf16[384,512]{1,0:T(8,128)(2,1)S(1)} %attend_back.2.refs_0_, bf16[384,512]{1,0:T(8,128)(2,1)S(1)} %attend_back.3.refs_1_, bf16[384,512]{1,0:T(8,128)(2,1)S(1)} %collective-permute-done.8.refs_2_, ...), custom_call_target="tpu_custom_call" | custom-call | flops 2147483648 | bytes 4194304 | tf_op jit(solution)/shard_map/chip_terms/pallas_call | solution.py:466
  79.3 1.5 %collective-permute-start.18 = (bf16[128,512]{1,0:T(8,128)(2,1)S(1)}, bf16[128,512]{1,0:T(8,128)(2,1)S(1)}, u32[]{:S(2)}, u32[]{:S(2)}) collective-permute-start(bf16[128,512]{1,0:T(8,128)(2,1)S(1)} %get-tuple-element.46), channel_id=1, source_target_pairs={{0,2},{1,3},{2,0},{3,1},{4,6},{5,7},{6,4},{7,5},{8,10},{9,11},{10,... | collective-permute-start | bytes 393224 | tf_op jit(solution)/shard_map/ppermute | solution.py:496
  80.7 1.5 %collective-permute-start.17 = (bf16[128,512]{1,0:T(8,128)(2,1)S(1)}, bf16[128,512]{1,0:T(8,128)(2,1)S(1)}, u32[]{:S(2)}, u32[]{:S(2)}) collective-permute-start(bf16[128,512]{1,0:T(8,128)(2,1)S(1)} %get-tuple-element.44), channel_id=1, source_target_pairs={{0,1},{1,0},{2,3},{3,2},{4,5},{5,4},{6,7},{7,6},{8,9},{9,8},{10,11... | collective-permute-start | bytes 393224 | tf_op jit(solution)/shard_map/ppermute | solution.py:496
  82.2 3.8 %collective-permute-done.19 = bf16[128,512]{1,0:T(8,128)(2,1)S(1)} collective-permute-done((bf16[128,512]{1,0:T(8,128)(2,1)S(1)}, bf16[128,512]{1,0:T(8,128)(2,1)S(1)}, u32[]{:S(2)}, u32[]{:S(2)}) %collective-permute-start.19) | collective-permute-done | bytes 131104 | tf_op jit(solution)/shard_map/ppermute | solution.py:496
  86.0 1.3 %collective-permute-done.18 = bf16[128,512]{1,0:T(8,128)(2,1)S(1)} collective-permute-done((bf16[128,512]{1,0:T(8,128)(2,1)S(1)}, bf16[128,512]{1,0:T(8,128)(2,1)S(1)}, u32[]{:S(2)}, u32[]{:S(2)}) %collective-permute-start.18) | collective-permute-done | bytes 131104 | tf_op jit(solution)/shard_map/ppermute | solution.py:496
  88.2 3.8 %collective-permute-start.20 = (bf16[32,512]{1,0:T(8,128)(2,1)S(1)}, bf16[32,512]{1,0:T(8,128)(2,1)S(1)}, u32[]{:S(2)}, u32[]{:S(2)}) collective-permute-start(bf16[32,512]{1,0:T(8,128)(2,1)S(1)} %get-tuple-element.47), channel_id=1, source_target_pairs={{0,4},{1,5},{2,6},{3,7},{4,0},{5,1},{6,2},{7,3},{8,12},{9,13},{10,... | collective-permute-start | bytes 98312 | tf_op jit(solution)/shard_map/ppermute | solution.py:496
  (80 shorter events, 11.0 us)
Async XLA Ops:
  0.7 42.2 %copy-start.4 = (s32[768]{0:T(1024)S(1)}, s32[768]{0:T(1024)}, u32[]{:S(2)}) copy-start(s32[768]{0:T(1024)} %param.23) | copy-start | bytes 9220
  21.4 5.6 %collective-permute-start = (bf16[32,512]{1,0:T(8,128)(2,1)S(1)}, bf16[32,512]{1,0:T(8,128)(2,1)S(1)}, u32[]{:S(2)}, u32[]{:S(2)}) collective-permute-start(bf16[32,512]{1,0:T(8,128)(2,1)S(1)} %get-tuple-element.22), channel_id=1, source_target_pairs={{0,4},{1,5},{2,6},{3,7},{4,0},{5,1},{6,2},{7,3},{8,12},{9,13},{10,... | collective-permute-start | bytes 98312 | tf_op jit(solution)/shard_map/ppermute | solution.py:496
  24.4 5.4 %collective-permute-start.1 = (bf16[32,512]{1,0:T(8,128)(2,1)S(1)}, bf16[32,512]{1,0:T(8,128)(2,1)S(1)}, u32[]{:S(2)}, u32[]{:S(2)}) collective-permute-start(bf16[32,512]{1,0:T(8,128)(2,1)S(1)} %get-tuple-element.22), channel_id=1, source_target_pairs={{0,8},{1,9},{2,10},{3,11},{4,12},{5,13},{6,14},{7,15},{8,0},{9,1},... | collective-permute-start | bytes 98312 | tf_op jit(solution)/shard_map/ppermute | solution.py:496
  27.0 5.7 %collective-permute-start.2 = (bf16[32,512]{1,0:T(8,128)(2,1)S(1)}, bf16[32,512]{1,0:T(8,128)(2,1)S(1)}, u32[]{:S(2)}, u32[]{:S(2)}) collective-permute-start(bf16[32,512]{1,0:T(8,128)(2,1)S(1)} %get-tuple-element.22), channel_id=1, source_target_pairs={{0,12},{1,13},{2,14},{3,15},{4,8},{5,9},{6,10},{7,11},{8,4},{9,5},... | collective-permute-start | bytes 98312 | tf_op jit(solution)/shard_map/ppermute | solution.py:496
  32.7 6.1 %collective-permute-start.3 = (bf16[128,512]{1,0:T(8,128)(2,1)S(1)}, bf16[128,512]{1,0:T(8,128)(2,1)S(1)}, u32[]{:S(2)}, u32[]{:S(2)}) collective-permute-start(bf16[128,512]{1,0:T(8,128)(2,1)S(1)} %get-tuple-element.50), channel_id=1, source_target_pairs={{0,1},{1,0},{2,3},{3,2},{4,5},{5,4},{6,7},{7,6},{8,9},{9,8},{10,11... | collective-permute-start | bytes 393224 | tf_op jit(solution)/shard_map/ppermute | solution.py:496
  34.2 5.8 %collective-permute-start.4 = (bf16[128,512]{1,0:T(8,128)(2,1)S(1)}, bf16[128,512]{1,0:T(8,128)(2,1)S(1)}, u32[]{:S(2)}, u32[]{:S(2)}) collective-permute-start(bf16[128,512]{1,0:T(8,128)(2,1)S(1)} %get-tuple-element.50), channel_id=1, source_target_pairs={{0,2},{1,3},{2,0},{3,1},{4,6},{5,7},{6,4},{7,5},{8,10},{9,11},{10,... | collective-permute-start | bytes 393224 | tf_op jit(solution)/shard_map/ppermute | solution.py:496
  35.8 5.9 %collective-permute-start.5 = (bf16[128,512]{1,0:T(8,128)(2,1)S(1)}, bf16[128,512]{1,0:T(8,128)(2,1)S(1)}, u32[]{:S(2)}, u32[]{:S(2)}) collective-permute-start(bf16[128,512]{1,0:T(8,128)(2,1)S(1)} %get-tuple-element.50), channel_id=1, source_target_pairs={{0,3},{1,2},{2,1},{3,0},{4,7},{5,6},{6,5},{7,4},{8,11},{9,10},{10,... | collective-permute-start | bytes 393224 | tf_op jit(solution)/shard_map/ppermute | solution.py:496
  41.7 6.5 %collective-permute-start.6 = (bf16[512,512]{1,0:T(8,128)(2,1)S(1)}, bf16[512,512]{1,0:T(8,128)(2,1)S(1)}, u32[]{:S(2)}, u32[]{:S(2)}) collective-permute-start(bf16[512,512]{1,0:T(8,128)(2,1)S(1)} %constant_dynamic-update-slice_fusion.4.near_ref), channel_id=1, source_target_pairs={{0,16},{16,0},{1,17},{17,1},{2,18},{18,2},{3,19},{19,3},{4,20},{20... | collective-permute-start | bytes 1572872 | tf_op jit(solution)/shard_map/ppermute | solution.py:496
  41.8 32.0 %collective-permute-start.7 = (s32[768]{0:T(1024)S(1)}, s32[768]{0:T(1024)S(1)}, u32[]{:S(2)}, u32[]{:S(2)}) collective-permute-start(s32[768]{0:T(1024)S(1)} %get-tuple-element.58), channel_id=1, source_target_pairs={{0,16},{16,0},{1,17},{17,1},{2,18},{18,2},{3,19},{19,3},{4,20},{20... | collective-permute-start | bytes 9224 | tf_op jit(solution)/shard_map/ppermute | solution.py:496
  42.4 1.4 %collective-permute-start.10 = (bf16[32,512]{1,0:T(8,128)(2,1)S(1)}, bf16[32,512]{1,0:T(8,128)(2,1)S(1)}, u32[]{:S(2)}, u32[]{:S(2)}) collective-permute-start(bf16[32,512]{1,0:T(8,128)(2,1)S(1)} %get-tuple-element.33), channel_id=1, source_target_pairs={{0,16},{16,0},{1,17},{17,1},{2,18},{18,2},{3,19},{19,3},{4,20},{20... | collective-permute-start | bytes 98312 | tf_op jit(solution)/shard_map/ppermute | solution.py:496
  43.7 14.2 %collective-permute-start.11 = (bf16[64,512]{1,0:T(8,128)(2,1)S(1)}, bf16[64,512]{1,0:T(8,128)(2,1)S(1)}, u32[]{:S(2)}, u32[]{:S(2)}) collective-permute-start(bf16[64,512]{1,0:T(8,128)(2,1)S(1)} %maximum_select_fusion), channel_id=1, source_target_pairs={{0,4},{1,5},{2,6},{3,7},{4,0},{5,1},{6,2},{7,3},{8,12},{9,13},{10,... | collective-permute-start | bytes 196616 | tf_op jit(solution)/shard_map/ppermute | solution.py:496
  43.8 14.1 %collective-permute-start.12 = (bf16[64,512]{1,0:T(8,128)(2,1)S(1)}, bf16[64,512]{1,0:T(8,128)(2,1)S(1)}, u32[]{:S(2)}, u32[]{:S(2)}) collective-permute-start(bf16[64,512]{1,0:T(8,128)(2,1)S(1)} %maximum_select_fusion), channel_id=1, source_target_pairs={{0,8},{1,9},{2,10},{3,11},{4,12},{5,13},{6,14},{7,15},{8,0},{9,1},... | collective-permute-start | bytes 196616 | tf_op jit(solution)/shard_map/ppermute | solution.py:496
  44.7 13.2 %collective-permute-start.13 = (bf16[64,512]{1,0:T(8,128)(2,1)S(1)}, bf16[64,512]{1,0:T(8,128)(2,1)S(1)}, u32[]{:S(2)}, u32[]{:S(2)}) collective-permute-start(bf16[64,512]{1,0:T(8,128)(2,1)S(1)} %maximum_select_fusion), channel_id=1, source_target_pairs={{0,12},{1,13},{2,14},{3,15},{4,8},{5,9},{6,10},{7,11},{8,4},{9,5},... | collective-permute-start | bytes 196616 | tf_op jit(solution)/shard_map/ppermute | solution.py:496
  58.0 16.4 %collective-permute-start.14 = (bf16[256,512]{1,0:T(8,128)(2,1)S(1)}, bf16[256,512]{1,0:T(8,128)(2,1)S(1)}, u32[]{:S(2)}, u32[]{:S(2)}) collective-permute-start(bf16[256,512]{1,0:T(8,128)(2,1)S(1)} %constant_dynamic-update-slice_fusion.11), channel_id=1, source_target_pairs={{0,1},{1,0},{2,3},{3,2},{4,5},{5,4},{6,7},{7,6},{8,9},{9,8},{10,11... | collective-permute-start | bytes 786440 | tf_op jit(solution)/shard_map/ppermute | solution.py:496
  58.6 15.8 %collective-permute-start.15 = (bf16[256,512]{1,0:T(8,128)(2,1)S(1)}, bf16[256,512]{1,0:T(8,128)(2,1)S(1)}, u32[]{:S(2)}, u32[]{:S(2)}) collective-permute-start(bf16[256,512]{1,0:T(8,128)(2,1)S(1)} %constant_dynamic-update-slice_fusion.11), channel_id=1, source_target_pairs={{0,2},{1,3},{2,0},{3,1},{4,6},{5,7},{6,4},{7,5},{8,10},{9,11},{10,... | collective-permute-start | bytes 786440 | tf_op jit(solution)/shard_map/ppermute | solution.py:496
  59.1 15.3 %collective-permute-start.16 = (bf16[256,512]{1,0:T(8,128)(2,1)S(1)}, bf16[256,512]{1,0:T(8,128)(2,1)S(1)}, u32[]{:S(2)}, u32[]{:S(2)}) collective-permute-start(bf16[256,512]{1,0:T(8,128)(2,1)S(1)} %constant_dynamic-update-slice_fusion.11), channel_id=1, source_target_pairs={{0,3},{1,2},{2,1},{3,0},{4,7},{5,6},{6,5},{7,4},{8,11},{9,10},{10,... | collective-permute-start | bytes 786440 | tf_op jit(solution)/shard_map/ppermute | solution.py:496
  73.8 1.8 %collective-permute-start.8 = (bf16[384,512]{1,0:T(8,128)(2,1)S(1)}, bf16[384,512]{1,0:T(8,128)(2,1)S(1)}, u32[]{:S(2)}, u32[]{:S(2)}) collective-permute-start(bf16[384,512]{1,0:T(8,128)(2,1)S(1)} %attend_back.2.refs_0_), channel_id=1, source_target_pairs={{0,16},{16,0},{1,17},{17,1},{2,18},{18,2},{3,19},{19,3},{4,20},{20... | collective-permute-start | bytes 1179656 | tf_op jit(solution)/shard_map/ppermute | solution.py:496
  73.8 2.3 %collective-permute-start.9 = (bf16[384,512]{1,0:T(8,128)(2,1)S(1)}, bf16[384,512]{1,0:T(8,128)(2,1)S(1)}, u32[]{:S(2)}, u32[]{:S(2)}) collective-permute-start(bf16[384,512]{1,0:T(8,128)(2,1)S(1)} %attend_back.3.refs_1_), channel_id=1, source_target_pairs={{0,16},{16,0},{1,17},{17,1},{2,18},{18,2},{3,19},{19,3},{4,20},{20... | collective-permute-start | bytes 1179656 | tf_op jit(solution)/shard_map/ppermute | solution.py:496
  78.7 7.4 %collective-permute-start.19 = (bf16[128,512]{1,0:T(8,128)(2,1)S(1)}, bf16[128,512]{1,0:T(8,128)(2,1)S(1)}, u32[]{:S(2)}, u32[]{:S(2)}) collective-permute-start(bf16[128,512]{1,0:T(8,128)(2,1)S(1)} %get-tuple-element.45), channel_id=1, source_target_pairs={{0,3},{1,2},{2,1},{3,0},{4,7},{5,6},{6,5},{7,4},{8,11},{9,10},{10,... | collective-permute-start | bytes 393224 | tf_op jit(solution)/shard_map/ppermute | solution.py:496
  79.3 8.1 %collective-permute-start.18 = (bf16[128,512]{1,0:T(8,128)(2,1)S(1)}, bf16[128,512]{1,0:T(8,128)(2,1)S(1)}, u32[]{:S(2)}, u32[]{:S(2)}) collective-permute-start(bf16[128,512]{1,0:T(8,128)(2,1)S(1)} %get-tuple-element.46), channel_id=1, source_target_pairs={{0,2},{1,3},{2,0},{3,1},{4,6},{5,7},{6,4},{7,5},{8,10},{9,11},{10,... | collective-permute-start | bytes 393224 | tf_op jit(solution)/shard_map/ppermute | solution.py:496
  80.7 6.7 %collective-permute-start.17 = (bf16[128,512]{1,0:T(8,128)(2,1)S(1)}, bf16[128,512]{1,0:T(8,128)(2,1)S(1)}, u32[]{:S(2)}, u32[]{:S(2)}) collective-permute-start(bf16[128,512]{1,0:T(8,128)(2,1)S(1)} %get-tuple-element.44), channel_id=1, source_target_pairs={{0,1},{1,0},{2,3},{3,2},{4,5},{5,4},{6,7},{7,6},{8,9},{9,8},{10,11... | collective-permute-start | bytes 393224 | tf_op jit(solution)/shard_map/ppermute | solution.py:496
  87.5 5.8 %collective-permute-start.22 = (bf16[32,512]{1,0:T(8,128)(2,1)S(1)}, bf16[32,512]{1,0:T(8,128)(2,1)S(1)}, u32[]{:S(2)}, u32[]{:S(2)}) collective-permute-start(bf16[32,512]{1,0:T(8,128)(2,1)S(1)} %get-tuple-element.48), channel_id=1, source_target_pairs={{0,12},{1,13},{2,14},{3,15},{4,8},{5,9},{6,10},{7,11},{8,4},{9,5},... | collective-permute-start | bytes 98312 | tf_op jit(solution)/shard_map/ppermute | solution.py:496
  88.1 5.2 %collective-permute-start.21 = (bf16[32,512]{1,0:T(8,128)(2,1)S(1)}, bf16[32,512]{1,0:T(8,128)(2,1)S(1)}, u32[]{:S(2)}, u32[]{:S(2)}) collective-permute-start(bf16[32,512]{1,0:T(8,128)(2,1)S(1)} %get-tuple-element.49), channel_id=1, source_target_pairs={{0,8},{1,9},{2,10},{3,11},{4,12},{5,13},{6,14},{7,15},{8,0},{9,1},... | collective-permute-start | bytes 98312 | tf_op jit(solution)/shard_map/ppermute | solution.py:496
  88.2 5.6 %collective-permute-start.20 = (bf16[32,512]{1,0:T(8,128)(2,1)S(1)}, bf16[32,512]{1,0:T(8,128)(2,1)S(1)}, u32[]{:S(2)}, u32[]{:S(2)}) collective-permute-start(bf16[32,512]{1,0:T(8,128)(2,1)S(1)} %get-tuple-element.47), channel_id=1, source_target_pairs={{0,4},{1,5},{2,6},{3,7},{4,0},{5,1},{6,2},{7,3},{8,12},{9,13},{10,... | collective-permute-start | bytes 98312 | tf_op jit(solution)/shard_map/ppermute | solution.py:496
  (10 other events, 213.1 us)
where the time goes:
time: 94.7 us; the launch traced here: 94.5 us
  Pallas kernels  38.4 us (41%)
  starting transfers between devices  26.4 us (28%)
  waiting for transfers between devices  19.6 us (21%)
  local copies, waits for them, and re-layouts  7.16 us (8%)
  other arithmetic  1.83 us (2%)
  between operations  1.02 us (1%)
    ppermute x23, starting transfers between devices, exchange(): lax.ppermute(values, axis_name, [(i, i ^ distance) for i in range(size)])  26.4 us
    ppermute x23, waiting for transfers between devices, exchange(): lax.ppermute(values, axis_name, [(i, i ^ distance) for i in range(size)])  19.6 us
    pallas_call x1, Pallas kernels, encode_block(): pl.pallas_call(functools.partial(encode_kernel, tokens), grid=(cand_count...  17.4 us
    pallas_call x1, Pallas kernels, score(): pl.pallas_call(score_kernel, grid=(steps,), in_specs=[pl.BlockSpec(memory...  7.49 us
    unnamed x30, local copies, waits for them, and re-layouts  6.74 us
    pallas_call x1, Pallas kernels, attend(): pl.pallas_call(attend_kernel, in_specs=[pl.BlockSpec(memory_space=pltpu.S...  6.31 us
    pallas_call x2, Pallas kernels, attend_back(): pl.pallas_call(functools.partial(attend_back_kernel, first), in_specs=[wh...  4.65 us
    pallas_call x1, Pallas kernels, chip_terms(): pl.pallas_call(functools.partial(terms_kernel, origins), in_specs=[pl.Blo...  2.53 us
  transfers between devices with their start and end apart: 23, of which 13 were waited for; matrix products, arithmetic and copies ran while one was open for 2% of the time, Pallas kernels for 20%

commit v1 on v0

v1 whole, which is shorter than its diff:
```python
import functools
import math

import jax
import jax.numpy as jnp
from jax import lax
from jax.experimental import pallas as pl
from jax.experimental.pallas import tpu as pltpu
from jax.sharding import PartitionSpec as P

HEADS = 16
FRAMES = 3


EPSILON = 1e-06
MIB = 1024 * 1024


def layer_norm(values):
    center = values - jnp.mean(values, axis=-1, keepdims=True)
    spread = jnp.mean(jnp.square(center), axis=-1, keepdims=True)
    return center * lax.rsqrt(spread + EPSILON)


def dot(left, right):
    return jnp.dot(left, right, preferred_element_type=jnp.float32)


def dot_rows(left, right):
    return lax.dot_general(left, right, (((1,), (1,)), ((), ())), preferred_element_type=jnp.float32)


def dot_columns(left, right):
    return lax.dot_general(left, right, (((0,), (0,)), ((), ())), preferred_element_type=jnp.float32)


def split_rows(values):
    high = values.astype(jnp.bfloat16)
    low = (values - high.astype(jnp.float32)).astype(jnp.bfloat16)
    return jnp.concatenate([high, low], axis=0)


def dot_split(values, right):
    both = dot(split_rows(values), right)
    rows = values.shape[0]
    return both[:rows] + both[rows:]


def encode_kernel(
    tokens,
    core_ref,
    frames_hbm,
    qkv_hbm,
    out_hbm,
    proj_hbm,
    keep_ref,
    send_ref,
    embedded_ref,
    frames_ref,
    qkv_ref,
    out_ref,
    proj_ref,
    sems,
    normed_ref,
    packed_ref,
    scores_ref,
    mixed_rows_ref,
    sums_ref,
):
    total = embedded_ref.shape[0]
    rows, width = packed_ref.shape[0], packed_ref.shape[1] // 2
    cands = rows // tokens
    groups = total // cands
    head_dim = width // HEADS
    patches = tokens // FRAMES
    lanes = 2 * head_dim
    blocks = rows // lanes
    pairs = HEADS // 2
    quad = 4
    span = quad * head_dim

    def group_rows(group):
        return pl.ds(group * rows, rows)

    def columns(part):
        return pl.ds(part * width, width)

    pieces = [(frames_hbm.at[group_rows(0)], frames_ref.at[group_rows(0)])]
    pieces += [(qkv_hbm.at[:, columns(part)], qkv_ref.at[:, columns(part)]) for part in range(2)]
    pieces += [
        (frames_hbm.at[group_rows(group)], frames_ref.at[group_rows(group)])
        for group in range(1, groups)
    ]
    pieces += [(qkv_hbm.at[:, columns(2)], qkv_ref.at[:, columns(2)])]
    pieces += [(out_hbm, out_ref), (proj_hbm, proj_ref)]
    copies = [
        pltpu.make_async_copy(source, target, sems.at[place])
        for place, (source, target) in enumerate(pieces)
    ]
    for copy in copies:
        copy.start()

    def norm_cand(cand):
        at = slice(cand * tokens, (cand + 1) * tokens)
        inputs = frames_ref[at, :].astype(jnp.float32)
        normed_ref[at, :] = layer_norm(inputs).astype(jnp.bfloat16)
        sums_ref[cand] = jnp.sum(inputs, axis=0, keepdims=True)

    exponent = math.log2(math.e) / math.sqrt(head_dim)
    frame_at = (lax.broadcasted_iota(jnp.int32, (patches, quad * lanes), 1) % lanes) // patches
    nothing = jnp.zeros((head_dim, lanes), jnp.bfloat16)
    ones_row = lax.broadcasted_iota(jnp.int32, (2 * lanes, 2 * lanes), 0) // patches
    ones_column = lax.broadcasted_iota(jnp.int32, (2 * lanes, 2 * lanes), 1) // patches
    frame_ones = (ones_row == ones_column).astype(jnp.bfloat16)
    own = lax.broadcasted_iota(jnp.int32, (cands, rows), 1) // tokens == lax.broadcasted_iota(
        jnp.int32, (cands, rows), 0
    )

    def own_scores(block, head):
        block_rows = slice(block * lanes, (block + 1) * lanes)
        start = head * head_dim
        query = packed_ref[block_rows, start : start + span]
        keys = packed_ref[block_rows, width + start : width + start + span].T
        keys = jnp.concatenate(
            [
                jnp.concatenate(
                    [nothing] * place
                    + [keys[place * head_dim : (place + 1) * head_dim]]
                    + [nothing] * (quad - 1 - place),
                    axis=1,
                )
                for place in range(quad)
            ],
            axis=0,
        )
        scores = dot(query, keys)
        found = scores[:patches]
        for frame in range(1, lanes // patches):
            found = jnp.where(
                frame_at == frame, scores[frame * patches : (frame + 1) * patches], found
            )
        for side in range(quad // 2):
            scores_ref[block, head // 2 + side] = found[
                :, side * 2 * lanes : (side + 1) * 2 * lanes
            ]

    copies[0].wait()
    for cand in range(cands):
        norm_cand(cand)
    copies[1].wait()
    copies[2].wait()
    for group in range(groups):
        at = slice(group * rows, (group + 1) * rows)
        for part in range(2):
            part_columns = slice(part * width, (part + 1) * width)
            packed_ref[:, part_columns] = dot(normed_ref[at, :], qkv_ref[:, part_columns]).astype(
                jnp.bfloat16
            )
        if group + 1 < groups:
            copies[3 + group].wait()
        for head in range(0, HEADS, quad):
            for block in range(blocks):
                own_scores(block, head)
            if group + 1 < groups:
                for cand in range(head * cands // HEADS, (head + quad) * cands // HEADS):
                    norm_cand((group + 1) * cands + cand)
        exp_scores = jnp.exp2(
            scores_ref[...].reshape(blocks * pairs * patches, 2 * lanes) * exponent
        )
        totals = dot(exp_scores.astype(jnp.bfloat16), frame_ones)
        probs = (exp_scores / totals).reshape(blocks * pairs, patches, 2 * lanes)
        sums = jnp.sum(probs, axis=1)
        key_sums = [
            jnp.concatenate(
                [
                    sums[block * pairs : (block + 1) * pairs, side * lanes : (side + 1) * lanes]
                    for block in range(blocks)
                ],
                axis=1,
            )
            for side in range(2)
        ]
        spread = jnp.concatenate(
            [
                jnp.where(own, key_sums[head % 2][head // 2 : head // 2 + 1], 0.0)
                for head in range(HEADS)
            ],
            axis=0,
        ).astype(jnp.bfloat16)
        mixed_rows = dot(spread, normed_ref[at, :])
        for head in range(HEADS):
            mixed_rows_ref[head, group * cands : (group + 1) * cands, :] = mixed_rows[
                head * cands : (head + 1) * cands
            ]

    for copy in copies[2 + groups :]:
        copy.wait()
    mixed = []
    for head in range(0, HEADS, quad):
        left = mixed_rows_ref[head : head + quad].reshape(quad * total, width)
        start = 2 * width + head * head_dim
        both = dot_split(left, qkv_ref[:, start : start + span])
        head_at = lax.broadcasted_iota(jnp.int32, (total, span), 1) // head_dim
        piece = jnp.zeros((total, span), jnp.float32)
        for place in range(quad):
            piece = jnp.where(head_at == place, both[place * total : (place + 1) * total], piece)
        mixed.append(piece)
    mixed_mean = jnp.concatenate(mixed, axis=1) * (1.0 / tokens)
    hidden = sums_ref[...].reshape(total, width) * (1.0 / tokens)
    hidden += dot_split(mixed_mean, out_ref[...])
    pooled = layer_norm(hidden).astype(jnp.bfloat16)
    first, second = pooled[:, : width // 2], pooled[:, width // 2 :]
    keep_ref[...] = jnp.where(core_ref[0] == 0, first, second)
    send_ref[...] = jnp.where(core_ref[0] == 0, second, first)
    embedded_ref[...] = dot(pooled, proj_ref[...]).astype(jnp.bfloat16)


def in_hbm(*arrays):
    return [pltpu.with_memory_space_constraint(array, pltpu.HBM) for array in arrays]


def encode_block(core, frames, qkv_weight, out_weight, proj_weight):
    cand_count, tokens, width = frames.shape
    key_width = proj_weight.shape[1]
    groups = 2
    rows = cand_count * tokens // groups
    lanes = 2 * width // HEADS
    patches = tokens // FRAMES
    flat = frames.reshape(cand_count * tokens, width)
    whole = pl.BlockSpec(memory_space=pltpu.VMEM)
    return pl.pallas_call(
        functools.partial(encode_kernel, tokens),
        in_specs=[pl.BlockSpec(memory_space=pltpu.SMEM)]
        + [pl.BlockSpec(memory_space=pltpu.HBM)] * 4,
        out_specs=[whole] * 3,
        out_shape=[
            jax.ShapeDtypeStruct((cand_count, width // 2), jnp.bfloat16),
            jax.ShapeDtypeStruct((cand_count, width // 2), jnp.bfloat16),
            jax.ShapeDtypeStruct((cand_count, key_width), jnp.bfloat16),
        ],
        scratch_shapes=[
            pltpu.VMEM(flat.shape, jnp.bfloat16),
            pltpu.VMEM(qkv_weight.shape, jnp.bfloat16),
            pltpu.VMEM(out_weight.shape, jnp.bfloat16),
            pltpu.VMEM(proj_weight.shape, jnp.bfloat16),
            pltpu.SemaphoreType.DMA((groups + 5,)),
            pltpu.VMEM(flat.shape, jnp.bfloat16),
            pltpu.VMEM((rows, 2 * width), jnp.bfloat16),
            pltpu.VMEM((rows // lanes, HEADS // 2, patches, 2 * lanes), jnp.float32),
            pltpu.VMEM((HEADS, cand_count, width), jnp.float32),
            pltpu.VMEM((cand_count, 1, width), jnp.float32),
        ],
        compiler_params=pltpu.CompilerParams(vmem_limit_bytes=44 * MIB),
        cost_estimate=pl.CostEstimate(
            flops=5 * cand_count * tokens * width * width, bytes_accessed=1 << 24, transcendentals=0
        ),
        name="encode",
    )(core, *in_hbm(flat, qkv_weight, out_weight, proj_weight))


def attend_kernel(
    inv_ref,
    slots_ref,
    near_ref,
    far_ref,
    usable_ref,
    history_hbm,
    queries_ref,
    attended_ref,
    slope_ref,
    history_ref,
    sems,
):
    users, events, _ = history_ref.shape
    chunk = math.gcd(events, 1024)
    copies = [
        [
            pltpu.make_async_copy(
                history_hbm.at[user, pl.ds(at, chunk)],
                history_ref.at[user, pl.ds(at, chunk)],
                sems.at[user, at // chunk],
            )
            for at in range(0, events, chunk)
        ]
        for user in range(users)
    ]
    for user_copies in copies:
        for copy in user_copies:
            copy.start()
    slots = slots_ref[...]
    half, key_width = near_ref.shape
    places = lax.broadcasted_iota(jnp.int32, (slots.shape[0], half), 1)
    queries = dot((slots == places).astype(jnp.bfloat16), near_ref[...])
    queries += dot((slots == places + half).astype(jnp.bfloat16), far_ref[...])
    queries_ref[...] = queries.astype(jnp.bfloat16)
    per_user = slots.shape[0] // users
    for user in range(users):
        rows = slice(user * per_user, (user + 1) * per_user)
        attended = jnp.zeros((per_user, key_width), jnp.float32)
        for at in range(0, events, chunk):
            copies[user][at // chunk].wait()
            keys = history_ref[user, at : at + chunk, :]
            usable = usable_ref[user, :, at : at + chunk]
            scores = dot_rows(queries_ref[rows, :], keys)
            half_gate = 0.5 * jnp.tanh(scores * (0.5 / math.sqrt(key_width)))
            weights = (0.5 + half_gate) * usable
            slope_ref[rows, at : at + chunk] = (weights * (0.5 - half_gate)).astype(jnp.bfloat16)
            attended += dot(weights.astype(jnp.bfloat16), keys)
        attended_ref[rows, :] = attended * inv_ref[user]


def attend(inv_count, slots, near, far, history, usable):
    users, events, key_width = history.shape
    requests = slots.shape[0]
    whole = pl.BlockSpec(memory_space=pltpu.VMEM)
    return pl.pallas_call(
        attend_kernel,
        in_specs=[pl.BlockSpec(memory_space=pltpu.SMEM)]
        + [whole] * 4
        + [pl.BlockSpec(memory_space=pltpu.HBM)],
        out_specs=[whole] * 3,
        out_shape=[
            jax.ShapeDtypeStruct((requests, key_width), jnp.bfloat16),
            jax.ShapeDtypeStruct((requests, key_width), jnp.float32),
            jax.ShapeDtypeStruct((requests, events), jnp.bfloat16),
        ],
        scratch_shapes=[
            pltpu.VMEM(history.shape, history.dtype),
            pltpu.SemaphoreType.DMA((users, events // math.gcd(events, 1024))),
        ],
        compiler_params=pltpu.CompilerParams(vmem_limit_bytes=32 * MIB),
        cost_estimate=pl.CostEstimate(
            flops=4 * requests * events * key_width, bytes_accessed=1 << 24, transcendentals=0
        ),
        name="attend",
    )(inv_count, slots, near, far, usable, *in_hbm(history))


def score_kernel(
    inv_ref,
    queries_ref,
    attended_ref,
    labels_ref,
    mlp_ref,
    logit_weight_ref,
    logits_ref,
    grad_att_ref,
    direct_ref,
):
    users = inv_ref.shape[0]
    per_user = queries_ref.shape[0] // users
    step_users = math.gcd(users, 2)
    step_rows = step_users * per_user
    weight = logit_weight_ref[...].astype(jnp.float32)
    for first in range(0, users, step_users):
        at = slice(first * per_user, first * per_user + step_rows)
        query_b = queries_ref[at, :]
        query_f = query_b.astype(jnp.float32)
        attended = attended_ref[at, :]
        key_width = query_f.shape[1]
        joined = jnp.concatenate(
            [query_b, attended.astype(jnp.bfloat16), (query_f * attended).astype(jnp.bfloat16)],
            axis=1,
        )
        pre_act = dot(joined, mlp_ref[...])
        act_sig = 0.5 * jnp.tanh(0.5 * pre_act) + 0.5
        hidden_units = (pre_act * act_sig).astype(jnp.bfloat16)
        logits = jnp.sum(hidden_units.astype(jnp.float32) * weight, axis=1, keepdims=True)
        logits_ref[at, :] = logits
        dlogit = (0.5 * jnp.tanh(0.5 * logits) + 0.5) - labels_ref[at, :].astype(jnp.float32)
        slope = act_sig * (1.0 + pre_act * (1.0 - act_sig))
        grad_pre = (dlogit * weight * slope).astype(jnp.bfloat16)
        djoined = dot_rows(grad_pre, mlp_ref[...])
        part_query = djoined[:, :key_width]
        part_att = djoined[:, key_width : 2 * key_width]
        part_prod = djoined[:, 2 * key_width :]
        grad_att = part_att + part_prod * query_f
        for user in range(step_users):
            grad_att_ref[pl.ds((first + user) * per_user, per_user), :] = (
                grad_att[user * per_user : (user + 1) * per_user] * inv_ref[first + user]
            ).astype(jnp.bfloat16)
        direct_ref[at, :] = part_query + part_prod * attended


def score(inv_count, queries, attended, labels, mlp_weight, logit_weight):
    requests, key_width = queries.shape
    whole = pl.BlockSpec(memory_space=pltpu.VMEM)
    return pl.pallas_call(
        score_kernel,
        in_specs=[pl.BlockSpec(memory_space=pltpu.SMEM)] + [whole] * 5,
        out_specs=[whole] * 3,
        out_shape=[
            jax.ShapeDtypeStruct((requests, 1), jnp.float32),
            jax.ShapeDtypeStruct((requests, key_width), jnp.bfloat16),
            jax.ShapeDtypeStruct((requests, key_width), jnp.float32),
        ],
        compiler_params=pltpu.CompilerParams(vmem_limit_bytes=32 * MIB),
        cost_estimate=pl.CostEstimate(
            flops=4 * requests * mlp_weight.shape[0] * mlp_weight.shape[1],
            bytes_accessed=1 << 23,
            transcendentals=0,
        ),
        name="score",
    )(inv_count, queries, attended, labels, mlp_weight, logit_weight)


def attend_back_kernel(first, grad_att_ref, direct_ref, slope_ref, history_ref, grad_rows_ref):
    users, events, key_width = history_ref.shape
    per_user = grad_att_ref.shape[0] // users
    chunk = math.gcd(events, 1024)
    for user in range(grad_rows_ref.shape[0] // per_user):
        rows = slice((first + user) * per_user, (first + user + 1) * per_user)
        back = jnp.zeros((per_user, key_width), jnp.float32)
        for at in range(0, events, chunk):
            keys = history_ref[first + user, at : at + chunk, :]
            slope = slope_ref[rows, at : at + chunk].astype(jnp.float32)
            grad_sig = (dot_rows(grad_att_ref[rows, :], keys) * slope).astype(jnp.bfloat16)
            back += dot(grad_sig, keys)
        grad_rows = direct_ref[rows, :] + back * (1.0 / math.sqrt(key_width))
        grad_rows_ref[user * per_user : (user + 1) * per_user, :] = grad_rows.astype(jnp.bfloat16)


def attend_back(first, count, grad_att, direct, slope, history):
    users, events, key_width = history.shape
    per_user = grad_att.shape[0] // users
    whole = pl.BlockSpec(memory_space=pltpu.VMEM)
    return pl.pallas_call(
        functools.partial(attend_back_kernel, first),
        in_specs=[whole] * 4,
        out_specs=whole,
        out_shape=jax.ShapeDtypeStruct((count * per_user, key_width), jnp.bfloat16),
        compiler_params=pltpu.CompilerParams(vmem_limit_bytes=20 * MIB),
        cost_estimate=pl.CostEstimate(
            flops=4 * count * per_user * events * key_width,
            bytes_accessed=1 << 23,
            transcendentals=0,
        ),
        name="attend_back",
    )(grad_att, direct, slope, history)


def terms_kernel(origins, wide_ref, slots_ref, *refs):
    grad_refs = refs[:-4]
    pooled_ref, out_ref, grad_rows_ref, terms_ref = refs[-4:]
    at = 0
    for grad_ref in grad_refs:
        grad_rows_ref[at : at + grad_ref.shape[0], :] = grad_ref[...]
        at += grad_ref.shape[0]
    cands = pooled_ref.shape[0]
    requests = slots_ref.shape[1]
    chunk = math.gcd(cands, 512)
    for at in range(0, cands, chunk):
        places = lax.broadcasted_iota(jnp.int32, (chunk, requests), 0) + at
        row_hot = (places == slots_ref[...]).astype(jnp.bfloat16)
        cand_grad = dot(row_hot, grad_rows_ref[...]).astype(jnp.bfloat16)
        term = dot_columns(pooled_ref[at : at + chunk, :], cand_grad)
        if at == 0:
            terms_ref[...] = term
        else:
            terms_ref[...] += term
    rows = terms_ref.shape[0] // len(origins)
    wide = wide_ref[0]
    batch = max(1, 32 // rows)
    for slot in range(0, len(origins), batch):
        found = [
            terms_ref[pl.ds(pl.multiple_of((wide ^ origins[slot + i]) * rows, rows), rows), :]
            for i in range(batch)
        ]
        found = found[0] if batch == 1 else jnp.concatenate(found, axis=0)
        out_ref[slot * rows : (slot + batch) * rows, :] = found.astype(jnp.bfloat16)


def chip_terms(origins, wide, slots, grad_parts, pooled):
    cands, width = pooled.shape
    requests = slots.shape[1]
    key_width = grad_parts[0].shape[1]
    whole = pl.BlockSpec(memory_space=pltpu.VMEM)
    return pl.pallas_call(
        functools.partial(terms_kernel, origins),
        in_specs=[pl.BlockSpec(memory_space=pltpu.SMEM)] + [whole] * (len(grad_parts) + 2),
        out_specs=whole,
        out_shape=jax.ShapeDtypeStruct((width, key_width), jnp.bfloat16),
        scratch_shapes=[
            pltpu.VMEM((requests, key_width), jnp.bfloat16),
            pltpu.VMEM((width, key_width), jnp.float32),
        ],
        compiler_params=pltpu.CompilerParams(vmem_limit_bytes=20 * MIB),
        cost_estimate=pl.CostEstimate(
            flops=2 * cands * key_width * (width + requests),
            bytes_accessed=1 << 22,
            transcendentals=0,
        ),
        name="chip_terms",
    )(wide, slots, *grad_parts, pooled)


def bit_groups(size):
    groups = []
    bit = 0
    while (1 << bit) < size:
        values = min(4, size >> bit)
        groups.append((bit, values))
        bit += values.bit_length() - 1
    return groups


def exchange(values, axis_name, size, distance):
    return lax.ppermute(values, axis_name, [(i, i ^ distance) for i in range(size)])


def send_stage(rows, wides, bit, values):
    return [exchange(rows, "wide", wides, step << bit) for step in range(1, values)]


def after(values, *others):
    return lax.optimization_barrier((tuple(values),) + others)[0]


def slot_of(distance, wides):
    slot = 0
    for bit, values in bit_groups(wides):
        slot = slot * values + ((distance >> bit) & (values - 1))
    return slot


def sum_blocks(blocks, wides, logits):
    total = blocks
    for bit, values in bit_groups(wides):
        if bit > 0:
            total, logits = lax.optimization_barrier((total, logits))
        parts = total.astype(jnp.bfloat16).reshape((values, -1) + blocks.shape[1:])
        found = [
            exchange(parts[step], "wide", wides, step << bit).astype(jnp.float32)
            for step in range(1, values)
        ]
        total = sum(found, parts[0].astype(jnp.float32))
    return total, logits


def body(
    frames,
    qkv_weight,
    out_weight,
    proj_weight,
    mlp_weight,
    logit_weight,
    history,
    hist_len,
    hist_mask,
    req_owner,
    req_local,
    labels,
):
    wides = lax.axis_size("wide")
    core, wide = lax.axis_index("section"), lax.axis_index("wide")
    cand_count = frames.shape[0]
    requests = req_local.shape[0]
    users, events, _ = history.shape
    keep, send, embedded = encode_block(
        core.reshape(1), frames, qkv_weight, out_weight, proj_weight
    )
    positions = jnp.arange(events, dtype=jnp.int32)[None, :]
    usable = (
        (positions < hist_len[:, None]) & ((hist_mask == 1) | (positions == 0))
    ).astype(jnp.float32)
    inv_count = lax.rsqrt(jnp.sum(usable, axis=1))
    usable = usable.reshape(users, 1, events)
    owner_core = req_owner[:, 0] // wides
    owner_slot = slot_of((req_owner[:, 0] % wides) ^ wide, wides)
    slots = ((owner_core ^ core) * wides + owner_slot) * cand_count + req_local
    pooled_slots = (owner_slot * 2 + owner_core) * cand_count + req_local
    stages = list(reversed(bit_groups(wides)))
    near = embedded
    for bit, values in stages:
        near = jnp.concatenate([near] + send_stage(near, wides, bit, values), axis=0)
        if bit == stages[0][0]:
            keep, send = after((keep, send), near)
    far = exchange(near, "section", 2, 1)
    far_slots = exchange(pooled_slots, "section", 2, 1)
    got = exchange(send, "section", 2, 1)
    pooled = jnp.where(
        core == 0, jnp.concatenate([keep, got], axis=0), jnp.concatenate([got, keep], axis=0)
    )
    found = send_stage(pooled, wides, *stages[0])
    queries, attended, slope = attend(
        inv_count, slots.reshape(requests, 1), near, far, history, usable
    )
    for stage in stages[1:]:
        pooled = jnp.concatenate(after([pooled] + found, attended), axis=0)
        found = send_stage(pooled, wides, *stage)
    logits, grad_att, direct = score(
        inv_count,
        queries,
        attended,
        labels.reshape(requests, 1),
        mlp_weight,
        logit_weight.reshape(1, -1),
    )
    half = users // 2
    grad_parts = [
        attend_back(0, half, grad_att, direct, slope, history),
        attend_back(half, users - half, grad_att, direct, slope, history),
    ]
    far_parts = [exchange(part, "section", 2, 1) for part in grad_parts]
    pooled = jnp.concatenate(after([pooled] + found, grad_parts[1]), axis=0)
    origins = [0] * wides
    for distance in range(wides):
        origins[slot_of(distance, wides)] = distance
    terms = chip_terms(
        origins,
        wide.reshape(1),
        jnp.concatenate([pooled_slots, far_slots]).reshape(1, 2 * requests),
        grad_parts + far_parts,
        pooled,
    )
    grad_proj, logits = sum_blocks(terms, wides, logits.reshape(requests))
    return (logits, grad_proj)


def solution(mesh):
    in_specs = (
        P(("section", "wide"), None, None),
        P(),
        P(),
        P(),
        P(),
        P(),
        P(("section", "wide"), None, None),
        P(("section", "wide")),
        P(("section", "wide"), None),
        P(("section", "wide"), None),
        P(("section", "wide")),
        P(("section", "wide")),
    )
    out_specs = (P(("section", "wide")), P(("section", "wide"), None))
    return jax.shard_map(body, mesh=mesh, in_specs=in_specs, out_specs=out_specs, check_vma=False)
```

time: 94.7 us -> 87.3 us (0.922)
  local copies, waits for them, and re-layouts: 7.16 us -> 0.52 us
    unnamed x30 -> x26, local copies, waits for them, and re-layouts: 6.74 us -> 0.1 us
    pallas_call x2, Pallas kernels: 24.9 us -> 22.1 us  [the longest x1 14.8 us: encode_block(): pl.pallas_call(functools.partial(encode_kernel, tokens), in_specs=[pl.Blo...]
    pallas_call x1, Pallas kernels: 6.31 us -> 8.15 us  [attend(): pl.pallas_call(attend_kernel, in_specs=[pl.BlockSpec(memory_space=pltpu.S...]
  transfers between devices with their start and end apart: 23 -> 23, of which waited for: 13 -> 13; matrix products, arithmetic and copies ran while one was open for 2% -> 2% of each run, Pallas kernels for 20% -> 23%
where the time goes in v1:
time: 87.3 us; the launch traced here: 87.2 us
  Pallas kernels  37.7 us (43%)
  starting transfers between devices  26.5 us (30%)
  waiting for transfers between devices  19.5 us (22%)
  other arithmetic  1.93 us (2%)
  between operations  1.02 us (1%)
    ppermute x23, starting transfers between devices, exchange(): lax.ppermute(values, axis_name, [(i, i ^ distance) for i in range(size)])  26.5 us
    ppermute x23, waiting for transfers between devices, exchange(): lax.ppermute(values, axis_name, [(i, i ^ distance) for i in range(size)])  19.5 us
    pallas_call x1, Pallas kernels, encode_block(): pl.pallas_call(functools.partial(encode_kernel, tokens), in_specs=[pl.Blo...  14.8 us
    pallas_call x1, Pallas kernels, attend(): pl.pallas_call(attend_kernel, in_specs=[pl.BlockSpec(memory_space=pltpu.S...  8.15 us
    pallas_call x1, Pallas kernels, score(): pl.pallas_call(score_kernel, in_specs=[pl.BlockSpec(memory_space=pltpu.SM...  7.27 us
    pallas_call x2, Pallas kernels, attend_back(): pl.pallas_call(functools.partial(attend_back_kernel, first), in_specs=[wh...  4.88 us
    pallas_call x1, Pallas kernels, chip_terms(): pl.pallas_call(functools.partial(terms_kernel, origins), in_specs=[pl.Blo...  2.53 us
  transfers between devices with their start and end apart: 23, of which 13 were waited for; matrix products, arithmetic and copies ran while one was open for 2% of the time, Pallas kernels for 23%

profile of v1, /device:TPU:0, one launch (start us, length us, event | category | flops | bytes accessed | tf_op | source)
XLA Modules:
  0.0 87.2 jit_solution(17520673263009468119)
XLA Ops:
  0.7 14.8 %encode.1 = (bf16[32,512]{1,0:T(8,128)(2,1)S(1)}, bf16[32,512]{1,0:T(8,128)(2,1)S(1)}, bf16[32,512]{1,0:T(8,128)(2,1)S(1)}) custom-call(s32[1]{0:T(128)} %bitcast.1.core_ref, bf16[1536,1024]{1,0:T(8,128)(2,1)} %bitcast.5, bf16[1024,3072]{1,0:T(8,128)(2,1)} %qkv_hbm.1, bf16[1024,1024]{1,0:T(8,128)(2,1)} %out_hbm.1, bf16[1024,512]{1,0:T(8,128)(2,1)} %proj_hbm.1), custom_call_target="tpu_custom_call" | custom-call | flops 8053063680 | bytes 16777216 | tf_op jit(solution)/shard_map/encode/pallas_call | solution.py:231
  15.5 3.1 %collective-permute-start.1 = (bf16[32,512]{1,0:T(8,128)(2,1)S(1)}, bf16[32,512]{1,0:T(8,128)(2,1)S(1)}, u32[]{:S(2)}, u32[]{:S(2)}) collective-permute-start(bf16[32,512]{1,0:T(8,128)(2,1)S(1)} %get-tuple-element.23), channel_id=1, source_target_pairs={{0,4},{1,5},{2,6},{3,7},{4,0},{5,1},{6,2},{7,3},{8,12},{9,13},{10,... | collective-permute-start | bytes 98312 | tf_op jit(solution)/shard_map/ppermute | solution.py:508
  18.6 2.6 %collective-permute-start.2 = (bf16[32,512]{1,0:T(8,128)(2,1)S(1)}, bf16[32,512]{1,0:T(8,128)(2,1)S(1)}, u32[]{:S(2)}, u32[]{:S(2)}) collective-permute-start(bf16[32,512]{1,0:T(8,128)(2,1)S(1)} %get-tuple-element.23), channel_id=1, source_target_pairs={{0,8},{1,9},{2,10},{3,11},{4,12},{5,13},{6,14},{7,15},{8,0},{9,1},... | collective-permute-start | bytes 98312 | tf_op jit(solution)/shard_map/ppermute | solution.py:508
  21.2 2.8 %collective-permute-done.2 = bf16[32,512]{1,0:T(8,128)(2,1)S(1)} collective-permute-done((bf16[32,512]{1,0:T(8,128)(2,1)S(1)}, bf16[32,512]{1,0:T(8,128)(2,1)S(1)}, u32[]{:S(2)}, u32[]{:S(2)}) %collective-permute-start.2) | collective-permute-done | bytes 32800 | tf_op jit(solution)/shard_map/ppermute | solution.py:508
  24.0 2.9 %collective-permute-done.3 = bf16[32,512]{1,0:T(8,128)(2,1)S(1)} collective-permute-done((bf16[32,512]{1,0:T(8,128)(2,1)S(1)}, bf16[32,512]{1,0:T(8,128)(2,1)S(1)}, u32[]{:S(2)}, u32[]{:S(2)}) %collective-permute-start.3) | collective-permute-done | bytes 32800 | tf_op jit(solution)/shard_map/ppermute | solution.py:508
  26.9 1.5 %collective-permute-start.4 = (bf16[128,512]{1,0:T(8,128)(2,1)S(1)}, bf16[128,512]{1,0:T(8,128)(2,1)S(1)}, u32[]{:S(2)}, u32[]{:S(2)}) collective-permute-start(bf16[128,512]{1,0:T(8,128)(2,1)S(1)} %get-tuple-element.52), channel_id=1, source_target_pairs={{0,1},{1,0},{2,3},{3,2},{4,5},{5,4},{6,7},{7,6},{8,9},{9,8},{10,11... | collective-permute-start | bytes 393224 | tf_op jit(solution)/shard_map/ppermute | solution.py:508
  28.4 1.5 %collective-permute-start.5 = (bf16[128,512]{1,0:T(8,128)(2,1)S(1)}, bf16[128,512]{1,0:T(8,128)(2,1)S(1)}, u32[]{:S(2)}, u32[]{:S(2)}) collective-permute-start(bf16[128,512]{1,0:T(8,128)(2,1)S(1)} %get-tuple-element.52), channel_id=1, source_target_pairs={{0,2},{1,3},{2,0},{3,1},{4,6},{5,7},{6,4},{7,5},{8,10},{9,11},{10,... | collective-permute-start | bytes 393224 | tf_op jit(solution)/shard_map/ppermute | solution.py:508
  30.5 2.5 %collective-permute-done.4 = bf16[128,512]{1,0:T(8,128)(2,1)S(1)} collective-permute-done((bf16[128,512]{1,0:T(8,128)(2,1)S(1)}, bf16[128,512]{1,0:T(8,128)(2,1)S(1)}, u32[]{:S(2)}, u32[]{:S(2)}) %collective-permute-start.4) | collective-permute-done | bytes 131104 | tf_op jit(solution)/shard_map/ppermute | solution.py:508
  33.1 1.2 %collective-permute-done.5 = bf16[128,512]{1,0:T(8,128)(2,1)S(1)} collective-permute-done((bf16[128,512]{1,0:T(8,128)(2,1)S(1)}, bf16[128,512]{1,0:T(8,128)(2,1)S(1)}, u32[]{:S(2)}, u32[]{:S(2)}) %collective-permute-start.5) | collective-permute-done | bytes 131104 | tf_op jit(solution)/shard_map/ppermute | solution.py:508
  34.3 1.6 %collective-permute-done.6 = bf16[128,512]{1,0:T(8,128)(2,1)S(1)} collective-permute-done((bf16[128,512]{1,0:T(8,128)(2,1)S(1)}, bf16[128,512]{1,0:T(8,128)(2,1)S(1)}, u32[]{:S(2)}, u32[]{:S(2)}) %collective-permute-start.6) | collective-permute-done | bytes 131104 | tf_op jit(solution)/shard_map/ppermute | solution.py:508
  38.9 3.5 %collective-permute-start.13 = (bf16[64,512]{1,0:T(8,128)(2,1)S(1)}, bf16[64,512]{1,0:T(8,128)(2,1)S(1)}, u32[]{:S(2)}, u32[]{:S(2)}) collective-permute-start(bf16[64,512]{1,0:T(8,128)(2,1)S(1)} %maximum_select_fusion), channel_id=1, source_target_pairs={{0,12},{1,13},{2,14},{3,15},{4,8},{5,9},{6,10},{7,11},{8,4},{9,5},... | collective-permute-start | bytes 196616 | tf_op jit(solution)/shard_map/ppermute | solution.py:508
  42.4 8.1 %attend.1 = (bf16[768,512]{1,0:T(8,128)(2,1)S(1)}, f32[768,512]{1,0:T(8,128)S(1)}, bf16[768,2048]{1,0:T(8,128)(2,1)S(1)}) custom-call(f32[4]{0:T(128)S(1)} %rsqrt.3.inv_ref, s32[768,1]{1,0:T(8,128)S(1)} %reshape.64.slots_ref, bf16[512,512]{1,0:T(8,128)(2,1)S(1)} %constant_dynamic-update-slice_fusion.4.near_ref, ...), custom_call_target="tpu_custom_call" | custom-call | flops 3221225472 | bytes 16777216 | tf_op jit(solution)/shard_map/attend/pallas_call | solution.py:316
  51.8 2.4 %collective-permute-start.16 = (bf16[256,512]{1,0:T(8,128)(2,1)S(1)}, bf16[256,512]{1,0:T(8,128)(2,1)S(1)}, u32[]{:S(2)}, u32[]{:S(2)}) collective-permute-start(bf16[256,512]{1,0:T(8,128)(2,1)S(1)} %constant_dynamic-update-slice_fusion.11), channel_id=1, source_target_pairs={{0,3},{1,2},{2,1},{3,0},{4,7},{5,6},{6,5},{7,4},{8,11},{9,10},{10,... | collective-permute-start | bytes 786440 | tf_op jit(solution)/shard_map/ppermute | solution.py:508
  54.2 7.3 %score.1 = (f32[768,1]{1,0:T(8,128)S(1)}, bf16[768,512]{1,0:T(8,128)(2,1)S(1)}, f32[768,512]{1,0:T(8,128)S(1)}) custom-call(f32[4]{0:T(128)S(1)} %rsqrt.3.inv_ref, bf16[768,512]{1,0:T(8,128)(2,1)S(1)} %get-tuple-element.24.queries_ref, f32[768,512]{1,0:T(8,128)S(1)} %get-tuple-element.25.attended_ref, s32[768,1]{1,0:T(8,128)S(1)} %reshape.65.labels_ref, ...), custom_call_target="tpu_custom_call" | custom-call | flops 4831838208 | bytes 8388608 | tf_op jit(solution)/shard_map/score/pallas_call | solution.py:388
  61.5 2.6 %attend_back.2.refs_0_ = bf16[384,512]{1,0:T(8,128)(2,1)S(1)} custom-call(bf16[768,512]{1,0:T(8,128)(2,1)S(1)} %get-tuple-element.26.grad_att_ref, f32[768,512]{1,0:T(8,128)S(1)} %get-tuple-element.27.direct_ref, bf16[768,2048]{1,0:T(8,128)(2,1)S(1)} %get-tuple-element.28.slope_ref, bf16[4,2048,512]{2,1,0:T(8,128)(2,1)S(1)} %bitcast.4), custom_call_target="tpu_custom_call" | custom-call | flops 1610612736 | bytes 8388608 | tf_op jit(solution)/shard_map/attend_back/pallas_call | solution.py:427
  64.1 2.3 %attend_back.3.refs_1_ = bf16[384,512]{1,0:T(8,128)(2,1)S(1)} custom-call(bf16[768,512]{1,0:T(8,128)(2,1)S(1)} %get-tuple-element.26.grad_att_ref, f32[768,512]{1,0:T(8,128)S(1)} %get-tuple-element.27.direct_ref, bf16[768,2048]{1,0:T(8,128)(2,1)S(1)} %get-tuple-element.28.slope_ref, bf16[4,2048,512]{2,1,0:T(8,128)(2,1)S(1)} %bitcast.4), custom_call_target="tpu_custom_call" | custom-call | flops 1610612736 | bytes 8388608 | tf_op jit(solution)/shard_map/attend_back/pallas_call | solution.py:427
  67.1 1.1 %collective-permute-done.8.refs_2_ = bf16[384,512]{1,0:T(8,128)(2,1)S(1)} collective-permute-done((bf16[384,512]{1,0:T(8,128)(2,1)S(1)}, bf16[384,512]{1,0:T(8,128)(2,1)S(1)}, u32[]{:S(2)}, u32[]{:S(2)}) %collective-permute-start.8) | collective-permute-done | bytes 393248 | tf_op jit(solution)/shard_map/ppermute | solution.py:508
  68.8 2.5 %chip_terms.1 = bf16[512,512]{1,0:T(8,128)(2,1)S(1)} custom-call(s32[1]{0:T(128)} %bitcast.wide_ref, s32[1,1536]{1,0:T(1,128)S(1)} %reshape.56.slots_ref, bf16[384,512]{1,0:T(8,128)(2,1)S(1)} %attend_back.2.refs_0_, bf16[384,512]{1,0:T(8,128)(2,1)S(1)} %attend_back.3.refs_1_, bf16[384,512]{1,0:T(8,128)(2,1)S(1)} %collective-permute-done.8.refs_2_, ...), custom_call_target="tpu_custom_call" | custom-call | flops 2147483648 | bytes 4194304 | tf_op jit(solution)/shard_map/chip_terms/pallas_call | solution.py:478
  71.9 1.5 %collective-permute-start.18 = (bf16[128,512]{1,0:T(8,128)(2,1)S(1)}, bf16[128,512]{1,0:T(8,128)(2,1)S(1)}, u32[]{:S(2)}, u32[]{:S(2)}) collective-permute-start(bf16[128,512]{1,0:T(8,128)(2,1)S(1)} %get-tuple-element.48), channel_id=1, source_target_pairs={{0,2},{1,3},{2,0},{3,1},{4,6},{5,7},{6,4},{7,5},{8,10},{9,11},{10,... | collective-permute-start | bytes 393224 | tf_op jit(solution)/shard_map/ppermute | solution.py:508
  73.4 1.5 %collective-permute-start.17 = (bf16[128,512]{1,0:T(8,128)(2,1)S(1)}, bf16[128,512]{1,0:T(8,128)(2,1)S(1)}, u32[]{:S(2)}, u32[]{:S(2)}) collective-permute-start(bf16[128,512]{1,0:T(8,128)(2,1)S(1)} %get-tuple-element.46), channel_id=1, source_target_pairs={{0,1},{1,0},{2,3},{3,2},{4,5},{5,4},{6,7},{7,6},{8,9},{9,8},{10,11... | collective-permute-start | bytes 393224 | tf_op jit(solution)/shard_map/ppermute | solution.py:508
  75.7 3.0 %collective-permute-done.19 = bf16[128,512]{1,0:T(8,128)(2,1)S(1)} collective-permute-done((bf16[128,512]{1,0:T(8,128)(2,1)S(1)}, bf16[128,512]{1,0:T(8,128)(2,1)S(1)}, u32[]{:S(2)}, u32[]{:S(2)}) %collective-permute-start.19) | collective-permute-done | bytes 131104 | tf_op jit(solution)/shard_map/ppermute | solution.py:508
  78.7 1.3 %collective-permute-done.18 = bf16[128,512]{1,0:T(8,128)(2,1)S(1)} collective-permute-done((bf16[128,512]{1,0:T(8,128)(2,1)S(1)}, bf16[128,512]{1,0:T(8,128)(2,1)S(1)}, u32[]{:S(2)}, u32[]{:S(2)}) %collective-permute-start.18) | collective-permute-done | bytes 131104 | tf_op jit(solution)/shard_map/ppermute | solution.py:508
  80.9 3.8 %collective-permute-start.20 = (bf16[32,512]{1,0:T(8,128)(2,1)S(1)}, bf16[32,512]{1,0:T(8,128)(2,1)S(1)}, u32[]{:S(2)}, u32[]{:S(2)}) collective-permute-start(bf16[32,512]{1,0:T(8,128)(2,1)S(1)} %get-tuple-element.49), channel_id=1, source_target_pairs={{0,4},{1,5},{2,6},{3,7},{4,0},{5,1},{6,2},{7,3},{8,12},{9,13},{10,... | collective-permute-start | bytes 98312 | tf_op jit(solution)/shard_map/ppermute | solution.py:508
  84.6 1.3 %collective-permute-done.22 = bf16[32,512]{1,0:T(8,128)(2,1)S(1)} collective-permute-done((bf16[32,512]{1,0:T(8,128)(2,1)S(1)}, bf16[32,512]{1,0:T(8,128)(2,1)S(1)}, u32[]{:S(2)}, u32[]{:S(2)}) %collective-permute-start.22) | collective-permute-done | bytes 32800 | tf_op jit(solution)/shard_map/ppermute | solution.py:508
  (76 shorter events, 9.4 us)
Async XLA Ops:
  0.7 36.5 %copy-start.2 = (s32[768]{0:T(1024)S(1)}, s32[768]{0:T(1024)}, u32[]{:S(2)}) copy-start(s32[768]{0:T(1024)} %param.23) | copy-start | bytes 9220
  15.5 5.7 %collective-permute-start.1 = (bf16[32,512]{1,0:T(8,128)(2,1)S(1)}, bf16[32,512]{1,0:T(8,128)(2,1)S(1)}, u32[]{:S(2)}, u32[]{:S(2)}) collective-permute-start(bf16[32,512]{1,0:T(8,128)(2,1)S(1)} %get-tuple-element.23), channel_id=1, source_target_pairs={{0,4},{1,5},{2,6},{3,7},{4,0},{5,1},{6,2},{7,3},{8,12},{9,13},{10,... | collective-permute-start | bytes 98312 | tf_op jit(solution)/shard_map/ppermute | solution.py:508
  18.6 5.4 %collective-permute-start.2 = (bf16[32,512]{1,0:T(8,128)(2,1)S(1)}, bf16[32,512]{1,0:T(8,128)(2,1)S(1)}, u32[]{:S(2)}, u32[]{:S(2)}) collective-permute-start(bf16[32,512]{1,0:T(8,128)(2,1)S(1)} %get-tuple-element.23), channel_id=1, source_target_pairs={{0,8},{1,9},{2,10},{3,11},{4,12},{5,13},{6,14},{7,15},{8,0},{9,1},... | collective-permute-start | bytes 98312 | tf_op jit(solution)/shard_map/ppermute | solution.py:508
  21.2 5.7 %collective-permute-start.3 = (bf16[32,512]{1,0:T(8,128)(2,1)S(1)}, bf16[32,512]{1,0:T(8,128)(2,1)S(1)}, u32[]{:S(2)}, u32[]{:S(2)}) collective-permute-start(bf16[32,512]{1,0:T(8,128)(2,1)S(1)} %get-tuple-element.23), channel_id=1, source_target_pairs={{0,12},{1,13},{2,14},{3,15},{4,8},{5,9},{6,10},{7,11},{8,4},{9,5},... | collective-permute-start | bytes 98312 | tf_op jit(solution)/shard_map/ppermute | solution.py:508
  26.9 6.1 %collective-permute-start.4 = (bf16[128,512]{1,0:T(8,128)(2,1)S(1)}, bf16[128,512]{1,0:T(8,128)(2,1)S(1)}, u32[]{:S(2)}, u32[]{:S(2)}) collective-permute-start(bf16[128,512]{1,0:T(8,128)(2,1)S(1)} %get-tuple-element.52), channel_id=1, source_target_pairs={{0,1},{1,0},{2,3},{3,2},{4,5},{5,4},{6,7},{7,6},{8,9},{9,8},{10,11... | collective-permute-start | bytes 393224 | tf_op jit(solution)/shard_map/ppermute | solution.py:508
  28.4 5.8 %collective-permute-start.5 = (bf16[128,512]{1,0:T(8,128)(2,1)S(1)}, bf16[128,512]{1,0:T(8,128)(2,1)S(1)}, u32[]{:S(2)}, u32[]{:S(2)}) collective-permute-start(bf16[128,512]{1,0:T(8,128)(2,1)S(1)} %get-tuple-element.52), channel_id=1, source_target_pairs={{0,2},{1,3},{2,0},{3,1},{4,6},{5,7},{6,4},{7,5},{8,10},{9,11},{10,... | collective-permute-start | bytes 393224 | tf_op jit(solution)/shard_map/ppermute | solution.py:508
  30.0 5.9 %collective-permute-start.6 = (bf16[128,512]{1,0:T(8,128)(2,1)S(1)}, bf16[128,512]{1,0:T(8,128)(2,1)S(1)}, u32[]{:S(2)}, u32[]{:S(2)}) collective-permute-start(bf16[128,512]{1,0:T(8,128)(2,1)S(1)} %get-tuple-element.52), channel_id=1, source_target_pairs={{0,3},{1,2},{2,1},{3,0},{4,7},{5,6},{6,5},{7,4},{8,11},{9,10},{10,... | collective-permute-start | bytes 393224 | tf_op jit(solution)/shard_map/ppermute | solution.py:508
  35.9 6.5 %collective-permute-start.7 = (bf16[512,512]{1,0:T(8,128)(2,1)S(1)}, bf16[512,512]{1,0:T(8,128)(2,1)S(1)}, u32[]{:S(2)}, u32[]{:S(2)}) collective-permute-start(bf16[512,512]{1,0:T(8,128)(2,1)S(1)} %constant_dynamic-update-slice_fusion.4.near_ref), channel_id=1, source_target_pairs={{0,16},{16,0},{1,17},{17,1},{2,18},{18,2},{3,19},{19,3},{4,20},{20... | collective-permute-start | bytes 1572872 | tf_op jit(solution)/shard_map/ppermute | solution.py:508
  36.0 30.5 %collective-permute-start = (s32[768]{0:T(1024)S(1)}, s32[768]{0:T(1024)S(1)}, u32[]{:S(2)}, u32[]{:S(2)}) collective-permute-start(s32[768]{0:T(1024)S(1)} %get-tuple-element.61), channel_id=1, source_target_pairs={{0,16},{16,0},{1,17},{17,1},{2,18},{18,2},{3,19},{19,3},{4,20},{20... | collective-permute-start | bytes 9224 | tf_op jit(solution)/shard_map/ppermute | solution.py:508
  36.6 1.4 %collective-permute-start.10 = (bf16[32,512]{1,0:T(8,128)(2,1)S(1)}, bf16[32,512]{1,0:T(8,128)(2,1)S(1)}, u32[]{:S(2)}, u32[]{:S(2)}) collective-permute-start(bf16[32,512]{1,0:T(8,128)(2,1)S(1)} %get-tuple-element.32), channel_id=1, source_target_pairs={{0,16},{16,0},{1,17},{17,1},{2,18},{18,2},{3,19},{19,3},{4,20},{20... | collective-permute-start | bytes 98312 | tf_op jit(solution)/shard_map/ppermute | solution.py:508
  38.0 12.6 %collective-permute-start.11 = (bf16[64,512]{1,0:T(8,128)(2,1)S(1)}, bf16[64,512]{1,0:T(8,128)(2,1)S(1)}, u32[]{:S(2)}, u32[]{:S(2)}) collective-permute-start(bf16[64,512]{1,0:T(8,128)(2,1)S(1)} %maximum_select_fusion), channel_id=1, source_target_pairs={{0,4},{1,5},{2,6},{3,7},{4,0},{5,1},{6,2},{7,3},{8,12},{9,13},{10,... | collective-permute-start | bytes 196616 | tf_op jit(solution)/shard_map/ppermute | solution.py:508
  38.0 12.5 %collective-permute-start.12 = (bf16[64,512]{1,0:T(8,128)(2,1)S(1)}, bf16[64,512]{1,0:T(8,128)(2,1)S(1)}, u32[]{:S(2)}, u32[]{:S(2)}) collective-permute-start(bf16[64,512]{1,0:T(8,128)(2,1)S(1)} %maximum_select_fusion), channel_id=1, source_target_pairs={{0,8},{1,9},{2,10},{3,11},{4,12},{5,13},{6,14},{7,15},{8,0},{9,1},... | collective-permute-start | bytes 196616 | tf_op jit(solution)/shard_map/ppermute | solution.py:508
  38.9 11.7 %collective-permute-start.13 = (bf16[64,512]{1,0:T(8,128)(2,1)S(1)}, bf16[64,512]{1,0:T(8,128)(2,1)S(1)}, u32[]{:S(2)}, u32[]{:S(2)}) collective-permute-start(bf16[64,512]{1,0:T(8,128)(2,1)S(1)} %maximum_select_fusion), channel_id=1, source_target_pairs={{0,12},{1,13},{2,14},{3,15},{4,8},{5,9},{6,10},{7,11},{8,4},{9,5},... | collective-permute-start | bytes 196616 | tf_op jit(solution)/shard_map/ppermute | solution.py:508
  50.7 16.4 %collective-permute-start.14 = (bf16[256,512]{1,0:T(8,128)(2,1)S(1)}, bf16[256,512]{1,0:T(8,128)(2,1)S(1)}, u32[]{:S(2)}, u32[]{:S(2)}) collective-permute-start(bf16[256,512]{1,0:T(8,128)(2,1)S(1)} %constant_dynamic-update-slice_fusion.11), channel_id=1, source_target_pairs={{0,1},{1,0},{2,3},{3,2},{4,5},{5,4},{6,7},{7,6},{8,9},{9,8},{10,11... | collective-permute-start | bytes 786440 | tf_op jit(solution)/shard_map/ppermute | solution.py:508
  51.3 15.8 %collective-permute-start.15 = (bf16[256,512]{1,0:T(8,128)(2,1)S(1)}, bf16[256,512]{1,0:T(8,128)(2,1)S(1)}, u32[]{:S(2)}, u32[]{:S(2)}) collective-permute-start(bf16[256,512]{1,0:T(8,128)(2,1)S(1)} %constant_dynamic-update-slice_fusion.11), channel_id=1, source_target_pairs={{0,2},{1,3},{2,0},{3,1},{4,6},{5,7},{6,4},{7,5},{8,10},{9,11},{10,... | collective-permute-start | bytes 786440 | tf_op jit(solution)/shard_map/ppermute | solution.py:508
  51.8 15.3 %collective-permute-start.16 = (bf16[256,512]{1,0:T(8,128)(2,1)S(1)}, bf16[256,512]{1,0:T(8,128)(2,1)S(1)}, u32[]{:S(2)}, u32[]{:S(2)}) collective-permute-start(bf16[256,512]{1,0:T(8,128)(2,1)S(1)} %constant_dynamic-update-slice_fusion.11), channel_id=1, source_target_pairs={{0,3},{1,2},{2,1},{3,0},{4,7},{5,6},{6,5},{7,4},{8,11},{9,10},{10,... | collective-permute-start | bytes 786440 | tf_op jit(solution)/shard_map/ppermute | solution.py:508
  66.4 1.8 %collective-permute-start.8 = (bf16[384,512]{1,0:T(8,128)(2,1)S(1)}, bf16[384,512]{1,0:T(8,128)(2,1)S(1)}, u32[]{:S(2)}, u32[]{:S(2)}) collective-permute-start(bf16[384,512]{1,0:T(8,128)(2,1)S(1)} %attend_back.2.refs_0_), channel_id=1, source_target_pairs={{0,16},{16,0},{1,17},{17,1},{2,18},{18,2},{3,19},{19,3},{4,20},{20... | collective-permute-start | bytes 1179656 | tf_op jit(solution)/shard_map/ppermute | solution.py:508
  66.5 2.3 %collective-permute-start.9 = (bf16[384,512]{1,0:T(8,128)(2,1)S(1)}, bf16[384,512]{1,0:T(8,128)(2,1)S(1)}, u32[]{:S(2)}, u32[]{:S(2)}) collective-permute-start(bf16[384,512]{1,0:T(8,128)(2,1)S(1)} %attend_back.3.refs_1_), channel_id=1, source_target_pairs={{0,16},{16,0},{1,17},{17,1},{2,18},{18,2},{3,19},{19,3},{4,20},{20... | collective-permute-start | bytes 1179656 | tf_op jit(solution)/shard_map/ppermute | solution.py:508
  71.4 7.4 %collective-permute-start.19 = (bf16[128,512]{1,0:T(8,128)(2,1)S(1)}, bf16[128,512]{1,0:T(8,128)(2,1)S(1)}, u32[]{:S(2)}, u32[]{:S(2)}) collective-permute-start(bf16[128,512]{1,0:T(8,128)(2,1)S(1)} %get-tuple-element.47), channel_id=1, source_target_pairs={{0,3},{1,2},{2,1},{3,0},{4,7},{5,6},{6,5},{7,4},{8,11},{9,10},{10,... | collective-permute-start | bytes 393224 | tf_op jit(solution)/shard_map/ppermute | solution.py:508
  71.9 8.1 %collective-permute-start.18 = (bf16[128,512]{1,0:T(8,128)(2,1)S(1)}, bf16[128,512]{1,0:T(8,128)(2,1)S(1)}, u32[]{:S(2)}, u32[]{:S(2)}) collective-permute-start(bf16[128,512]{1,0:T(8,128)(2,1)S(1)} %get-tuple-element.48), channel_id=1, source_target_pairs={{0,2},{1,3},{2,0},{3,1},{4,6},{5,7},{6,4},{7,5},{8,10},{9,11},{10,... | collective-permute-start | bytes 393224 | tf_op jit(solution)/shard_map/ppermute | solution.py:508
  73.4 6.7 %collective-permute-start.17 = (bf16[128,512]{1,0:T(8,128)(2,1)S(1)}, bf16[128,512]{1,0:T(8,128)(2,1)S(1)}, u32[]{:S(2)}, u32[]{:S(2)}) collective-permute-start(bf16[128,512]{1,0:T(8,128)(2,1)S(1)} %get-tuple-element.46), channel_id=1, source_target_pairs={{0,1},{1,0},{2,3},{3,2},{4,5},{5,4},{6,7},{7,6},{8,9},{9,8},{10,11... | collective-permute-start | bytes 393224 | tf_op jit(solution)/shard_map/ppermute | solution.py:508
  80.2 5.8 %collective-permute-start.22 = (bf16[32,512]{1,0:T(8,128)(2,1)S(1)}, bf16[32,512]{1,0:T(8,128)(2,1)S(1)}, u32[]{:S(2)}, u32[]{:S(2)}) collective-permute-start(bf16[32,512]{1,0:T(8,128)(2,1)S(1)} %get-tuple-element.51), channel_id=1, source_target_pairs={{0,12},{1,13},{2,14},{3,15},{4,8},{5,9},{6,10},{7,11},{8,4},{9,5},... | collective-permute-start | bytes 98312 | tf_op jit(solution)/shard_map/ppermute | solution.py:508
  80.8 5.2 %collective-permute-start.21 = (bf16[32,512]{1,0:T(8,128)(2,1)S(1)}, bf16[32,512]{1,0:T(8,128)(2,1)S(1)}, u32[]{:S(2)}, u32[]{:S(2)}) collective-permute-start(bf16[32,512]{1,0:T(8,128)(2,1)S(1)} %get-tuple-element.50), channel_id=1, source_target_pairs={{0,8},{1,9},{2,10},{3,11},{4,12},{5,13},{6,14},{7,15},{8,0},{9,1},... | collective-permute-start | bytes 98312 | tf_op jit(solution)/shard_map/ppermute | solution.py:508
  80.9 5.6 %collective-permute-start.20 = (bf16[32,512]{1,0:T(8,128)(2,1)S(1)}, bf16[32,512]{1,0:T(8,128)(2,1)S(1)}, u32[]{:S(2)}, u32[]{:S(2)}) collective-permute-start(bf16[32,512]{1,0:T(8,128)(2,1)S(1)} %get-tuple-element.49), channel_id=1, source_target_pairs={{0,4},{1,5},{2,6},{3,7},{4,0},{5,1},{6,2},{7,3},{8,12},{9,13},{10,... | collective-permute-start | bytes 98312 | tf_op jit(solution)/shard_map/ppermute | solution.py:508
  (8 other events, 189.3 us)

commit v2 on v1

--- a/solution.py
+++ b/solution.py
@@ -273,20 +273,17 @@
 ):
     users, events, _ = history_ref.shape
     chunk = math.gcd(events, 1024)
+    half_users = max(1, users // 2)
     copies = [
-        [
-            pltpu.make_async_copy(
-                history_hbm.at[user, pl.ds(at, chunk)],
-                history_ref.at[user, pl.ds(at, chunk)],
-                sems.at[user, at // chunk],
-            )
-            for at in range(0, events, chunk)
-        ]
-        for user in range(users)
+        pltpu.make_async_copy(
+            history_hbm.at[pl.ds(user, half_users)],
+            history_ref.at[pl.ds(user, half_users)],
+            sems.at[user],
+        )
+        for user in range(0, users, half_users)
     ]
-    for user_copies in copies:
-        for copy in user_copies:
-            copy.start()
+    for copy in copies:
+        copy.start()
     slots = slots_ref[...]
     half, key_width = near_ref.shape
     places = lax.broadcasted_iota(jnp.int32, (slots.shape[0], half), 1)
@@ -295,10 +292,11 @@
     queries_ref[...] = queries.astype(jnp.bfloat16)
     per_user = slots.shape[0] // users
     for user in range(users):
+        if user % half_users == 0:
+            copies[user // half_users].wait()
         rows = slice(user * per_user, (user + 1) * per_user)
         attended = jnp.zeros((per_user, key_width), jnp.float32)
         for at in range(0, events, chunk):
-            copies[user][at // chunk].wait()
             keys = history_ref[user, at : at + chunk, :]
             usable = usable_ref[user, :, at : at + chunk]
             scores = dot_rows(queries_ref[rows, :], keys)
@@ -326,7 +324,7 @@
         ],
         scratch_shapes=[
             pltpu.VMEM(history.shape, history.dtype),
-            pltpu.SemaphoreType.DMA((users, events // math.gcd(events, 1024))),
+            pltpu.SemaphoreType.DMA((users,)),
         ],
         compiler_params=pltpu.CompilerParams(vmem_limit_bytes=32 * MIB),
         cost_estimate=pl.CostEstimate(
@@ -346,18 +344,19 @@
     logits_ref,
     grad_att_ref,
     direct_ref,
+    grad_pre_ref,
 ):
     users = inv_ref.shape[0]
     per_user = queries_ref.shape[0] // users
     step_users = math.gcd(users, 2)
     step_rows = step_users * per_user
+    key_width = queries_ref.shape[1]
     weight = logit_weight_ref[...].astype(jnp.float32)
     for first in range(0, users, step_users):
         at = slice(first * per_user, first * per_user + step_rows)
         query_b = queries_ref[at, :]
         query_f = query_b.astype(jnp.float32)
         attended = attended_ref[at, :]
-        key_width = query_f.shape[1]
         joined = jnp.concatenate(
             [query_b, attended.astype(jnp.bfloat16), (query_f * attended).astype(jnp.bfloat16)],
             axis=1,
@@ -370,16 +369,15 @@
         dlogit = (0.5 * jnp.tanh(0.5 * logits) + 0.5) - labels_ref[at, :].astype(jnp.float32)
         slope = act_sig * (1.0 + pre_act * (1.0 - act_sig))
         grad_pre = (dlogit * weight * slope).astype(jnp.bfloat16)
-        djoined = dot_rows(grad_pre, mlp_ref[...])
-        part_query = djoined[:, :key_width]
-        part_att = djoined[:, key_width : 2 * key_width]
-        part_prod = djoined[:, 2 * key_width :]
-        grad_att = part_att + part_prod * query_f
-        for user in range(step_users):
-            grad_att_ref[pl.ds((first + user) * per_user, per_user), :] = (
-                grad_att[user * per_user : (user + 1) * per_user] * inv_ref[first + user]
-            ).astype(jnp.bfloat16)
-        direct_ref[at, :] = part_query + part_prod * attended
+        grad_pre_ref[at, :] = grad_pre
+    djoined = dot_rows(grad_pre_ref[...], mlp_ref[...])
+    part_att = djoined[:, key_width : 2 * key_width]
+    part_prod = djoined[:, 2 * key_width :]
+    for user in range(users):
+        at = slice(user * per_user, (user + 1) * per_user)
+        grad_att = part_att[at] + part_prod[at] * queries_ref[at, :].astype(jnp.float32)
+        grad_att_ref[at, :] = (grad_att * inv_ref[user]).astype(jnp.bfloat16)
+    direct_ref[...] = djoined[:, :key_width] + part_prod * attended_ref[...]
 
 
 def score(inv_count, queries, attended, labels, mlp_weight, logit_weight):
@@ -394,6 +392,7 @@
             jax.ShapeDtypeStruct((requests, key_width), jnp.bfloat16),
             jax.ShapeDtypeStruct((requests, key_width), jnp.float32),
         ],
+        scratch_shapes=[pltpu.VMEM((requests, mlp_weight.shape[1]), jnp.bfloat16)],
         compiler_params=pltpu.CompilerParams(vmem_limit_bytes=32 * MIB),
         cost_estimate=pl.CostEstimate(
             flops=4 * requests * mlp_weight.shape[0] * mlp_weight.shape[1],
@@ -404,56 +403,77 @@
     )(inv_count, queries, attended, labels, mlp_weight, logit_weight)
 
 
-def attend_back_kernel(first, grad_att_ref, direct_ref, slope_ref, history_ref, grad_rows_ref):
+def attend_back_kernel(grad_att_ref, direct_ref, slope_ref, history_ref, grad_rows_ref):
     users, events, key_width = history_ref.shape
     per_user = grad_att_ref.shape[0] // users
     chunk = math.gcd(events, 1024)
-    for user in range(grad_rows_ref.shape[0] // per_user):
-        rows = slice((first + user) * per_user, (first + user + 1) * per_user)
+    for user in range(users):
+        rows = slice(user * per_user, (user + 1) * per_user)
         back = jnp.zeros((per_user, key_width), jnp.float32)
         for at in range(0, events, chunk):
-            keys = history_ref[first + user, at : at + chunk, :]
+            keys = history_ref[user, at : at + chunk, :]
             slope = slope_ref[rows, at : at + chunk].astype(jnp.float32)
             grad_sig = (dot_rows(grad_att_ref[rows, :], keys) * slope).astype(jnp.bfloat16)
             back += dot(grad_sig, keys)
         grad_rows = direct_ref[rows, :] + back * (1.0 / math.sqrt(key_width))
-        grad_rows_ref[user * per_user : (user + 1) * per_user, :] = grad_rows.astype(jnp.bfloat16)
-
-
-def attend_back(first, count, grad_att, direct, slope, history):
-    users, events, key_width = history.shape
-    per_user = grad_att.shape[0] // users
+        grad_rows_ref[rows, :] = grad_rows.astype(jnp.bfloat16)
+
+
+def attend_back(grad_att, direct, slope, history):
+    _, events, key_width = history.shape
+    requests = grad_att.shape[0]
     whole = pl.BlockSpec(memory_space=pltpu.VMEM)
     return pl.pallas_call(
-        functools.partial(attend_back_kernel, first),
+        attend_back_kernel,
         in_specs=[whole] * 4,
         out_specs=whole,
-        out_shape=jax.ShapeDtypeStruct((count * per_user, key_width), jnp.bfloat16),
+        out_shape=jax.ShapeDtypeStruct((requests, key_width), jnp.bfloat16),
         compiler_params=pltpu.CompilerParams(vmem_limit_bytes=20 * MIB),
         cost_estimate=pl.CostEstimate(
-            flops=4 * count * per_user * events * key_width,
-            bytes_accessed=1 << 23,
-            transcendentals=0,
+            flops=4 * requests * events * key_width, bytes_accessed=1 << 23, transcendentals=0
         ),
         name="attend_back",
     )(grad_att, direct, slope, history)
 
 
-def terms_kernel(origins, wide_ref, slots_ref, *refs):
-    grad_refs = refs[:-4]
-    pooled_ref, out_ref, grad_rows_ref, terms_ref = refs[-4:]
-    at = 0
-    for grad_ref in grad_refs:
-        grad_rows_ref[at : at + grad_ref.shape[0], :] = grad_ref[...]
-        at += grad_ref.shape[0]
-    cands = pooled_ref.shape[0]
-    requests = slots_ref.shape[1]
+def sum_rows(cands, at, slots_ref, grad_rows_ref):
+    places = lax.broadcasted_iota(jnp.int32, (cands, slots_ref.shape[1]), 0) + at
+    return dot((places == slots_ref[...]).astype(jnp.bfloat16), grad_rows_ref[...])
+
+
+def cand_grad_kernel(slots_ref, grad_rows_ref, cand_grad_ref):
+    cands = cand_grad_ref.shape[0]
     chunk = math.gcd(cands, 512)
     for at in range(0, cands, chunk):
-        places = lax.broadcasted_iota(jnp.int32, (chunk, requests), 0) + at
-        row_hot = (places == slots_ref[...]).astype(jnp.bfloat16)
-        cand_grad = dot(row_hot, grad_rows_ref[...]).astype(jnp.bfloat16)
-        term = dot_columns(pooled_ref[at : at + chunk, :], cand_grad)
+        cand_grad_ref[at : at + chunk, :] = sum_rows(chunk, at, slots_ref, grad_rows_ref)
+
+
+def own_cand_grad(cands, slots, grad_rows):
+    requests, key_width = grad_rows.shape
+    whole = pl.BlockSpec(memory_space=pltpu.VMEM)
+    return pl.pallas_call(
+        cand_grad_kernel,
+        in_specs=[whole] * 2,
+        out_specs=whole,
+        out_shape=jax.ShapeDtypeStruct((cands, key_width), jnp.float32),
+        compiler_params=pltpu.CompilerParams(vmem_limit_bytes=20 * MIB),
+        cost_estimate=pl.CostEstimate(
+            flops=2 * cands * key_width * requests, bytes_accessed=1 << 22, transcendentals=0
+        ),
+        name="own_cand_grad",
+    )(slots, grad_rows)
+
+
+def terms_kernel(
+    origins, wide_ref, cand_grad_ref, slots_ref, grad_rows_ref, pooled_ref, out_ref, terms_ref
+):
+    cands = pooled_ref.shape[0]
+    chunk = math.gcd(cands, 512)
+    for at in range(0, cands, chunk):
+        cand_grad = cand_grad_ref[at : at + chunk, :] + sum_rows(
+            chunk, at, slots_ref, grad_rows_ref
+        )
+        term = dot_columns(pooled_ref[at : at + chunk, :], cand_grad.astype(jnp.bfloat16))
         if at == 0:
             terms_ref[...] = term
         else:
@@ -470,20 +490,16 @@
         out_ref[slot * rows : (slot + batch) * rows, :] = found.astype(jnp.bfloat16)
 
 
-def chip_terms(origins, wide, slots, grad_parts, pooled):
+def chip_terms(origins, wide, cand_grad, far_slots, far_grad_rows, pooled):
     cands, width = pooled.shape
-    requests = slots.shape[1]
-    key_width = grad_parts[0].shape[1]
+    requests, key_width = far_grad_rows.shape
     whole = pl.BlockSpec(memory_space=pltpu.VMEM)
     return pl.pallas_call(
         functools.partial(terms_kernel, origins),
-        in_specs=[pl.BlockSpec(memory_space=pltpu.SMEM)] + [whole] * (len(grad_parts) + 2),
+        in_specs=[pl.BlockSpec(memory_space=pltpu.SMEM)] + [whole] * 4,
         out_specs=whole,
         out_shape=jax.ShapeDtypeStruct((width, key_width), jnp.bfloat16),
-        scratch_shapes=[
-            pltpu.VMEM((requests, key_width), jnp.bfloat16),
-            pltpu.VMEM((width, key_width), jnp.float32),
-        ],
+        scratch_shapes=[pltpu.VMEM((width, key_width), jnp.float32)],
         compiler_params=pltpu.CompilerParams(vmem_limit_bytes=20 * MIB),
         cost_estimate=pl.CostEstimate(
             flops=2 * cands * key_width * (width + requests),
@@ -491,7 +507,7 @@
             transcendentals=0,
         ),
         name="chip_terms",
-    )(wide, slots, *grad_parts, pooled)
+    )(wide, cand_grad, far_slots, far_grad_rows, pooled)
 
 
 def bit_groups(size):
@@ -570,24 +586,28 @@
     slots = ((owner_core ^ core) * wides + owner_slot) * cand_count + req_local
     pooled_slots = (owner_slot * 2 + owner_core) * cand_count + req_local
     stages = list(reversed(bit_groups(wides)))
-    near = embedded
-    for bit, values in stages:
-        near = jnp.concatenate([near] + send_stage(near, wides, bit, values), axis=0)
-        if bit == stages[0][0]:
-            keep, send = after((keep, send), near)
+    near, pooled = embedded, None
+    for place, stage in enumerate(stages):
+        found = send_stage(near, wides, *stage)
+        if place == 0:
+            got = exchange(send, "section", 2, 1)
+            far_slots = exchange(pooled_slots, "section", 2, 1)
+            found, keep, got, far_slots = lax.optimization_barrier((found, keep, got, far_slots))
+            pooled = jnp.where(
+                core == 0,
+                jnp.concatenate([keep, got], axis=0),
+                jnp.concatenate([got, keep], axis=0),
+            )
+        else:
+            found_pooled = send_stage(pooled, wides, *stages[place - 1])
+            found, found_pooled = lax.optimization_barrier((found, found_pooled))
+            pooled = jnp.concatenate([pooled] + found_pooled, axis=0)
+        near = jnp.concatenate([near] + found, axis=0)
     far = exchange(near, "section", 2, 1)
-    far_slots = exchange(pooled_slots, "section", 2, 1)
-    got = exchange(send, "section", 2, 1)
-    pooled = jnp.where(
-        core == 0, jnp.concatenate([keep, got], axis=0), jnp.concatenate([got, keep], axis=0)
-    )
-    found = send_stage(pooled, wides, *stages[0])
+    found_pooled = send_stage(pooled, wides, *stages[-1])
     queries, attended, slope = attend(
         inv_count, slots.reshape(requests, 1), near, far, history, usable
     )
-    for stage in stages[1:]:
-        pooled = jnp.concatenate(after([pooled] + found, attended), axis=0)
-        found = send_stage(pooled, wides, *stage)
     logits, grad_att, direct = score(
         inv_count,
         queries,
@@ -596,21 +616,20 @@
         mlp_weight,
         logit_weight.reshape(1, -1),
     )
-    half = users // 2
-    grad_parts = [
-        attend_back(0, half, grad_att, direct, slope, history),
-        attend_back(half, users - half, grad_att, direct, slope, history),
-    ]
-    far_parts = [exchange(part, "section", 2, 1) for part in grad_parts]
-    pooled = jnp.concatenate(after([pooled] + found, grad_parts[1]), axis=0)
+    found_pooled, grad_att = lax.optimization_barrier((found_pooled, grad_att))
+    grad_rows = attend_back(grad_att, direct, slope, history)
+    far_grad_rows = exchange(grad_rows, "section", 2, 1)
+    pooled = jnp.concatenate(after([pooled] + found_pooled, grad_rows), axis=0)
+    cand_grad = own_cand_grad(pooled.shape[0], pooled_slots.reshape(1, requests), grad_rows)
     origins = [0] * wides
     for distance in range(wides):
         origins[slot_of(distance, wides)] = distance
     terms = chip_terms(
         origins,
         wide.reshape(1),
-        jnp.concatenate([pooled_slots, far_slots]).reshape(1, 2 * requests),
-        grad_parts + far_parts,
+        cand_grad,
+        far_slots.reshape(1, requests),
+        far_grad_rows,
         pooled,
     )
     grad_proj, logits = sum_blocks(terms, wides, logits.reshape(requests))

time: 87.3 us -> 85.3 us (0.977)
  starting transfers between devices: 26.5 us -> 23.1 us
  waiting for transfers between devices: 19.5 us -> 21.1 us
    ppermute x23 -> x22, starting transfers between devices: 26.5 us -> 23.1 us  [exchange(): lax.ppermute(values, axis_name, [(i, i ^ distance) for i in range(size)])]
    ppermute x23 -> x22, waiting for transfers between devices: 19.5 us -> 21.1 us  [exchange(): lax.ppermute(values, axis_name, [(i, i ^ distance) for i in range(size)])]
  transfers between devices with their start and end apart: 23 -> 22, of which waited for: 13 -> 11; matrix products, arithmetic and copies ran while one was open for 2% -> 2% of each run, Pallas kernels for 23% -> 19%
where the time goes in v2:
time: 85.3 us; the launch traced here: 85.1 us
  Pallas kernels  37.6 us (44%)
  starting transfers between devices  23.1 us (27%)
  waiting for transfers between devices  21.1 us (25%)
  other arithmetic  1.83 us (2%)
  between operations  1.04 us (1%)
    ppermute x22, starting transfers between devices, exchange(): lax.ppermute(values, axis_name, [(i, i ^ distance) for i in range(size)])  23.1 us
    ppermute x22, waiting for transfers between devices, exchange(): lax.ppermute(values, axis_name, [(i, i ^ distance) for i in range(size)])  21.1 us
    pallas_call x1, Pallas kernels, encode_block(): pl.pallas_call(functools.partial(encode_kernel, tokens), in_specs=[pl.Blo...  14.8 us
    pallas_call x1, Pallas kernels, attend(): pl.pallas_call(attend_kernel, in_specs=[pl.BlockSpec(memory_space=pltpu.S...  8.45 us
    pallas_call x1, Pallas kernels, score(): pl.pallas_call(score_kernel, in_specs=[pl.BlockSpec(memory_space=pltpu.SM...  6.88 us
    pallas_call x1, Pallas kernels, attend_back(): pl.pallas_call(attend_back_kernel, in_specs=[whole] * 4, out_specs=whole,...  4.68 us
    pallas_call x1, Pallas kernels, chip_terms(): pl.pallas_call(functools.partial(terms_kernel, origins), in_specs=[pl.Blo...  1.75 us
  transfers between devices with their start and end apart: 22, of which 11 were waited for; matrix products, arithmetic and copies ran while one was open for 2% of the time, Pallas kernels for 19%

profile of v2, /device:TPU:0, one launch (start us, length us, event | category | flops | bytes accessed | tf_op | source)
XLA Modules:
  0.0 85.1 jit_solution(6111415294929263214)
XLA Ops:
  0.7 14.8 %encode.1 = (bf16[32,512]{1,0:T(8,128)(2,1)S(1)}, bf16[32,512]{1,0:T(8,128)(2,1)S(1)}, bf16[32,512]{1,0:T(8,128)(2,1)S(1)}) custom-call(s32[1]{0:T(128)} %bitcast.1.core_ref, bf16[1536,1024]{1,0:T(8,128)(2,1)} %bitcast.5, bf16[1024,3072]{1,0:T(8,128)(2,1)} %qkv_hbm.1, bf16[1024,1024]{1,0:T(8,128)(2,1)} %out_hbm.1, bf16[1024,512]{1,0:T(8,128)(2,1)} %proj_hbm.1), custom_call_target="tpu_custom_call" | custom-call | flops 8053063680 | bytes 16777216 | tf_op jit(solution)/shard_map/encode/pallas_call | solution.py:231
  15.5 3.1 %collective-permute-start = (bf16[32,512]{1,0:T(8,128)(2,1)S(1)}, bf16[32,512]{1,0:T(8,128)(2,1)S(1)}, u32[]{:S(2)}, u32[]{:S(2)}) collective-permute-start(bf16[32,512]{1,0:T(8,128)(2,1)S(1)} %get-tuple-element.33), channel_id=1, source_target_pairs={{0,4},{1,5},{2,6},{3,7},{4,0},{5,1},{6,2},{7,3},{8,12},{9,13},{10,... | collective-permute-start | bytes 98312 | tf_op jit(solution)/shard_map/ppermute | solution.py:524
  18.6 2.6 %collective-permute-start.1 = (bf16[32,512]{1,0:T(8,128)(2,1)S(1)}, bf16[32,512]{1,0:T(8,128)(2,1)S(1)}, u32[]{:S(2)}, u32[]{:S(2)}) collective-permute-start(bf16[32,512]{1,0:T(8,128)(2,1)S(1)} %get-tuple-element.33), channel_id=1, source_target_pairs={{0,8},{1,9},{2,10},{3,11},{4,12},{5,13},{6,14},{7,15},{8,0},{9,1},... | collective-permute-start | bytes 98312 | tf_op jit(solution)/shard_map/ppermute | solution.py:524
  22.5 1.5 %collective-permute-done.1 = bf16[32,512]{1,0:T(8,128)(2,1)S(1)} collective-permute-done((bf16[32,512]{1,0:T(8,128)(2,1)S(1)}, bf16[32,512]{1,0:T(8,128)(2,1)S(1)}, u32[]{:S(2)}, u32[]{:S(2)}) %collective-permute-start.1) | collective-permute-done | bytes 32800 | tf_op jit(solution)/shard_map/ppermute | solution.py:524
  24.0 3.0 %collective-permute-done.2 = bf16[32,512]{1,0:T(8,128)(2,1)S(1)} collective-permute-done((bf16[32,512]{1,0:T(8,128)(2,1)S(1)}, bf16[32,512]{1,0:T(8,128)(2,1)S(1)}, u32[]{:S(2)}, u32[]{:S(2)}) %collective-permute-start.2) | collective-permute-done | bytes 32800 | tf_op jit(solution)/shard_map/ppermute | solution.py:524
  27.4 1.6 %collective-permute-start.5 = (bf16[128,512]{1,0:T(8,128)(2,1)S(1)}, bf16[128,512]{1,0:T(8,128)(2,1)S(1)}, u32[]{:S(2)}, u32[]{:S(2)}) collective-permute-start(bf16[128,512]{1,0:T(8,128)(2,1)S(1)} %get-tuple-element.73), channel_id=1, source_target_pairs={{0,1},{1,0},{2,3},{3,2},{4,5},{5,4},{6,7},{7,6},{8,9},{9,8},{10,11... | collective-permute-start | bytes 393224 | tf_op jit(solution)/shard_map/ppermute | solution.py:524
  28.9 1.5 %collective-permute-start.6 = (bf16[128,512]{1,0:T(8,128)(2,1)S(1)}, bf16[128,512]{1,0:T(8,128)(2,1)S(1)}, u32[]{:S(2)}, u32[]{:S(2)}) collective-permute-start(bf16[128,512]{1,0:T(8,128)(2,1)S(1)} %get-tuple-element.73), channel_id=1, source_target_pairs={{0,2},{1,3},{2,0},{3,1},{4,6},{5,7},{6,4},{7,5},{8,10},{9,11},{10,... | collective-permute-start | bytes 393224 | tf_op jit(solution)/shard_map/ppermute | solution.py:524
  30.9 2.8 %collective-permute-done.10 = bf16[64,512]{1,0:T(8,128)(2,1)S(1)} collective-permute-done((bf16[64,512]{1,0:T(8,128)(2,1)S(1)}, bf16[64,512]{1,0:T(8,128)(2,1)S(1)}, u32[]{:S(2)}, u32[]{:S(2)}) %collective-permute-start.10) | collective-permute-done | bytes 65568 | tf_op jit(solution)/shard_map/ppermute | solution.py:524
  33.8 1.3 %collective-permute-start.9 = (bf16[64,512]{1,0:T(8,128)(2,1)S(1)}, bf16[64,512]{1,0:T(8,128)(2,1)S(1)}, u32[]{:S(2)}, u32[]{:S(2)}) collective-permute-start(bf16[64,512]{1,0:T(8,128)(2,1)S(1)} %maximum_select_fusion), channel_id=1, source_target_pairs={{0,8},{1,9},{2,10},{3,11},{4,12},{5,13},{6,14},{7,15},{8,0},{9,1},... | collective-permute-start | bytes 196616 | tf_op jit(solution)/shard_map/ppermute | solution.py:524
  35.6 3.4 %collective-permute-done.9 = bf16[64,512]{1,0:T(8,128)(2,1)S(1)} collective-permute-done((bf16[64,512]{1,0:T(8,128)(2,1)S(1)}, bf16[64,512]{1,0:T(8,128)(2,1)S(1)}, u32[]{:S(2)}, u32[]{:S(2)}) %collective-permute-start.9) | collective-permute-done | bytes 65568 | tf_op jit(solution)/shard_map/ppermute | solution.py:524
  39.8 1.6 %collective-permute-start.11 = (bf16[256,512]{1,0:T(8,128)(2,1)S(1)}, bf16[256,512]{1,0:T(8,128)(2,1)S(1)}, u32[]{:S(2)}, u32[]{:S(2)}) collective-permute-start(bf16[256,512]{1,0:T(8,128)(2,1)S(1)} %pad_maximum_fusion.1), channel_id=1, source_target_pairs={{0,1},{1,0},{2,3},{3,2},{4,5},{5,4},{6,7},{7,6},{8,9},{9,8},{10,11... | collective-permute-start | bytes 786440 | tf_op jit(solution)/shard_map/ppermute | solution.py:524
  41.3 1.5 %collective-permute-start.12 = (bf16[256,512]{1,0:T(8,128)(2,1)S(1)}, bf16[256,512]{1,0:T(8,128)(2,1)S(1)}, u32[]{:S(2)}, u32[]{:S(2)}) collective-permute-start(bf16[256,512]{1,0:T(8,128)(2,1)S(1)} %pad_maximum_fusion.1), channel_id=1, source_target_pairs={{0,2},{1,3},{2,0},{3,1},{4,6},{5,7},{6,4},{7,5},{8,10},{9,11},{10,... | collective-permute-start | bytes 786440 | tf_op jit(solution)/shard_map/ppermute | solution.py:524
  43.3 8.5 %attend.1 = (bf16[768,512]{1,0:T(8,128)(2,1)S(1)}, f32[768,512]{1,0:T(8,128)S(1)}, bf16[768,2048]{1,0:T(8,128)(2,1)S(1)}) custom-call(f32[4]{0:T(128)S(1)} %rsqrt.3.inv_ref, s32[768,1]{1,0:T(8,128)S(1)} %reshape.68.slots_ref, bf16[512,512]{1,0:T(8,128)(2,1)S(1)} %constant_dynamic-update-slice_fusion.4.near_ref, ...), custom_call_target="tpu_custom_call" | custom-call | flops 3221225472 | bytes 16777216 | tf_op jit(solution)/shard_map/attend/pallas_call | solution.py:314
  51.8 6.9 %score.1 = (f32[768,1]{1,0:T(8,128)S(1)}, bf16[768,512]{1,0:T(8,128)(2,1)S(1)}, f32[768,512]{1,0:T(8,128)S(1)}) custom-call(f32[4]{0:T(128)S(1)} %rsqrt.3.inv_ref, bf16[768,512]{1,0:T(8,128)(2,1)S(1)} %get-tuple-element.47.queries_ref, f32[768,512]{1,0:T(8,128)S(1)} %get-tuple-element.48.attended_ref, s32[768,1]{1,0:T(8,128)S(1)} %reshape.69.labels_ref, ...), custom_call_target="tpu_custom_call" | custom-call | flops 4831838208 | bytes 8388608 | tf_op jit(solution)/shard_map/score/pallas_call | solution.py:386
  58.8 4.7 %attend_back.1.grad_rows_ref = bf16[768,512]{1,0:T(8,128)(2,1)S(1)} custom-call(bf16[768,512]{1,0:T(8,128)(2,1)S(1)} %get-tuple-element.50.grad_att_ref, f32[768,512]{1,0:T(8,128)S(1)} %get-tuple-element.51.direct_ref, bf16[768,2048]{1,0:T(8,128)(2,1)S(1)} %get-tuple-element.52.slope_ref, bf16[4,2048,512]{2,1,0:T(8,128)(2,1)S(1)} %bitcast.4), custom_call_target="tpu_custom_call" | custom-call | flops 3221225472 | bytes 8388608 | tf_op jit(solution)/shard_map/attend_back/pallas_call | solution.py:426
  64.6 1.2 %collective-permute-done.15.grad_rows_ref = bf16[768,512]{1,0:T(8,128)(2,1)S(1)} collective-permute-done((bf16[768,512]{1,0:T(8,128)(2,1)S(1)}, bf16[768,512]{1,0:T(8,128)(2,1)S(1)}, u32[]{:S(2)}, u32[]{:S(2)}) %collective-permute-start.15) | collective-permute-done | bytes 786464 | tf_op jit(solution)/shard_map/ppermute | solution.py:524
  65.8 1.8 %chip_terms.1 = bf16[512,512]{1,0:T(8,128)(2,1)S(1)} custom-call(s32[1]{0:T(128)} %bitcast.wide_ref, f32[1024,512]{1,0:T(8,128)S(1)} %own_cand_grad.1.cand_grad_ref, s32[1,768]{1,0:T(1,128)S(1)} %reshape.66.slots_ref, bf16[768,512]{1,0:T(8,128)(2,1)S(1)} %collective-permute-done.15.grad_rows_ref, bf16[1024,512]{1,0:T(8,128)(2,1)S(1)} %pad_maximum_fusion.pooled_ref), custom_call_target="tpu_custom_call" | custom-call | flops 1342177280 | bytes 4194304 | tf_op jit(solution)/shard_map/chip_terms/pallas_call | solution.py:497
  67.6 1.5 %collective-permute-start.16 = (bf16[128,512]{1,0:T(8,128)(2,1)S(1)}, bf16[128,512]{1,0:T(8,128)(2,1)S(1)}, u32[]{:S(2)}, u32[]{:S(2)}) collective-permute-start(bf16[128,512]{1,0:T(8,128)(2,1)S(1)} %get-tuple-element.66), channel_id=1, source_target_pairs={{0,1},{1,0},{2,3},{3,2},{4,5},{5,4},{6,7},{7,6},{8,9},{9,8},{10,11... | collective-permute-start | bytes 393224 | tf_op jit(solution)/shard_map/ppermute | solution.py:524
  69.1 1.5 %collective-permute-start.17 = (bf16[128,512]{1,0:T(8,128)(2,1)S(1)}, bf16[128,512]{1,0:T(8,128)(2,1)S(1)}, u32[]{:S(2)}, u32[]{:S(2)}) collective-permute-start(bf16[128,512]{1,0:T(8,128)(2,1)S(1)} %get-tuple-element.68), channel_id=1, source_target_pairs={{0,2},{1,3},{2,0},{3,1},{4,6},{5,7},{6,4},{7,5},{8,10},{9,11},{10,... | collective-permute-start | bytes 393224 | tf_op jit(solution)/shard_map/ppermute | solution.py:524
  71.9 1.7 %collective-permute-done.16 = bf16[128,512]{1,0:T(8,128)(2,1)S(1)} collective-permute-done((bf16[128,512]{1,0:T(8,128)(2,1)S(1)}, bf16[128,512]{1,0:T(8,128)(2,1)S(1)}, u32[]{:S(2)}, u32[]{:S(2)}) %collective-permute-start.16) | collective-permute-done | bytes 131104 | tf_op jit(solution)/shard_map/ppermute | solution.py:524
  73.6 3.6 %collective-permute-done.17 = bf16[128,512]{1,0:T(8,128)(2,1)S(1)} collective-permute-done((bf16[128,512]{1,0:T(8,128)(2,1)S(1)}, bf16[128,512]{1,0:T(8,128)(2,1)S(1)}, u32[]{:S(2)}, u32[]{:S(2)}) %collective-permute-start.17) | collective-permute-done | bytes 131104 | tf_op jit(solution)/shard_map/ppermute | solution.py:524
  77.3 1.4 %collective-permute-start.20 = (bf16[32,512]{1,0:T(8,128)(2,1)S(1)}, bf16[32,512]{1,0:T(8,128)(2,1)S(1)}, u32[]{:S(2)}, u32[]{:S(2)}) collective-permute-start(bf16[32,512]{1,0:T(8,128)(2,1)S(1)} %get-tuple-element.70), channel_id=1, source_target_pairs={{0,8},{1,9},{2,10},{3,11},{4,12},{5,13},{6,14},{7,15},{8,0},{9,1},... | collective-permute-start | bytes 98312 | tf_op jit(solution)/shard_map/ppermute | solution.py:524
  78.8 3.0 %collective-permute-start.21 = (bf16[32,512]{1,0:T(8,128)(2,1)S(1)}, bf16[32,512]{1,0:T(8,128)(2,1)S(1)}, u32[]{:S(2)}, u32[]{:S(2)}) collective-permute-start(bf16[32,512]{1,0:T(8,128)(2,1)S(1)} %get-tuple-element.71), channel_id=1, source_target_pairs={{0,12},{1,13},{2,14},{3,15},{4,8},{5,9},{6,10},{7,11},{8,4},{9,5},... | collective-permute-start | bytes 98312 | tf_op jit(solution)/shard_map/ppermute | solution.py:524
  82.5 1.9 %collective-permute-done.21 = bf16[32,512]{1,0:T(8,128)(2,1)S(1)} collective-permute-done((bf16[32,512]{1,0:T(8,128)(2,1)S(1)}, bf16[32,512]{1,0:T(8,128)(2,1)S(1)}, u32[]{:S(2)}, u32[]{:S(2)}) %collective-permute-start.21) | collective-permute-done | bytes 32800 | tf_op jit(solution)/shard_map/ppermute | solution.py:524
  (71 shorter events, 7.9 us)
Async XLA Ops:
  0.7 38.6 %copy-start.1 = (s32[4,2048]{1,0:T(4,128)S(1)}, s32[4,2048]{1,0:T(4,128)}, u32[]{:S(2)}) copy-start(s32[4,2048]{1,0:T(4,128)} %param.20) | copy-start | bytes 98308
  0.7 38.9 %copy-start.2 = (s32[768]{0:T(1024)S(1)}, s32[768]{0:T(1024)}, u32[]{:S(2)}) copy-start(s32[768]{0:T(1024)} %param.23) | copy-start | bytes 9220
  15.5 7.0 %collective-permute-start = (bf16[32,512]{1,0:T(8,128)(2,1)S(1)}, bf16[32,512]{1,0:T(8,128)(2,1)S(1)}, u32[]{:S(2)}, u32[]{:S(2)}) collective-permute-start(bf16[32,512]{1,0:T(8,128)(2,1)S(1)} %get-tuple-element.33), channel_id=1, source_target_pairs={{0,4},{1,5},{2,6},{3,7},{4,0},{5,1},{6,2},{7,3},{8,12},{9,13},{10,... | collective-permute-start | bytes 98312 | tf_op jit(solution)/shard_map/ppermute | solution.py:524
  18.6 5.4 %collective-permute-start.1 = (bf16[32,512]{1,0:T(8,128)(2,1)S(1)}, bf16[32,512]{1,0:T(8,128)(2,1)S(1)}, u32[]{:S(2)}, u32[]{:S(2)}) collective-permute-start(bf16[32,512]{1,0:T(8,128)(2,1)S(1)} %get-tuple-element.33), channel_id=1, source_target_pairs={{0,8},{1,9},{2,10},{3,11},{4,12},{5,13},{6,14},{7,15},{8,0},{9,1},... | collective-permute-start | bytes 98312 | tf_op jit(solution)/shard_map/ppermute | solution.py:524
  21.2 5.8 %collective-permute-start.2 = (bf16[32,512]{1,0:T(8,128)(2,1)S(1)}, bf16[32,512]{1,0:T(8,128)(2,1)S(1)}, u32[]{:S(2)}, u32[]{:S(2)}) collective-permute-start(bf16[32,512]{1,0:T(8,128)(2,1)S(1)} %get-tuple-element.33), channel_id=1, source_target_pairs={{0,12},{1,13},{2,14},{3,15},{4,8},{5,9},{6,10},{7,11},{8,4},{9,5},... | collective-permute-start | bytes 98312 | tf_op jit(solution)/shard_map/ppermute | solution.py:524
  21.3 1.2 %collective-permute-start.4 = (s32[768]{0:T(1024)S(1)}, s32[768]{0:T(1024)S(1)}, u32[]{:S(2)}, u32[]{:S(2)}) collective-permute-start(s32[768]{0:T(1024)S(1)} %get-tuple-element.81), channel_id=1, source_target_pairs={{0,16},{16,0},{1,17},{17,1},{2,18},{18,2},{3,19},{19,3},{4,20},{20... | collective-permute-start | bytes 9224 | tf_op jit(solution)/shard_map/ppermute | solution.py:524
  21.3 5.7 %collective-permute-start.3 = (bf16[32,512]{1,0:T(8,128)(2,1)S(1)}, bf16[32,512]{1,0:T(8,128)(2,1)S(1)}, u32[]{:S(2)}, u32[]{:S(2)}) collective-permute-start(bf16[32,512]{1,0:T(8,128)(2,1)S(1)} %get-tuple-element.35), channel_id=1, source_target_pairs={{0,16},{16,0},{1,17},{17,1},{2,18},{18,2},{3,19},{19,3},{4,20},{20... | collective-permute-start | bytes 98312 | tf_op jit(solution)/shard_map/ppermute | solution.py:524
  27.0 6.7 %collective-permute-start.10 = (bf16[64,512]{1,0:T(8,128)(2,1)S(1)}, bf16[64,512]{1,0:T(8,128)(2,1)S(1)}, u32[]{:S(2)}, u32[]{:S(2)}) collective-permute-start(bf16[64,512]{1,0:T(8,128)(2,1)S(1)} %maximum_select_fusion), channel_id=1, source_target_pairs={{0,12},{1,13},{2,14},{3,15},{4,8},{5,9},{6,10},{7,11},{8,4},{9,5},... | collective-permute-start | bytes 196616 | tf_op jit(solution)/shard_map/ppermute | solution.py:524
  27.4 11.6 %collective-permute-start.5 = (bf16[128,512]{1,0:T(8,128)(2,1)S(1)}, bf16[128,512]{1,0:T(8,128)(2,1)S(1)}, u32[]{:S(2)}, u32[]{:S(2)}) collective-permute-start(bf16[128,512]{1,0:T(8,128)(2,1)S(1)} %get-tuple-element.73), channel_id=1, source_target_pairs={{0,1},{1,0},{2,3},{3,2},{4,5},{5,4},{6,7},{7,6},{8,9},{9,8},{10,11... | collective-permute-start | bytes 393224 | tf_op jit(solution)/shard_map/ppermute | solution.py:524
  28.9 10.0 %collective-permute-start.6 = (bf16[128,512]{1,0:T(8,128)(2,1)S(1)}, bf16[128,512]{1,0:T(8,128)(2,1)S(1)}, u32[]{:S(2)}, u32[]{:S(2)}) collective-permute-start(bf16[128,512]{1,0:T(8,128)(2,1)S(1)} %get-tuple-element.73), channel_id=1, source_target_pairs={{0,2},{1,3},{2,0},{3,1},{4,6},{5,7},{6,4},{7,5},{8,10},{9,11},{10,... | collective-permute-start | bytes 393224 | tf_op jit(solution)/shard_map/ppermute | solution.py:524
  30.5 8.5 %collective-permute-start.7 = (bf16[128,512]{1,0:T(8,128)(2,1)S(1)}, bf16[128,512]{1,0:T(8,128)(2,1)S(1)}, u32[]{:S(2)}, u32[]{:S(2)}) collective-permute-start(bf16[128,512]{1,0:T(8,128)(2,1)S(1)} %get-tuple-element.73), channel_id=1, source_target_pairs={{0,3},{1,2},{2,1},{3,0},{4,7},{5,6},{6,5},{7,4},{8,11},{9,10},{10,... | collective-permute-start | bytes 393224 | tf_op jit(solution)/shard_map/ppermute | solution.py:524
  30.9 4.6 %collective-permute-start.8 = (bf16[64,512]{1,0:T(8,128)(2,1)S(1)}, bf16[64,512]{1,0:T(8,128)(2,1)S(1)}, u32[]{:S(2)}, u32[]{:S(2)}) collective-permute-start(bf16[64,512]{1,0:T(8,128)(2,1)S(1)} %maximum_select_fusion), channel_id=1, source_target_pairs={{0,4},{1,5},{2,6},{3,7},{4,0},{5,1},{6,2},{7,3},{8,12},{9,13},{10,... | collective-permute-start | bytes 196616 | tf_op jit(solution)/shard_map/ppermute | solution.py:524
  33.8 5.2 %collective-permute-start.9 = (bf16[64,512]{1,0:T(8,128)(2,1)S(1)}, bf16[64,512]{1,0:T(8,128)(2,1)S(1)}, u32[]{:S(2)}, u32[]{:S(2)}) collective-permute-start(bf16[64,512]{1,0:T(8,128)(2,1)S(1)} %maximum_select_fusion), channel_id=1, source_target_pairs={{0,8},{1,9},{2,10},{3,11},{4,12},{5,13},{6,14},{7,15},{8,0},{9,1},... | collective-permute-start | bytes 196616 | tf_op jit(solution)/shard_map/ppermute | solution.py:524
  39.0 4.3 %collective-permute-start.14 = (bf16[512,512]{1,0:T(8,128)(2,1)S(1)}, bf16[512,512]{1,0:T(8,128)(2,1)S(1)}, u32[]{:S(2)}, u32[]{:S(2)}) collective-permute-start(bf16[512,512]{1,0:T(8,128)(2,1)S(1)} %constant_dynamic-update-slice_fusion.4.near_ref), channel_id=1, source_target_pairs={{0,16},{16,0},{1,17},{17,1},{2,18},{18,2},{3,19},{19,3},{4,20},{20... | collective-permute-start | bytes 1572872 | tf_op jit(solution)/shard_map/ppermute | solution.py:524
  39.8 18.9 %collective-permute-start.11 = (bf16[256,512]{1,0:T(8,128)(2,1)S(1)}, bf16[256,512]{1,0:T(8,128)(2,1)S(1)}, u32[]{:S(2)}, u32[]{:S(2)}) collective-permute-start(bf16[256,512]{1,0:T(8,128)(2,1)S(1)} %pad_maximum_fusion.1), channel_id=1, source_target_pairs={{0,1},{1,0},{2,3},{3,2},{4,5},{5,4},{6,7},{7,6},{8,9},{9,8},{10,11... | collective-permute-start | bytes 786440 | tf_op jit(solution)/shard_map/ppermute | solution.py:524
  41.3 17.4 %collective-permute-start.12 = (bf16[256,512]{1,0:T(8,128)(2,1)S(1)}, bf16[256,512]{1,0:T(8,128)(2,1)S(1)}, u32[]{:S(2)}, u32[]{:S(2)}) collective-permute-start(bf16[256,512]{1,0:T(8,128)(2,1)S(1)} %pad_maximum_fusion.1), channel_id=1, source_target_pairs={{0,2},{1,3},{2,0},{3,1},{4,6},{5,7},{6,4},{7,5},{8,10},{9,11},{10,... | collective-permute-start | bytes 786440 | tf_op jit(solution)/shard_map/ppermute | solution.py:524
  42.8 15.9 %collective-permute-start.13 = (bf16[256,512]{1,0:T(8,128)(2,1)S(1)}, bf16[256,512]{1,0:T(8,128)(2,1)S(1)}, u32[]{:S(2)}, u32[]{:S(2)}) collective-permute-start(bf16[256,512]{1,0:T(8,128)(2,1)S(1)} %pad_maximum_fusion.1), channel_id=1, source_target_pairs={{0,3},{1,2},{2,1},{3,0},{4,7},{5,6},{6,5},{7,4},{8,11},{9,10},{10,... | collective-permute-start | bytes 786440 | tf_op jit(solution)/shard_map/ppermute | solution.py:524
  63.5 2.4 %collective-permute-start.15 = (bf16[768,512]{1,0:T(8,128)(2,1)S(1)}, bf16[768,512]{1,0:T(8,128)(2,1)S(1)}, u32[]{:S(2)}, u32[]{:S(2)}) collective-permute-start(bf16[768,512]{1,0:T(8,128)(2,1)S(1)} %attend_back.1.grad_rows_ref), channel_id=1, source_target_pairs={{0,16},{16,0},{1,17},{17,1},{2,18},{18,2},{3,19},{19,3},{4,20},{20... | collective-permute-start | bytes 2359304 | tf_op jit(solution)/shard_map/ppermute | solution.py:524
  67.6 6.0 %collective-permute-start.16 = (bf16[128,512]{1,0:T(8,128)(2,1)S(1)}, bf16[128,512]{1,0:T(8,128)(2,1)S(1)}, u32[]{:S(2)}, u32[]{:S(2)}) collective-permute-start(bf16[128,512]{1,0:T(8,128)(2,1)S(1)} %get-tuple-element.66), channel_id=1, source_target_pairs={{0,1},{1,0},{2,3},{3,2},{4,5},{5,4},{6,7},{7,6},{8,9},{9,8},{10,11... | collective-permute-start | bytes 393224 | tf_op jit(solution)/shard_map/ppermute | solution.py:524
  69.1 8.1 %collective-permute-start.17 = (bf16[128,512]{1,0:T(8,128)(2,1)S(1)}, bf16[128,512]{1,0:T(8,128)(2,1)S(1)}, u32[]{:S(2)}, u32[]{:S(2)}) collective-permute-start(bf16[128,512]{1,0:T(8,128)(2,1)S(1)} %get-tuple-element.68), channel_id=1, source_target_pairs={{0,2},{1,3},{2,0},{3,1},{4,6},{5,7},{6,4},{7,5},{8,10},{9,11},{10,... | collective-permute-start | bytes 393224 | tf_op jit(solution)/shard_map/ppermute | solution.py:524
  70.6 6.5 %collective-permute-start.18 = (bf16[128,512]{1,0:T(8,128)(2,1)S(1)}, bf16[128,512]{1,0:T(8,128)(2,1)S(1)}, u32[]{:S(2)}, u32[]{:S(2)}) collective-permute-start(bf16[128,512]{1,0:T(8,128)(2,1)S(1)} %get-tuple-element.67), channel_id=1, source_target_pairs={{0,3},{1,2},{2,1},{3,0},{4,7},{5,6},{6,5},{7,4},{8,11},{9,10},{10,... | collective-permute-start | bytes 393224 | tf_op jit(solution)/shard_map/ppermute | solution.py:524
  77.3 4.5 %collective-permute-start.19 = (bf16[32,512]{1,0:T(8,128)(2,1)S(1)}, bf16[32,512]{1,0:T(8,128)(2,1)S(1)}, u32[]{:S(2)}, u32[]{:S(2)}) collective-permute-start(bf16[32,512]{1,0:T(8,128)(2,1)S(1)} %get-tuple-element.69), channel_id=1, source_target_pairs={{0,4},{1,5},{2,6},{3,7},{4,0},{5,1},{6,2},{7,3},{8,12},{9,13},{10,... | collective-permute-start | bytes 98312 | tf_op jit(solution)/shard_map/ppermute | solution.py:524
  77.3 5.2 %collective-permute-start.20 = (bf16[32,512]{1,0:T(8,128)(2,1)S(1)}, bf16[32,512]{1,0:T(8,128)(2,1)S(1)}, u32[]{:S(2)}, u32[]{:S(2)}) collective-permute-start(bf16[32,512]{1,0:T(8,128)(2,1)S(1)} %get-tuple-element.70), channel_id=1, source_target_pairs={{0,8},{1,9},{2,10},{3,11},{4,12},{5,13},{6,14},{7,15},{8,0},{9,1},... | collective-permute-start | bytes 98312 | tf_op jit(solution)/shard_map/ppermute | solution.py:524
  78.8 5.7 %collective-permute-start.21 = (bf16[32,512]{1,0:T(8,128)(2,1)S(1)}, bf16[32,512]{1,0:T(8,128)(2,1)S(1)}, u32[]{:S(2)}, u32[]{:S(2)}) collective-permute-start(bf16[32,512]{1,0:T(8,128)(2,1)S(1)} %get-tuple-element.71), channel_id=1, source_target_pairs={{0,12},{1,13},{2,14},{3,15},{4,8},{5,9},{6,10},{7,11},{8,4},{9,5},... | collective-permute-start | bytes 98312 | tf_op jit(solution)/shard_map/ppermute | solution.py:524
  (7 other events, 129.9 us)

commit v3 on v2

--- a/solution.py
+++ b/solution.py
@@ -107,7 +107,11 @@
         sums_ref[cand] = jnp.sum(inputs, axis=0, keepdims=True)
 
     exponent = math.log2(math.e) / math.sqrt(head_dim)
-    frame_at = (lax.broadcasted_iota(jnp.int32, (patches, quad * lanes), 1) % lanes) // patches
+    half = lanes // 2
+    frame_at = (lax.broadcasted_iota(jnp.int32, (patches, 2 * lanes), 1) % half) // patches
+    even_lanes = lax.broadcasted_iota(jnp.int32, (half, 2 * lanes), 1) % lanes < half
+    first_half = lax.broadcasted_iota(jnp.int32, (head_dim, lanes), 1) < half
+    low_lanes = lax.broadcasted_iota(jnp.int32, (HEADS // quad, lanes), 1) < half
     nothing = jnp.zeros((head_dim, lanes), jnp.bfloat16)
     ones_row = lax.broadcasted_iota(jnp.int32, (2 * lanes, 2 * lanes), 0) // patches
     ones_column = lax.broadcasted_iota(jnp.int32, (2 * lanes, 2 * lanes), 1) // patches
@@ -117,32 +121,32 @@
     )
 
     def own_scores(block, head):
-        block_rows = slice(block * lanes, (block + 1) * lanes)
         start = head * head_dim
-        query = packed_ref[block_rows, start : start + span]
-        keys = packed_ref[block_rows, width + start : width + start + span].T
-        keys = jnp.concatenate(
-            [
-                jnp.concatenate(
-                    [nothing] * place
-                    + [keys[place * head_dim : (place + 1) * head_dim]]
-                    + [nothing] * (quad - 1 - place),
-                    axis=1,
+        low, high = (
+            packed_ref[block * lanes + side * half : block * lanes + (side + 1) * half, start : start + span]
+            for side in range(2)
+        )
+        keys = packed_ref[
+            block * lanes : (block + 1) * lanes, width + start : width + start + span
+        ].T
+        for turn in range(2):
+            query = jnp.where(even_lanes, low, high) if turn == 0 else jnp.where(even_lanes, high, low)
+            rows_of = []
+            for place in range(quad):
+                own_keys = keys[place * head_dim : (place + 1) * head_dim]
+                if (place + turn) % 2 == 0:
+                    own_keys = jnp.where(first_half, own_keys, nothing)
+                else:
+                    own_keys = jnp.where(first_half, nothing, own_keys)
+                both = [own_keys, nothing] if place < 2 else [nothing, own_keys]
+                rows_of.append(jnp.concatenate(both, axis=1))
+            scores = dot(query, jnp.concatenate(rows_of, axis=0))
+            found = scores[:patches]
+            for frame in range(1, half // patches):
+                found = jnp.where(
+                    frame_at == frame, scores[frame * patches : (frame + 1) * patches], found
                 )
-                for place in range(quad)
-            ],
-            axis=0,
-        )
-        scores = dot(query, keys)
-        found = scores[:patches]
-        for frame in range(1, lanes // patches):
-            found = jnp.where(
-                frame_at == frame, scores[frame * patches : (frame + 1) * patches], found
-            )
-        for side in range(quad // 2):
-            scores_ref[block, head // 2 + side] = found[
-                :, side * 2 * lanes : (side + 1) * 2 * lanes
-            ]
+            scores_ref[block, turn * (HEADS // quad) + head // quad] = found
 
     copies[0].wait()
     for cand in range(cands):
@@ -170,19 +174,27 @@
         totals = dot(exp_scores.astype(jnp.bfloat16), frame_ones)
         probs = (exp_scores / totals).reshape(blocks * pairs, patches, 2 * lanes)
         sums = jnp.sum(probs, axis=1)
-        key_sums = [
-            jnp.concatenate(
-                [
-                    sums[block * pairs : (block + 1) * pairs, side * lanes : (side + 1) * lanes]
-                    for block in range(blocks)
-                ],
-                axis=1,
-            )
-            for side in range(2)
-        ]
+        quads = HEADS // quad
+        key_sums = []
+        for pair in range(quad // 2):
+            sides = []
+            for side in range(2):
+                found = []
+                for block in range(blocks):
+                    first = sums[block * pairs : block * pairs + quads, pair * lanes : (pair + 1) * lanes]
+                    second = sums[
+                        block * pairs + quads : (block + 1) * pairs, pair * lanes : (pair + 1) * lanes
+                    ]
+                    if side == 1:
+                        first, second = second, first
+                    found.append(jnp.where(low_lanes, first, second))
+                sides.append(jnp.concatenate(found, axis=1))
+            key_sums.append(sides)
         spread = jnp.concatenate(
             [
-                jnp.where(own, key_sums[head % 2][head // 2 : head // 2 + 1], 0.0)
+                jnp.where(
+                    own, key_sums[head % quad // 2][head % 2][head // quad : head // quad + 1], 0.0
+                )
                 for head in range(HEADS)
             ],
             axis=0,
@@ -265,23 +277,21 @@
     far_ref,
     usable_ref,
     history_hbm,
+    mlp_hbm,
     queries_ref,
     attended_ref,
     slope_ref,
+    mlp_ref,
     history_ref,
     sems,
 ):
     users, events, _ = history_ref.shape
     chunk = math.gcd(events, 1024)
-    half_users = max(1, users // 2)
     copies = [
-        pltpu.make_async_copy(
-            history_hbm.at[pl.ds(user, half_users)],
-            history_ref.at[pl.ds(user, half_users)],
-            sems.at[user],
-        )
-        for user in range(0, users, half_users)
+        pltpu.make_async_copy(history_hbm.at[user], history_ref.at[user], sems.at[user])
+        for user in range(users)
     ]
+    copies.append(pltpu.make_async_copy(mlp_hbm, mlp_ref, sems.at[users]))
     for copy in copies:
         copy.start()
     slots = slots_ref[...]
@@ -292,8 +302,7 @@
     queries_ref[...] = queries.astype(jnp.bfloat16)
     per_user = slots.shape[0] // users
     for user in range(users):
-        if user % half_users == 0:
-            copies[user // half_users].wait()
+        copies[user].wait()
         rows = slice(user * per_user, (user + 1) * per_user)
         attended = jnp.zeros((per_user, key_width), jnp.float32)
         for at in range(0, events, chunk):
@@ -305,9 +314,10 @@
             slope_ref[rows, at : at + chunk] = (weights * (0.5 - half_gate)).astype(jnp.bfloat16)
             attended += dot(weights.astype(jnp.bfloat16), keys)
         attended_ref[rows, :] = attended * inv_ref[user]
-
-
-def attend(inv_count, slots, near, far, history, usable):
+    copies[users].wait()
+
+
+def attend(inv_count, slots, near, far, history, usable, mlp_weight):
     users, events, key_width = history.shape
     requests = slots.shape[0]
     whole = pl.BlockSpec(memory_space=pltpu.VMEM)
@@ -315,23 +325,24 @@
         attend_kernel,
         in_specs=[pl.BlockSpec(memory_space=pltpu.SMEM)]
         + [whole] * 4
-        + [pl.BlockSpec(memory_space=pltpu.HBM)],
-        out_specs=[whole] * 3,
+        + [pl.BlockSpec(memory_space=pltpu.HBM)] * 2,
+        out_specs=[whole] * 4,
         out_shape=[
             jax.ShapeDtypeStruct((requests, key_width), jnp.bfloat16),
             jax.ShapeDtypeStruct((requests, key_width), jnp.float32),
             jax.ShapeDtypeStruct((requests, events), jnp.bfloat16),
+            pltpu.VMEM(mlp_weight.shape, mlp_weight.dtype),
         ],
         scratch_shapes=[
             pltpu.VMEM(history.shape, history.dtype),
-            pltpu.SemaphoreType.DMA((users,)),
+            pltpu.SemaphoreType.DMA((users + 1,)),
         ],
         compiler_params=pltpu.CompilerParams(vmem_limit_bytes=32 * MIB),
         cost_estimate=pl.CostEstimate(
             flops=4 * requests * events * key_width, bytes_accessed=1 << 24, transcendentals=0
         ),
         name="attend",
-    )(inv_count, slots, near, far, usable, *in_hbm(history))
+    )(inv_count, slots, near, far, usable, *in_hbm(history, mlp_weight))
 
 
 def score_kernel(
@@ -605,8 +616,8 @@
         near = jnp.concatenate([near] + found, axis=0)
     far = exchange(near, "section", 2, 1)
     found_pooled = send_stage(pooled, wides, *stages[-1])
-    queries, attended, slope = attend(
-        inv_count, slots.reshape(requests, 1), near, far, history, usable
+    queries, attended, slope, mlp_weight = attend(
+        inv_count, slots.reshape(requests, 1), near, far, history, usable, mlp_weight
     )
     logits, grad_att, direct = score(
         inv_count,

time: 85.3 us -> 85.2 us (level)
  transfers between devices with their start and end apart: 22 -> 22, of which waited for: 11 -> 11; matrix products, arithmetic and copies ran while one was open for 2% -> 2% of each run, Pallas kernels for 19% -> 18%
where the time goes in v3:
time: 85.2 us; the launch traced here: 85.1 us
  Pallas kernels  37.3 us (44%)
  starting transfers between devices  23.3 us (27%)
  waiting for transfers between devices  21.1 us (25%)
  other arithmetic  1.83 us (2%)
  between operations  1.02 us (1%)
    ppermute x22, starting transfers between devices, exchange(): lax.ppermute(values, axis_name, [(i, i ^ distance) for i in range(size)])  23.3 us
    ppermute x22, waiting for transfers between devices, exchange(): lax.ppermute(values, axis_name, [(i, i ^ distance) for i in range(size)])  21.1 us
    pallas_call x1, Pallas kernels, encode_block(): pl.pallas_call(functools.partial(encode_kernel, tokens), in_specs=[pl.Blo...  15.3 us
    pallas_call x1, Pallas kernels, attend(): pl.pallas_call(attend_kernel, in_specs=[pl.BlockSpec(memory_space=pltpu.S...  7.75 us
    pallas_call x1, Pallas kernels, score(): pl.pallas_call(score_kernel, in_specs=[pl.BlockSpec(memory_space=pltpu.SM...  6.88 us
    pallas_call x1, Pallas kernels, attend_back(): pl.pallas_call(attend_back_kernel, in_specs=[whole] * 4, out_specs=whole,...  4.69 us
    pallas_call x1, Pallas kernels, chip_terms(): pl.pallas_call(functools.partial(terms_kernel, origins), in_specs=[pl.Blo...  1.75 us
  transfers between devices with their start and end apart: 22, of which 11 were waited for; matrix products, arithmetic and copies ran while one was open for 2% of the time, Pallas kernels for 18%

profile of v3, /device:TPU:0, one launch (start us, length us, event | category | flops | bytes accessed | tf_op | source)
XLA Modules:
  0.0 85.1 jit_solution(8046503174109159133)
XLA Ops:
  0.7 15.3 %encode.1 = (bf16[32,512]{1,0:T(8,128)(2,1)S(1)}, bf16[32,512]{1,0:T(8,128)(2,1)S(1)}, bf16[32,512]{1,0:T(8,128)(2,1)S(1)}) custom-call(s32[1]{0:T(128)} %bitcast.1.core_ref, bf16[1536,1024]{1,0:T(8,128)(2,1)} %bitcast.5, bf16[1024,3072]{1,0:T(8,128)(2,1)} %qkv_hbm.1, bf16[1024,1024]{1,0:T(8,128)(2,1)} %out_hbm.1, bf16[1024,512]{1,0:T(8,128)(2,1)} %proj_hbm.1), custom_call_target="tpu_custom_call" | custom-call | flops 8053063680 | bytes 16777216 | tf_op jit(solution)/shard_map/encode/pallas_call | solution.py:243
  16.0 3.1 %collective-permute-start = (bf16[32,512]{1,0:T(8,128)(2,1)S(1)}, bf16[32,512]{1,0:T(8,128)(2,1)S(1)}, u32[]{:S(2)}, u32[]{:S(2)}) collective-permute-start(bf16[32,512]{1,0:T(8,128)(2,1)S(1)} %get-tuple-element.34), channel_id=1, source_target_pairs={{0,4},{1,5},{2,6},{3,7},{4,0},{5,1},{6,2},{7,3},{8,12},{9,13},{10,... | collective-permute-start | bytes 98312 | tf_op jit(solution)/shard_map/ppermute | solution.py:535
  19.1 2.6 %collective-permute-start.1 = (bf16[32,512]{1,0:T(8,128)(2,1)S(1)}, bf16[32,512]{1,0:T(8,128)(2,1)S(1)}, u32[]{:S(2)}, u32[]{:S(2)}) collective-permute-start(bf16[32,512]{1,0:T(8,128)(2,1)S(1)} %get-tuple-element.34), channel_id=1, source_target_pairs={{0,8},{1,9},{2,10},{3,11},{4,12},{5,13},{6,14},{7,15},{8,0},{9,1},... | collective-permute-start | bytes 98312 | tf_op jit(solution)/shard_map/ppermute | solution.py:535
  23.0 1.5 %collective-permute-done.1 = bf16[32,512]{1,0:T(8,128)(2,1)S(1)} collective-permute-done((bf16[32,512]{1,0:T(8,128)(2,1)S(1)}, bf16[32,512]{1,0:T(8,128)(2,1)S(1)}, u32[]{:S(2)}, u32[]{:S(2)}) %collective-permute-start.1) | collective-permute-done | bytes 32800 | tf_op jit(solution)/shard_map/ppermute | solution.py:535
  24.5 3.0 %collective-permute-done.2 = bf16[32,512]{1,0:T(8,128)(2,1)S(1)} collective-permute-done((bf16[32,512]{1,0:T(8,128)(2,1)S(1)}, bf16[32,512]{1,0:T(8,128)(2,1)S(1)}, u32[]{:S(2)}, u32[]{:S(2)}) %collective-permute-start.2) | collective-permute-done | bytes 32800 | tf_op jit(solution)/shard_map/ppermute | solution.py:535
  27.8 1.6 %collective-permute-start.5 = (bf16[128,512]{1,0:T(8,128)(2,1)S(1)}, bf16[128,512]{1,0:T(8,128)(2,1)S(1)}, u32[]{:S(2)}, u32[]{:S(2)}) collective-permute-start(bf16[128,512]{1,0:T(8,128)(2,1)S(1)} %get-tuple-element.75), channel_id=1, source_target_pairs={{0,1},{1,0},{2,3},{3,2},{4,5},{5,4},{6,7},{7,6},{8,9},{9,8},{10,11... | collective-permute-start | bytes 393224 | tf_op jit(solution)/shard_map/ppermute | solution.py:535
  29.4 1.5 %collective-permute-start.6 = (bf16[128,512]{1,0:T(8,128)(2,1)S(1)}, bf16[128,512]{1,0:T(8,128)(2,1)S(1)}, u32[]{:S(2)}, u32[]{:S(2)}) collective-permute-start(bf16[128,512]{1,0:T(8,128)(2,1)S(1)} %get-tuple-element.75), channel_id=1, source_target_pairs={{0,2},{1,3},{2,0},{3,1},{4,6},{5,7},{6,4},{7,5},{8,10},{9,11},{10,... | collective-permute-start | bytes 393224 | tf_op jit(solution)/shard_map/ppermute | solution.py:535
  31.4 2.8 %collective-permute-done.10 = bf16[64,512]{1,0:T(8,128)(2,1)S(1)} collective-permute-done((bf16[64,512]{1,0:T(8,128)(2,1)S(1)}, bf16[64,512]{1,0:T(8,128)(2,1)S(1)}, u32[]{:S(2)}, u32[]{:S(2)}) %collective-permute-start.10) | collective-permute-done | bytes 65568 | tf_op jit(solution)/shard_map/ppermute | solution.py:535
  34.2 1.3 %collective-permute-start.9 = (bf16[64,512]{1,0:T(8,128)(2,1)S(1)}, bf16[64,512]{1,0:T(8,128)(2,1)S(1)}, u32[]{:S(2)}, u32[]{:S(2)}) collective-permute-start(bf16[64,512]{1,0:T(8,128)(2,1)S(1)} %maximum_select_fusion), channel_id=1, source_target_pairs={{0,8},{1,9},{2,10},{3,11},{4,12},{5,13},{6,14},{7,15},{8,0},{9,1},... | collective-permute-start | bytes 196616 | tf_op jit(solution)/shard_map/ppermute | solution.py:535
  36.1 3.4 %collective-permute-done.9 = bf16[64,512]{1,0:T(8,128)(2,1)S(1)} collective-permute-done((bf16[64,512]{1,0:T(8,128)(2,1)S(1)}, bf16[64,512]{1,0:T(8,128)(2,1)S(1)}, u32[]{:S(2)}, u32[]{:S(2)}) %collective-permute-start.9) | collective-permute-done | bytes 65568 | tf_op jit(solution)/shard_map/ppermute | solution.py:535
  40.4 1.6 %collective-permute-start.11 = (bf16[256,512]{1,0:T(8,128)(2,1)S(1)}, bf16[256,512]{1,0:T(8,128)(2,1)S(1)}, u32[]{:S(2)}, u32[]{:S(2)}) collective-permute-start(bf16[256,512]{1,0:T(8,128)(2,1)S(1)} %pad_maximum_fusion.1), channel_id=1, source_target_pairs={{0,1},{1,0},{2,3},{3,2},{4,5},{5,4},{6,7},{7,6},{8,9},{9,8},{10,11... | collective-permute-start | bytes 786440 | tf_op jit(solution)/shard_map/ppermute | solution.py:535
  42.0 1.5 %collective-permute-start.12 = (bf16[256,512]{1,0:T(8,128)(2,1)S(1)}, bf16[256,512]{1,0:T(8,128)(2,1)S(1)}, u32[]{:S(2)}, u32[]{:S(2)}) collective-permute-start(bf16[256,512]{1,0:T(8,128)(2,1)S(1)} %pad_maximum_fusion.1), channel_id=1, source_target_pairs={{0,2},{1,3},{2,0},{3,1},{4,6},{5,7},{6,4},{7,5},{8,10},{9,11},{10,... | collective-permute-start | bytes 786440 | tf_op jit(solution)/shard_map/ppermute | solution.py:535
  44.0 7.8 %attend.1 = (bf16[768,512]{1,0:T(8,128)(2,1)S(1)}, f32[768,512]{1,0:T(8,128)S(1)}, bf16[768,2048]{1,0:T(8,128)(2,1)S(1)}, bf16[1536,1024]{1,0:T(8,128)(2,1)S(1)}) custom-call(f32[4]{0:T(128)S(1)} %rsqrt.3.inv_ref, s32[768,1]{1,0:T(8,128)S(1)} %reshape.68.slots_ref, bf16[512,512]{1,0:T(8,128)(2,1)S(1)} %constant_dynamic-update-slice_fusion.4.near_ref, ...), custom_call_target="tpu_custom_call" | custom-call | flops 3221225472 | bytes 16777216 | tf_op jit(solution)/shard_map/attend/pallas_call | solution.py:324
  51.7 6.9 %score.1 = (f32[768,1]{1,0:T(8,128)S(1)}, bf16[768,512]{1,0:T(8,128)(2,1)S(1)}, f32[768,512]{1,0:T(8,128)S(1)}) custom-call(f32[4]{0:T(128)S(1)} %rsqrt.3.inv_ref, bf16[768,512]{1,0:T(8,128)(2,1)S(1)} %get-tuple-element.48.queries_ref, f32[768,512]{1,0:T(8,128)S(1)} %get-tuple-element.49.attended_ref, s32[768,1]{1,0:T(8,128)S(1)} %reshape.69.labels_ref, ...), custom_call_target="tpu_custom_call" | custom-call | flops 4831838208 | bytes 8388608 | tf_op jit(solution)/shard_map/score/pallas_call | solution.py:397
  58.7 4.7 %attend_back.1.grad_rows_ref = bf16[768,512]{1,0:T(8,128)(2,1)S(1)} custom-call(bf16[768,512]{1,0:T(8,128)(2,1)S(1)} %get-tuple-element.52.grad_att_ref, f32[768,512]{1,0:T(8,128)S(1)} %get-tuple-element.53.direct_ref, bf16[768,2048]{1,0:T(8,128)(2,1)S(1)} %get-tuple-element.54.slope_ref, bf16[4,2048,512]{2,1,0:T(8,128)(2,1)S(1)} %bitcast.4), custom_call_target="tpu_custom_call" | custom-call | flops 3221225472 | bytes 8388608 | tf_op jit(solution)/shard_map/attend_back/pallas_call | solution.py:437
  64.5 1.2 %collective-permute-done.15.grad_rows_ref = bf16[768,512]{1,0:T(8,128)(2,1)S(1)} collective-permute-done((bf16[768,512]{1,0:T(8,128)(2,1)S(1)}, bf16[768,512]{1,0:T(8,128)(2,1)S(1)}, u32[]{:S(2)}, u32[]{:S(2)}) %collective-permute-start.15) | collective-permute-done | bytes 786464 | tf_op jit(solution)/shard_map/ppermute | solution.py:535
  65.7 1.7 %chip_terms.1 = bf16[512,512]{1,0:T(8,128)(2,1)S(1)} custom-call(s32[1]{0:T(128)} %bitcast.wide_ref, f32[1024,512]{1,0:T(8,128)S(1)} %own_cand_grad.1.cand_grad_ref, s32[1,768]{1,0:T(1,128)S(1)} %reshape.66.slots_ref, bf16[768,512]{1,0:T(8,128)(2,1)S(1)} %collective-permute-done.15.grad_rows_ref, bf16[1024,512]{1,0:T(8,128)(2,1)S(1)} %pad_maximum_fusion.pooled_ref), custom_call_target="tpu_custom_call" | custom-call | flops 1342177280 | bytes 4194304 | tf_op jit(solution)/shard_map/chip_terms/pallas_call | solution.py:508
  67.5 1.6 %collective-permute-start.16 = (bf16[128,512]{1,0:T(8,128)(2,1)S(1)}, bf16[128,512]{1,0:T(8,128)(2,1)S(1)}, u32[]{:S(2)}, u32[]{:S(2)}) collective-permute-start(bf16[128,512]{1,0:T(8,128)(2,1)S(1)} %get-tuple-element.68), channel_id=1, source_target_pairs={{0,1},{1,0},{2,3},{3,2},{4,5},{5,4},{6,7},{7,6},{8,9},{9,8},{10,11... | collective-permute-start | bytes 393224 | tf_op jit(solution)/shard_map/ppermute | solution.py:535
  69.1 1.5 %collective-permute-start.17 = (bf16[128,512]{1,0:T(8,128)(2,1)S(1)}, bf16[128,512]{1,0:T(8,128)(2,1)S(1)}, u32[]{:S(2)}, u32[]{:S(2)}) collective-permute-start(bf16[128,512]{1,0:T(8,128)(2,1)S(1)} %get-tuple-element.70), channel_id=1, source_target_pairs={{0,2},{1,3},{2,0},{3,1},{4,6},{5,7},{6,4},{7,5},{8,10},{9,11},{10,... | collective-permute-start | bytes 393224 | tf_op jit(solution)/shard_map/ppermute | solution.py:535
  71.9 1.6 %collective-permute-done.16 = bf16[128,512]{1,0:T(8,128)(2,1)S(1)} collective-permute-done((bf16[128,512]{1,0:T(8,128)(2,1)S(1)}, bf16[128,512]{1,0:T(8,128)(2,1)S(1)}, u32[]{:S(2)}, u32[]{:S(2)}) %collective-permute-start.16) | collective-permute-done | bytes 131104 | tf_op jit(solution)/shard_map/ppermute | solution.py:535
  73.5 3.7 %collective-permute-done.17 = bf16[128,512]{1,0:T(8,128)(2,1)S(1)} collective-permute-done((bf16[128,512]{1,0:T(8,128)(2,1)S(1)}, bf16[128,512]{1,0:T(8,128)(2,1)S(1)}, u32[]{:S(2)}, u32[]{:S(2)}) %collective-permute-start.17) | collective-permute-done | bytes 131104 | tf_op jit(solution)/shard_map/ppermute | solution.py:535
  77.3 1.4 %collective-permute-start.20 = (bf16[32,512]{1,0:T(8,128)(2,1)S(1)}, bf16[32,512]{1,0:T(8,128)(2,1)S(1)}, u32[]{:S(2)}, u32[]{:S(2)}) collective-permute-start(bf16[32,512]{1,0:T(8,128)(2,1)S(1)} %get-tuple-element.72), channel_id=1, source_target_pairs={{0,8},{1,9},{2,10},{3,11},{4,12},{5,13},{6,14},{7,15},{8,0},{9,1},... | collective-permute-start | bytes 98312 | tf_op jit(solution)/shard_map/ppermute | solution.py:535
  78.7 3.0 %collective-permute-start.21 = (bf16[32,512]{1,0:T(8,128)(2,1)S(1)}, bf16[32,512]{1,0:T(8,128)(2,1)S(1)}, u32[]{:S(2)}, u32[]{:S(2)}) collective-permute-start(bf16[32,512]{1,0:T(8,128)(2,1)S(1)} %get-tuple-element.73), channel_id=1, source_target_pairs={{0,12},{1,13},{2,14},{3,15},{4,8},{5,9},{6,10},{7,11},{8,4},{9,5},... | collective-permute-start | bytes 98312 | tf_op jit(solution)/shard_map/ppermute | solution.py:535
  82.5 1.9 %collective-permute-done.21 = bf16[32,512]{1,0:T(8,128)(2,1)S(1)} collective-permute-done((bf16[32,512]{1,0:T(8,128)(2,1)S(1)}, bf16[32,512]{1,0:T(8,128)(2,1)S(1)}, u32[]{:S(2)}, u32[]{:S(2)}) %collective-permute-start.21) | collective-permute-done | bytes 32800 | tf_op jit(solution)/shard_map/ppermute | solution.py:535
  (69 shorter events, 8.0 us)
Async XLA Ops:
  0.7 39.3 %copy-start = (s32[4,2048]{1,0:T(4,128)S(1)}, s32[4,2048]{1,0:T(4,128)}, u32[]{:S(2)}) copy-start(s32[4,2048]{1,0:T(4,128)} %param.20) | copy-start | bytes 98308
  0.7 39.5 %copy-start.1 = (s32[768]{0:T(1024)S(1)}, s32[768]{0:T(1024)}, u32[]{:S(2)}) copy-start(s32[768]{0:T(1024)} %param.23) | copy-start | bytes 9220
  16.0 7.0 %collective-permute-start = (bf16[32,512]{1,0:T(8,128)(2,1)S(1)}, bf16[32,512]{1,0:T(8,128)(2,1)S(1)}, u32[]{:S(2)}, u32[]{:S(2)}) collective-permute-start(bf16[32,512]{1,0:T(8,128)(2,1)S(1)} %get-tuple-element.34), channel_id=1, source_target_pairs={{0,4},{1,5},{2,6},{3,7},{4,0},{5,1},{6,2},{7,3},{8,12},{9,13},{10,... | collective-permute-start | bytes 98312 | tf_op jit(solution)/shard_map/ppermute | solution.py:535
  19.1 5.4 %collective-permute-start.1 = (bf16[32,512]{1,0:T(8,128)(2,1)S(1)}, bf16[32,512]{1,0:T(8,128)(2,1)S(1)}, u32[]{:S(2)}, u32[]{:S(2)}) collective-permute-start(bf16[32,512]{1,0:T(8,128)(2,1)S(1)} %get-tuple-element.34), channel_id=1, source_target_pairs={{0,8},{1,9},{2,10},{3,11},{4,12},{5,13},{6,14},{7,15},{8,0},{9,1},... | collective-permute-start | bytes 98312 | tf_op jit(solution)/shard_map/ppermute | solution.py:535
  21.7 5.8 %collective-permute-start.2 = (bf16[32,512]{1,0:T(8,128)(2,1)S(1)}, bf16[32,512]{1,0:T(8,128)(2,1)S(1)}, u32[]{:S(2)}, u32[]{:S(2)}) collective-permute-start(bf16[32,512]{1,0:T(8,128)(2,1)S(1)} %get-tuple-element.34), channel_id=1, source_target_pairs={{0,12},{1,13},{2,14},{3,15},{4,8},{5,9},{6,10},{7,11},{8,4},{9,5},... | collective-permute-start | bytes 98312 | tf_op jit(solution)/shard_map/ppermute | solution.py:535
  21.7 1.2 %collective-permute-start.4 = (s32[768]{0:T(1024)S(1)}, s32[768]{0:T(1024)S(1)}, u32[]{:S(2)}, u32[]{:S(2)}) collective-permute-start(s32[768]{0:T(1024)S(1)} %get-tuple-element.83), channel_id=1, source_target_pairs={{0,16},{16,0},{1,17},{17,1},{2,18},{18,2},{3,19},{19,3},{4,20},{20... | collective-permute-start | bytes 9224 | tf_op jit(solution)/shard_map/ppermute | solution.py:535
  21.8 5.7 %collective-permute-start.3 = (bf16[32,512]{1,0:T(8,128)(2,1)S(1)}, bf16[32,512]{1,0:T(8,128)(2,1)S(1)}, u32[]{:S(2)}, u32[]{:S(2)}) collective-permute-start(bf16[32,512]{1,0:T(8,128)(2,1)S(1)} %get-tuple-element.36), channel_id=1, source_target_pairs={{0,16},{16,0},{1,17},{17,1},{2,18},{18,2},{3,19},{19,3},{4,20},{20... | collective-permute-start | bytes 98312 | tf_op jit(solution)/shard_map/ppermute | solution.py:535
  27.5 6.7 %collective-permute-start.10 = (bf16[64,512]{1,0:T(8,128)(2,1)S(1)}, bf16[64,512]{1,0:T(8,128)(2,1)S(1)}, u32[]{:S(2)}, u32[]{:S(2)}) collective-permute-start(bf16[64,512]{1,0:T(8,128)(2,1)S(1)} %maximum_select_fusion), channel_id=1, source_target_pairs={{0,12},{1,13},{2,14},{3,15},{4,8},{5,9},{6,10},{7,11},{8,4},{9,5},... | collective-permute-start | bytes 196616 | tf_op jit(solution)/shard_map/ppermute | solution.py:535
  27.8 11.6 %collective-permute-start.5 = (bf16[128,512]{1,0:T(8,128)(2,1)S(1)}, bf16[128,512]{1,0:T(8,128)(2,1)S(1)}, u32[]{:S(2)}, u32[]{:S(2)}) collective-permute-start(bf16[128,512]{1,0:T(8,128)(2,1)S(1)} %get-tuple-element.75), channel_id=1, source_target_pairs={{0,1},{1,0},{2,3},{3,2},{4,5},{5,4},{6,7},{7,6},{8,9},{9,8},{10,11... | collective-permute-start | bytes 393224 | tf_op jit(solution)/shard_map/ppermute | solution.py:535
  29.4 10.0 %collective-permute-start.6 = (bf16[128,512]{1,0:T(8,128)(2,1)S(1)}, bf16[128,512]{1,0:T(8,128)(2,1)S(1)}, u32[]{:S(2)}, u32[]{:S(2)}) collective-permute-start(bf16[128,512]{1,0:T(8,128)(2,1)S(1)} %get-tuple-element.75), channel_id=1, source_target_pairs={{0,2},{1,3},{2,0},{3,1},{4,6},{5,7},{6,4},{7,5},{8,10},{9,11},{10,... | collective-permute-start | bytes 393224 | tf_op jit(solution)/shard_map/ppermute | solution.py:535
  30.9 8.5 %collective-permute-start.7 = (bf16[128,512]{1,0:T(8,128)(2,1)S(1)}, bf16[128,512]{1,0:T(8,128)(2,1)S(1)}, u32[]{:S(2)}, u32[]{:S(2)}) collective-permute-start(bf16[128,512]{1,0:T(8,128)(2,1)S(1)} %get-tuple-element.75), channel_id=1, source_target_pairs={{0,3},{1,2},{2,1},{3,0},{4,7},{5,6},{6,5},{7,4},{8,11},{9,10},{10,... | collective-permute-start | bytes 393224 | tf_op jit(solution)/shard_map/ppermute | solution.py:535
  31.4 4.7 %collective-permute-start.8 = (bf16[64,512]{1,0:T(8,128)(2,1)S(1)}, bf16[64,512]{1,0:T(8,128)(2,1)S(1)}, u32[]{:S(2)}, u32[]{:S(2)}) collective-permute-start(bf16[64,512]{1,0:T(8,128)(2,1)S(1)} %maximum_select_fusion), channel_id=1, source_target_pairs={{0,4},{1,5},{2,6},{3,7},{4,0},{5,1},{6,2},{7,3},{8,12},{9,13},{10,... | collective-permute-start | bytes 196616 | tf_op jit(solution)/shard_map/ppermute | solution.py:535
  34.2 5.2 %collective-permute-start.9 = (bf16[64,512]{1,0:T(8,128)(2,1)S(1)}, bf16[64,512]{1,0:T(8,128)(2,1)S(1)}, u32[]{:S(2)}, u32[]{:S(2)}) collective-permute-start(bf16[64,512]{1,0:T(8,128)(2,1)S(1)} %maximum_select_fusion), channel_id=1, source_target_pairs={{0,8},{1,9},{2,10},{3,11},{4,12},{5,13},{6,14},{7,15},{8,0},{9,1},... | collective-permute-start | bytes 196616 | tf_op jit(solution)/shard_map/ppermute | solution.py:535
  39.5 4.5 %collective-permute-start.14 = (bf16[512,512]{1,0:T(8,128)(2,1)S(1)}, bf16[512,512]{1,0:T(8,128)(2,1)S(1)}, u32[]{:S(2)}, u32[]{:S(2)}) collective-permute-start(bf16[512,512]{1,0:T(8,128)(2,1)S(1)} %constant_dynamic-update-slice_fusion.4.near_ref), channel_id=1, source_target_pairs={{0,16},{16,0},{1,17},{17,1},{2,18},{18,2},{3,19},{19,3},{4,20},{20... | collective-permute-start | bytes 1572872 | tf_op jit(solution)/shard_map/ppermute | solution.py:535
  40.4 18.2 %collective-permute-start.11 = (bf16[256,512]{1,0:T(8,128)(2,1)S(1)}, bf16[256,512]{1,0:T(8,128)(2,1)S(1)}, u32[]{:S(2)}, u32[]{:S(2)}) collective-permute-start(bf16[256,512]{1,0:T(8,128)(2,1)S(1)} %pad_maximum_fusion.1), channel_id=1, source_target_pairs={{0,1},{1,0},{2,3},{3,2},{4,5},{5,4},{6,7},{7,6},{8,9},{9,8},{10,11... | collective-permute-start | bytes 786440 | tf_op jit(solution)/shard_map/ppermute | solution.py:535
  42.0 16.7 %collective-permute-start.12 = (bf16[256,512]{1,0:T(8,128)(2,1)S(1)}, bf16[256,512]{1,0:T(8,128)(2,1)S(1)}, u32[]{:S(2)}, u32[]{:S(2)}) collective-permute-start(bf16[256,512]{1,0:T(8,128)(2,1)S(1)} %pad_maximum_fusion.1), channel_id=1, source_target_pairs={{0,2},{1,3},{2,0},{3,1},{4,6},{5,7},{6,4},{7,5},{8,10},{9,11},{10,... | collective-permute-start | bytes 786440 | tf_op jit(solution)/shard_map/ppermute | solution.py:535
  43.5 15.2 %collective-permute-start.13 = (bf16[256,512]{1,0:T(8,128)(2,1)S(1)}, bf16[256,512]{1,0:T(8,128)(2,1)S(1)}, u32[]{:S(2)}, u32[]{:S(2)}) collective-permute-start(bf16[256,512]{1,0:T(8,128)(2,1)S(1)} %pad_maximum_fusion.1), channel_id=1, source_target_pairs={{0,3},{1,2},{2,1},{3,0},{4,7},{5,6},{6,5},{7,4},{8,11},{9,10},{10,... | collective-permute-start | bytes 786440 | tf_op jit(solution)/shard_map/ppermute | solution.py:535
  63.4 2.4 %collective-permute-start.15 = (bf16[768,512]{1,0:T(8,128)(2,1)S(1)}, bf16[768,512]{1,0:T(8,128)(2,1)S(1)}, u32[]{:S(2)}, u32[]{:S(2)}) collective-permute-start(bf16[768,512]{1,0:T(8,128)(2,1)S(1)} %attend_back.1.grad_rows_ref), channel_id=1, source_target_pairs={{0,16},{16,0},{1,17},{17,1},{2,18},{18,2},{3,19},{19,3},{4,20},{20... | collective-permute-start | bytes 2359304 | tf_op jit(solution)/shard_map/ppermute | solution.py:535
  67.5 6.0 %collective-permute-start.16 = (bf16[128,512]{1,0:T(8,128)(2,1)S(1)}, bf16[128,512]{1,0:T(8,128)(2,1)S(1)}, u32[]{:S(2)}, u32[]{:S(2)}) collective-permute-start(bf16[128,512]{1,0:T(8,128)(2,1)S(1)} %get-tuple-element.68), channel_id=1, source_target_pairs={{0,1},{1,0},{2,3},{3,2},{4,5},{5,4},{6,7},{7,6},{8,9},{9,8},{10,11... | collective-permute-start | bytes 393224 | tf_op jit(solution)/shard_map/ppermute | solution.py:535
  69.1 8.1 %collective-permute-start.17 = (bf16[128,512]{1,0:T(8,128)(2,1)S(1)}, bf16[128,512]{1,0:T(8,128)(2,1)S(1)}, u32[]{:S(2)}, u32[]{:S(2)}) collective-permute-start(bf16[128,512]{1,0:T(8,128)(2,1)S(1)} %get-tuple-element.70), channel_id=1, source_target_pairs={{0,2},{1,3},{2,0},{3,1},{4,6},{5,7},{6,4},{7,5},{8,10},{9,11},{10,... | collective-permute-start | bytes 393224 | tf_op jit(solution)/shard_map/ppermute | solution.py:535
  70.6 6.6 %collective-permute-start.18 = (bf16[128,512]{1,0:T(8,128)(2,1)S(1)}, bf16[128,512]{1,0:T(8,128)(2,1)S(1)}, u32[]{:S(2)}, u32[]{:S(2)}) collective-permute-start(bf16[128,512]{1,0:T(8,128)(2,1)S(1)} %get-tuple-element.69), channel_id=1, source_target_pairs={{0,3},{1,2},{2,1},{3,0},{4,7},{5,6},{6,5},{7,4},{8,11},{9,10},{10,... | collective-permute-start | bytes 393224 | tf_op jit(solution)/shard_map/ppermute | solution.py:535
  77.2 4.5 %collective-permute-start.19 = (bf16[32,512]{1,0:T(8,128)(2,1)S(1)}, bf16[32,512]{1,0:T(8,128)(2,1)S(1)}, u32[]{:S(2)}, u32[]{:S(2)}) collective-permute-start(bf16[32,512]{1,0:T(8,128)(2,1)S(1)} %get-tuple-element.71), channel_id=1, source_target_pairs={{0,4},{1,5},{2,6},{3,7},{4,0},{5,1},{6,2},{7,3},{8,12},{9,13},{10,... | collective-permute-start | bytes 98312 | tf_op jit(solution)/shard_map/ppermute | solution.py:535
  77.3 5.2 %collective-permute-start.20 = (bf16[32,512]{1,0:T(8,128)(2,1)S(1)}, bf16[32,512]{1,0:T(8,128)(2,1)S(1)}, u32[]{:S(2)}, u32[]{:S(2)}) collective-permute-start(bf16[32,512]{1,0:T(8,128)(2,1)S(1)} %get-tuple-element.72), channel_id=1, source_target_pairs={{0,8},{1,9},{2,10},{3,11},{4,12},{5,13},{6,14},{7,15},{8,0},{9,1},... | collective-permute-start | bytes 98312 | tf_op jit(solution)/shard_map/ppermute | solution.py:535
  78.7 5.7 %collective-permute-start.21 = (bf16[32,512]{1,0:T(8,128)(2,1)S(1)}, bf16[32,512]{1,0:T(8,128)(2,1)S(1)}, u32[]{:S(2)}, u32[]{:S(2)}) collective-permute-start(bf16[32,512]{1,0:T(8,128)(2,1)S(1)} %get-tuple-element.73), channel_id=1, source_target_pairs={{0,12},{1,13},{2,14},{3,15},{4,8},{5,9},{6,10},{7,11},{8,4},{9,5},... | collective-permute-start | bytes 98312 | tf_op jit(solution)/shard_map/ppermute | solution.py:535
  (6 other events, 119.6 us)

commit v4 on v2

--- a/solution.py
+++ b/solution.py
@@ -97,8 +97,8 @@
         pltpu.make_async_copy(source, target, sems.at[place])
         for place, (source, target) in enumerate(pieces)
     ]
-    for copy in copies:
-        copy.start()
+    copies[0].start()
+    copies[1].start()
 
     def norm_cand(cand):
         at = slice(cand * tokens, (cand + 1) * tokens)
@@ -145,13 +145,19 @@
             ]
 
     copies[0].wait()
+    copies[2].start()
     for cand in range(cands):
         norm_cand(cand)
     copies[1].wait()
-    copies[2].wait()
+    for copy in copies[3 : 2 + groups]:
+        copy.start()
     for group in range(groups):
         at = slice(group * rows, (group + 1) * rows)
         for part in range(2):
+            if group == 0 and part == 1:
+                copies[2].wait()
+                for copy in copies[2 + groups :]:
+                    copy.start()
             part_columns = slice(part * width, (part + 1) * width)
             packed_ref[:, part_columns] = dot(normed_ref[at, :], qkv_ref[:, part_columns]).astype(
                 jnp.bfloat16
@@ -265,24 +271,22 @@
     far_ref,
     usable_ref,
     history_hbm,
+    mlp_hbm,
     queries_ref,
     attended_ref,
     slope_ref,
+    mlp_ref,
     history_ref,
     sems,
 ):
     users, events, _ = history_ref.shape
     chunk = math.gcd(events, 1024)
-    half_users = max(1, users // 2)
     copies = [
-        pltpu.make_async_copy(
-            history_hbm.at[pl.ds(user, half_users)],
-            history_ref.at[pl.ds(user, half_users)],
-            sems.at[user],
-        )
-        for user in range(0, users, half_users)
+        pltpu.make_async_copy(history_hbm.at[user], history_ref.at[user], sems.at[user])
+        for user in range(users)
     ]
-    for copy in copies:
+    copies.append(pltpu.make_async_copy(mlp_hbm, mlp_ref, sems.at[users]))
+    for copy in copies[:2]:
         copy.start()
     slots = slots_ref[...]
     half, key_width = near_ref.shape
@@ -292,8 +296,9 @@
     queries_ref[...] = queries.astype(jnp.bfloat16)
     per_user = slots.shape[0] // users
     for user in range(users):
-        if user % half_users == 0:
-            copies[user // half_users].wait()
+        copies[user].wait()
+        if user + 2 < len(copies):
+            copies[user + 2].start()
         rows = slice(user * per_user, (user + 1) * per_user)
         attended = jnp.zeros((per_user, key_width), jnp.float32)
         for at in range(0, events, chunk):
@@ -305,9 +310,10 @@
             slope_ref[rows, at : at + chunk] = (weights * (0.5 - half_gate)).astype(jnp.bfloat16)
             attended += dot(weights.astype(jnp.bfloat16), keys)
         attended_ref[rows, :] = attended * inv_ref[user]
-
-
-def attend(inv_count, slots, near, far, history, usable):
+    copies[users].wait()
+
+
+def attend(inv_count, slots, near, far, history, usable, mlp_weight):
     users, events, key_width = history.shape
     requests = slots.shape[0]
     whole = pl.BlockSpec(memory_space=pltpu.VMEM)
@@ -315,23 +321,24 @@
         attend_kernel,
         in_specs=[pl.BlockSpec(memory_space=pltpu.SMEM)]
         + [whole] * 4
-        + [pl.BlockSpec(memory_space=pltpu.HBM)],
-        out_specs=[whole] * 3,
+        + [pl.BlockSpec(memory_space=pltpu.HBM)] * 2,
+        out_specs=[whole] * 4,
         out_shape=[
             jax.ShapeDtypeStruct((requests, key_width), jnp.bfloat16),
             jax.ShapeDtypeStruct((requests, key_width), jnp.float32),
             jax.ShapeDtypeStruct((requests, events), jnp.bfloat16),
+            pltpu.VMEM(mlp_weight.shape, mlp_weight.dtype),
         ],
         scratch_shapes=[
             pltpu.VMEM(history.shape, history.dtype),
-            pltpu.SemaphoreType.DMA((users,)),
+            pltpu.SemaphoreType.DMA((users + 1,)),
         ],
         compiler_params=pltpu.CompilerParams(vmem_limit_bytes=32 * MIB),
         cost_estimate=pl.CostEstimate(
             flops=4 * requests * events * key_width, bytes_accessed=1 << 24, transcendentals=0
         ),
         name="attend",
-    )(inv_count, slots, near, far, usable, *in_hbm(history))
+    )(inv_count, slots, near, far, usable, *in_hbm(history, mlp_weight))
 
 
 def score_kernel(
@@ -605,8 +612,8 @@
         near = jnp.concatenate([near] + found, axis=0)
     far = exchange(near, "section", 2, 1)
     found_pooled = send_stage(pooled, wides, *stages[-1])
-    queries, attended, slope = attend(
-        inv_count, slots.reshape(requests, 1), near, far, history, usable
+    queries, attended, slope, mlp_weight = attend(
+        inv_count, slots.reshape(requests, 1), near, far, history, usable, mlp_weight
     )
     logits, grad_att, direct = score(
         inv_count,

time: 85.3 us -> 84.7 us (level)
  transfers between devices with their start and end apart: 22 -> 22, of which waited for: 11 -> 11; matrix products, arithmetic and copies ran while one was open for 2% -> 2% of each run, Pallas kernels for 19% -> 18%
where the time goes in v4:
time: 84.7 us; the launch traced here: 84.5 us
  Pallas kernels  36.8 us (43%)
  starting transfers between devices  23.3 us (28%)
  waiting for transfers between devices  21.1 us (25%)
  other arithmetic  1.83 us (2%)
  between operations  1.02 us (1%)
    ppermute x22, starting transfers between devices, exchange(): lax.ppermute(values, axis_name, [(i, i ^ distance) for i in range(size)])  23.3 us
    ppermute x22, waiting for transfers between devices, exchange(): lax.ppermute(values, axis_name, [(i, i ^ distance) for i in range(size)])  21.1 us
    pallas_call x1, Pallas kernels, encode_block(): pl.pallas_call(functools.partial(encode_kernel, tokens), in_specs=[pl.Blo...  14.7 us
    pallas_call x1, Pallas kernels, attend(): pl.pallas_call(attend_kernel, in_specs=[pl.BlockSpec(memory_space=pltpu.S...  7.75 us
    pallas_call x1, Pallas kernels, score(): pl.pallas_call(score_kernel, in_specs=[pl.BlockSpec(memory_space=pltpu.SM...  6.88 us
    pallas_call x1, Pallas kernels, attend_back(): pl.pallas_call(attend_back_kernel, in_specs=[whole] * 4, out_specs=whole,...  4.71 us
    pallas_call x1, Pallas kernels, chip_terms(): pl.pallas_call(functools.partial(terms_kernel, origins), in_specs=[pl.Blo...  1.75 us
  transfers between devices with their start and end apart: 22, of which 11 were waited for; matrix products, arithmetic and copies ran while one was open for 2% of the time, Pallas kernels for 18%

profile of v4, /device:TPU:0, one launch (start us, length us, event | category | flops | bytes accessed | tf_op | source)
XLA Modules:
  0.0 84.5 jit_solution(4817211498132099183)
XLA Ops:
  0.7 14.7 %encode.1 = (bf16[32,512]{1,0:T(8,128)(2,1)S(1)}, bf16[32,512]{1,0:T(8,128)(2,1)S(1)}, bf16[32,512]{1,0:T(8,128)(2,1)S(1)}) custom-call(s32[1]{0:T(128)} %bitcast.1.core_ref, bf16[1536,1024]{1,0:T(8,128)(2,1)} %bitcast.5, bf16[1024,3072]{1,0:T(8,128)(2,1)} %qkv_hbm.1, bf16[1024,1024]{1,0:T(8,128)(2,1)} %out_hbm.1, bf16[1024,512]{1,0:T(8,128)(2,1)} %proj_hbm.1), custom_call_target="tpu_custom_call" | custom-call | flops 8053063680 | bytes 16777216 | tf_op jit(solution)/shard_map/encode/pallas_call | solution.py:237
  15.4 3.1 %collective-permute-start = (bf16[32,512]{1,0:T(8,128)(2,1)S(1)}, bf16[32,512]{1,0:T(8,128)(2,1)S(1)}, u32[]{:S(2)}, u32[]{:S(2)}) collective-permute-start(bf16[32,512]{1,0:T(8,128)(2,1)S(1)} %get-tuple-element.34), channel_id=1, source_target_pairs={{0,4},{1,5},{2,6},{3,7},{4,0},{5,1},{6,2},{7,3},{8,12},{9,13},{10,... | collective-permute-start | bytes 98312 | tf_op jit(solution)/shard_map/ppermute | solution.py:531
  18.5 2.6 %collective-permute-start.1 = (bf16[32,512]{1,0:T(8,128)(2,1)S(1)}, bf16[32,512]{1,0:T(8,128)(2,1)S(1)}, u32[]{:S(2)}, u32[]{:S(2)}) collective-permute-start(bf16[32,512]{1,0:T(8,128)(2,1)S(1)} %get-tuple-element.34), channel_id=1, source_target_pairs={{0,8},{1,9},{2,10},{3,11},{4,12},{5,13},{6,14},{7,15},{8,0},{9,1},... | collective-permute-start | bytes 98312 | tf_op jit(solution)/shard_map/ppermute | solution.py:531
  22.4 1.5 %collective-permute-done.1 = bf16[32,512]{1,0:T(8,128)(2,1)S(1)} collective-permute-done((bf16[32,512]{1,0:T(8,128)(2,1)S(1)}, bf16[32,512]{1,0:T(8,128)(2,1)S(1)}, u32[]{:S(2)}, u32[]{:S(2)}) %collective-permute-start.1) | collective-permute-done | bytes 32800 | tf_op jit(solution)/shard_map/ppermute | solution.py:531
  23.9 3.0 %collective-permute-done.2 = bf16[32,512]{1,0:T(8,128)(2,1)S(1)} collective-permute-done((bf16[32,512]{1,0:T(8,128)(2,1)S(1)}, bf16[32,512]{1,0:T(8,128)(2,1)S(1)}, u32[]{:S(2)}, u32[]{:S(2)}) %collective-permute-start.2) | collective-permute-done | bytes 32800 | tf_op jit(solution)/shard_map/ppermute | solution.py:531
  27.3 1.6 %collective-permute-start.5 = (bf16[128,512]{1,0:T(8,128)(2,1)S(1)}, bf16[128,512]{1,0:T(8,128)(2,1)S(1)}, u32[]{:S(2)}, u32[]{:S(2)}) collective-permute-start(bf16[128,512]{1,0:T(8,128)(2,1)S(1)} %get-tuple-element.75), channel_id=1, source_target_pairs={{0,1},{1,0},{2,3},{3,2},{4,5},{5,4},{6,7},{7,6},{8,9},{9,8},{10,11... | collective-permute-start | bytes 393224 | tf_op jit(solution)/shard_map/ppermute | solution.py:531
  28.9 1.5 %collective-permute-start.6 = (bf16[128,512]{1,0:T(8,128)(2,1)S(1)}, bf16[128,512]{1,0:T(8,128)(2,1)S(1)}, u32[]{:S(2)}, u32[]{:S(2)}) collective-permute-start(bf16[128,512]{1,0:T(8,128)(2,1)S(1)} %get-tuple-element.75), channel_id=1, source_target_pairs={{0,2},{1,3},{2,0},{3,1},{4,6},{5,7},{6,4},{7,5},{8,10},{9,11},{10,... | collective-permute-start | bytes 393224 | tf_op jit(solution)/shard_map/ppermute | solution.py:531
  30.9 2.8 %collective-permute-done.10 = bf16[64,512]{1,0:T(8,128)(2,1)S(1)} collective-permute-done((bf16[64,512]{1,0:T(8,128)(2,1)S(1)}, bf16[64,512]{1,0:T(8,128)(2,1)S(1)}, u32[]{:S(2)}, u32[]{:S(2)}) %collective-permute-start.10) | collective-permute-done | bytes 65568 | tf_op jit(solution)/shard_map/ppermute | solution.py:531
  33.7 1.3 %collective-permute-start.9 = (bf16[64,512]{1,0:T(8,128)(2,1)S(1)}, bf16[64,512]{1,0:T(8,128)(2,1)S(1)}, u32[]{:S(2)}, u32[]{:S(2)}) collective-permute-start(bf16[64,512]{1,0:T(8,128)(2,1)S(1)} %maximum_select_fusion), channel_id=1, source_target_pairs={{0,8},{1,9},{2,10},{3,11},{4,12},{5,13},{6,14},{7,15},{8,0},{9,1},... | collective-permute-start | bytes 196616 | tf_op jit(solution)/shard_map/ppermute | solution.py:531
  35.5 3.4 %collective-permute-done.9 = bf16[64,512]{1,0:T(8,128)(2,1)S(1)} collective-permute-done((bf16[64,512]{1,0:T(8,128)(2,1)S(1)}, bf16[64,512]{1,0:T(8,128)(2,1)S(1)}, u32[]{:S(2)}, u32[]{:S(2)}) %collective-permute-start.9) | collective-permute-done | bytes 65568 | tf_op jit(solution)/shard_map/ppermute | solution.py:531
  39.9 1.6 %collective-permute-start.11 = (bf16[256,512]{1,0:T(8,128)(2,1)S(1)}, bf16[256,512]{1,0:T(8,128)(2,1)S(1)}, u32[]{:S(2)}, u32[]{:S(2)}) collective-permute-start(bf16[256,512]{1,0:T(8,128)(2,1)S(1)} %pad_maximum_fusion.1), channel_id=1, source_target_pairs={{0,1},{1,0},{2,3},{3,2},{4,5},{5,4},{6,7},{7,6},{8,9},{9,8},{10,11... | collective-permute-start | bytes 786440 | tf_op jit(solution)/shard_map/ppermute | solution.py:531
  41.4 1.5 %collective-permute-start.12 = (bf16[256,512]{1,0:T(8,128)(2,1)S(1)}, bf16[256,512]{1,0:T(8,128)(2,1)S(1)}, u32[]{:S(2)}, u32[]{:S(2)}) collective-permute-start(bf16[256,512]{1,0:T(8,128)(2,1)S(1)} %pad_maximum_fusion.1), channel_id=1, source_target_pairs={{0,2},{1,3},{2,0},{3,1},{4,6},{5,7},{6,4},{7,5},{8,10},{9,11},{10,... | collective-permute-start | bytes 786440 | tf_op jit(solution)/shard_map/ppermute | solution.py:531
  43.4 7.8 %attend.1 = (bf16[768,512]{1,0:T(8,128)(2,1)S(1)}, f32[768,512]{1,0:T(8,128)S(1)}, bf16[768,2048]{1,0:T(8,128)(2,1)S(1)}, bf16[1536,1024]{1,0:T(8,128)(2,1)S(1)}) custom-call(f32[4]{0:T(128)S(1)} %rsqrt.3.inv_ref, s32[768,1]{1,0:T(8,128)S(1)} %reshape.68.slots_ref, bf16[512,512]{1,0:T(8,128)(2,1)S(1)} %constant_dynamic-update-slice_fusion.4.near_ref, ...), custom_call_target="tpu_custom_call" | custom-call | flops 3221225472 | bytes 16777216 | tf_op jit(solution)/shard_map/attend/pallas_call | solution.py:320
  51.2 6.9 %score.1 = (f32[768,1]{1,0:T(8,128)S(1)}, bf16[768,512]{1,0:T(8,128)(2,1)S(1)}, f32[768,512]{1,0:T(8,128)S(1)}) custom-call(f32[4]{0:T(128)S(1)} %rsqrt.3.inv_ref, bf16[768,512]{1,0:T(8,128)(2,1)S(1)} %get-tuple-element.48.queries_ref, f32[768,512]{1,0:T(8,128)S(1)} %get-tuple-element.49.attended_ref, s32[768,1]{1,0:T(8,128)S(1)} %reshape.69.labels_ref, ...), custom_call_target="tpu_custom_call" | custom-call | flops 4831838208 | bytes 8388608 | tf_op jit(solution)/shard_map/score/pallas_call | solution.py:393
  58.1 4.7 %attend_back.1.grad_rows_ref = bf16[768,512]{1,0:T(8,128)(2,1)S(1)} custom-call(bf16[768,512]{1,0:T(8,128)(2,1)S(1)} %get-tuple-element.52.grad_att_ref, f32[768,512]{1,0:T(8,128)S(1)} %get-tuple-element.53.direct_ref, bf16[768,2048]{1,0:T(8,128)(2,1)S(1)} %get-tuple-element.54.slope_ref, bf16[4,2048,512]{2,1,0:T(8,128)(2,1)S(1)} %bitcast.4), custom_call_target="tpu_custom_call" | custom-call | flops 3221225472 | bytes 8388608 | tf_op jit(solution)/shard_map/attend_back/pallas_call | solution.py:433
  64.0 1.2 %collective-permute-done.15.grad_rows_ref = bf16[768,512]{1,0:T(8,128)(2,1)S(1)} collective-permute-done((bf16[768,512]{1,0:T(8,128)(2,1)S(1)}, bf16[768,512]{1,0:T(8,128)(2,1)S(1)}, u32[]{:S(2)}, u32[]{:S(2)}) %collective-permute-start.15) | collective-permute-done | bytes 786464 | tf_op jit(solution)/shard_map/ppermute | solution.py:531
  65.2 1.8 %chip_terms.1 = bf16[512,512]{1,0:T(8,128)(2,1)S(1)} custom-call(s32[1]{0:T(128)} %bitcast.wide_ref, f32[1024,512]{1,0:T(8,128)S(1)} %own_cand_grad.1.cand_grad_ref, s32[1,768]{1,0:T(1,128)S(1)} %reshape.66.slots_ref, bf16[768,512]{1,0:T(8,128)(2,1)S(1)} %collective-permute-done.15.grad_rows_ref, bf16[1024,512]{1,0:T(8,128)(2,1)S(1)} %pad_maximum_fusion.pooled_ref), custom_call_target="tpu_custom_call" | custom-call | flops 1342177280 | bytes 4194304 | tf_op jit(solution)/shard_map/chip_terms/pallas_call | solution.py:504
  67.0 1.6 %collective-permute-start.16 = (bf16[128,512]{1,0:T(8,128)(2,1)S(1)}, bf16[128,512]{1,0:T(8,128)(2,1)S(1)}, u32[]{:S(2)}, u32[]{:S(2)}) collective-permute-start(bf16[128,512]{1,0:T(8,128)(2,1)S(1)} %get-tuple-element.68), channel_id=1, source_target_pairs={{0,1},{1,0},{2,3},{3,2},{4,5},{5,4},{6,7},{7,6},{8,9},{9,8},{10,11... | collective-permute-start | bytes 393224 | tf_op jit(solution)/shard_map/ppermute | solution.py:531
  68.6 1.5 %collective-permute-start.17 = (bf16[128,512]{1,0:T(8,128)(2,1)S(1)}, bf16[128,512]{1,0:T(8,128)(2,1)S(1)}, u32[]{:S(2)}, u32[]{:S(2)}) collective-permute-start(bf16[128,512]{1,0:T(8,128)(2,1)S(1)} %get-tuple-element.70), channel_id=1, source_target_pairs={{0,2},{1,3},{2,0},{3,1},{4,6},{5,7},{6,4},{7,5},{8,10},{9,11},{10,... | collective-permute-start | bytes 393224 | tf_op jit(solution)/shard_map/ppermute | solution.py:531
  71.3 1.6 %collective-permute-done.16 = bf16[128,512]{1,0:T(8,128)(2,1)S(1)} collective-permute-done((bf16[128,512]{1,0:T(8,128)(2,1)S(1)}, bf16[128,512]{1,0:T(8,128)(2,1)S(1)}, u32[]{:S(2)}, u32[]{:S(2)}) %collective-permute-start.16) | collective-permute-done | bytes 131104 | tf_op jit(solution)/shard_map/ppermute | solution.py:531
  73.0 3.7 %collective-permute-done.17 = bf16[128,512]{1,0:T(8,128)(2,1)S(1)} collective-permute-done((bf16[128,512]{1,0:T(8,128)(2,1)S(1)}, bf16[128,512]{1,0:T(8,128)(2,1)S(1)}, u32[]{:S(2)}, u32[]{:S(2)}) %collective-permute-start.17) | collective-permute-done | bytes 131104 | tf_op jit(solution)/shard_map/ppermute | solution.py:531
  76.8 1.4 %collective-permute-start.20 = (bf16[32,512]{1,0:T(8,128)(2,1)S(1)}, bf16[32,512]{1,0:T(8,128)(2,1)S(1)}, u32[]{:S(2)}, u32[]{:S(2)}) collective-permute-start(bf16[32,512]{1,0:T(8,128)(2,1)S(1)} %get-tuple-element.72), channel_id=1, source_target_pairs={{0,8},{1,9},{2,10},{3,11},{4,12},{5,13},{6,14},{7,15},{8,0},{9,1},... | collective-permute-start | bytes 98312 | tf_op jit(solution)/shard_map/ppermute | solution.py:531
  78.2 3.0 %collective-permute-start.21 = (bf16[32,512]{1,0:T(8,128)(2,1)S(1)}, bf16[32,512]{1,0:T(8,128)(2,1)S(1)}, u32[]{:S(2)}, u32[]{:S(2)}) collective-permute-start(bf16[32,512]{1,0:T(8,128)(2,1)S(1)} %get-tuple-element.73), channel_id=1, source_target_pairs={{0,12},{1,13},{2,14},{3,15},{4,8},{5,9},{6,10},{7,11},{8,4},{9,5},... | collective-permute-start | bytes 98312 | tf_op jit(solution)/shard_map/ppermute | solution.py:531
  81.9 2.0 %collective-permute-done.21 = bf16[32,512]{1,0:T(8,128)(2,1)S(1)} collective-permute-done((bf16[32,512]{1,0:T(8,128)(2,1)S(1)}, bf16[32,512]{1,0:T(8,128)(2,1)S(1)}, u32[]{:S(2)}, u32[]{:S(2)}) %collective-permute-start.21) | collective-permute-done | bytes 32800 | tf_op jit(solution)/shard_map/ppermute | solution.py:531
  (69 shorter events, 7.9 us)
Async XLA Ops:
  0.7 38.7 %copy-start = (s32[4,2048]{1,0:T(4,128)S(1)}, s32[4,2048]{1,0:T(4,128)}, u32[]{:S(2)}) copy-start(s32[4,2048]{1,0:T(4,128)} %param.20) | copy-start | bytes 98308
  0.7 39.0 %copy-start.1 = (s32[768]{0:T(1024)S(1)}, s32[768]{0:T(1024)}, u32[]{:S(2)}) copy-start(s32[768]{0:T(1024)} %param.23) | copy-start | bytes 9220
  15.4 7.0 %collective-permute-start = (bf16[32,512]{1,0:T(8,128)(2,1)S(1)}, bf16[32,512]{1,0:T(8,128)(2,1)S(1)}, u32[]{:S(2)}, u32[]{:S(2)}) collective-permute-start(bf16[32,512]{1,0:T(8,128)(2,1)S(1)} %get-tuple-element.34), channel_id=1, source_target_pairs={{0,4},{1,5},{2,6},{3,7},{4,0},{5,1},{6,2},{7,3},{8,12},{9,13},{10,... | collective-permute-start | bytes 98312 | tf_op jit(solution)/shard_map/ppermute | solution.py:531
  18.5 5.4 %collective-permute-start.1 = (bf16[32,512]{1,0:T(8,128)(2,1)S(1)}, bf16[32,512]{1,0:T(8,128)(2,1)S(1)}, u32[]{:S(2)}, u32[]{:S(2)}) collective-permute-start(bf16[32,512]{1,0:T(8,128)(2,1)S(1)} %get-tuple-element.34), channel_id=1, source_target_pairs={{0,8},{1,9},{2,10},{3,11},{4,12},{5,13},{6,14},{7,15},{8,0},{9,1},... | collective-permute-start | bytes 98312 | tf_op jit(solution)/shard_map/ppermute | solution.py:531
  21.1 5.8 %collective-permute-start.2 = (bf16[32,512]{1,0:T(8,128)(2,1)S(1)}, bf16[32,512]{1,0:T(8,128)(2,1)S(1)}, u32[]{:S(2)}, u32[]{:S(2)}) collective-permute-start(bf16[32,512]{1,0:T(8,128)(2,1)S(1)} %get-tuple-element.34), channel_id=1, source_target_pairs={{0,12},{1,13},{2,14},{3,15},{4,8},{5,9},{6,10},{7,11},{8,4},{9,5},... | collective-permute-start | bytes 98312 | tf_op jit(solution)/shard_map/ppermute | solution.py:531
  21.2 1.2 %collective-permute-start.4 = (s32[768]{0:T(1024)S(1)}, s32[768]{0:T(1024)S(1)}, u32[]{:S(2)}, u32[]{:S(2)}) collective-permute-start(s32[768]{0:T(1024)S(1)} %get-tuple-element.83), channel_id=1, source_target_pairs={{0,16},{16,0},{1,17},{17,1},{2,18},{18,2},{3,19},{19,3},{4,20},{20... | collective-permute-start | bytes 9224 | tf_op jit(solution)/shard_map/ppermute | solution.py:531
  21.3 5.7 %collective-permute-start.3 = (bf16[32,512]{1,0:T(8,128)(2,1)S(1)}, bf16[32,512]{1,0:T(8,128)(2,1)S(1)}, u32[]{:S(2)}, u32[]{:S(2)}) collective-permute-start(bf16[32,512]{1,0:T(8,128)(2,1)S(1)} %get-tuple-element.36), channel_id=1, source_target_pairs={{0,16},{16,0},{1,17},{17,1},{2,18},{18,2},{3,19},{19,3},{4,20},{20... | collective-permute-start | bytes 98312 | tf_op jit(solution)/shard_map/ppermute | solution.py:531
  27.0 6.7 %collective-permute-start.10 = (bf16[64,512]{1,0:T(8,128)(2,1)S(1)}, bf16[64,512]{1,0:T(8,128)(2,1)S(1)}, u32[]{:S(2)}, u32[]{:S(2)}) collective-permute-start(bf16[64,512]{1,0:T(8,128)(2,1)S(1)} %maximum_select_fusion), channel_id=1, source_target_pairs={{0,12},{1,13},{2,14},{3,15},{4,8},{5,9},{6,10},{7,11},{8,4},{9,5},... | collective-permute-start | bytes 196616 | tf_op jit(solution)/shard_map/ppermute | solution.py:531
  27.3 11.6 %collective-permute-start.5 = (bf16[128,512]{1,0:T(8,128)(2,1)S(1)}, bf16[128,512]{1,0:T(8,128)(2,1)S(1)}, u32[]{:S(2)}, u32[]{:S(2)}) collective-permute-start(bf16[128,512]{1,0:T(8,128)(2,1)S(1)} %get-tuple-element.75), channel_id=1, source_target_pairs={{0,1},{1,0},{2,3},{3,2},{4,5},{5,4},{6,7},{7,6},{8,9},{9,8},{10,11... | collective-permute-start | bytes 393224 | tf_op jit(solution)/shard_map/ppermute | solution.py:531
  28.9 10.0 %collective-permute-start.6 = (bf16[128,512]{1,0:T(8,128)(2,1)S(1)}, bf16[128,512]{1,0:T(8,128)(2,1)S(1)}, u32[]{:S(2)}, u32[]{:S(2)}) collective-permute-start(bf16[128,512]{1,0:T(8,128)(2,1)S(1)} %get-tuple-element.75), channel_id=1, source_target_pairs={{0,2},{1,3},{2,0},{3,1},{4,6},{5,7},{6,4},{7,5},{8,10},{9,11},{10,... | collective-permute-start | bytes 393224 | tf_op jit(solution)/shard_map/ppermute | solution.py:531
  30.4 8.5 %collective-permute-start.7 = (bf16[128,512]{1,0:T(8,128)(2,1)S(1)}, bf16[128,512]{1,0:T(8,128)(2,1)S(1)}, u32[]{:S(2)}, u32[]{:S(2)}) collective-permute-start(bf16[128,512]{1,0:T(8,128)(2,1)S(1)} %get-tuple-element.75), channel_id=1, source_target_pairs={{0,3},{1,2},{2,1},{3,0},{4,7},{5,6},{6,5},{7,4},{8,11},{9,10},{10,... | collective-permute-start | bytes 393224 | tf_op jit(solution)/shard_map/ppermute | solution.py:531
  30.9 4.6 %collective-permute-start.8 = (bf16[64,512]{1,0:T(8,128)(2,1)S(1)}, bf16[64,512]{1,0:T(8,128)(2,1)S(1)}, u32[]{:S(2)}, u32[]{:S(2)}) collective-permute-start(bf16[64,512]{1,0:T(8,128)(2,1)S(1)} %maximum_select_fusion), channel_id=1, source_target_pairs={{0,4},{1,5},{2,6},{3,7},{4,0},{5,1},{6,2},{7,3},{8,12},{9,13},{10,... | collective-permute-start | bytes 196616 | tf_op jit(solution)/shard_map/ppermute | solution.py:531
  33.7 5.2 %collective-permute-start.9 = (bf16[64,512]{1,0:T(8,128)(2,1)S(1)}, bf16[64,512]{1,0:T(8,128)(2,1)S(1)}, u32[]{:S(2)}, u32[]{:S(2)}) collective-permute-start(bf16[64,512]{1,0:T(8,128)(2,1)S(1)} %maximum_select_fusion), channel_id=1, source_target_pairs={{0,8},{1,9},{2,10},{3,11},{4,12},{5,13},{6,14},{7,15},{8,0},{9,1},... | collective-permute-start | bytes 196616 | tf_op jit(solution)/shard_map/ppermute | solution.py:531
  38.9 4.5 %collective-permute-start.14 = (bf16[512,512]{1,0:T(8,128)(2,1)S(1)}, bf16[512,512]{1,0:T(8,128)(2,1)S(1)}, u32[]{:S(2)}, u32[]{:S(2)}) collective-permute-start(bf16[512,512]{1,0:T(8,128)(2,1)S(1)} %constant_dynamic-update-slice_fusion.4.near_ref), channel_id=1, source_target_pairs={{0,16},{16,0},{1,17},{17,1},{2,18},{18,2},{3,19},{19,3},{4,20},{20... | collective-permute-start | bytes 1572872 | tf_op jit(solution)/shard_map/ppermute | solution.py:531
  39.9 18.2 %collective-permute-start.11 = (bf16[256,512]{1,0:T(8,128)(2,1)S(1)}, bf16[256,512]{1,0:T(8,128)(2,1)S(1)}, u32[]{:S(2)}, u32[]{:S(2)}) collective-permute-start(bf16[256,512]{1,0:T(8,128)(2,1)S(1)} %pad_maximum_fusion.1), channel_id=1, source_target_pairs={{0,1},{1,0},{2,3},{3,2},{4,5},{5,4},{6,7},{7,6},{8,9},{9,8},{10,11... | collective-permute-start | bytes 786440 | tf_op jit(solution)/shard_map/ppermute | solution.py:531
  41.4 16.7 %collective-permute-start.12 = (bf16[256,512]{1,0:T(8,128)(2,1)S(1)}, bf16[256,512]{1,0:T(8,128)(2,1)S(1)}, u32[]{:S(2)}, u32[]{:S(2)}) collective-permute-start(bf16[256,512]{1,0:T(8,128)(2,1)S(1)} %pad_maximum_fusion.1), channel_id=1, source_target_pairs={{0,2},{1,3},{2,0},{3,1},{4,6},{5,7},{6,4},{7,5},{8,10},{9,11},{10,... | collective-permute-start | bytes 786440 | tf_op jit(solution)/shard_map/ppermute | solution.py:531
  42.9 15.2 %collective-permute-start.13 = (bf16[256,512]{1,0:T(8,128)(2,1)S(1)}, bf16[256,512]{1,0:T(8,128)(2,1)S(1)}, u32[]{:S(2)}, u32[]{:S(2)}) collective-permute-start(bf16[256,512]{1,0:T(8,128)(2,1)S(1)} %pad_maximum_fusion.1), channel_id=1, source_target_pairs={{0,3},{1,2},{2,1},{3,0},{4,7},{5,6},{6,5},{7,4},{8,11},{9,10},{10,... | collective-permute-start | bytes 786440 | tf_op jit(solution)/shard_map/ppermute | solution.py:531
  62.9 2.4 %collective-permute-start.15 = (bf16[768,512]{1,0:T(8,128)(2,1)S(1)}, bf16[768,512]{1,0:T(8,128)(2,1)S(1)}, u32[]{:S(2)}, u32[]{:S(2)}) collective-permute-start(bf16[768,512]{1,0:T(8,128)(2,1)S(1)} %attend_back.1.grad_rows_ref), channel_id=1, source_target_pairs={{0,16},{16,0},{1,17},{17,1},{2,18},{18,2},{3,19},{19,3},{4,20},{20... | collective-permute-start | bytes 2359304 | tf_op jit(solution)/shard_map/ppermute | solution.py:531
  67.0 5.9 %collective-permute-start.16 = (bf16[128,512]{1,0:T(8,128)(2,1)S(1)}, bf16[128,512]{1,0:T(8,128)(2,1)S(1)}, u32[]{:S(2)}, u32[]{:S(2)}) collective-permute-start(bf16[128,512]{1,0:T(8,128)(2,1)S(1)} %get-tuple-element.68), channel_id=1, source_target_pairs={{0,1},{1,0},{2,3},{3,2},{4,5},{5,4},{6,7},{7,6},{8,9},{9,8},{10,11... | collective-permute-start | bytes 393224 | tf_op jit(solution)/shard_map/ppermute | solution.py:531
  68.6 8.1 %collective-permute-start.17 = (bf16[128,512]{1,0:T(8,128)(2,1)S(1)}, bf16[128,512]{1,0:T(8,128)(2,1)S(1)}, u32[]{:S(2)}, u32[]{:S(2)}) collective-permute-start(bf16[128,512]{1,0:T(8,128)(2,1)S(1)} %get-tuple-element.70), channel_id=1, source_target_pairs={{0,2},{1,3},{2,0},{3,1},{4,6},{5,7},{6,4},{7,5},{8,10},{9,11},{10,... | collective-permute-start | bytes 393224 | tf_op jit(solution)/shard_map/ppermute | solution.py:531
  70.1 6.5 %collective-permute-start.18 = (bf16[128,512]{1,0:T(8,128)(2,1)S(1)}, bf16[128,512]{1,0:T(8,128)(2,1)S(1)}, u32[]{:S(2)}, u32[]{:S(2)}) collective-permute-start(bf16[128,512]{1,0:T(8,128)(2,1)S(1)} %get-tuple-element.69), channel_id=1, source_target_pairs={{0,3},{1,2},{2,1},{3,0},{4,7},{5,6},{6,5},{7,4},{8,11},{9,10},{10,... | collective-permute-start | bytes 393224 | tf_op jit(solution)/shard_map/ppermute | solution.py:531
  76.7 4.5 %collective-permute-start.19 = (bf16[32,512]{1,0:T(8,128)(2,1)S(1)}, bf16[32,512]{1,0:T(8,128)(2,1)S(1)}, u32[]{:S(2)}, u32[]{:S(2)}) collective-permute-start(bf16[32,512]{1,0:T(8,128)(2,1)S(1)} %get-tuple-element.71), channel_id=1, source_target_pairs={{0,4},{1,5},{2,6},{3,7},{4,0},{5,1},{6,2},{7,3},{8,12},{9,13},{10,... | collective-permute-start | bytes 98312 | tf_op jit(solution)/shard_map/ppermute | solution.py:531
  76.8 5.1 %collective-permute-start.20 = (bf16[32,512]{1,0:T(8,128)(2,1)S(1)}, bf16[32,512]{1,0:T(8,128)(2,1)S(1)}, u32[]{:S(2)}, u32[]{:S(2)}) collective-permute-start(bf16[32,512]{1,0:T(8,128)(2,1)S(1)} %get-tuple-element.72), channel_id=1, source_target_pairs={{0,8},{1,9},{2,10},{3,11},{4,12},{5,13},{6,14},{7,15},{8,0},{9,1},... | collective-permute-start | bytes 98312 | tf_op jit(solution)/shard_map/ppermute | solution.py:531
  78.2 5.7 %collective-permute-start.21 = (bf16[32,512]{1,0:T(8,128)(2,1)S(1)}, bf16[32,512]{1,0:T(8,128)(2,1)S(1)}, u32[]{:S(2)}, u32[]{:S(2)}) collective-permute-start(bf16[32,512]{1,0:T(8,128)(2,1)S(1)} %get-tuple-element.73), channel_id=1, source_target_pairs={{0,12},{1,13},{2,14},{3,15},{4,8},{5,9},{6,10},{7,11},{8,4},{9,5},... | collective-permute-start | bytes 98312 | tf_op jit(solution)/shard_map/ppermute | solution.py:531
  (6 other events, 118.0 us)

commit v5 on v4

--- a/solution.py
+++ b/solution.py
@@ -410,70 +410,91 @@
     )(inv_count, queries, attended, labels, mlp_weight, logit_weight)
 
 
-def attend_back_kernel(grad_att_ref, direct_ref, slope_ref, history_ref, grad_rows_ref):
+def attend_back_kernel(first, grad_att_ref, direct_ref, slope_ref, history_ref, grad_rows_ref):
     users, events, key_width = history_ref.shape
     per_user = grad_att_ref.shape[0] // users
     chunk = math.gcd(events, 1024)
-    for user in range(users):
-        rows = slice(user * per_user, (user + 1) * per_user)
+    for user in range(grad_rows_ref.shape[0] // per_user):
+        rows = slice((first + user) * per_user, (first + user + 1) * per_user)
         back = jnp.zeros((per_user, key_width), jnp.float32)
         for at in range(0, events, chunk):
-            keys = history_ref[user, at : at + chunk, :]
+            keys = history_ref[first + user, at : at + chunk, :]
             slope = slope_ref[rows, at : at + chunk].astype(jnp.float32)
             grad_sig = (dot_rows(grad_att_ref[rows, :], keys) * slope).astype(jnp.bfloat16)
             back += dot(grad_sig, keys)
         grad_rows = direct_ref[rows, :] + back * (1.0 / math.sqrt(key_width))
-        grad_rows_ref[rows, :] = grad_rows.astype(jnp.bfloat16)
-
-
-def attend_back(grad_att, direct, slope, history):
-    _, events, key_width = history.shape
-    requests = grad_att.shape[0]
+        grad_rows_ref[user * per_user : (user + 1) * per_user, :] = grad_rows.astype(jnp.bfloat16)
+
+
+def attend_back(first, count, grad_att, direct, slope, history):
+    users, events, key_width = history.shape
+    per_user = grad_att.shape[0] // users
     whole = pl.BlockSpec(memory_space=pltpu.VMEM)
     return pl.pallas_call(
-        attend_back_kernel,
+        functools.partial(attend_back_kernel, first),
         in_specs=[whole] * 4,
         out_specs=whole,
-        out_shape=jax.ShapeDtypeStruct((requests, key_width), jnp.bfloat16),
+        out_shape=jax.ShapeDtypeStruct((count * per_user, key_width), jnp.bfloat16),
         compiler_params=pltpu.CompilerParams(vmem_limit_bytes=20 * MIB),
         cost_estimate=pl.CostEstimate(
-            flops=4 * requests * events * key_width, bytes_accessed=1 << 23, transcendentals=0
+            flops=4 * count * per_user * events * key_width,
+            bytes_accessed=1 << 23,
+            transcendentals=0,
         ),
         name="attend_back",
     )(grad_att, direct, slope, history)
 
 
+def join_rows(parts, joined_ref):
+    at = 0
+    for part in parts:
+        joined_ref[at : at + part.shape[0], :] = part[...]
+        at += part.shape[0]
+
+
 def sum_rows(cands, at, slots_ref, grad_rows_ref):
     places = lax.broadcasted_iota(jnp.int32, (cands, slots_ref.shape[1]), 0) + at
     return dot((places == slots_ref[...]).astype(jnp.bfloat16), grad_rows_ref[...])
 
 
-def cand_grad_kernel(slots_ref, grad_rows_ref, cand_grad_ref):
+def cand_grad_kernel(slots_ref, first_ref, second_ref, cand_grad_ref, grad_rows_ref):
+    join_rows((first_ref, second_ref), grad_rows_ref)
     cands = cand_grad_ref.shape[0]
     chunk = math.gcd(cands, 512)
     for at in range(0, cands, chunk):
         cand_grad_ref[at : at + chunk, :] = sum_rows(chunk, at, slots_ref, grad_rows_ref)
 
 
-def own_cand_grad(cands, slots, grad_rows):
-    requests, key_width = grad_rows.shape
+def own_cand_grad(cands, slots, grad_parts):
+    requests, key_width = slots.shape[1], grad_parts[0].shape[1]
     whole = pl.BlockSpec(memory_space=pltpu.VMEM)
     return pl.pallas_call(
         cand_grad_kernel,
-        in_specs=[whole] * 2,
+        in_specs=[whole] * 3,
         out_specs=whole,
         out_shape=jax.ShapeDtypeStruct((cands, key_width), jnp.float32),
+        scratch_shapes=[pltpu.VMEM((requests, key_width), jnp.bfloat16)],
         compiler_params=pltpu.CompilerParams(vmem_limit_bytes=20 * MIB),
         cost_estimate=pl.CostEstimate(
             flops=2 * cands * key_width * requests, bytes_accessed=1 << 22, transcendentals=0
         ),
         name="own_cand_grad",
-    )(slots, grad_rows)
+    )(slots, *grad_parts)
 
 
 def terms_kernel(
-    origins, wide_ref, cand_grad_ref, slots_ref, grad_rows_ref, pooled_ref, out_ref, terms_ref
+    origins,
+    wide_ref,
+    cand_grad_ref,
+    slots_ref,
+    first_ref,
+    second_ref,
+    pooled_ref,
+    out_ref,
+    grad_rows_ref,
+    terms_ref,
 ):
+    join_rows((first_ref, second_ref), grad_rows_ref)
     cands = pooled_ref.shape[0]
     chunk = math.gcd(cands, 512)
     for at in range(0, cands, chunk):
@@ -497,16 +518,19 @@
         out_ref[slot * rows : (slot + batch) * rows, :] = found.astype(jnp.bfloat16)
 
 
-def chip_terms(origins, wide, cand_grad, far_slots, far_grad_rows, pooled):
+def chip_terms(origins, wide, cand_grad, far_slots, far_parts, pooled):
     cands, width = pooled.shape
-    requests, key_width = far_grad_rows.shape
+    requests, key_width = far_slots.shape[1], cand_grad.shape[1]
     whole = pl.BlockSpec(memory_space=pltpu.VMEM)
     return pl.pallas_call(
         functools.partial(terms_kernel, origins),
-        in_specs=[pl.BlockSpec(memory_space=pltpu.SMEM)] + [whole] * 4,
+        in_specs=[pl.BlockSpec(memory_space=pltpu.SMEM)] + [whole] * 5,
         out_specs=whole,
         out_shape=jax.ShapeDtypeStruct((width, key_width), jnp.bfloat16),
-        scratch_shapes=[pltpu.VMEM((width, key_width), jnp.float32)],
+        scratch_shapes=[
+            pltpu.VMEM((requests, key_width), jnp.bfloat16),
+            pltpu.VMEM((width, key_width), jnp.float32),
+        ],
         compiler_params=pltpu.CompilerParams(vmem_limit_bytes=20 * MIB),
         cost_estimate=pl.CostEstimate(
             flops=2 * cands * key_width * (width + requests),
@@ -514,7 +538,7 @@
             transcendentals=0,
         ),
         name="chip_terms",
-    )(wide, cand_grad, far_slots, far_grad_rows, pooled)
+    )(wide, cand_grad, far_slots, *far_parts, pooled)
 
 
 def bit_groups(size):
@@ -606,15 +630,19 @@
                 jnp.concatenate([got, keep], axis=0),
             )
         else:
-            found_pooled = send_stage(pooled, wides, *stages[place - 1])
-            found, found_pooled = lax.optimization_barrier((found, found_pooled))
-            pooled = jnp.concatenate([pooled] + found_pooled, axis=0)
+            bit, values = stages[place - 1]
+            early = send_stage(pooled, wides, bit, values - 1)
+            found, early = lax.optimization_barrier((found, early))
+            late = exchange(after([pooled], *found)[0], "wide", wides, (values - 1) << bit)
+            if place + 1 < len(stages):
+                pooled = jnp.concatenate([pooled] + early + [late], axis=0)
         near = jnp.concatenate([near] + found, axis=0)
     far = exchange(near, "section", 2, 1)
-    found_pooled = send_stage(pooled, wides, *stages[-1])
     queries, attended, slope, mlp_weight = attend(
         inv_count, slots.reshape(requests, 1), near, far, history, usable, mlp_weight
     )
+    pooled = jnp.concatenate(after([pooled] + early + [late], attended), axis=0)
+    found_pooled = send_stage(pooled, wides, *stages[-1])
     logits, grad_att, direct = score(
         inv_count,
         queries,
@@ -623,11 +651,15 @@
         mlp_weight,
         logit_weight.reshape(1, -1),
     )
-    found_pooled, grad_att = lax.optimization_barrier((found_pooled, grad_att))
-    grad_rows = attend_back(grad_att, direct, slope, history)
-    far_grad_rows = exchange(grad_rows, "section", 2, 1)
-    pooled = jnp.concatenate(after([pooled] + found_pooled, grad_rows), axis=0)
-    cand_grad = own_cand_grad(pooled.shape[0], pooled_slots.reshape(1, requests), grad_rows)
+    half = users // 2
+    first_rows = attend_back(0, half, grad_att, direct, slope, history)
+    found_pooled, grad_att, first_rows = lax.optimization_barrier(
+        (found_pooled, grad_att, first_rows)
+    )
+    pooled = jnp.concatenate([pooled] + found_pooled, axis=0)
+    grad_parts = [first_rows, attend_back(half, users - half, grad_att, direct, slope, history)]
+    far_parts = [exchange(part, "section", 2, 1) for part in grad_parts]
+    cand_grad = own_cand_grad(pooled.shape[0], pooled_slots.reshape(1, requests), grad_parts)
     origins = [0] * wides
     for distance in range(wides):
         origins[slot_of(distance, wides)] = distance
@@ -636,7 +668,7 @@
         wide.reshape(1),
         cand_grad,
         far_slots.reshape(1, requests),
-        far_grad_rows,
+        far_parts,
         pooled,
     )
     grad_proj, logits = sum_blocks(terms, wides, logits.reshape(requests))

time: 84.7 us -> 87.8 us (1.037)
  starting transfers between devices: 23.3 us -> 25.3 us
    ppermute x22 -> x23, starting transfers between devices: 23.3 us -> 25.3 us  [exchange(): lax.ppermute(values, axis_name, [(i, i ^ distance) for i in range(size)])]
    ppermute x22 -> x23, waiting for transfers between devices: 21.1 us -> 21.9 us  [exchange(): lax.ppermute(values, axis_name, [(i, i ^ distance) for i in range(size)])]
    pallas_call x2 -> x3, Pallas kernels: 5.69 us -> 5.84 us  [the longest x2 4.86 us: attend_back(): pl.pallas_call(functools.partial(attend_back_kernel, first), in_specs=[wh...]
  transfers between devices with their start and end apart: 22 -> 23, of which waited for: 11 -> 14; matrix products, arithmetic and copies ran while one was open for 2% -> 2% of each run, Pallas kernels for 18% -> 20%
where the time goes in v5:
time: 87.8 us; the launch traced here: 87.6 us
  Pallas kernels  36.9 us (42%)
  starting transfers between devices  25.3 us (29%)
  waiting for transfers between devices  21.9 us (25%)
  other arithmetic  1.74 us (2%)
  between operations  1.23 us (1%)
    ppermute x23, starting transfers between devices, exchange(): lax.ppermute(values, axis_name, [(i, i ^ distance) for i in range(size)])  25.3 us
    ppermute x23, waiting for transfers between devices, exchange(): lax.ppermute(values, axis_name, [(i, i ^ distance) for i in range(size)])  21.9 us
    pallas_call x1, Pallas kernels, encode_block(): pl.pallas_call(functools.partial(encode_kernel, tokens), in_specs=[pl.Blo...  14.7 us
    pallas_call x1, Pallas kernels, attend(): pl.pallas_call(attend_kernel, in_specs=[pl.BlockSpec(memory_space=pltpu.S...  7.76 us
    pallas_call x1, Pallas kernels, score(): pl.pallas_call(score_kernel, in_specs=[pl.BlockSpec(memory_space=pltpu.SM...  6.87 us
    pallas_call x2, Pallas kernels, attend_back(): pl.pallas_call(functools.partial(attend_back_kernel, first), in_specs=[wh...  4.86 us
  transfers between devices with their start and end apart: 23, of which 14 were waited for; matrix products, arithmetic and copies ran while one was open for 2% of the time, Pallas kernels for 20%

profile of v5, /device:TPU:0, one launch (start us, length us, event | category | flops | bytes accessed | tf_op | source)
XLA Modules:
  0.0 87.6 jit_solution(10149019069652559764)
XLA Ops:
  0.7 14.7 %encode.1 = (bf16[32,512]{1,0:T(8,128)(2,1)S(1)}, bf16[32,512]{1,0:T(8,128)(2,1)S(1)}, bf16[32,512]{1,0:T(8,128)(2,1)S(1)}) custom-call(s32[1]{0:T(128)} %bitcast.1.core_ref, bf16[1536,1024]{1,0:T(8,128)(2,1)} %bitcast.5, bf16[1024,3072]{1,0:T(8,128)(2,1)} %qkv_hbm.1, bf16[1024,1024]{1,0:T(8,128)(2,1)} %out_hbm.1, bf16[1024,512]{1,0:T(8,128)(2,1)} %proj_hbm.1), custom_call_target="tpu_custom_call" | custom-call | flops 8053063680 | bytes 16777216 | tf_op jit(solution)/shard_map/encode/pallas_call | solution.py:237
  15.4 5.1 %collective-permute-start.2 = (bf16[32,512]{1,0:T(8,128)(2,1)S(1)}, bf16[32,512]{1,0:T(8,128)(2,1)S(1)}, u32[]{:S(2)}, u32[]{:S(2)}) collective-permute-start(bf16[32,512]{1,0:T(8,128)(2,1)S(1)} %get-tuple-element.35), channel_id=1, source_target_pairs={{0,12},{1,13},{2,14},{3,15},{4,8},{5,9},{6,10},{7,11},{8,4},{9,5},... | collective-permute-start | bytes 98312 | tf_op jit(solution)/shard_map/ppermute | solution.py:555
  22.7 2.7 %collective-permute-done.1 = bf16[32,512]{1,0:T(8,128)(2,1)S(1)} collective-permute-done((bf16[32,512]{1,0:T(8,128)(2,1)S(1)}, bf16[32,512]{1,0:T(8,128)(2,1)S(1)}, u32[]{:S(2)}, u32[]{:S(2)}) %collective-permute-start.1) | collective-permute-done | bytes 32800 | tf_op jit(solution)/shard_map/ppermute | solution.py:555
  25.4 2.5 %collective-permute-start.7 = (bf16[128,512]{1,0:T(8,128)(2,1)S(1)}, bf16[128,512]{1,0:T(8,128)(2,1)S(1)}, u32[]{:S(2)}, u32[]{:S(2)}) collective-permute-start(bf16[128,512]{1,0:T(8,128)(2,1)S(1)} %get-tuple-element.85), channel_id=1, source_target_pairs={{0,3},{1,2},{2,1},{3,0},{4,7},{5,6},{6,5},{7,4},{8,11},{9,10},{10,... | collective-permute-start | bytes 393224 | tf_op jit(solution)/shard_map/ppermute | solution.py:555
  29.0 2.1 %collective-permute-start.9 = (bf16[64,512]{1,0:T(8,128)(2,1)S(1)}, bf16[64,512]{1,0:T(8,128)(2,1)S(1)}, u32[]{:S(2)}, u32[]{:S(2)}) collective-permute-start(bf16[64,512]{1,0:T(8,128)(2,1)S(1)} %maximum_select_fusion), channel_id=1, source_target_pairs={{0,8},{1,9},{2,10},{3,11},{4,12},{5,13},{6,14},{7,15},{8,0},{9,1},... | collective-permute-start | bytes 196616 | tf_op jit(solution)/shard_map/ppermute | solution.py:555
  31.1 3.1 %collective-permute-done.9 = bf16[64,512]{1,0:T(8,128)(2,1)S(1)} collective-permute-done((bf16[64,512]{1,0:T(8,128)(2,1)S(1)}, bf16[64,512]{1,0:T(8,128)(2,1)S(1)}, u32[]{:S(2)}, u32[]{:S(2)}) %collective-permute-start.9) | collective-permute-done | bytes 65568 | tf_op jit(solution)/shard_map/ppermute | solution.py:555
  34.2 1.1 %collective-permute-done.8 = bf16[64,512]{1,0:T(8,128)(2,1)S(1)} collective-permute-done((bf16[64,512]{1,0:T(8,128)(2,1)S(1)}, bf16[64,512]{1,0:T(8,128)(2,1)S(1)}, u32[]{:S(2)}, u32[]{:S(2)}) %collective-permute-start.8) | collective-permute-done | bytes 65568 | tf_op jit(solution)/shard_map/ppermute | solution.py:555
  36.3 1.1 %collective-permute-start.10 = (bf16[64,512]{1,0:T(8,128)(2,1)S(1)}, bf16[64,512]{1,0:T(8,128)(2,1)S(1)}, u32[]{:S(2)}, u32[]{:S(2)}) collective-permute-start(bf16[64,512]{1,0:T(8,128)(2,1)S(1)} %maximum_select_fusion), channel_id=1, source_target_pairs={{0,12},{1,13},{2,14},{3,15},{4,8},{5,9},{6,10},{7,11},{8,4},{9,5},... | collective-permute-start | bytes 196616 | tf_op jit(solution)/shard_map/ppermute | solution.py:555
  37.4 7.8 %attend.1 = (bf16[768,512]{1,0:T(8,128)(2,1)S(1)}, f32[768,512]{1,0:T(8,128)S(1)}, bf16[768,2048]{1,0:T(8,128)(2,1)S(1)}, bf16[1536,1024]{1,0:T(8,128)(2,1)S(1)}) custom-call(f32[4]{0:T(128)S(1)} %rsqrt.3.inv_ref, s32[768,1]{1,0:T(8,128)S(1)} %reshape.68.slots_ref, bf16[512,512]{1,0:T(8,128)(2,1)S(1)} %constant_dynamic-update-slice_fusion.4.near_ref, ...), custom_call_target="tpu_custom_call" | custom-call | flops 3221225472 | bytes 16777216 | tf_op jit(solution)/shard_map/attend/pallas_call | solution.py:320
  45.3 2.5 %collective-permute-start.14 = (bf16[256,512]{1,0:T(8,128)(2,1)S(1)}, bf16[256,512]{1,0:T(8,128)(2,1)S(1)}, u32[]{:S(2)}, u32[]{:S(2)}) collective-permute-start(bf16[256,512]{1,0:T(8,128)(2,1)S(1)} %get-tuple-element.77), channel_id=1, source_target_pairs={{0,3},{1,2},{2,1},{3,0},{4,7},{5,6},{6,5},{7,4},{8,11},{9,10},{10,... | collective-permute-start | bytes 786440 | tf_op jit(solution)/shard_map/ppermute | solution.py:555
  48.8 6.9 %score.1 = (f32[768,1]{1,0:T(8,128)S(1)}, bf16[768,512]{1,0:T(8,128)(2,1)S(1)}, f32[768,512]{1,0:T(8,128)S(1)}) custom-call(f32[4]{0:T(128)S(1)} %rsqrt.3.inv_ref, bf16[768,512]{1,0:T(8,128)(2,1)S(1)} %get-tuple-element.54.queries_ref, f32[768,512]{1,0:T(8,128)S(1)} %get-tuple-element.49.attended_ref, s32[768,1]{1,0:T(8,128)S(1)} %reshape.69.labels_ref, ...), custom_call_target="tpu_custom_call" | custom-call | flops 4831838208 | bytes 8388608 | tf_op jit(solution)/shard_map/score/pallas_call | solution.py:393
  55.7 2.3 %attend_back.2.first_ref = bf16[384,512]{1,0:T(8,128)(2,1)S(1)} custom-call(bf16[768,512]{1,0:T(8,128)(2,1)S(1)} %get-tuple-element.60.grad_att_ref, f32[768,512]{1,0:T(8,128)S(1)} %get-tuple-element.57.direct_ref, bf16[768,2048]{1,0:T(8,128)(2,1)S(1)} %get-tuple-element.58.slope_ref, bf16[4,2048,512]{2,1,0:T(8,128)(2,1)S(1)} %bitcast.4), custom_call_target="tpu_custom_call" | custom-call | flops 1610612736 | bytes 8388608 | tf_op jit(solution)/shard_map/attend_back/pallas_call | solution.py:433
  58.1 2.2 %collective-permute-done.13 = bf16[256,512]{1,0:T(8,128)(2,1)S(1)} collective-permute-done((bf16[256,512]{1,0:T(8,128)(2,1)S(1)}, bf16[256,512]{1,0:T(8,128)(2,1)S(1)}, u32[]{:S(2)}, u32[]{:S(2)}) %collective-permute-start.13) | collective-permute-done | bytes 262176 | tf_op jit(solution)/shard_map/ppermute | solution.py:555
  60.4 2.5 %attend_back.3.second_ref = bf16[384,512]{1,0:T(8,128)(2,1)S(1)} custom-call(bf16[768,512]{1,0:T(8,128)(2,1)S(1)} %get-tuple-element.60.grad_att_ref, f32[768,512]{1,0:T(8,128)S(1)} %get-tuple-element.57.direct_ref, bf16[768,2048]{1,0:T(8,128)(2,1)S(1)} %get-tuple-element.58.slope_ref, bf16[4,2048,512]{2,1,0:T(8,128)(2,1)S(1)} %bitcast.4), custom_call_target="tpu_custom_call" | custom-call | flops 1610612736 | bytes 8388608 | tf_op jit(solution)/shard_map/attend_back/pallas_call | solution.py:433
  65.3 1.7 %chip_terms.1 = bf16[512,512]{1,0:T(8,128)(2,1)S(1)} custom-call(s32[1]{0:T(128)} %bitcast.wide_ref, f32[1024,512]{1,0:T(8,128)S(1)} %own_cand_grad.1.cand_grad_ref, s32[1,768]{1,0:T(1,128)S(1)} %reshape.66.slots_ref, bf16[384,512]{1,0:T(8,128)(2,1)S(1)} %collective-permute-done.15.first_ref, bf16[384,512]{1,0:T(8,128)(2,1)S(1)} %collective-permute-done.16.second_ref, ...), custom_call_target="tpu_custom_call" | custom-call | flops 1342177280 | bytes 4194304 | tf_op jit(solution)/shard_map/chip_terms/pallas_call | solution.py:525
  67.0 1.6 %collective-permute-start.17 = (bf16[128,512]{1,0:T(8,128)(2,1)S(1)}, bf16[128,512]{1,0:T(8,128)(2,1)S(1)}, u32[]{:S(2)}, u32[]{:S(2)}) collective-permute-start(bf16[128,512]{1,0:T(8,128)(2,1)S(1)} %get-tuple-element.70), channel_id=1, source_target_pairs={{0,1},{1,0},{2,3},{3,2},{4,5},{5,4},{6,7},{7,6},{8,9},{9,8},{10,11... | collective-permute-start | bytes 393224 | tf_op jit(solution)/shard_map/ppermute | solution.py:555
  68.6 1.4 %collective-permute-start.19 = (bf16[128,512]{1,0:T(8,128)(2,1)S(1)}, bf16[128,512]{1,0:T(8,128)(2,1)S(1)}, u32[]{:S(2)}, u32[]{:S(2)}) collective-permute-start(bf16[128,512]{1,0:T(8,128)(2,1)S(1)} %get-tuple-element.71), channel_id=1, source_target_pairs={{0,3},{1,2},{2,1},{3,0},{4,7},{5,6},{6,5},{7,4},{8,11},{9,10},{10,... | collective-permute-start | bytes 393224 | tf_op jit(solution)/shard_map/ppermute | solution.py:555
  71.3 2.1 %collective-permute-done.17 = bf16[128,512]{1,0:T(8,128)(2,1)S(1)} collective-permute-done((bf16[128,512]{1,0:T(8,128)(2,1)S(1)}, bf16[128,512]{1,0:T(8,128)(2,1)S(1)}, u32[]{:S(2)}, u32[]{:S(2)}) %collective-permute-start.17) | collective-permute-done | bytes 131104 | tf_op jit(solution)/shard_map/ppermute | solution.py:555
  73.4 3.0 %collective-permute-done.19 = bf16[128,512]{1,0:T(8,128)(2,1)S(1)} collective-permute-done((bf16[128,512]{1,0:T(8,128)(2,1)S(1)}, bf16[128,512]{1,0:T(8,128)(2,1)S(1)}, u32[]{:S(2)}, u32[]{:S(2)}) %collective-permute-start.19) | collective-permute-done | bytes 131104 | tf_op jit(solution)/shard_map/ppermute | solution.py:555
  76.4 1.4 %collective-permute-done.18 = bf16[128,512]{1,0:T(8,128)(2,1)S(1)} collective-permute-done((bf16[128,512]{1,0:T(8,128)(2,1)S(1)}, bf16[128,512]{1,0:T(8,128)(2,1)S(1)}, u32[]{:S(2)}, u32[]{:S(2)}) %collective-permute-start.18) | collective-permute-done | bytes 131104 | tf_op jit(solution)/shard_map/ppermute | solution.py:555
  78.5 2.8 %collective-permute-start.21 = (bf16[32,512]{1,0:T(8,128)(2,1)S(1)}, bf16[32,512]{1,0:T(8,128)(2,1)S(1)}, u32[]{:S(2)}, u32[]{:S(2)}) collective-permute-start(bf16[32,512]{1,0:T(8,128)(2,1)S(1)} %get-tuple-element.74), channel_id=1, source_target_pairs={{0,8},{1,9},{2,10},{3,11},{4,12},{5,13},{6,14},{7,15},{8,0},{9,1},... | collective-permute-start | bytes 98312 | tf_op jit(solution)/shard_map/ppermute | solution.py:555
  81.3 1.0 %collective-permute-start.22 = (bf16[32,512]{1,0:T(8,128)(2,1)S(1)}, bf16[32,512]{1,0:T(8,128)(2,1)S(1)}, u32[]{:S(2)}, u32[]{:S(2)}) collective-permute-start(bf16[32,512]{1,0:T(8,128)(2,1)S(1)} %get-tuple-element.75), channel_id=1, source_target_pairs={{0,12},{1,13},{2,14},{3,15},{4,8},{5,9},{6,10},{7,11},{8,4},{9,5},... | collective-permute-start | bytes 98312 | tf_op jit(solution)/shard_map/ppermute | solution.py:555
  82.3 1.0 %collective-permute-done.21 = bf16[32,512]{1,0:T(8,128)(2,1)S(1)} collective-permute-done((bf16[32,512]{1,0:T(8,128)(2,1)S(1)}, bf16[32,512]{1,0:T(8,128)(2,1)S(1)}, u32[]{:S(2)}, u32[]{:S(2)}) %collective-permute-start.21) | collective-permute-done | bytes 32800 | tf_op jit(solution)/shard_map/ppermute | solution.py:555
  83.3 3.6 %collective-permute-done.22 = bf16[32,512]{1,0:T(8,128)(2,1)S(1)} collective-permute-done((bf16[32,512]{1,0:T(8,128)(2,1)S(1)}, bf16[32,512]{1,0:T(8,128)(2,1)S(1)}, u32[]{:S(2)}, u32[]{:S(2)}) %collective-permute-start.22) | collective-permute-done | bytes 32800 | tf_op jit(solution)/shard_map/ppermute | solution.py:555
  (77 shorter events, 10.2 us)
Async XLA Ops:
  0.7 35.4 %copy-start.1 = (s32[768]{0:T(1024)S(1)}, s32[768]{0:T(1024)}, u32[]{:S(2)}) copy-start(s32[768]{0:T(1024)} %param.23) | copy-start | bytes 9220
  15.4 7.3 %collective-permute-start.2 = (bf16[32,512]{1,0:T(8,128)(2,1)S(1)}, bf16[32,512]{1,0:T(8,128)(2,1)S(1)}, u32[]{:S(2)}, u32[]{:S(2)}) collective-permute-start(bf16[32,512]{1,0:T(8,128)(2,1)S(1)} %get-tuple-element.35), channel_id=1, source_target_pairs={{0,12},{1,13},{2,14},{3,15},{4,8},{5,9},{6,10},{7,11},{8,4},{9,5},... | collective-permute-start | bytes 98312 | tf_op jit(solution)/shard_map/ppermute | solution.py:555
  20.6 4.8 %collective-permute-start.1 = (bf16[32,512]{1,0:T(8,128)(2,1)S(1)}, bf16[32,512]{1,0:T(8,128)(2,1)S(1)}, u32[]{:S(2)}, u32[]{:S(2)}) collective-permute-start(bf16[32,512]{1,0:T(8,128)(2,1)S(1)} %get-tuple-element.35), channel_id=1, source_target_pairs={{0,8},{1,9},{2,10},{3,11},{4,12},{5,13},{6,14},{7,15},{8,0},{9,1},... | collective-permute-start | bytes 98312 | tf_op jit(solution)/shard_map/ppermute | solution.py:555
  20.6 4.8 %collective-permute-start = (bf16[32,512]{1,0:T(8,128)(2,1)S(1)}, bf16[32,512]{1,0:T(8,128)(2,1)S(1)}, u32[]{:S(2)}, u32[]{:S(2)}) collective-permute-start(bf16[32,512]{1,0:T(8,128)(2,1)S(1)} %get-tuple-element.35), channel_id=1, source_target_pairs={{0,4},{1,5},{2,6},{3,7},{4,0},{5,1},{6,2},{7,3},{8,12},{9,13},{10,... | collective-permute-start | bytes 98312 | tf_op jit(solution)/shard_map/ppermute | solution.py:555
  21.3 1.2 %collective-permute-start.4 = (s32[768]{0:T(1024)S(1)}, s32[768]{0:T(1024)S(1)}, u32[]{:S(2)}, u32[]{:S(2)}) collective-permute-start(s32[768]{0:T(1024)S(1)} %get-tuple-element.93), channel_id=1, source_target_pairs={{0,16},{16,0},{1,17},{17,1},{2,18},{18,2},{3,19},{19,3},{4,20},{20... | collective-permute-start | bytes 9224 | tf_op jit(solution)/shard_map/ppermute | solution.py:555
  21.3 1.4 %collective-permute-start.3 = (bf16[32,512]{1,0:T(8,128)(2,1)S(1)}, bf16[32,512]{1,0:T(8,128)(2,1)S(1)}, u32[]{:S(2)}, u32[]{:S(2)}) collective-permute-start(bf16[32,512]{1,0:T(8,128)(2,1)S(1)} %get-tuple-element.37), channel_id=1, source_target_pairs={{0,16},{16,0},{1,17},{17,1},{2,18},{18,2},{3,19},{19,3},{4,20},{20... | collective-permute-start | bytes 98312 | tf_op jit(solution)/shard_map/ppermute | solution.py:555
  25.4 9.9 %collective-permute-start.7 = (bf16[128,512]{1,0:T(8,128)(2,1)S(1)}, bf16[128,512]{1,0:T(8,128)(2,1)S(1)}, u32[]{:S(2)}, u32[]{:S(2)}) collective-permute-start(bf16[128,512]{1,0:T(8,128)(2,1)S(1)} %get-tuple-element.85), channel_id=1, source_target_pairs={{0,3},{1,2},{2,1},{3,0},{4,7},{5,6},{6,5},{7,4},{8,11},{9,10},{10,... | collective-permute-start | bytes 393224 | tf_op jit(solution)/shard_map/ppermute | solution.py:555
  27.9 7.4 %collective-permute-start.6 = (bf16[128,512]{1,0:T(8,128)(2,1)S(1)}, bf16[128,512]{1,0:T(8,128)(2,1)S(1)}, u32[]{:S(2)}, u32[]{:S(2)}) collective-permute-start(bf16[128,512]{1,0:T(8,128)(2,1)S(1)} %get-tuple-element.85), channel_id=1, source_target_pairs={{0,2},{1,3},{2,0},{3,1},{4,6},{5,7},{6,4},{7,5},{8,10},{9,11},{10,... | collective-permute-start | bytes 393224 | tf_op jit(solution)/shard_map/ppermute | solution.py:555
  28.4 6.9 %collective-permute-start.5 = (bf16[128,512]{1,0:T(8,128)(2,1)S(1)}, bf16[128,512]{1,0:T(8,128)(2,1)S(1)}, u32[]{:S(2)}, u32[]{:S(2)}) collective-permute-start(bf16[128,512]{1,0:T(8,128)(2,1)S(1)} %get-tuple-element.85), channel_id=1, source_target_pairs={{0,1},{1,0},{2,3},{3,2},{4,5},{5,4},{6,7},{7,6},{8,9},{9,8},{10,11... | collective-permute-start | bytes 393224 | tf_op jit(solution)/shard_map/ppermute | solution.py:555
  29.0 5.2 %collective-permute-start.9 = (bf16[64,512]{1,0:T(8,128)(2,1)S(1)}, bf16[64,512]{1,0:T(8,128)(2,1)S(1)}, u32[]{:S(2)}, u32[]{:S(2)}) collective-permute-start(bf16[64,512]{1,0:T(8,128)(2,1)S(1)} %maximum_select_fusion), channel_id=1, source_target_pairs={{0,8},{1,9},{2,10},{3,11},{4,12},{5,13},{6,14},{7,15},{8,0},{9,1},... | collective-permute-start | bytes 196616 | tf_op jit(solution)/shard_map/ppermute | solution.py:555
  31.1 4.3 %collective-permute-start.8 = (bf16[64,512]{1,0:T(8,128)(2,1)S(1)}, bf16[64,512]{1,0:T(8,128)(2,1)S(1)}, u32[]{:S(2)}, u32[]{:S(2)}) collective-permute-start(bf16[64,512]{1,0:T(8,128)(2,1)S(1)} %maximum_select_fusion), channel_id=1, source_target_pairs={{0,4},{1,5},{2,6},{3,7},{4,0},{5,1},{6,2},{7,3},{8,12},{9,13},{10,... | collective-permute-start | bytes 196616 | tf_op jit(solution)/shard_map/ppermute | solution.py:555
  35.4 2.0 %collective-permute-start.11 = (bf16[512,512]{1,0:T(8,128)(2,1)S(1)}, bf16[512,512]{1,0:T(8,128)(2,1)S(1)}, u32[]{:S(2)}, u32[]{:S(2)}) collective-permute-start(bf16[512,512]{1,0:T(8,128)(2,1)S(1)} %constant_dynamic-update-slice_fusion.4.near_ref), channel_id=1, source_target_pairs={{0,16},{16,0},{1,17},{17,1},{2,18},{18,2},{3,19},{19,3},{4,20},{20... | collective-permute-start | bytes 1572872 | tf_op jit(solution)/shard_map/ppermute | solution.py:555
  36.3 8.9 %collective-permute-start.10 = (bf16[64,512]{1,0:T(8,128)(2,1)S(1)}, bf16[64,512]{1,0:T(8,128)(2,1)S(1)}, u32[]{:S(2)}, u32[]{:S(2)}) collective-permute-start(bf16[64,512]{1,0:T(8,128)(2,1)S(1)} %maximum_select_fusion), channel_id=1, source_target_pairs={{0,12},{1,13},{2,14},{3,15},{4,8},{5,9},{6,10},{7,11},{8,4},{9,5},... | collective-permute-start | bytes 196616 | tf_op jit(solution)/shard_map/ppermute | solution.py:555
  45.3 12.8 %collective-permute-start.14 = (bf16[256,512]{1,0:T(8,128)(2,1)S(1)}, bf16[256,512]{1,0:T(8,128)(2,1)S(1)}, u32[]{:S(2)}, u32[]{:S(2)}) collective-permute-start(bf16[256,512]{1,0:T(8,128)(2,1)S(1)} %get-tuple-element.77), channel_id=1, source_target_pairs={{0,3},{1,2},{2,1},{3,0},{4,7},{5,6},{6,5},{7,4},{8,11},{9,10},{10,... | collective-permute-start | bytes 786440 | tf_op jit(solution)/shard_map/ppermute | solution.py:555
  47.8 12.5 %collective-permute-start.13 = (bf16[256,512]{1,0:T(8,128)(2,1)S(1)}, bf16[256,512]{1,0:T(8,128)(2,1)S(1)}, u32[]{:S(2)}, u32[]{:S(2)}) collective-permute-start(bf16[256,512]{1,0:T(8,128)(2,1)S(1)} %get-tuple-element.77), channel_id=1, source_target_pairs={{0,2},{1,3},{2,0},{3,1},{4,6},{5,7},{6,4},{7,5},{8,10},{9,11},{10,... | collective-permute-start | bytes 786440 | tf_op jit(solution)/shard_map/ppermute | solution.py:555
  48.3 12.1 %collective-permute-start.12 = (bf16[256,512]{1,0:T(8,128)(2,1)S(1)}, bf16[256,512]{1,0:T(8,128)(2,1)S(1)}, u32[]{:S(2)}, u32[]{:S(2)}) collective-permute-start(bf16[256,512]{1,0:T(8,128)(2,1)S(1)} %get-tuple-element.77), channel_id=1, source_target_pairs={{0,1},{1,0},{2,3},{3,2},{4,5},{5,4},{6,7},{7,6},{8,9},{9,8},{10,11... | collective-permute-start | bytes 786440 | tf_op jit(solution)/shard_map/ppermute | solution.py:555
  62.9 1.8 %collective-permute-start.16 = (bf16[384,512]{1,0:T(8,128)(2,1)S(1)}, bf16[384,512]{1,0:T(8,128)(2,1)S(1)}, u32[]{:S(2)}, u32[]{:S(2)}) collective-permute-start(bf16[384,512]{1,0:T(8,128)(2,1)S(1)} %attend_back.3.second_ref), channel_id=1, source_target_pairs={{0,16},{16,0},{1,17},{17,1},{2,18},{18,2},{3,19},{19,3},{4,20},{20... | collective-permute-start | bytes 1179656 | tf_op jit(solution)/shard_map/ppermute | solution.py:555
  63.0 2.3 %collective-permute-start.15 = (bf16[384,512]{1,0:T(8,128)(2,1)S(1)}, bf16[384,512]{1,0:T(8,128)(2,1)S(1)}, u32[]{:S(2)}, u32[]{:S(2)}) collective-permute-start(bf16[384,512]{1,0:T(8,128)(2,1)S(1)} %attend_back.2.first_ref), channel_id=1, source_target_pairs={{0,16},{16,0},{1,17},{17,1},{2,18},{18,2},{3,19},{19,3},{4,20},{20... | collective-permute-start | bytes 1179656 | tf_op jit(solution)/shard_map/ppermute | solution.py:555
  67.0 6.4 %collective-permute-start.17 = (bf16[128,512]{1,0:T(8,128)(2,1)S(1)}, bf16[128,512]{1,0:T(8,128)(2,1)S(1)}, u32[]{:S(2)}, u32[]{:S(2)}) collective-permute-start(bf16[128,512]{1,0:T(8,128)(2,1)S(1)} %get-tuple-element.70), channel_id=1, source_target_pairs={{0,1},{1,0},{2,3},{3,2},{4,5},{5,4},{6,7},{7,6},{8,9},{9,8},{10,11... | collective-permute-start | bytes 393224 | tf_op jit(solution)/shard_map/ppermute | solution.py:555
  68.6 7.8 %collective-permute-start.19 = (bf16[128,512]{1,0:T(8,128)(2,1)S(1)}, bf16[128,512]{1,0:T(8,128)(2,1)S(1)}, u32[]{:S(2)}, u32[]{:S(2)}) collective-permute-start(bf16[128,512]{1,0:T(8,128)(2,1)S(1)} %get-tuple-element.71), channel_id=1, source_target_pairs={{0,3},{1,2},{2,1},{3,0},{4,7},{5,6},{6,5},{7,4},{8,11},{9,10},{10,... | collective-permute-start | bytes 393224 | tf_op jit(solution)/shard_map/ppermute | solution.py:555
  70.0 7.8 %collective-permute-start.18 = (bf16[128,512]{1,0:T(8,128)(2,1)S(1)}, bf16[128,512]{1,0:T(8,128)(2,1)S(1)}, u32[]{:S(2)}, u32[]{:S(2)}) collective-permute-start(bf16[128,512]{1,0:T(8,128)(2,1)S(1)} %get-tuple-element.72), channel_id=1, source_target_pairs={{0,2},{1,3},{2,0},{3,1},{4,6},{5,7},{6,4},{7,5},{8,10},{9,11},{10,... | collective-permute-start | bytes 393224 | tf_op jit(solution)/shard_map/ppermute | solution.py:555
  77.9 4.5 %collective-permute-start.20 = (bf16[32,512]{1,0:T(8,128)(2,1)S(1)}, bf16[32,512]{1,0:T(8,128)(2,1)S(1)}, u32[]{:S(2)}, u32[]{:S(2)}) collective-permute-start(bf16[32,512]{1,0:T(8,128)(2,1)S(1)} %get-tuple-element.73), channel_id=1, source_target_pairs={{0,4},{1,5},{2,6},{3,7},{4,0},{5,1},{6,2},{7,3},{8,12},{9,13},{10,... | collective-permute-start | bytes 98312 | tf_op jit(solution)/shard_map/ppermute | solution.py:555
  78.5 4.8 %collective-permute-start.21 = (bf16[32,512]{1,0:T(8,128)(2,1)S(1)}, bf16[32,512]{1,0:T(8,128)(2,1)S(1)}, u32[]{:S(2)}, u32[]{:S(2)}) collective-permute-start(bf16[32,512]{1,0:T(8,128)(2,1)S(1)} %get-tuple-element.74), channel_id=1, source_target_pairs={{0,8},{1,9},{2,10},{3,11},{4,12},{5,13},{6,14},{7,15},{8,0},{9,1},... | collective-permute-start | bytes 98312 | tf_op jit(solution)/shard_map/ppermute | solution.py:555
  81.3 5.7 %collective-permute-start.22 = (bf16[32,512]{1,0:T(8,128)(2,1)S(1)}, bf16[32,512]{1,0:T(8,128)(2,1)S(1)}, u32[]{:S(2)}, u32[]{:S(2)}) collective-permute-start(bf16[32,512]{1,0:T(8,128)(2,1)S(1)} %get-tuple-element.75), channel_id=1, source_target_pairs={{0,12},{1,13},{2,14},{3,15},{4,8},{5,9},{6,10},{7,11},{8,4},{9,5},... | collective-permute-start | bytes 98312 | tf_op jit(solution)/shard_map/ppermute | solution.py:555
  (7 other events, 159.8 us)

commit v6 on v5

--- a/solution.py
+++ b/solution.py
@@ -556,7 +556,8 @@
 
 
 def send_stage(rows, wides, bit, values):
-    return [exchange(rows, "wide", wides, step << bit) for step in range(1, values)]
+    found = [exchange(rows, "wide", wides, step << bit) for step in reversed(range(1, values))]
+    return found[::-1]
 
 
 def after(values, *others):
@@ -578,7 +579,7 @@
         parts = total.astype(jnp.bfloat16).reshape((values, -1) + blocks.shape[1:])
         found = [
             exchange(parts[step], "wide", wides, step << bit).astype(jnp.float32)
-            for step in range(1, values)
+            for step in reversed(range(1, values))
         ]
         total = sum(found, parts[0].astype(jnp.float32))
     return total, logits
@@ -651,7 +652,7 @@
         mlp_weight,
         logit_weight.reshape(1, -1),
     )
-    half = users // 2
+    half = max(1, users - 1)
     first_rows = attend_back(0, half, grad_att, direct, slope, history)
     found_pooled, grad_att, first_rows = lax.optimization_barrier(
         (found_pooled, grad_att, first_rows)

time: 87.8 us -> 83.3 us (0.949)
  waiting for transfers between devices: 21.9 us -> 17.4 us
    ppermute x23, waiting for transfers between devices: 21.9 us -> 17.4 us  [exchange(): lax.ppermute(values, axis_name, [(i, i ^ distance) for i in range(size)])]
  transfers between devices with their start and end apart: 23 -> 23, of which waited for: 14 -> 11; matrix products, arithmetic and copies ran while one was open for 2% -> 2% of each run, Pallas kernels for 20% -> 25%
where the time goes in v6:
time: 83.3 us; the launch traced here: 83.2 us
  Pallas kernels  36.9 us (44%)
  starting transfers between devices  25.3 us (30%)
  waiting for transfers between devices  17.4 us (21%)
  other arithmetic  1.74 us (2%)
  between operations  1.03 us (1%)
    ppermute x23, starting transfers between devices, exchange(): lax.ppermute(values, axis_name, [(i, i ^ distance) for i in range(size)])  25.3 us
    ppermute x23, waiting for transfers between devices, exchange(): lax.ppermute(values, axis_name, [(i, i ^ distance) for i in range(size)])  17.4 us
    pallas_call x1, Pallas kernels, encode_block(): pl.pallas_call(functools.partial(encode_kernel, tokens), in_specs=[pl.Blo...  14.7 us
    pallas_call x1, Pallas kernels, attend(): pl.pallas_call(attend_kernel, in_specs=[pl.BlockSpec(memory_space=pltpu.S...  7.75 us
    pallas_call x1, Pallas kernels, score(): pl.pallas_call(score_kernel, in_specs=[pl.BlockSpec(memory_space=pltpu.SM...  6.87 us
    pallas_call x2, Pallas kernels, attend_back(): pl.pallas_call(functools.partial(attend_back_kernel, first), in_specs=[wh...  4.85 us
    pallas_call x1, Pallas kernels, chip_terms(): pl.pallas_call(functools.partial(terms_kernel, origins), in_specs=[pl.Blo...  1.73 us
  transfers between devices with their start and end apart: 23, of which 11 were waited for; matrix products, arithmetic and copies ran while one was open for 2% of the time, Pallas kernels for 25%

profile of v6, /device:TPU:0, one launch (start us, length us, event | category | flops | bytes accessed | tf_op | source)
XLA Modules:
  0.0 83.2 jit_solution(15265100250759330456)
XLA Ops:
  0.7 14.7 %encode.1 = (bf16[32,512]{1,0:T(8,128)(2,1)S(1)}, bf16[32,512]{1,0:T(8,128)(2,1)S(1)}, bf16[32,512]{1,0:T(8,128)(2,1)S(1)}) custom-call(s32[1]{0:T(128)} %bitcast.1.core_ref, bf16[1536,1024]{1,0:T(8,128)(2,1)} %bitcast.5, bf16[1024,3072]{1,0:T(8,128)(2,1)} %qkv_hbm.1, bf16[1024,1024]{1,0:T(8,128)(2,1)} %out_hbm.1, bf16[1024,512]{1,0:T(8,128)(2,1)} %proj_hbm.1), custom_call_target="tpu_custom_call" | custom-call | flops 8053063680 | bytes 16777216 | tf_op jit(solution)/shard_map/encode/pallas_call | solution.py:237
  15.4 5.1 %collective-permute-start.2 = (bf16[32,512]{1,0:T(8,128)(2,1)S(1)}, bf16[32,512]{1,0:T(8,128)(2,1)S(1)}, u32[]{:S(2)}, u32[]{:S(2)}) collective-permute-start(bf16[32,512]{1,0:T(8,128)(2,1)S(1)} %get-tuple-element.35), channel_id=1, source_target_pairs={{0,12},{1,13},{2,14},{3,15},{4,8},{5,9},{6,10},{7,11},{8,4},{9,5},... | collective-permute-start | bytes 98312 | tf_op jit(solution)/shard_map/ppermute | solution.py:555
  22.7 2.7 %collective-permute-done.1 = bf16[32,512]{1,0:T(8,128)(2,1)S(1)} collective-permute-done((bf16[32,512]{1,0:T(8,128)(2,1)S(1)}, bf16[32,512]{1,0:T(8,128)(2,1)S(1)}, u32[]{:S(2)}, u32[]{:S(2)}) %collective-permute-start.1) | collective-permute-done | bytes 32800 | tf_op jit(solution)/shard_map/ppermute | solution.py:555
  25.4 2.5 %collective-permute-start.7 = (bf16[128,512]{1,0:T(8,128)(2,1)S(1)}, bf16[128,512]{1,0:T(8,128)(2,1)S(1)}, u32[]{:S(2)}, u32[]{:S(2)}) collective-permute-start(bf16[128,512]{1,0:T(8,128)(2,1)S(1)} %get-tuple-element.85), channel_id=1, source_target_pairs={{0,3},{1,2},{2,1},{3,0},{4,7},{5,6},{6,5},{7,4},{8,11},{9,10},{10,... | collective-permute-start | bytes 393224 | tf_op jit(solution)/shard_map/ppermute | solution.py:555
  29.0 2.1 %collective-permute-start.9 = (bf16[64,512]{1,0:T(8,128)(2,1)S(1)}, bf16[64,512]{1,0:T(8,128)(2,1)S(1)}, u32[]{:S(2)}, u32[]{:S(2)}) collective-permute-start(bf16[64,512]{1,0:T(8,128)(2,1)S(1)} %maximum_select_fusion), channel_id=1, source_target_pairs={{0,8},{1,9},{2,10},{3,11},{4,12},{5,13},{6,14},{7,15},{8,0},{9,1},... | collective-permute-start | bytes 196616 | tf_op jit(solution)/shard_map/ppermute | solution.py:555
  31.1 3.1 %collective-permute-done.9 = bf16[64,512]{1,0:T(8,128)(2,1)S(1)} collective-permute-done((bf16[64,512]{1,0:T(8,128)(2,1)S(1)}, bf16[64,512]{1,0:T(8,128)(2,1)S(1)}, u32[]{:S(2)}, u32[]{:S(2)}) %collective-permute-start.9) | collective-permute-done | bytes 65568 | tf_op jit(solution)/shard_map/ppermute | solution.py:555
  34.2 1.1 %collective-permute-done.8 = bf16[64,512]{1,0:T(8,128)(2,1)S(1)} collective-permute-done((bf16[64,512]{1,0:T(8,128)(2,1)S(1)}, bf16[64,512]{1,0:T(8,128)(2,1)S(1)}, u32[]{:S(2)}, u32[]{:S(2)}) %collective-permute-start.8) | collective-permute-done | bytes 65568 | tf_op jit(solution)/shard_map/ppermute | solution.py:555
  36.3 1.1 %collective-permute-start.10 = (bf16[64,512]{1,0:T(8,128)(2,1)S(1)}, bf16[64,512]{1,0:T(8,128)(2,1)S(1)}, u32[]{:S(2)}, u32[]{:S(2)}) collective-permute-start(bf16[64,512]{1,0:T(8,128)(2,1)S(1)} %maximum_select_fusion), channel_id=1, source_target_pairs={{0,12},{1,13},{2,14},{3,15},{4,8},{5,9},{6,10},{7,11},{8,4},{9,5},... | collective-permute-start | bytes 196616 | tf_op jit(solution)/shard_map/ppermute | solution.py:555
  37.4 7.8 %attend.1 = (bf16[768,512]{1,0:T(8,128)(2,1)S(1)}, f32[768,512]{1,0:T(8,128)S(1)}, bf16[768,2048]{1,0:T(8,128)(2,1)S(1)}, bf16[1536,1024]{1,0:T(8,128)(2,1)S(1)}) custom-call(f32[4]{0:T(128)S(1)} %rsqrt.3.inv_ref, s32[768,1]{1,0:T(8,128)S(1)} %reshape.68.slots_ref, bf16[512,512]{1,0:T(8,128)(2,1)S(1)} %constant_dynamic-update-slice_fusion.4.near_ref, ...), custom_call_target="tpu_custom_call" | custom-call | flops 3221225472 | bytes 16777216 | tf_op jit(solution)/shard_map/attend/pallas_call | solution.py:320
  45.3 2.5 %collective-permute-start.14 = (bf16[256,512]{1,0:T(8,128)(2,1)S(1)}, bf16[256,512]{1,0:T(8,128)(2,1)S(1)}, u32[]{:S(2)}, u32[]{:S(2)}) collective-permute-start(bf16[256,512]{1,0:T(8,128)(2,1)S(1)} %get-tuple-element.77), channel_id=1, source_target_pairs={{0,3},{1,2},{2,1},{3,0},{4,7},{5,6},{6,5},{7,4},{8,11},{9,10},{10,... | collective-permute-start | bytes 786440 | tf_op jit(solution)/shard_map/ppermute | solution.py:555
  48.8 6.9 %score.1 = (f32[768,1]{1,0:T(8,128)S(1)}, bf16[768,512]{1,0:T(8,128)(2,1)S(1)}, f32[768,512]{1,0:T(8,128)S(1)}) custom-call(f32[4]{0:T(128)S(1)} %rsqrt.3.inv_ref, bf16[768,512]{1,0:T(8,128)(2,1)S(1)} %get-tuple-element.54.queries_ref, f32[768,512]{1,0:T(8,128)S(1)} %get-tuple-element.49.attended_ref, s32[768,1]{1,0:T(8,128)S(1)} %reshape.69.labels_ref, ...), custom_call_target="tpu_custom_call" | custom-call | flops 4831838208 | bytes 8388608 | tf_op jit(solution)/shard_map/score/pallas_call | solution.py:393
  55.7 3.4 %attend_back.2.first_ref = bf16[576,512]{1,0:T(8,128)(2,1)S(1)} custom-call(bf16[768,512]{1,0:T(8,128)(2,1)S(1)} %get-tuple-element.60.grad_att_ref, f32[768,512]{1,0:T(8,128)S(1)} %get-tuple-element.57.direct_ref, bf16[768,2048]{1,0:T(8,128)(2,1)S(1)} %get-tuple-element.58.slope_ref, bf16[4,2048,512]{2,1,0:T(8,128)(2,1)S(1)} %bitcast.4), custom_call_target="tpu_custom_call" | custom-call | flops 2415919104 | bytes 8388608 | tf_op jit(solution)/shard_map/attend_back/pallas_call | solution.py:433
  59.1 1.1 %collective-permute-done.13 = bf16[256,512]{1,0:T(8,128)(2,1)S(1)} collective-permute-done((bf16[256,512]{1,0:T(8,128)(2,1)S(1)}, bf16[256,512]{1,0:T(8,128)(2,1)S(1)}, u32[]{:S(2)}, u32[]{:S(2)}) %collective-permute-start.13) | collective-permute-done | bytes 262176 | tf_op jit(solution)/shard_map/ppermute | solution.py:555
  60.4 1.4 %attend_back.3.second_ref = bf16[192,512]{1,0:T(8,128)(2,1)S(1)} custom-call(bf16[768,512]{1,0:T(8,128)(2,1)S(1)} %get-tuple-element.60.grad_att_ref, f32[768,512]{1,0:T(8,128)S(1)} %get-tuple-element.57.direct_ref, bf16[768,2048]{1,0:T(8,128)(2,1)S(1)} %get-tuple-element.58.slope_ref, bf16[4,2048,512]{2,1,0:T(8,128)(2,1)S(1)} %bitcast.4), custom_call_target="tpu_custom_call" | custom-call | flops 805306368 | bytes 8388608 | tf_op jit(solution)/shard_map/attend_back/pallas_call | solution.py:433
  62.4 1.0 %own_cand_grad.1.cand_grad_ref = f32[1024,512]{1,0:T(8,128)S(1)} custom-call(s32[1,768]{1,0:T(1,128)S(1)} %reshape.59.slots_ref, bf16[576,512]{1,0:T(8,128)(2,1)S(1)} %attend_back.2.first_ref, bf16[192,512]{1,0:T(8,128)(2,1)S(1)} %attend_back.3.second_ref), custom_call_target="tpu_custom_call" | custom-call | flops 805306368 | bytes 4194304 | tf_op jit(solution)/shard_map/own_cand_grad/pallas_call | solution.py:471
  63.5 1.7 %chip_terms.1 = bf16[512,512]{1,0:T(8,128)(2,1)S(1)} custom-call(s32[1]{0:T(128)} %bitcast.wide_ref, f32[1024,512]{1,0:T(8,128)S(1)} %own_cand_grad.1.cand_grad_ref, s32[1,768]{1,0:T(1,128)S(1)} %reshape.66.slots_ref, bf16[576,512]{1,0:T(8,128)(2,1)S(1)} %collective-permute-done.15.first_ref, bf16[192,512]{1,0:T(8,128)(2,1)S(1)} %collective-permute-done.16.second_ref, ...), custom_call_target="tpu_custom_call" | custom-call | flops 1342177280 | bytes 4194304 | tf_op jit(solution)/shard_map/chip_terms/pallas_call | solution.py:525
  65.2 1.7 %collective-permute-start.17 = (bf16[128,512]{1,0:T(8,128)(2,1)S(1)}, bf16[128,512]{1,0:T(8,128)(2,1)S(1)}, u32[]{:S(2)}, u32[]{:S(2)}) collective-permute-start(bf16[128,512]{1,0:T(8,128)(2,1)S(1)} %get-tuple-element.70), channel_id=1, source_target_pairs={{0,3},{1,2},{2,1},{3,0},{4,7},{5,6},{6,5},{7,4},{8,11},{9,10},{10,... | collective-permute-start | bytes 393224 | tf_op jit(solution)/shard_map/ppermute | solution.py:555
  67.0 1.2 %collective-permute-start.19 = (bf16[128,512]{1,0:T(8,128)(2,1)S(1)}, bf16[128,512]{1,0:T(8,128)(2,1)S(1)}, u32[]{:S(2)}, u32[]{:S(2)}) collective-permute-start(bf16[128,512]{1,0:T(8,128)(2,1)S(1)} %get-tuple-element.71), channel_id=1, source_target_pairs={{0,1},{1,0},{2,3},{3,2},{4,5},{5,4},{6,7},{7,6},{8,9},{9,8},{10,11... | collective-permute-start | bytes 393224 | tf_op jit(solution)/shard_map/ppermute | solution.py:555
  69.6 3.0 %collective-permute-done.17 = bf16[128,512]{1,0:T(8,128)(2,1)S(1)} collective-permute-done((bf16[128,512]{1,0:T(8,128)(2,1)S(1)}, bf16[128,512]{1,0:T(8,128)(2,1)S(1)}, u32[]{:S(2)}, u32[]{:S(2)}) %collective-permute-start.17) | collective-permute-done | bytes 131104 | tf_op jit(solution)/shard_map/ppermute | solution.py:555
  72.5 2.2 %collective-permute-done.19 = bf16[128,512]{1,0:T(8,128)(2,1)S(1)} collective-permute-done((bf16[128,512]{1,0:T(8,128)(2,1)S(1)}, bf16[128,512]{1,0:T(8,128)(2,1)S(1)}, u32[]{:S(2)}, u32[]{:S(2)}) %collective-permute-start.19) | collective-permute-done | bytes 131104 | tf_op jit(solution)/shard_map/ppermute | solution.py:555
  74.9 2.8 %collective-permute-start.20 = (bf16[32,512]{1,0:T(8,128)(2,1)S(1)}, bf16[32,512]{1,0:T(8,128)(2,1)S(1)}, u32[]{:S(2)}, u32[]{:S(2)}) collective-permute-start(bf16[32,512]{1,0:T(8,128)(2,1)S(1)} %get-tuple-element.73), channel_id=1, source_target_pairs={{0,12},{1,13},{2,14},{3,15},{4,8},{5,9},{6,10},{7,11},{8,4},{9,5},... | collective-permute-start | bytes 98312 | tf_op jit(solution)/shard_map/ppermute | solution.py:555
  77.7 1.6 %collective-permute-start.22 = (bf16[32,512]{1,0:T(8,128)(2,1)S(1)}, bf16[32,512]{1,0:T(8,128)(2,1)S(1)}, u32[]{:S(2)}, u32[]{:S(2)}) collective-permute-start(bf16[32,512]{1,0:T(8,128)(2,1)S(1)} %get-tuple-element.75), channel_id=1, source_target_pairs={{0,4},{1,5},{2,6},{3,7},{4,0},{5,1},{6,2},{7,3},{8,12},{9,13},{10,... | collective-permute-start | bytes 98312 | tf_op jit(solution)/shard_map/ppermute | solution.py:555
  79.3 1.3 %collective-permute-done.20 = bf16[32,512]{1,0:T(8,128)(2,1)S(1)} collective-permute-done((bf16[32,512]{1,0:T(8,128)(2,1)S(1)}, bf16[32,512]{1,0:T(8,128)(2,1)S(1)}, u32[]{:S(2)}, u32[]{:S(2)}) %collective-permute-start.20) | collective-permute-done | bytes 32800 | tf_op jit(solution)/shard_map/ppermute | solution.py:555
  80.6 1.9 %collective-permute-done.21 = bf16[32,512]{1,0:T(8,128)(2,1)S(1)} collective-permute-done((bf16[32,512]{1,0:T(8,128)(2,1)S(1)}, bf16[32,512]{1,0:T(8,128)(2,1)S(1)}, u32[]{:S(2)}, u32[]{:S(2)}) %collective-permute-start.21) | collective-permute-done | bytes 32800 | tf_op jit(solution)/shard_map/ppermute | solution.py:555
  (77 shorter events, 8.1 us)
Async XLA Ops:
  0.7 35.4 %copy-start.1 = (s32[768]{0:T(1024)S(1)}, s32[768]{0:T(1024)}, u32[]{:S(2)}) copy-start(s32[768]{0:T(1024)} %param.23) | copy-start | bytes 9220
  15.4 7.3 %collective-permute-start.2 = (bf16[32,512]{1,0:T(8,128)(2,1)S(1)}, bf16[32,512]{1,0:T(8,128)(2,1)S(1)}, u32[]{:S(2)}, u32[]{:S(2)}) collective-permute-start(bf16[32,512]{1,0:T(8,128)(2,1)S(1)} %get-tuple-element.35), channel_id=1, source_target_pairs={{0,12},{1,13},{2,14},{3,15},{4,8},{5,9},{6,10},{7,11},{8,4},{9,5},... | collective-permute-start | bytes 98312 | tf_op jit(solution)/shard_map/ppermute | solution.py:555
  20.6 4.8 %collective-permute-start.1 = (bf16[32,512]{1,0:T(8,128)(2,1)S(1)}, bf16[32,512]{1,0:T(8,128)(2,1)S(1)}, u32[]{:S(2)}, u32[]{:S(2)}) collective-permute-start(bf16[32,512]{1,0:T(8,128)(2,1)S(1)} %get-tuple-element.35), channel_id=1, source_target_pairs={{0,8},{1,9},{2,10},{3,11},{4,12},{5,13},{6,14},{7,15},{8,0},{9,1},... | collective-permute-start | bytes 98312 | tf_op jit(solution)/shard_map/ppermute | solution.py:555
  20.6 4.8 %collective-permute-start = (bf16[32,512]{1,0:T(8,128)(2,1)S(1)}, bf16[32,512]{1,0:T(8,128)(2,1)S(1)}, u32[]{:S(2)}, u32[]{:S(2)}) collective-permute-start(bf16[32,512]{1,0:T(8,128)(2,1)S(1)} %get-tuple-element.35), channel_id=1, source_target_pairs={{0,4},{1,5},{2,6},{3,7},{4,0},{5,1},{6,2},{7,3},{8,12},{9,13},{10,... | collective-permute-start | bytes 98312 | tf_op jit(solution)/shard_map/ppermute | solution.py:555
  21.3 1.2 %collective-permute-start.4 = (s32[768]{0:T(1024)S(1)}, s32[768]{0:T(1024)S(1)}, u32[]{:S(2)}, u32[]{:S(2)}) collective-permute-start(s32[768]{0:T(1024)S(1)} %get-tuple-element.93), channel_id=1, source_target_pairs={{0,16},{16,0},{1,17},{17,1},{2,18},{18,2},{3,19},{19,3},{4,20},{20... | collective-permute-start | bytes 9224 | tf_op jit(solution)/shard_map/ppermute | solution.py:555
  21.3 1.4 %collective-permute-start.3 = (bf16[32,512]{1,0:T(8,128)(2,1)S(1)}, bf16[32,512]{1,0:T(8,128)(2,1)S(1)}, u32[]{:S(2)}, u32[]{:S(2)}) collective-permute-start(bf16[32,512]{1,0:T(8,128)(2,1)S(1)} %get-tuple-element.37), channel_id=1, source_target_pairs={{0,16},{16,0},{1,17},{17,1},{2,18},{18,2},{3,19},{19,3},{4,20},{20... | collective-permute-start | bytes 98312 | tf_op jit(solution)/shard_map/ppermute | solution.py:555
  25.4 9.9 %collective-permute-start.7 = (bf16[128,512]{1,0:T(8,128)(2,1)S(1)}, bf16[128,512]{1,0:T(8,128)(2,1)S(1)}, u32[]{:S(2)}, u32[]{:S(2)}) collective-permute-start(bf16[128,512]{1,0:T(8,128)(2,1)S(1)} %get-tuple-element.85), channel_id=1, source_target_pairs={{0,3},{1,2},{2,1},{3,0},{4,7},{5,6},{6,5},{7,4},{8,11},{9,10},{10,... | collective-permute-start | bytes 393224 | tf_op jit(solution)/shard_map/ppermute | solution.py:555
  27.9 7.4 %collective-permute-start.6 = (bf16[128,512]{1,0:T(8,128)(2,1)S(1)}, bf16[128,512]{1,0:T(8,128)(2,1)S(1)}, u32[]{:S(2)}, u32[]{:S(2)}) collective-permute-start(bf16[128,512]{1,0:T(8,128)(2,1)S(1)} %get-tuple-element.85), channel_id=1, source_target_pairs={{0,2},{1,3},{2,0},{3,1},{4,6},{5,7},{6,4},{7,5},{8,10},{9,11},{10,... | collective-permute-start | bytes 393224 | tf_op jit(solution)/shard_map/ppermute | solution.py:555
  28.4 6.9 %collective-permute-start.5 = (bf16[128,512]{1,0:T(8,128)(2,1)S(1)}, bf16[128,512]{1,0:T(8,128)(2,1)S(1)}, u32[]{:S(2)}, u32[]{:S(2)}) collective-permute-start(bf16[128,512]{1,0:T(8,128)(2,1)S(1)} %get-tuple-element.85), channel_id=1, source_target_pairs={{0,1},{1,0},{2,3},{3,2},{4,5},{5,4},{6,7},{7,6},{8,9},{9,8},{10,11... | collective-permute-start | bytes 393224 | tf_op jit(solution)/shard_map/ppermute | solution.py:555
  29.0 5.2 %collective-permute-start.9 = (bf16[64,512]{1,0:T(8,128)(2,1)S(1)}, bf16[64,512]{1,0:T(8,128)(2,1)S(1)}, u32[]{:S(2)}, u32[]{:S(2)}) collective-permute-start(bf16[64,512]{1,0:T(8,128)(2,1)S(1)} %maximum_select_fusion), channel_id=1, source_target_pairs={{0,8},{1,9},{2,10},{3,11},{4,12},{5,13},{6,14},{7,15},{8,0},{9,1},... | collective-permute-start | bytes 196616 | tf_op jit(solution)/shard_map/ppermute | solution.py:555
  31.1 4.3 %collective-permute-start.8 = (bf16[64,512]{1,0:T(8,128)(2,1)S(1)}, bf16[64,512]{1,0:T(8,128)(2,1)S(1)}, u32[]{:S(2)}, u32[]{:S(2)}) collective-permute-start(bf16[64,512]{1,0:T(8,128)(2,1)S(1)} %maximum_select_fusion), channel_id=1, source_target_pairs={{0,4},{1,5},{2,6},{3,7},{4,0},{5,1},{6,2},{7,3},{8,12},{9,13},{10,... | collective-permute-start | bytes 196616 | tf_op jit(solution)/shard_map/ppermute | solution.py:555
  35.4 2.0 %collective-permute-start.11 = (bf16[512,512]{1,0:T(8,128)(2,1)S(1)}, bf16[512,512]{1,0:T(8,128)(2,1)S(1)}, u32[]{:S(2)}, u32[]{:S(2)}) collective-permute-start(bf16[512,512]{1,0:T(8,128)(2,1)S(1)} %constant_dynamic-update-slice_fusion.4.near_ref), channel_id=1, source_target_pairs={{0,16},{16,0},{1,17},{17,1},{2,18},{18,2},{3,19},{19,3},{4,20},{20... | collective-permute-start | bytes 1572872 | tf_op jit(solution)/shard_map/ppermute | solution.py:555
  36.3 8.9 %collective-permute-start.10 = (bf16[64,512]{1,0:T(8,128)(2,1)S(1)}, bf16[64,512]{1,0:T(8,128)(2,1)S(1)}, u32[]{:S(2)}, u32[]{:S(2)}) collective-permute-start(bf16[64,512]{1,0:T(8,128)(2,1)S(1)} %maximum_select_fusion), channel_id=1, source_target_pairs={{0,12},{1,13},{2,14},{3,15},{4,8},{5,9},{6,10},{7,11},{8,4},{9,5},... | collective-permute-start | bytes 196616 | tf_op jit(solution)/shard_map/ppermute | solution.py:555
  45.3 13.9 %collective-permute-start.14 = (bf16[256,512]{1,0:T(8,128)(2,1)S(1)}, bf16[256,512]{1,0:T(8,128)(2,1)S(1)}, u32[]{:S(2)}, u32[]{:S(2)}) collective-permute-start(bf16[256,512]{1,0:T(8,128)(2,1)S(1)} %get-tuple-element.77), channel_id=1, source_target_pairs={{0,3},{1,2},{2,1},{3,0},{4,7},{5,6},{6,5},{7,4},{8,11},{9,10},{10,... | collective-permute-start | bytes 786440 | tf_op jit(solution)/shard_map/ppermute | solution.py:555
  47.8 12.5 %collective-permute-start.13 = (bf16[256,512]{1,0:T(8,128)(2,1)S(1)}, bf16[256,512]{1,0:T(8,128)(2,1)S(1)}, u32[]{:S(2)}, u32[]{:S(2)}) collective-permute-start(bf16[256,512]{1,0:T(8,128)(2,1)S(1)} %get-tuple-element.77), channel_id=1, source_target_pairs={{0,2},{1,3},{2,0},{3,1},{4,6},{5,7},{6,4},{7,5},{8,10},{9,11},{10,... | collective-permute-start | bytes 786440 | tf_op jit(solution)/shard_map/ppermute | solution.py:555
  48.3 12.1 %collective-permute-start.12 = (bf16[256,512]{1,0:T(8,128)(2,1)S(1)}, bf16[256,512]{1,0:T(8,128)(2,1)S(1)}, u32[]{:S(2)}, u32[]{:S(2)}) collective-permute-start(bf16[256,512]{1,0:T(8,128)(2,1)S(1)} %get-tuple-element.77), channel_id=1, source_target_pairs={{0,1},{1,0},{2,3},{3,2},{4,5},{5,4},{6,7},{7,6},{8,9},{9,8},{10,11... | collective-permute-start | bytes 786440 | tf_op jit(solution)/shard_map/ppermute | solution.py:555
  60.3 3.1 %collective-permute-start.15 = (bf16[576,512]{1,0:T(8,128)(2,1)S(1)}, bf16[576,512]{1,0:T(8,128)(2,1)S(1)}, u32[]{:S(2)}, u32[]{:S(2)}) collective-permute-start(bf16[576,512]{1,0:T(8,128)(2,1)S(1)} %attend_back.2.first_ref), channel_id=1, source_target_pairs={{0,16},{16,0},{1,17},{17,1},{2,18},{18,2},{3,19},{19,3},{4,20},{20... | collective-permute-start | bytes 1769480 | tf_op jit(solution)/shard_map/ppermute | solution.py:555
  61.8 1.6 %collective-permute-start.16 = (bf16[192,512]{1,0:T(8,128)(2,1)S(1)}, bf16[192,512]{1,0:T(8,128)(2,1)S(1)}, u32[]{:S(2)}, u32[]{:S(2)}) collective-permute-start(bf16[192,512]{1,0:T(8,128)(2,1)S(1)} %attend_back.3.second_ref), channel_id=1, source_target_pairs={{0,16},{16,0},{1,17},{17,1},{2,18},{18,2},{3,19},{19,3},{4,20},{20... | collective-permute-start | bytes 589832 | tf_op jit(solution)/shard_map/ppermute | solution.py:555
  65.2 7.3 %collective-permute-start.17 = (bf16[128,512]{1,0:T(8,128)(2,1)S(1)}, bf16[128,512]{1,0:T(8,128)(2,1)S(1)}, u32[]{:S(2)}, u32[]{:S(2)}) collective-permute-start(bf16[128,512]{1,0:T(8,128)(2,1)S(1)} %get-tuple-element.70), channel_id=1, source_target_pairs={{0,3},{1,2},{2,1},{3,0},{4,7},{5,6},{6,5},{7,4},{8,11},{9,10},{10,... | collective-permute-start | bytes 393224 | tf_op jit(solution)/shard_map/ppermute | solution.py:555
  67.0 7.8 %collective-permute-start.19 = (bf16[128,512]{1,0:T(8,128)(2,1)S(1)}, bf16[128,512]{1,0:T(8,128)(2,1)S(1)}, u32[]{:S(2)}, u32[]{:S(2)}) collective-permute-start(bf16[128,512]{1,0:T(8,128)(2,1)S(1)} %get-tuple-element.71), channel_id=1, source_target_pairs={{0,1},{1,0},{2,3},{3,2},{4,5},{5,4},{6,7},{7,6},{8,9},{9,8},{10,11... | collective-permute-start | bytes 393224 | tf_op jit(solution)/shard_map/ppermute | solution.py:555
  68.2 6.6 %collective-permute-start.18 = (bf16[128,512]{1,0:T(8,128)(2,1)S(1)}, bf16[128,512]{1,0:T(8,128)(2,1)S(1)}, u32[]{:S(2)}, u32[]{:S(2)}) collective-permute-start(bf16[128,512]{1,0:T(8,128)(2,1)S(1)} %get-tuple-element.72), channel_id=1, source_target_pairs={{0,2},{1,3},{2,0},{3,1},{4,6},{5,7},{6,4},{7,5},{8,10},{9,11},{10,... | collective-permute-start | bytes 393224 | tf_op jit(solution)/shard_map/ppermute | solution.py:555
  74.9 5.8 %collective-permute-start.20 = (bf16[32,512]{1,0:T(8,128)(2,1)S(1)}, bf16[32,512]{1,0:T(8,128)(2,1)S(1)}, u32[]{:S(2)}, u32[]{:S(2)}) collective-permute-start(bf16[32,512]{1,0:T(8,128)(2,1)S(1)} %get-tuple-element.73), channel_id=1, source_target_pairs={{0,12},{1,13},{2,14},{3,15},{4,8},{5,9},{6,10},{7,11},{8,4},{9,5},... | collective-permute-start | bytes 98312 | tf_op jit(solution)/shard_map/ppermute | solution.py:555
  77.7 4.8 %collective-permute-start.21 = (bf16[32,512]{1,0:T(8,128)(2,1)S(1)}, bf16[32,512]{1,0:T(8,128)(2,1)S(1)}, u32[]{:S(2)}, u32[]{:S(2)}) collective-permute-start(bf16[32,512]{1,0:T(8,128)(2,1)S(1)} %get-tuple-element.74), channel_id=1, source_target_pairs={{0,8},{1,9},{2,10},{3,11},{4,12},{5,13},{6,14},{7,15},{8,0},{9,1},... | collective-permute-start | bytes 98312 | tf_op jit(solution)/shard_map/ppermute | solution.py:555
  77.7 4.8 %collective-permute-start.22 = (bf16[32,512]{1,0:T(8,128)(2,1)S(1)}, bf16[32,512]{1,0:T(8,128)(2,1)S(1)}, u32[]{:S(2)}, u32[]{:S(2)}) collective-permute-start(bf16[32,512]{1,0:T(8,128)(2,1)S(1)} %get-tuple-element.75), channel_id=1, source_target_pairs={{0,4},{1,5},{2,6},{3,7},{4,0},{5,1},{6,2},{7,3},{8,12},{9,13},{10,... | collective-permute-start | bytes 98312 | tf_op jit(solution)/shard_map/ppermute | solution.py:555
  (7 other events, 159.6 us)

commit v7 on v6

--- a/solution.py
+++ b/solution.py
@@ -162,14 +162,14 @@
             packed_ref[:, part_columns] = dot(normed_ref[at, :], qkv_ref[:, part_columns]).astype(
                 jnp.bfloat16
             )
-        if group + 1 < groups:
-            copies[3 + group].wait()
+            if group + 1 < groups:
+                if part == 0:
+                    copies[3 + group].wait()
+                for cand in range(part * cands // 2, (part + 1) * cands // 2):
+                    norm_cand((group + 1) * cands + cand)
         for head in range(0, HEADS, quad):
             for block in range(blocks):
                 own_scores(block, head)
-            if group + 1 < groups:
-                for cand in range(head * cands // HEADS, (head + quad) * cands // HEADS):
-                    norm_cand((group + 1) * cands + cand)
         exp_scores = jnp.exp2(
             scores_ref[...].reshape(blocks * pairs * patches, 2 * lanes) * exponent
         )
@@ -624,7 +624,8 @@
         if place == 0:
             got = exchange(send, "section", 2, 1)
             far_slots = exchange(pooled_slots, "section", 2, 1)
-            found, keep, got, far_slots = lax.optimization_barrier((found, keep, got, far_slots))
+            found, keep, got, far_slots = lax.optimization_barrier((found[::-1], keep, got, far_slots))
+            found = found[::-1]
             pooled = jnp.where(
                 core == 0,
                 jnp.concatenate([keep, got], axis=0),
@@ -632,17 +633,20 @@
             )
         else:
             bit, values = stages[place - 1]
-            early = send_stage(pooled, wides, bit, values - 1)
-            found, early = lax.optimization_barrier((found, early))
-            late = exchange(after([pooled], *found)[0], "wide", wides, (values - 1) << bit)
+            paired = exchange(pooled, "wide", wides, 1 << bit)
+            found, paired = lax.optimization_barrier((found[::-1], paired))
+            found = found[::-1]
+            pooled_parts = [jnp.concatenate([pooled, paired], axis=0)]
+            if values > 2:
+                pooled_parts.append(exchange(pooled_parts[0], "wide", wides, 2 << bit))
             if place + 1 < len(stages):
-                pooled = jnp.concatenate([pooled] + early + [late], axis=0)
+                pooled = jnp.concatenate(pooled_parts, axis=0)
         near = jnp.concatenate([near] + found, axis=0)
     far = exchange(near, "section", 2, 1)
     queries, attended, slope, mlp_weight = attend(
         inv_count, slots.reshape(requests, 1), near, far, history, usable, mlp_weight
     )
-    pooled = jnp.concatenate(after([pooled] + early + [late], attended), axis=0)
+    pooled = jnp.concatenate(after(pooled_parts, attended), axis=0)
     found_pooled = send_stage(pooled, wides, *stages[-1])
     logits, grad_att, direct = score(
         inv_count,
@@ -655,9 +659,9 @@
     half = max(1, users - 1)
     first_rows = attend_back(0, half, grad_att, direct, slope, history)
     found_pooled, grad_att, first_rows = lax.optimization_barrier(
-        (found_pooled, grad_att, first_rows)
+        (found_pooled[::-1], grad_att, first_rows)
     )
-    pooled = jnp.concatenate([pooled] + found_pooled, axis=0)
+    pooled = jnp.concatenate([pooled] + found_pooled[::-1], axis=0)
     grad_parts = [first_rows, attend_back(half, users - half, grad_att, direct, slope, history)]
     far_parts = [exchange(part, "section", 2, 1) for part in grad_parts]
     cand_grad = own_cand_grad(pooled.shape[0], pooled_slots.reshape(1, requests), grad_parts)

time: 83.3 us -> 81.6 us (0.980)
  starting transfers between devices: 25.3 us -> 24.3 us
    ppermute x23 -> x22, starting transfers between devices: 25.3 us -> 24.3 us  [exchange(): lax.ppermute(values, axis_name, [(i, i ^ distance) for i in range(size)])]
    ppermute x23 -> x22, waiting for transfers between devices: 17.4 us -> 16.9 us  [exchange(): lax.ppermute(values, axis_name, [(i, i ^ distance) for i in range(size)])]
  transfers between devices with their start and end apart: 23 -> 22, of which waited for: 11 -> 10; matrix products, arithmetic and copies ran while one was open for 2% -> 2% of each run, Pallas kernels for 25% -> 25%
where the time goes in v7:
time: 81.6 us; the launch traced here: 81.5 us
  Pallas kernels  36.8 us (45%)
  starting transfers between devices  24.3 us (30%)
  waiting for transfers between devices  16.9 us (21%)
  other arithmetic  1.93 us (2%)
  between operations  1.02 us (1%)
    ppermute x22, starting transfers between devices, exchange(): lax.ppermute(values, axis_name, [(i, i ^ distance) for i in range(size)])  24.3 us
    ppermute x22, waiting for transfers between devices, exchange(): lax.ppermute(values, axis_name, [(i, i ^ distance) for i in range(size)])  16.9 us
    pallas_call x1, Pallas kernels, encode_block(): pl.pallas_call(functools.partial(encode_kernel, tokens), in_specs=[pl.Blo...  14.6 us
    pallas_call x1, Pallas kernels, attend(): pl.pallas_call(attend_kernel, in_specs=[pl.BlockSpec(memory_space=pltpu.S...  7.75 us
    pallas_call x1, Pallas kernels, score(): pl.pallas_call(score_kernel, in_specs=[pl.BlockSpec(memory_space=pltpu.SM...  6.86 us
    pallas_call x2, Pallas kernels, attend_back(): pl.pallas_call(functools.partial(attend_back_kernel, first), in_specs=[wh...  4.86 us
    pallas_call x1, Pallas kernels, chip_terms(): pl.pallas_call(functools.partial(terms_kernel, origins), in_specs=[pl.Blo...  1.73 us
  transfers between devices with their start and end apart: 22, of which 10 were waited for; matrix products, arithmetic and copies ran while one was open for 2% of the time, Pallas kernels for 25%

profile of v7, /device:TPU:0, one launch (start us, length us, event | category | flops | bytes accessed | tf_op | source)
XLA Modules:
  0.0 81.5 jit_solution(18444463549281244956)
XLA Ops:
  0.7 14.6 %encode.1 = (bf16[32,512]{1,0:T(8,128)(2,1)S(1)}, bf16[32,512]{1,0:T(8,128)(2,1)S(1)}, bf16[32,512]{1,0:T(8,128)(2,1)S(1)}) custom-call(s32[1]{0:T(128)} %bitcast.1.core_ref, bf16[1536,1024]{1,0:T(8,128)(2,1)} %bitcast.5, bf16[1024,3072]{1,0:T(8,128)(2,1)} %qkv_hbm.1, bf16[1024,1024]{1,0:T(8,128)(2,1)} %out_hbm.1, bf16[1024,512]{1,0:T(8,128)(2,1)} %proj_hbm.1), custom_call_target="tpu_custom_call" | custom-call | flops 8053063680 | bytes 16777216 | tf_op jit(solution)/shard_map/encode/pallas_call | solution.py:237
  15.3 5.1 %collective-permute-start = (bf16[32,512]{1,0:T(8,128)(2,1)S(1)}, bf16[32,512]{1,0:T(8,128)(2,1)S(1)}, u32[]{:S(2)}, u32[]{:S(2)}) collective-permute-start(bf16[32,512]{1,0:T(8,128)(2,1)S(1)} %get-tuple-element.31), channel_id=1, source_target_pairs={{0,12},{1,13},{2,14},{3,15},{4,8},{5,9},{6,10},{7,11},{8,4},{9,5},... | collective-permute-start | bytes 98312 | tf_op jit(solution)/shard_map/ppermute | solution.py:555
  22.4 2.9 %collective-permute-done.1 = bf16[32,512]{1,0:T(8,128)(2,1)S(1)} collective-permute-done((bf16[32,512]{1,0:T(8,128)(2,1)S(1)}, bf16[32,512]{1,0:T(8,128)(2,1)S(1)}, u32[]{:S(2)}, u32[]{:S(2)}) %collective-permute-start.1) | collective-permute-done | bytes 32800 | tf_op jit(solution)/shard_map/ppermute | solution.py:555
  25.3 2.5 %collective-permute-start.5 = (bf16[128,512]{1,0:T(8,128)(2,1)S(1)}, bf16[128,512]{1,0:T(8,128)(2,1)S(1)}, u32[]{:S(2)}, u32[]{:S(2)}) collective-permute-start(bf16[128,512]{1,0:T(8,128)(2,1)S(1)} %get-tuple-element.73), channel_id=1, source_target_pairs={{0,3},{1,2},{2,1},{3,0},{4,7},{5,6},{6,5},{7,4},{8,11},{9,10},{10,... | collective-permute-start | bytes 393224 | tf_op jit(solution)/shard_map/ppermute | solution.py:555
  29.0 4.3 %collective-permute-done.8 = bf16[64,512]{1,0:T(8,128)(2,1)S(1)} collective-permute-done((bf16[64,512]{1,0:T(8,128)(2,1)S(1)}, bf16[64,512]{1,0:T(8,128)(2,1)S(1)}, u32[]{:S(2)}, u32[]{:S(2)}) %collective-permute-start.8) | collective-permute-done | bytes 65568 | tf_op jit(solution)/shard_map/ppermute | solution.py:555
  34.4 2.1 %collective-permute-start.9 = (bf16[128,512]{1,0:T(8,128)(2,1)S(1)}, bf16[128,512]{1,0:T(8,128)(2,1)S(1)}, u32[]{:S(2)}, u32[]{:S(2)}) collective-permute-start(bf16[128,512]{1,0:T(8,128)(2,1)S(1)} %pad_maximum_fusion), channel_id=1, source_target_pairs={{0,8},{1,9},{2,10},{3,11},{4,12},{5,13},{6,14},{7,15},{8,0},{9,1},... | collective-permute-start | bytes 393224 | tf_op jit(solution)/shard_map/ppermute | solution.py:555
  36.5 7.8 %attend.1 = (bf16[768,512]{1,0:T(8,128)(2,1)S(1)}, f32[768,512]{1,0:T(8,128)S(1)}, bf16[768,2048]{1,0:T(8,128)(2,1)S(1)}, bf16[1536,1024]{1,0:T(8,128)(2,1)S(1)}) custom-call(f32[4]{0:T(128)S(1)} %rsqrt.3.inv_ref, s32[768,1]{1,0:T(8,128)S(1)} %reshape.68.slots_ref, bf16[512,512]{1,0:T(8,128)(2,1)S(1)} %constant_dynamic-update-slice_fusion.4.near_ref, ...), custom_call_target="tpu_custom_call" | custom-call | flops 3221225472 | bytes 16777216 | tf_op jit(solution)/shard_map/attend/pallas_call | solution.py:320
  44.3 2.3 %collective-permute-start.11 = (bf16[256,512]{1,0:T(8,128)(2,1)S(1)}, bf16[256,512]{1,0:T(8,128)(2,1)S(1)}, u32[]{:S(2)}, u32[]{:S(2)}) collective-permute-start(bf16[256,512]{1,0:T(8,128)(2,1)S(1)} %get-tuple-element.69), channel_id=1, source_target_pairs={{0,3},{1,2},{2,1},{3,0},{4,7},{5,6},{6,5},{7,4},{8,11},{9,10},{10,... | collective-permute-start | bytes 786440 | tf_op jit(solution)/shard_map/ppermute | solution.py:555
  47.1 0.7 collective-permute-start.13
  47.9 6.9 %score.1 = (f32[768,1]{1,0:T(8,128)S(1)}, bf16[768,512]{1,0:T(8,128)(2,1)S(1)}, f32[768,512]{1,0:T(8,128)S(1)}) custom-call(f32[4]{0:T(128)S(1)} %rsqrt.3.inv_ref, bf16[768,512]{1,0:T(8,128)(2,1)S(1)} %get-tuple-element.46.queries_ref, f32[768,512]{1,0:T(8,128)S(1)} %get-tuple-element.43.attended_ref, s32[768,1]{1,0:T(8,128)S(1)} %reshape.69.labels_ref, ...), custom_call_target="tpu_custom_call" | custom-call | flops 4831838208 | bytes 8388608 | tf_op jit(solution)/shard_map/score/pallas_call | solution.py:393
  54.8 3.4 %attend_back.2.first_ref = bf16[576,512]{1,0:T(8,128)(2,1)S(1)} custom-call(bf16[768,512]{1,0:T(8,128)(2,1)S(1)} %get-tuple-element.52.grad_att_ref, f32[768,512]{1,0:T(8,128)S(1)} %get-tuple-element.49.direct_ref, bf16[768,2048]{1,0:T(8,128)(2,1)S(1)} %get-tuple-element.50.slope_ref, bf16[4,2048,512]{2,1,0:T(8,128)(2,1)S(1)} %bitcast.4), custom_call_target="tpu_custom_call" | custom-call | flops 2415919104 | bytes 8388608 | tf_op jit(solution)/shard_map/attend_back/pallas_call | solution.py:433
  58.2 1.1 %collective-permute-done.12 = bf16[256,512]{1,0:T(8,128)(2,1)S(1)} collective-permute-done((bf16[256,512]{1,0:T(8,128)(2,1)S(1)}, bf16[256,512]{1,0:T(8,128)(2,1)S(1)}, u32[]{:S(2)}, u32[]{:S(2)}) %collective-permute-start.12) | collective-permute-done | bytes 262176 | tf_op jit(solution)/shard_map/ppermute | solution.py:555
  59.3 1.5 %attend_back.3.second_ref = bf16[192,512]{1,0:T(8,128)(2,1)S(1)} custom-call(bf16[768,512]{1,0:T(8,128)(2,1)S(1)} %get-tuple-element.52.grad_att_ref, f32[768,512]{1,0:T(8,128)S(1)} %get-tuple-element.49.direct_ref, bf16[768,2048]{1,0:T(8,128)(2,1)S(1)} %get-tuple-element.50.slope_ref, bf16[4,2048,512]{2,1,0:T(8,128)(2,1)S(1)} %bitcast.4), custom_call_target="tpu_custom_call" | custom-call | flops 805306368 | bytes 8388608 | tf_op jit(solution)/shard_map/attend_back/pallas_call | solution.py:433
  61.4 1.0 %own_cand_grad.1.cand_grad_ref = f32[1024,512]{1,0:T(8,128)S(1)} custom-call(s32[1,768]{1,0:T(1,128)S(1)} %reshape.59.slots_ref, bf16[576,512]{1,0:T(8,128)(2,1)S(1)} %attend_back.2.first_ref, bf16[192,512]{1,0:T(8,128)(2,1)S(1)} %attend_back.3.second_ref), custom_call_target="tpu_custom_call" | custom-call | flops 805306368 | bytes 4194304 | tf_op jit(solution)/shard_map/own_cand_grad/pallas_call | solution.py:471
  62.5 1.7 %chip_terms.1 = bf16[512,512]{1,0:T(8,128)(2,1)S(1)} custom-call(s32[1]{0:T(128)} %bitcast.wide_ref, f32[1024,512]{1,0:T(8,128)S(1)} %own_cand_grad.1.cand_grad_ref, s32[1,768]{1,0:T(1,128)S(1)} %reshape.66.slots_ref, bf16[576,512]{1,0:T(8,128)(2,1)S(1)} %collective-permute-done.14.first_ref, bf16[192,512]{1,0:T(8,128)(2,1)S(1)} %collective-permute-done.15.second_ref, ...), custom_call_target="tpu_custom_call" | custom-call | flops 1342177280 | bytes 4194304 | tf_op jit(solution)/shard_map/chip_terms/pallas_call | solution.py:525
  64.2 1.8 %collective-permute-start.16 = (bf16[128,512]{1,0:T(8,128)(2,1)S(1)}, bf16[128,512]{1,0:T(8,128)(2,1)S(1)}, u32[]{:S(2)}, u32[]{:S(2)}) collective-permute-start(bf16[128,512]{1,0:T(8,128)(2,1)S(1)} %get-tuple-element.62), channel_id=1, source_target_pairs={{0,3},{1,2},{2,1},{3,0},{4,7},{5,6},{6,5},{7,4},{8,11},{9,10},{10,... | collective-permute-start | bytes 393224 | tf_op jit(solution)/shard_map/ppermute | solution.py:555
  66.1 1.1 %collective-permute-start.17 = (bf16[128,512]{1,0:T(8,128)(2,1)S(1)}, bf16[128,512]{1,0:T(8,128)(2,1)S(1)}, u32[]{:S(2)}, u32[]{:S(2)}) collective-permute-start(bf16[128,512]{1,0:T(8,128)(2,1)S(1)} %get-tuple-element.64), channel_id=1, source_target_pairs={{0,2},{1,3},{2,0},{3,1},{4,6},{5,7},{6,4},{7,5},{8,10},{9,11},{10,... | collective-permute-start | bytes 393224 | tf_op jit(solution)/shard_map/ppermute | solution.py:555
  67.8 0.8 reduce.1
  68.6 3.0 %collective-permute-done.16 = bf16[128,512]{1,0:T(8,128)(2,1)S(1)} collective-permute-done((bf16[128,512]{1,0:T(8,128)(2,1)S(1)}, bf16[128,512]{1,0:T(8,128)(2,1)S(1)}, u32[]{:S(2)}, u32[]{:S(2)}) %collective-permute-start.16) | collective-permute-done | bytes 131104 | tf_op jit(solution)/shard_map/ppermute | solution.py:555
  71.5 2.2 %collective-permute-done.17 = bf16[128,512]{1,0:T(8,128)(2,1)S(1)} collective-permute-done((bf16[128,512]{1,0:T(8,128)(2,1)S(1)}, bf16[128,512]{1,0:T(8,128)(2,1)S(1)}, u32[]{:S(2)}, u32[]{:S(2)}) %collective-permute-start.17) | collective-permute-done | bytes 131104 | tf_op jit(solution)/shard_map/ppermute | solution.py:555
  73.9 2.0 %collective-permute-start.19 = (bf16[32,512]{1,0:T(8,128)(2,1)S(1)}, bf16[32,512]{1,0:T(8,128)(2,1)S(1)}, u32[]{:S(2)}, u32[]{:S(2)}) collective-permute-start(bf16[32,512]{1,0:T(8,128)(2,1)S(1)} %get-tuple-element.65), channel_id=1, source_target_pairs={{0,12},{1,13},{2,14},{3,15},{4,8},{5,9},{6,10},{7,11},{8,4},{9,5},... | collective-permute-start | bytes 98312 | tf_op jit(solution)/shard_map/ppermute | solution.py:555
  76.5 1.8 %collective-permute-start.21 = (bf16[32,512]{1,0:T(8,128)(2,1)S(1)}, bf16[32,512]{1,0:T(8,128)(2,1)S(1)}, u32[]{:S(2)}, u32[]{:S(2)}) collective-permute-start(bf16[32,512]{1,0:T(8,128)(2,1)S(1)} %get-tuple-element.67), channel_id=1, source_target_pairs={{0,4},{1,5},{2,6},{3,7},{4,0},{5,1},{6,2},{7,3},{8,12},{9,13},{10,... | collective-permute-start | bytes 98312 | tf_op jit(solution)/shard_map/ppermute | solution.py:555
  78.3 1.3 %collective-permute-done.19 = bf16[32,512]{1,0:T(8,128)(2,1)S(1)} collective-permute-done((bf16[32,512]{1,0:T(8,128)(2,1)S(1)}, bf16[32,512]{1,0:T(8,128)(2,1)S(1)}, u32[]{:S(2)}, u32[]{:S(2)}) %collective-permute-start.19) | collective-permute-done | bytes 32800 | tf_op jit(solution)/shard_map/ppermute | solution.py:555
  79.6 1.1 %collective-permute-done.20 = bf16[32,512]{1,0:T(8,128)(2,1)S(1)} collective-permute-done((bf16[32,512]{1,0:T(8,128)(2,1)S(1)}, bf16[32,512]{1,0:T(8,128)(2,1)S(1)}, u32[]{:S(2)}, u32[]{:S(2)}) %collective-permute-start.20) | collective-permute-done | bytes 32800 | tf_op jit(solution)/shard_map/ppermute | solution.py:555
  (74 shorter events, 7.5 us)
Async XLA Ops:
  0.7 33.5 %copy-start.1 = (s32[768]{0:T(1024)S(1)}, s32[768]{0:T(1024)}, u32[]{:S(2)}) copy-start(s32[768]{0:T(1024)} %param.23) | copy-start | bytes 9220
  0.7 33.7 %copy-start.4 = (bf16[1024]{0:T(1024)(128)(2,1)S(1)}, bf16[1024]{0:T(1024)(128)(2,1)}, u32[]{:S(2)}) copy-start(bf16[1024]{0:T(1024)(128)(2,1)} %param.17) | copy-start | bytes 6148
  15.3 7.0 %collective-permute-start = (bf16[32,512]{1,0:T(8,128)(2,1)S(1)}, bf16[32,512]{1,0:T(8,128)(2,1)S(1)}, u32[]{:S(2)}, u32[]{:S(2)}) collective-permute-start(bf16[32,512]{1,0:T(8,128)(2,1)S(1)} %get-tuple-element.31), channel_id=1, source_target_pairs={{0,12},{1,13},{2,14},{3,15},{4,8},{5,9},{6,10},{7,11},{8,4},{9,5},... | collective-permute-start | bytes 98312 | tf_op jit(solution)/shard_map/ppermute | solution.py:555
  20.5 4.8 %collective-permute-start.1 = (bf16[32,512]{1,0:T(8,128)(2,1)S(1)}, bf16[32,512]{1,0:T(8,128)(2,1)S(1)}, u32[]{:S(2)}, u32[]{:S(2)}) collective-permute-start(bf16[32,512]{1,0:T(8,128)(2,1)S(1)} %get-tuple-element.31), channel_id=1, source_target_pairs={{0,8},{1,9},{2,10},{3,11},{4,12},{5,13},{6,14},{7,15},{8,0},{9,1},... | collective-permute-start | bytes 98312 | tf_op jit(solution)/shard_map/ppermute | solution.py:555
  20.5 4.8 %collective-permute-start.2 = (bf16[32,512]{1,0:T(8,128)(2,1)S(1)}, bf16[32,512]{1,0:T(8,128)(2,1)S(1)}, u32[]{:S(2)}, u32[]{:S(2)}) collective-permute-start(bf16[32,512]{1,0:T(8,128)(2,1)S(1)} %get-tuple-element.31), channel_id=1, source_target_pairs={{0,4},{1,5},{2,6},{3,7},{4,0},{5,1},{6,2},{7,3},{8,12},{9,13},{10,... | collective-permute-start | bytes 98312 | tf_op jit(solution)/shard_map/ppermute | solution.py:555
  21.2 1.2 %collective-permute-start.4 = (s32[768]{0:T(1024)S(1)}, s32[768]{0:T(1024)S(1)}, u32[]{:S(2)}, u32[]{:S(2)}) collective-permute-start(s32[768]{0:T(1024)S(1)} %get-tuple-element.81), channel_id=1, source_target_pairs={{0,16},{16,0},{1,17},{17,1},{2,18},{18,2},{3,19},{19,3},{4,20},{20... | collective-permute-start | bytes 9224 | tf_op jit(solution)/shard_map/ppermute | solution.py:555
  21.2 4.0 %collective-permute-start.3 = (bf16[32,512]{1,0:T(8,128)(2,1)S(1)}, bf16[32,512]{1,0:T(8,128)(2,1)S(1)}, u32[]{:S(2)}, u32[]{:S(2)}) collective-permute-start(bf16[32,512]{1,0:T(8,128)(2,1)S(1)} %get-tuple-element.33), channel_id=1, source_target_pairs={{0,16},{16,0},{1,17},{17,1},{2,18},{18,2},{3,19},{19,3},{4,20},{20... | collective-permute-start | bytes 98312 | tf_op jit(solution)/shard_map/ppermute | solution.py:555
  25.3 7.9 %collective-permute-start.5 = (bf16[128,512]{1,0:T(8,128)(2,1)S(1)}, bf16[128,512]{1,0:T(8,128)(2,1)S(1)}, u32[]{:S(2)}, u32[]{:S(2)}) collective-permute-start(bf16[128,512]{1,0:T(8,128)(2,1)S(1)} %get-tuple-element.73), channel_id=1, source_target_pairs={{0,3},{1,2},{2,1},{3,0},{4,7},{5,6},{6,5},{7,4},{8,11},{9,10},{10,... | collective-permute-start | bytes 393224 | tf_op jit(solution)/shard_map/ppermute | solution.py:555
  27.8 5.6 %collective-permute-start.6 = (bf16[128,512]{1,0:T(8,128)(2,1)S(1)}, bf16[128,512]{1,0:T(8,128)(2,1)S(1)}, u32[]{:S(2)}, u32[]{:S(2)}) collective-permute-start(bf16[128,512]{1,0:T(8,128)(2,1)S(1)} %get-tuple-element.73), channel_id=1, source_target_pairs={{0,2},{1,3},{2,0},{3,1},{4,6},{5,7},{6,4},{7,5},{8,10},{9,11},{10,... | collective-permute-start | bytes 393224 | tf_op jit(solution)/shard_map/ppermute | solution.py:555
  28.3 5.1 %collective-permute-start.7 = (bf16[128,512]{1,0:T(8,128)(2,1)S(1)}, bf16[128,512]{1,0:T(8,128)(2,1)S(1)}, u32[]{:S(2)}, u32[]{:S(2)}) collective-permute-start(bf16[128,512]{1,0:T(8,128)(2,1)S(1)} %get-tuple-element.73), channel_id=1, source_target_pairs={{0,1},{1,0},{2,3},{3,2},{4,5},{5,4},{6,7},{7,6},{8,9},{9,8},{10,11... | collective-permute-start | bytes 393224 | tf_op jit(solution)/shard_map/ppermute | solution.py:555
  28.9 4.3 %collective-permute-start.8 = (bf16[64,512]{1,0:T(8,128)(2,1)S(1)}, bf16[64,512]{1,0:T(8,128)(2,1)S(1)}, u32[]{:S(2)}, u32[]{:S(2)}) collective-permute-start(bf16[64,512]{1,0:T(8,128)(2,1)S(1)} %maximum_select_fusion), channel_id=1, source_target_pairs={{0,4},{1,5},{2,6},{3,7},{4,0},{5,1},{6,2},{7,3},{8,12},{9,13},{10,... | collective-permute-start | bytes 196616 | tf_op jit(solution)/shard_map/ppermute | solution.py:555
  33.5 3.0 %collective-permute-start.10 = (bf16[512,512]{1,0:T(8,128)(2,1)S(1)}, bf16[512,512]{1,0:T(8,128)(2,1)S(1)}, u32[]{:S(2)}, u32[]{:S(2)}) collective-permute-start(bf16[512,512]{1,0:T(8,128)(2,1)S(1)} %constant_dynamic-update-slice_fusion.4.near_ref), channel_id=1, source_target_pairs={{0,16},{16,0},{1,17},{17,1},{2,18},{18,2},{3,19},{19,3},{4,20},{20... | collective-permute-start | bytes 1572872 | tf_op jit(solution)/shard_map/ppermute | solution.py:555
  34.4 9.9 %collective-permute-start.9 = (bf16[128,512]{1,0:T(8,128)(2,1)S(1)}, bf16[128,512]{1,0:T(8,128)(2,1)S(1)}, u32[]{:S(2)}, u32[]{:S(2)}) collective-permute-start(bf16[128,512]{1,0:T(8,128)(2,1)S(1)} %pad_maximum_fusion), channel_id=1, source_target_pairs={{0,8},{1,9},{2,10},{3,11},{4,12},{5,13},{6,14},{7,15},{8,0},{9,1},... | collective-permute-start | bytes 393224 | tf_op jit(solution)/shard_map/ppermute | solution.py:555
  44.3 13.9 %collective-permute-start.11 = (bf16[256,512]{1,0:T(8,128)(2,1)S(1)}, bf16[256,512]{1,0:T(8,128)(2,1)S(1)}, u32[]{:S(2)}, u32[]{:S(2)}) collective-permute-start(bf16[256,512]{1,0:T(8,128)(2,1)S(1)} %get-tuple-element.69), channel_id=1, source_target_pairs={{0,3},{1,2},{2,1},{3,0},{4,7},{5,6},{6,5},{7,4},{8,11},{9,10},{10,... | collective-permute-start | bytes 786440 | tf_op jit(solution)/shard_map/ppermute | solution.py:555
  46.6 12.7 %collective-permute-start.12 = (bf16[256,512]{1,0:T(8,128)(2,1)S(1)}, bf16[256,512]{1,0:T(8,128)(2,1)S(1)}, u32[]{:S(2)}, u32[]{:S(2)}) collective-permute-start(bf16[256,512]{1,0:T(8,128)(2,1)S(1)} %get-tuple-element.69), channel_id=1, source_target_pairs={{0,2},{1,3},{2,0},{3,1},{4,6},{5,7},{6,4},{7,5},{8,10},{9,11},{10,... | collective-permute-start | bytes 786440 | tf_op jit(solution)/shard_map/ppermute | solution.py:555
  47.1 12.2 %collective-permute-start.13 = (bf16[256,512]{1,0:T(8,128)(2,1)S(1)}, bf16[256,512]{1,0:T(8,128)(2,1)S(1)}, u32[]{:S(2)}, u32[]{:S(2)}) collective-permute-start(bf16[256,512]{1,0:T(8,128)(2,1)S(1)} %get-tuple-element.69), channel_id=1, source_target_pairs={{0,1},{1,0},{2,3},{3,2},{4,5},{5,4},{6,7},{7,6},{8,9},{9,8},{10,11... | collective-permute-start | bytes 786440 | tf_op jit(solution)/shard_map/ppermute | solution.py:555
  59.3 3.1 %collective-permute-start.14 = (bf16[576,512]{1,0:T(8,128)(2,1)S(1)}, bf16[576,512]{1,0:T(8,128)(2,1)S(1)}, u32[]{:S(2)}, u32[]{:S(2)}) collective-permute-start(bf16[576,512]{1,0:T(8,128)(2,1)S(1)} %attend_back.2.first_ref), channel_id=1, source_target_pairs={{0,16},{16,0},{1,17},{17,1},{2,18},{18,2},{3,19},{19,3},{4,20},{20... | collective-permute-start | bytes 1769480 | tf_op jit(solution)/shard_map/ppermute | solution.py:555
  60.8 1.6 %collective-permute-start.15 = (bf16[192,512]{1,0:T(8,128)(2,1)S(1)}, bf16[192,512]{1,0:T(8,128)(2,1)S(1)}, u32[]{:S(2)}, u32[]{:S(2)}) collective-permute-start(bf16[192,512]{1,0:T(8,128)(2,1)S(1)} %attend_back.3.second_ref), channel_id=1, source_target_pairs={{0,16},{16,0},{1,17},{17,1},{2,18},{18,2},{3,19},{19,3},{4,20},{20... | collective-permute-start | bytes 589832 | tf_op jit(solution)/shard_map/ppermute | solution.py:555
  64.2 7.3 %collective-permute-start.16 = (bf16[128,512]{1,0:T(8,128)(2,1)S(1)}, bf16[128,512]{1,0:T(8,128)(2,1)S(1)}, u32[]{:S(2)}, u32[]{:S(2)}) collective-permute-start(bf16[128,512]{1,0:T(8,128)(2,1)S(1)} %get-tuple-element.62), channel_id=1, source_target_pairs={{0,3},{1,2},{2,1},{3,0},{4,7},{5,6},{6,5},{7,4},{8,11},{9,10},{10,... | collective-permute-start | bytes 393224 | tf_op jit(solution)/shard_map/ppermute | solution.py:555
  66.1 7.7 %collective-permute-start.17 = (bf16[128,512]{1,0:T(8,128)(2,1)S(1)}, bf16[128,512]{1,0:T(8,128)(2,1)S(1)}, u32[]{:S(2)}, u32[]{:S(2)}) collective-permute-start(bf16[128,512]{1,0:T(8,128)(2,1)S(1)} %get-tuple-element.64), channel_id=1, source_target_pairs={{0,2},{1,3},{2,0},{3,1},{4,6},{5,7},{6,4},{7,5},{8,10},{9,11},{10,... | collective-permute-start | bytes 393224 | tf_op jit(solution)/shard_map/ppermute | solution.py:555
  67.2 6.6 %collective-permute-start.18 = (bf16[128,512]{1,0:T(8,128)(2,1)S(1)}, bf16[128,512]{1,0:T(8,128)(2,1)S(1)}, u32[]{:S(2)}, u32[]{:S(2)}) collective-permute-start(bf16[128,512]{1,0:T(8,128)(2,1)S(1)} %get-tuple-element.63), channel_id=1, source_target_pairs={{0,1},{1,0},{2,3},{3,2},{4,5},{5,4},{6,7},{7,6},{8,9},{9,8},{10,11... | collective-permute-start | bytes 393224 | tf_op jit(solution)/shard_map/ppermute | solution.py:555
  73.9 5.8 %collective-permute-start.19 = (bf16[32,512]{1,0:T(8,128)(2,1)S(1)}, bf16[32,512]{1,0:T(8,128)(2,1)S(1)}, u32[]{:S(2)}, u32[]{:S(2)}) collective-permute-start(bf16[32,512]{1,0:T(8,128)(2,1)S(1)} %get-tuple-element.65), channel_id=1, source_target_pairs={{0,12},{1,13},{2,14},{3,15},{4,8},{5,9},{6,10},{7,11},{8,4},{9,5},... | collective-permute-start | bytes 98312 | tf_op jit(solution)/shard_map/ppermute | solution.py:555
  75.8 4.9 %collective-permute-start.20 = (bf16[32,512]{1,0:T(8,128)(2,1)S(1)}, bf16[32,512]{1,0:T(8,128)(2,1)S(1)}, u32[]{:S(2)}, u32[]{:S(2)}) collective-permute-start(bf16[32,512]{1,0:T(8,128)(2,1)S(1)} %get-tuple-element.66), channel_id=1, source_target_pairs={{0,8},{1,9},{2,10},{3,11},{4,12},{5,13},{6,14},{7,15},{8,0},{9,1},... | collective-permute-start | bytes 98312 | tf_op jit(solution)/shard_map/ppermute | solution.py:555
  76.5 4.3 %collective-permute-start.21 = (bf16[32,512]{1,0:T(8,128)(2,1)S(1)}, bf16[32,512]{1,0:T(8,128)(2,1)S(1)}, u32[]{:S(2)}, u32[]{:S(2)}) collective-permute-start(bf16[32,512]{1,0:T(8,128)(2,1)S(1)} %get-tuple-element.67), channel_id=1, source_target_pairs={{0,4},{1,5},{2,6},{3,7},{4,0},{5,1},{6,2},{7,3},{8,12},{9,13},{10,... | collective-permute-start | bytes 98312 | tf_op jit(solution)/shard_map/ppermute | solution.py:555
  (6 other events, 121.2 us)

commit v8 on v7

--- a/solution.py
+++ b/solution.py
@@ -205,7 +205,7 @@
     for head in range(0, HEADS, quad):
         left = mixed_rows_ref[head : head + quad].reshape(quad * total, width)
         start = 2 * width + head * head_dim
-        both = dot_split(left, qkv_ref[:, start : start + span])
+        both = dot(left.astype(jnp.bfloat16), qkv_ref[:, start : start + span])
         head_at = lax.broadcasted_iota(jnp.int32, (total, span), 1) // head_dim
         piece = jnp.zeros((total, span), jnp.float32)
         for place in range(quad):
@@ -280,7 +280,7 @@
     sems,
 ):
     users, events, _ = history_ref.shape
-    chunk = math.gcd(events, 1024)
+    chunk = math.gcd(events, 2048)
     copies = [
         pltpu.make_async_copy(history_hbm.at[user], history_ref.at[user], sems.at[user])
         for user in range(users)
@@ -413,7 +413,7 @@
 def attend_back_kernel(first, grad_att_ref, direct_ref, slope_ref, history_ref, grad_rows_ref):
     users, events, key_width = history_ref.shape
     per_user = grad_att_ref.shape[0] // users
-    chunk = math.gcd(events, 1024)
+    chunk = math.gcd(events, 2048)
     for user in range(grad_rows_ref.shape[0] // per_user):
         rows = slice((first + user) * per_user, (first + user + 1) * per_user)
         back = jnp.zeros((per_user, key_width), jnp.float32)
@@ -457,29 +457,27 @@
     return dot((places == slots_ref[...]).astype(jnp.bfloat16), grad_rows_ref[...])
 
 
-def cand_grad_kernel(slots_ref, first_ref, second_ref, cand_grad_ref, grad_rows_ref):
-    join_rows((first_ref, second_ref), grad_rows_ref)
+def cand_grad_kernel(slots_ref, grad_rows_ref, cand_grad_ref):
     cands = cand_grad_ref.shape[0]
     chunk = math.gcd(cands, 512)
     for at in range(0, cands, chunk):
         cand_grad_ref[at : at + chunk, :] = sum_rows(chunk, at, slots_ref, grad_rows_ref)
 
 
-def own_cand_grad(cands, slots, grad_parts):
-    requests, key_width = slots.shape[1], grad_parts[0].shape[1]
+def sum_by_cand(cands, slots, grad_rows):
+    requests, key_width = grad_rows.shape
     whole = pl.BlockSpec(memory_space=pltpu.VMEM)
     return pl.pallas_call(
         cand_grad_kernel,
-        in_specs=[whole] * 3,
+        in_specs=[whole] * 2,
         out_specs=whole,
         out_shape=jax.ShapeDtypeStruct((cands, key_width), jnp.float32),
-        scratch_shapes=[pltpu.VMEM((requests, key_width), jnp.bfloat16)],
         compiler_params=pltpu.CompilerParams(vmem_limit_bytes=20 * MIB),
         cost_estimate=pl.CostEstimate(
             flops=2 * cands * key_width * requests, bytes_accessed=1 << 22, transcendentals=0
         ),
-        name="own_cand_grad",
-    )(slots, *grad_parts)
+        name="sum_by_cand",
+    )(slots, grad_rows)
 
 
 def terms_kernel(
@@ -487,14 +485,11 @@
     wide_ref,
     cand_grad_ref,
     slots_ref,
-    first_ref,
-    second_ref,
     pooled_ref,
-    out_ref,
-    grad_rows_ref,
-    terms_ref,
+    *refs,
 ):
-    join_rows((first_ref, second_ref), grad_rows_ref)
+    *parts, out_ref, grad_rows_ref, terms_ref = refs
+    join_rows(parts, grad_rows_ref)
     cands = pooled_ref.shape[0]
     chunk = math.gcd(cands, 512)
     for at in range(0, cands, chunk):
@@ -518,13 +513,13 @@
         out_ref[slot * rows : (slot + batch) * rows, :] = found.astype(jnp.bfloat16)
 
 
-def chip_terms(origins, wide, cand_grad, far_slots, far_parts, pooled):
+def chip_terms(origins, wide, cand_grad, slots, grad_parts, pooled):
     cands, width = pooled.shape
-    requests, key_width = far_slots.shape[1], cand_grad.shape[1]
+    requests, key_width = slots.shape[1], cand_grad.shape[1]
     whole = pl.BlockSpec(memory_space=pltpu.VMEM)
     return pl.pallas_call(
         functools.partial(terms_kernel, origins),
-        in_specs=[pl.BlockSpec(memory_space=pltpu.SMEM)] + [whole] * 5,
+        in_specs=[pl.BlockSpec(memory_space=pltpu.SMEM)] + [whole] * (3 + len(grad_parts)),
         out_specs=whole,
         out_shape=jax.ShapeDtypeStruct((width, key_width), jnp.bfloat16),
         scratch_shapes=[
@@ -538,7 +533,7 @@
             transcendentals=0,
         ),
         name="chip_terms",
-    )(wide, cand_grad, far_slots, *far_parts, pooled)
+    )(wide, cand_grad, slots, pooled, *grad_parts)
 
 
 def bit_groups(size):
@@ -658,13 +653,16 @@
     )
     half = max(1, users - 1)
     first_rows = attend_back(0, half, grad_att, direct, slope, history)
-    found_pooled, grad_att, first_rows = lax.optimization_barrier(
-        (found_pooled[::-1], grad_att, first_rows)
+    first_count = first_rows.shape[0]
+    cands = cand_count * wides * 2
+    cand_grad = sum_by_cand(cands, pooled_slots[:first_count].reshape(1, first_count), first_rows)
+    found_pooled, grad_att, first_rows, cand_grad = lax.optimization_barrier(
+        (found_pooled[::-1], grad_att, first_rows, cand_grad)
     )
     pooled = jnp.concatenate([pooled] + found_pooled[::-1], axis=0)
-    grad_parts = [first_rows, attend_back(half, users - half, grad_att, direct, slope, history)]
-    far_parts = [exchange(part, "section", 2, 1) for part in grad_parts]
-    cand_grad = own_cand_grad(pooled.shape[0], pooled_slots.reshape(1, requests), grad_parts)
+    second_rows = attend_back(half, users - half, grad_att, direct, slope, history)
+    far_parts = [exchange(part, "section", 2, 1) for part in (first_rows, second_rows)]
+    rest_slots = jnp.concatenate([pooled_slots[first_count:], far_slots])
     origins = [0] * wides
     for distance in range(wides):
         origins[slot_of(distance, wides)] = distance
@@ -672,8 +670,8 @@
         origins,
         wide.reshape(1),
         cand_grad,
-        far_slots.reshape(1, requests),
-        far_parts,
+        rest_slots.reshape(1, -1),
+        [second_rows] + far_parts,
         pooled,
     )
     grad_proj, logits = sum_blocks(terms, wides, logits.reshape(requests))

time: 81.6 us -> 82 us (level)
  no operation moved by 1% of the time
where the time goes in v8:
time: 82 us; the launch traced here: 81.8 us
  Pallas kernels  36.5 us (45%)
  starting transfers between devices  24.3 us (30%)
  waiting for transfers between devices  17.4 us (21%)
  other arithmetic  1.83 us (2%)
  between operations  1.04 us (1%)
  local copies, waits for them, and re-layouts  0.83 us (1%)
    ppermute x22, starting transfers between devices, exchange(): lax.ppermute(values, axis_name, [(i, i ^ distance) for i in range(size)])  24.3 us
    ppermute x22, waiting for transfers between devices, exchange(): lax.ppermute(values, axis_name, [(i, i ^ distance) for i in range(size)])  17.4 us
    pallas_call x1, Pallas kernels, encode_block(): pl.pallas_call(functools.partial(encode_kernel, tokens), in_specs=[pl.Blo...  14.3 us
    pallas_call x1, Pallas kernels, attend(): pl.pallas_call(attend_kernel, in_specs=[pl.BlockSpec(memory_space=pltpu.S...  7.62 us
    pallas_call x1, Pallas kernels, score(): pl.pallas_call(score_kernel, in_specs=[pl.BlockSpec(memory_space=pltpu.SM...  6.88 us
    pallas_call x2, Pallas kernels, attend_back(): pl.pallas_call(functools.partial(attend_back_kernel, first), in_specs=[wh...  4.65 us
    pallas_call x1, Pallas kernels, chip_terms(): pl.pallas_call(functools.partial(terms_kernel, origins), in_specs=[pl.Blo...  1.99 us
  transfers between devices with their start and end apart: 22, of which 10 were waited for; matrix products, arithmetic and copies ran while one was open for 2% of the time, Pallas kernels for 25%

profile of v8, /device:TPU:0, one launch (start us, length us, event | category | flops | bytes accessed | tf_op | source)
XLA Modules:
  0.0 81.8 jit_solution(958753208123185855)
XLA Ops:
  0.7 14.3 %encode.1 = (bf16[32,512]{1,0:T(8,128)(2,1)S(1)}, bf16[32,512]{1,0:T(8,128)(2,1)S(1)}, bf16[32,512]{1,0:T(8,128)(2,1)S(1)}) custom-call(s32[1]{0:T(128)} %bitcast.1.core_ref, bf16[1536,1024]{1,0:T(8,128)(2,1)} %bitcast.9, bf16[1024,3072]{1,0:T(8,128)(2,1)} %qkv_hbm.1, bf16[1024,1024]{1,0:T(8,128)(2,1)} %out_hbm.1, bf16[1024,512]{1,0:T(8,128)(2,1)} %proj_hbm.1), custom_call_target="tpu_custom_call" | custom-call | flops 8053063680 | bytes 16777216 | tf_op jit(solution)/shard_map/encode/pallas_call | solution.py:237
  15.0 5.1 %collective-permute-start = (bf16[32,512]{1,0:T(8,128)(2,1)S(1)}, bf16[32,512]{1,0:T(8,128)(2,1)S(1)}, u32[]{:S(2)}, u32[]{:S(2)}) collective-permute-start(bf16[32,512]{1,0:T(8,128)(2,1)S(1)} %get-tuple-element.32), channel_id=1, source_target_pairs={{0,12},{1,13},{2,14},{3,15},{4,8},{5,9},{6,10},{7,11},{8,4},{9,5},... | collective-permute-start | bytes 98312 | tf_op jit(solution)/shard_map/ppermute | solution.py:550
  22.1 2.9 %collective-permute-done.1 = bf16[32,512]{1,0:T(8,128)(2,1)S(1)} collective-permute-done((bf16[32,512]{1,0:T(8,128)(2,1)S(1)}, bf16[32,512]{1,0:T(8,128)(2,1)S(1)}, u32[]{:S(2)}, u32[]{:S(2)}) %collective-permute-start.1) | collective-permute-done | bytes 32800 | tf_op jit(solution)/shard_map/ppermute | solution.py:550
  25.0 2.5 %collective-permute-start.5 = (bf16[128,512]{1,0:T(8,128)(2,1)S(1)}, bf16[128,512]{1,0:T(8,128)(2,1)S(1)}, u32[]{:S(2)}, u32[]{:S(2)}) collective-permute-start(bf16[128,512]{1,0:T(8,128)(2,1)S(1)} %get-tuple-element.75), channel_id=1, source_target_pairs={{0,3},{1,2},{2,1},{3,0},{4,7},{5,6},{6,5},{7,4},{8,11},{9,10},{10,... | collective-permute-start | bytes 393224 | tf_op jit(solution)/shard_map/ppermute | solution.py:550
  28.7 4.3 %collective-permute-done.8 = bf16[64,512]{1,0:T(8,128)(2,1)S(1)} collective-permute-done((bf16[64,512]{1,0:T(8,128)(2,1)S(1)}, bf16[64,512]{1,0:T(8,128)(2,1)S(1)}, u32[]{:S(2)}, u32[]{:S(2)}) %collective-permute-start.8) | collective-permute-done | bytes 65568 | tf_op jit(solution)/shard_map/ppermute | solution.py:550
  34.1 2.1 %collective-permute-start.9 = (bf16[128,512]{1,0:T(8,128)(2,1)S(1)}, bf16[128,512]{1,0:T(8,128)(2,1)S(1)}, u32[]{:S(2)}, u32[]{:S(2)}) collective-permute-start(bf16[128,512]{1,0:T(8,128)(2,1)S(1)} %pad_maximum_fusion), channel_id=1, source_target_pairs={{0,8},{1,9},{2,10},{3,11},{4,12},{5,13},{6,14},{7,15},{8,0},{9,1},... | collective-permute-start | bytes 393224 | tf_op jit(solution)/shard_map/ppermute | solution.py:550
  36.2 7.6 %attend.1 = (bf16[768,512]{1,0:T(8,128)(2,1)S(1)}, f32[768,512]{1,0:T(8,128)S(1)}, bf16[768,2048]{1,0:T(8,128)(2,1)S(1)}, bf16[1536,1024]{1,0:T(8,128)(2,1)S(1)}) custom-call(f32[4]{0:T(128)S(1)} %rsqrt.3.inv_ref, s32[768,1]{1,0:T(8,128)S(1)} %reshape.68.slots_ref, bf16[512,512]{1,0:T(8,128)(2,1)S(1)} %constant_dynamic-update-slice_fusion.4.near_ref, ...), custom_call_target="tpu_custom_call" | custom-call | flops 3221225472 | bytes 16777216 | tf_op jit(solution)/shard_map/attend/pallas_call | solution.py:320
  43.9 2.3 %collective-permute-start.11 = (bf16[256,512]{1,0:T(8,128)(2,1)S(1)}, bf16[256,512]{1,0:T(8,128)(2,1)S(1)}, u32[]{:S(2)}, u32[]{:S(2)}) collective-permute-start(bf16[256,512]{1,0:T(8,128)(2,1)S(1)} %get-tuple-element.71), channel_id=1, source_target_pairs={{0,3},{1,2},{2,1},{3,0},{4,7},{5,6},{6,5},{7,4},{8,11},{9,10},{10,... | collective-permute-start | bytes 786440 | tf_op jit(solution)/shard_map/ppermute | solution.py:550
  46.7 0.7 collective-permute-start.13
  47.4 6.9 %score.1 = (f32[768,1]{1,0:T(8,128)S(1)}, bf16[768,512]{1,0:T(8,128)(2,1)S(1)}, f32[768,512]{1,0:T(8,128)S(1)}) custom-call(f32[4]{0:T(128)S(1)} %rsqrt.3.inv_ref, bf16[768,512]{1,0:T(8,128)(2,1)S(1)} %get-tuple-element.47.queries_ref, f32[768,512]{1,0:T(8,128)S(1)} %get-tuple-element.44.attended_ref, s32[768,1]{1,0:T(8,128)S(1)} %reshape.69.labels_ref, ...), custom_call_target="tpu_custom_call" | custom-call | flops 4831838208 | bytes 8388608 | tf_op jit(solution)/shard_map/score/pallas_call | solution.py:393
  54.4 3.4 %attend_back.2.grad_rows_ref = bf16[576,512]{1,0:T(8,128)(2,1)S(1)} custom-call(bf16[768,512]{1,0:T(8,128)(2,1)S(1)} %get-tuple-element.57.grad_att_ref, f32[768,512]{1,0:T(8,128)S(1)} %get-tuple-element.50.direct_ref, bf16[768,2048]{1,0:T(8,128)(2,1)S(1)} %get-tuple-element.51.slope_ref, bf16[4,2048,512]{2,1,0:T(8,128)(2,1)S(1)} %bitcast.6), custom_call_target="tpu_custom_call" | custom-call | flops 2415919104 | bytes 8388608 | tf_op jit(solution)/shard_map/attend_back/pallas_call | solution.py:433
  57.8 1.0 %sum_by_cand.1.cand_grad_ref = f32[1024,512]{1,0:T(8,128)S(1)} custom-call(s32[1,576]{1,0:T(1,128)S(1)} %reshape.65.slots_ref, bf16[576,512]{1,0:T(8,128)(2,1)S(1)} %attend_back.2.grad_rows_ref), custom_call_target="tpu_custom_call" | custom-call | flops 603979776 | bytes 4194304 | tf_op jit(solution)/shard_map/sum_by_cand/pallas_call | solution.py:470
  59.2 1.2 %attend_back.3.refs_0_ = bf16[192,512]{1,0:T(8,128)(2,1)S(1)} custom-call(bf16[768,512]{1,0:T(8,128)(2,1)S(1)} %get-tuple-element.57.grad_att_ref, f32[768,512]{1,0:T(8,128)S(1)} %get-tuple-element.50.direct_ref, bf16[768,2048]{1,0:T(8,128)(2,1)S(1)} %get-tuple-element.51.slope_ref, bf16[4,2048,512]{2,1,0:T(8,128)(2,1)S(1)} %bitcast.6), custom_call_target="tpu_custom_call" | custom-call | flops 805306368 | bytes 8388608 | tf_op jit(solution)/shard_map/attend_back/pallas_call | solution.py:433
  61.1 1.0 %collective-permute-done.15.refs_2_ = bf16[192,512]{1,0:T(8,128)(2,1)S(1)} collective-permute-done((bf16[192,512]{1,0:T(8,128)(2,1)S(1)}, bf16[192,512]{1,0:T(8,128)(2,1)S(1)}, u32[]{:S(2)}, u32[]{:S(2)}) %collective-permute-start.15) | collective-permute-done | bytes 196640 | tf_op jit(solution)/shard_map/ppermute | solution.py:550
  62.1 2.0 %chip_terms.1 = bf16[512,512]{1,0:T(8,128)(2,1)S(1)} custom-call(s32[1]{0:T(128)} %bitcast.wide_ref, f32[1024,512]{1,0:T(8,128)S(1)} %sum_by_cand.1.cand_grad_ref, s32[1,960]{1,0:T(1,128)S(1)} %bitcast.7, bf16[1024,512]{1,0:T(8,128)(2,1)S(1)} %constant_dynamic-update-slice_fusion.13.pooled_ref, bf16[192,512]{1,0:T(8,128)(2,1)S(1)} %attend_back.3.refs_0_, ...), custom_call_target="tpu_custom_call" | custom-call | flops 1543503872 | bytes 4194304 | tf_op jit(solution)/shard_map/chip_terms/pallas_call | solution.py:520
  64.2 2.3 %collective-permute-start.16 = (bf16[128,512]{1,0:T(8,128)(2,1)S(1)}, bf16[128,512]{1,0:T(8,128)(2,1)S(1)}, u32[]{:S(2)}, u32[]{:S(2)}) collective-permute-start(bf16[128,512]{1,0:T(8,128)(2,1)S(1)} %get-tuple-element.64), channel_id=1, source_target_pairs={{0,3},{1,2},{2,1},{3,0},{4,7},{5,6},{6,5},{7,4},{8,11},{9,10},{10,... | collective-permute-start | bytes 393224 | tf_op jit(solution)/shard_map/ppermute | solution.py:550
  67.0 0.7 collective-permute-start.18
  67.7 0.8 reduce.1
  68.5 3.0 %collective-permute-done.16 = bf16[128,512]{1,0:T(8,128)(2,1)S(1)} collective-permute-done((bf16[128,512]{1,0:T(8,128)(2,1)S(1)}, bf16[128,512]{1,0:T(8,128)(2,1)S(1)}, u32[]{:S(2)}, u32[]{:S(2)}) %collective-permute-start.16) | collective-permute-done | bytes 131104 | tf_op jit(solution)/shard_map/ppermute | solution.py:550
  71.4 2.3 %collective-permute-done.17 = bf16[128,512]{1,0:T(8,128)(2,1)S(1)} collective-permute-done((bf16[128,512]{1,0:T(8,128)(2,1)S(1)}, bf16[128,512]{1,0:T(8,128)(2,1)S(1)}, u32[]{:S(2)}, u32[]{:S(2)}) %collective-permute-start.17) | collective-permute-done | bytes 131104 | tf_op jit(solution)/shard_map/ppermute | solution.py:550
  73.8 2.6 %collective-permute-start.19 = (bf16[32,512]{1,0:T(8,128)(2,1)S(1)}, bf16[32,512]{1,0:T(8,128)(2,1)S(1)}, u32[]{:S(2)}, u32[]{:S(2)}) collective-permute-start(bf16[32,512]{1,0:T(8,128)(2,1)S(1)} %get-tuple-element.67), channel_id=1, source_target_pairs={{0,12},{1,13},{2,14},{3,15},{4,8},{5,9},{6,10},{7,11},{8,4},{9,5},... | collective-permute-start | bytes 98312 | tf_op jit(solution)/shard_map/ppermute | solution.py:550
  76.4 1.8 %collective-permute-start.21 = (bf16[32,512]{1,0:T(8,128)(2,1)S(1)}, bf16[32,512]{1,0:T(8,128)(2,1)S(1)}, u32[]{:S(2)}, u32[]{:S(2)}) collective-permute-start(bf16[32,512]{1,0:T(8,128)(2,1)S(1)} %get-tuple-element.69), channel_id=1, source_target_pairs={{0,4},{1,5},{2,6},{3,7},{4,0},{5,1},{6,2},{7,3},{8,12},{9,13},{10,... | collective-permute-start | bytes 98312 | tf_op jit(solution)/shard_map/ppermute | solution.py:550
  78.2 1.3 %collective-permute-done.19 = bf16[32,512]{1,0:T(8,128)(2,1)S(1)} collective-permute-done((bf16[32,512]{1,0:T(8,128)(2,1)S(1)}, bf16[32,512]{1,0:T(8,128)(2,1)S(1)}, u32[]{:S(2)}, u32[]{:S(2)}) %collective-permute-start.19) | collective-permute-done | bytes 32800 | tf_op jit(solution)/shard_map/ppermute | solution.py:550
  79.6 1.6 %collective-permute-done.20 = bf16[32,512]{1,0:T(8,128)(2,1)S(1)} collective-permute-done((bf16[32,512]{1,0:T(8,128)(2,1)S(1)}, bf16[32,512]{1,0:T(8,128)(2,1)S(1)}, u32[]{:S(2)}, u32[]{:S(2)}) %collective-permute-start.20) | collective-permute-done | bytes 32800 | tf_op jit(solution)/shard_map/ppermute | solution.py:550
  (75 shorter events, 7.1 us)
Async XLA Ops:
  0.7 33.0 %copy-start.1 = (s32[768]{0:T(1024)S(1)}, s32[768]{0:T(1024)}, u32[]{:S(2)}) copy-start(s32[768]{0:T(1024)} %param.23) | copy-start | bytes 9220
  0.7 33.2 %copy-start.4 = (bf16[1024]{0:T(1024)(128)(2,1)S(1)}, bf16[1024]{0:T(1024)(128)(2,1)}, u32[]{:S(2)}) copy-start(bf16[1024]{0:T(1024)(128)(2,1)} %param.17) | copy-start | bytes 6148
  15.0 7.0 %collective-permute-start = (bf16[32,512]{1,0:T(8,128)(2,1)S(1)}, bf16[32,512]{1,0:T(8,128)(2,1)S(1)}, u32[]{:S(2)}, u32[]{:S(2)}) collective-permute-start(bf16[32,512]{1,0:T(8,128)(2,1)S(1)} %get-tuple-element.32), channel_id=1, source_target_pairs={{0,12},{1,13},{2,14},{3,15},{4,8},{5,9},{6,10},{7,11},{8,4},{9,5},... | collective-permute-start | bytes 98312 | tf_op jit(solution)/shard_map/ppermute | solution.py:550
  20.1 4.8 %collective-permute-start.1 = (bf16[32,512]{1,0:T(8,128)(2,1)S(1)}, bf16[32,512]{1,0:T(8,128)(2,1)S(1)}, u32[]{:S(2)}, u32[]{:S(2)}) collective-permute-start(bf16[32,512]{1,0:T(8,128)(2,1)S(1)} %get-tuple-element.32), channel_id=1, source_target_pairs={{0,8},{1,9},{2,10},{3,11},{4,12},{5,13},{6,14},{7,15},{8,0},{9,1},... | collective-permute-start | bytes 98312 | tf_op jit(solution)/shard_map/ppermute | solution.py:550
  20.2 4.8 %collective-permute-start.2 = (bf16[32,512]{1,0:T(8,128)(2,1)S(1)}, bf16[32,512]{1,0:T(8,128)(2,1)S(1)}, u32[]{:S(2)}, u32[]{:S(2)}) collective-permute-start(bf16[32,512]{1,0:T(8,128)(2,1)S(1)} %get-tuple-element.32), channel_id=1, source_target_pairs={{0,4},{1,5},{2,6},{3,7},{4,0},{5,1},{6,2},{7,3},{8,12},{9,13},{10,... | collective-permute-start | bytes 98312 | tf_op jit(solution)/shard_map/ppermute | solution.py:550
  20.8 1.2 %collective-permute-start.4 = (s32[768]{0:T(1024)S(1)}, s32[768]{0:T(1024)S(1)}, u32[]{:S(2)}, u32[]{:S(2)}) collective-permute-start(s32[768]{0:T(1024)S(1)} %get-tuple-element.83), channel_id=1, source_target_pairs={{0,16},{16,0},{1,17},{17,1},{2,18},{18,2},{3,19},{19,3},{4,20},{20... | collective-permute-start | bytes 9224 | tf_op jit(solution)/shard_map/ppermute | solution.py:550
  20.9 4.0 %collective-permute-start.3 = (bf16[32,512]{1,0:T(8,128)(2,1)S(1)}, bf16[32,512]{1,0:T(8,128)(2,1)S(1)}, u32[]{:S(2)}, u32[]{:S(2)}) collective-permute-start(bf16[32,512]{1,0:T(8,128)(2,1)S(1)} %get-tuple-element.34), channel_id=1, source_target_pairs={{0,16},{16,0},{1,17},{17,1},{2,18},{18,2},{3,19},{19,3},{4,20},{20... | collective-permute-start | bytes 98312 | tf_op jit(solution)/shard_map/ppermute | solution.py:550
  25.0 7.9 %collective-permute-start.5 = (bf16[128,512]{1,0:T(8,128)(2,1)S(1)}, bf16[128,512]{1,0:T(8,128)(2,1)S(1)}, u32[]{:S(2)}, u32[]{:S(2)}) collective-permute-start(bf16[128,512]{1,0:T(8,128)(2,1)S(1)} %get-tuple-element.75), channel_id=1, source_target_pairs={{0,3},{1,2},{2,1},{3,0},{4,7},{5,6},{6,5},{7,4},{8,11},{9,10},{10,... | collective-permute-start | bytes 393224 | tf_op jit(solution)/shard_map/ppermute | solution.py:550
  27.5 5.6 %collective-permute-start.6 = (bf16[128,512]{1,0:T(8,128)(2,1)S(1)}, bf16[128,512]{1,0:T(8,128)(2,1)S(1)}, u32[]{:S(2)}, u32[]{:S(2)}) collective-permute-start(bf16[128,512]{1,0:T(8,128)(2,1)S(1)} %get-tuple-element.75), channel_id=1, source_target_pairs={{0,2},{1,3},{2,0},{3,1},{4,6},{5,7},{6,4},{7,5},{8,10},{9,11},{10,... | collective-permute-start | bytes 393224 | tf_op jit(solution)/shard_map/ppermute | solution.py:550
  28.0 5.1 %collective-permute-start.7 = (bf16[128,512]{1,0:T(8,128)(2,1)S(1)}, bf16[128,512]{1,0:T(8,128)(2,1)S(1)}, u32[]{:S(2)}, u32[]{:S(2)}) collective-permute-start(bf16[128,512]{1,0:T(8,128)(2,1)S(1)} %get-tuple-element.75), channel_id=1, source_target_pairs={{0,1},{1,0},{2,3},{3,2},{4,5},{5,4},{6,7},{7,6},{8,9},{9,8},{10,11... | collective-permute-start | bytes 393224 | tf_op jit(solution)/shard_map/ppermute | solution.py:550
  28.6 4.3 %collective-permute-start.8 = (bf16[64,512]{1,0:T(8,128)(2,1)S(1)}, bf16[64,512]{1,0:T(8,128)(2,1)S(1)}, u32[]{:S(2)}, u32[]{:S(2)}) collective-permute-start(bf16[64,512]{1,0:T(8,128)(2,1)S(1)} %maximum_select_fusion), channel_id=1, source_target_pairs={{0,4},{1,5},{2,6},{3,7},{4,0},{5,1},{6,2},{7,3},{8,12},{9,13},{10,... | collective-permute-start | bytes 196616 | tf_op jit(solution)/shard_map/ppermute | solution.py:550
  33.2 3.0 %collective-permute-start.10 = (bf16[512,512]{1,0:T(8,128)(2,1)S(1)}, bf16[512,512]{1,0:T(8,128)(2,1)S(1)}, u32[]{:S(2)}, u32[]{:S(2)}) collective-permute-start(bf16[512,512]{1,0:T(8,128)(2,1)S(1)} %constant_dynamic-update-slice_fusion.4.near_ref), channel_id=1, source_target_pairs={{0,16},{16,0},{1,17},{17,1},{2,18},{18,2},{3,19},{19,3},{4,20},{20... | collective-permute-start | bytes 1572872 | tf_op jit(solution)/shard_map/ppermute | solution.py:550
  34.1 9.7 %collective-permute-start.9 = (bf16[128,512]{1,0:T(8,128)(2,1)S(1)}, bf16[128,512]{1,0:T(8,128)(2,1)S(1)}, u32[]{:S(2)}, u32[]{:S(2)}) collective-permute-start(bf16[128,512]{1,0:T(8,128)(2,1)S(1)} %pad_maximum_fusion), channel_id=1, source_target_pairs={{0,8},{1,9},{2,10},{3,11},{4,12},{5,13},{6,14},{7,15},{8,0},{9,1},... | collective-permute-start | bytes 393224 | tf_op jit(solution)/shard_map/ppermute | solution.py:550
  43.9 15.1 %collective-permute-start.11 = (bf16[256,512]{1,0:T(8,128)(2,1)S(1)}, bf16[256,512]{1,0:T(8,128)(2,1)S(1)}, u32[]{:S(2)}, u32[]{:S(2)}) collective-permute-start(bf16[256,512]{1,0:T(8,128)(2,1)S(1)} %get-tuple-element.71), channel_id=1, source_target_pairs={{0,3},{1,2},{2,1},{3,0},{4,7},{5,6},{6,5},{7,4},{8,11},{9,10},{10,... | collective-permute-start | bytes 786440 | tf_op jit(solution)/shard_map/ppermute | solution.py:550
  46.2 12.8 %collective-permute-start.12 = (bf16[256,512]{1,0:T(8,128)(2,1)S(1)}, bf16[256,512]{1,0:T(8,128)(2,1)S(1)}, u32[]{:S(2)}, u32[]{:S(2)}) collective-permute-start(bf16[256,512]{1,0:T(8,128)(2,1)S(1)} %get-tuple-element.71), channel_id=1, source_target_pairs={{0,2},{1,3},{2,0},{3,1},{4,6},{5,7},{6,4},{7,5},{8,10},{9,11},{10,... | collective-permute-start | bytes 786440 | tf_op jit(solution)/shard_map/ppermute | solution.py:550
  46.7 12.3 %collective-permute-start.13 = (bf16[256,512]{1,0:T(8,128)(2,1)S(1)}, bf16[256,512]{1,0:T(8,128)(2,1)S(1)}, u32[]{:S(2)}, u32[]{:S(2)}) collective-permute-start(bf16[256,512]{1,0:T(8,128)(2,1)S(1)} %get-tuple-element.71), channel_id=1, source_target_pairs={{0,1},{1,0},{2,3},{3,2},{4,5},{5,4},{6,7},{7,6},{8,9},{9,8},{10,11... | collective-permute-start | bytes 786440 | tf_op jit(solution)/shard_map/ppermute | solution.py:550
  59.0 3.1 %collective-permute-start.14 = (bf16[576,512]{1,0:T(8,128)(2,1)S(1)}, bf16[576,512]{1,0:T(8,128)(2,1)S(1)}, u32[]{:S(2)}, u32[]{:S(2)}) collective-permute-start(bf16[576,512]{1,0:T(8,128)(2,1)S(1)} %attend_back.2.grad_rows_ref), channel_id=1, source_target_pairs={{0,16},{16,0},{1,17},{17,1},{2,18},{18,2},{3,19},{19,3},{4,20},{20... | collective-permute-start | bytes 1769480 | tf_op jit(solution)/shard_map/ppermute | solution.py:550
  60.5 1.6 %collective-permute-start.15 = (bf16[192,512]{1,0:T(8,128)(2,1)S(1)}, bf16[192,512]{1,0:T(8,128)(2,1)S(1)}, u32[]{:S(2)}, u32[]{:S(2)}) collective-permute-start(bf16[192,512]{1,0:T(8,128)(2,1)S(1)} %attend_back.3.refs_0_), channel_id=1, source_target_pairs={{0,16},{16,0},{1,17},{17,1},{2,18},{18,2},{3,19},{19,3},{4,20},{20... | collective-permute-start | bytes 589832 | tf_op jit(solution)/shard_map/ppermute | solution.py:550
  64.2 7.3 %collective-permute-start.16 = (bf16[128,512]{1,0:T(8,128)(2,1)S(1)}, bf16[128,512]{1,0:T(8,128)(2,1)S(1)}, u32[]{:S(2)}, u32[]{:S(2)}) collective-permute-start(bf16[128,512]{1,0:T(8,128)(2,1)S(1)} %get-tuple-element.64), channel_id=1, source_target_pairs={{0,3},{1,2},{2,1},{3,0},{4,7},{5,6},{6,5},{7,4},{8,11},{9,10},{10,... | collective-permute-start | bytes 393224 | tf_op jit(solution)/shard_map/ppermute | solution.py:550
  66.5 7.2 %collective-permute-start.17 = (bf16[128,512]{1,0:T(8,128)(2,1)S(1)}, bf16[128,512]{1,0:T(8,128)(2,1)S(1)}, u32[]{:S(2)}, u32[]{:S(2)}) collective-permute-start(bf16[128,512]{1,0:T(8,128)(2,1)S(1)} %get-tuple-element.66), channel_id=1, source_target_pairs={{0,2},{1,3},{2,0},{3,1},{4,6},{5,7},{6,4},{7,5},{8,10},{9,11},{10,... | collective-permute-start | bytes 393224 | tf_op jit(solution)/shard_map/ppermute | solution.py:550
  67.0 6.7 %collective-permute-start.18 = (bf16[128,512]{1,0:T(8,128)(2,1)S(1)}, bf16[128,512]{1,0:T(8,128)(2,1)S(1)}, u32[]{:S(2)}, u32[]{:S(2)}) collective-permute-start(bf16[128,512]{1,0:T(8,128)(2,1)S(1)} %get-tuple-element.65), channel_id=1, source_target_pairs={{0,1},{1,0},{2,3},{3,2},{4,5},{5,4},{6,7},{7,6},{8,9},{9,8},{10,11... | collective-permute-start | bytes 393224 | tf_op jit(solution)/shard_map/ppermute | solution.py:550
  73.8 5.8 %collective-permute-start.19 = (bf16[32,512]{1,0:T(8,128)(2,1)S(1)}, bf16[32,512]{1,0:T(8,128)(2,1)S(1)}, u32[]{:S(2)}, u32[]{:S(2)}) collective-permute-start(bf16[32,512]{1,0:T(8,128)(2,1)S(1)} %get-tuple-element.67), channel_id=1, source_target_pairs={{0,12},{1,13},{2,14},{3,15},{4,8},{5,9},{6,10},{7,11},{8,4},{9,5},... | collective-permute-start | bytes 98312 | tf_op jit(solution)/shard_map/ppermute | solution.py:550
  76.3 4.8 %collective-permute-start.20 = (bf16[32,512]{1,0:T(8,128)(2,1)S(1)}, bf16[32,512]{1,0:T(8,128)(2,1)S(1)}, u32[]{:S(2)}, u32[]{:S(2)}) collective-permute-start(bf16[32,512]{1,0:T(8,128)(2,1)S(1)} %get-tuple-element.68), channel_id=1, source_target_pairs={{0,8},{1,9},{2,10},{3,11},{4,12},{5,13},{6,14},{7,15},{8,0},{9,1},... | collective-permute-start | bytes 98312 | tf_op jit(solution)/shard_map/ppermute | solution.py:550
  76.4 4.7 %collective-permute-start.21 = (bf16[32,512]{1,0:T(8,128)(2,1)S(1)}, bf16[32,512]{1,0:T(8,128)(2,1)S(1)}, u32[]{:S(2)}, u32[]{:S(2)}) collective-permute-start(bf16[32,512]{1,0:T(8,128)(2,1)S(1)} %get-tuple-element.69), channel_id=1, source_target_pairs={{0,4},{1,5},{2,6},{3,7},{4,0},{5,1},{6,2},{7,3},{8,12},{9,13},{10,... | collective-permute-start | bytes 98312 | tf_op jit(solution)/shard_map/ppermute | solution.py:550
  (6 other events, 119.7 us)

commit v9 on v7

--- a/solution.py
+++ b/solution.py
@@ -85,7 +85,11 @@
     def columns(part):
         return pl.ds(part * width, width)
 
-    pieces = [(frames_hbm.at[group_rows(0)], frames_ref.at[group_rows(0)])]
+    first_rows = cands // 2 * tokens
+    pieces = [
+        (frames_hbm.at[pl.ds(at, count)], frames_ref.at[pl.ds(at, count)])
+        for at, count in ((0, first_rows), (first_rows, rows - first_rows))
+    ]
     pieces += [(qkv_hbm.at[:, columns(part)], qkv_ref.at[:, columns(part)]) for part in range(2)]
     pieces += [
         (frames_hbm.at[group_rows(group)], frames_ref.at[group_rows(group)])
@@ -144,19 +148,20 @@
                 :, side * 2 * lanes : (side + 1) * 2 * lanes
             ]
 
-    copies[0].wait()
-    copies[2].start()
-    for cand in range(cands):
-        norm_cand(cand)
-    copies[1].wait()
-    for copy in copies[3 : 2 + groups]:
+    for side in range(2):
+        copies[side].wait()
+        copies[2 + side].start()
+        for cand in range(side * (cands // 2), cands if side else cands // 2):
+            norm_cand(cand)
+    copies[2].wait()
+    for copy in copies[4 : 3 + groups]:
         copy.start()
     for group in range(groups):
         at = slice(group * rows, (group + 1) * rows)
         for part in range(2):
             if group == 0 and part == 1:
-                copies[2].wait()
-                for copy in copies[2 + groups :]:
+                copies[3].wait()
+                for copy in copies[3 + groups :]:
                     copy.start()
             part_columns = slice(part * width, (part + 1) * width)
             packed_ref[:, part_columns] = dot(normed_ref[at, :], qkv_ref[:, part_columns]).astype(
@@ -164,7 +169,7 @@
             )
             if group + 1 < groups:
                 if part == 0:
-                    copies[3 + group].wait()
+                    copies[4 + group].wait()
                 for cand in range(part * cands // 2, (part + 1) * cands // 2):
                     norm_cand((group + 1) * cands + cand)
         for head in range(0, HEADS, quad):
@@ -199,13 +204,13 @@
                 head * cands : (head + 1) * cands
             ]
 
-    for copy in copies[2 + groups :]:
+    for copy in copies[3 + groups :]:
         copy.wait()
     mixed = []
     for head in range(0, HEADS, quad):
         left = mixed_rows_ref[head : head + quad].reshape(quad * total, width)
         start = 2 * width + head * head_dim
-        both = dot_split(left, qkv_ref[:, start : start + span])
+        both = dot(left.astype(jnp.bfloat16), qkv_ref[:, start : start + span])
         head_at = lax.broadcasted_iota(jnp.int32, (total, span), 1) // head_dim
         piece = jnp.zeros((total, span), jnp.float32)
         for place in range(quad):
@@ -249,7 +254,7 @@
             pltpu.VMEM(qkv_weight.shape, jnp.bfloat16),
             pltpu.VMEM(out_weight.shape, jnp.bfloat16),
             pltpu.VMEM(proj_weight.shape, jnp.bfloat16),
-            pltpu.SemaphoreType.DMA((groups + 5,)),
+            pltpu.SemaphoreType.DMA((groups + 6,)),
             pltpu.VMEM(flat.shape, jnp.bfloat16),
             pltpu.VMEM((rows, 2 * width), jnp.bfloat16),
             pltpu.VMEM((rows // lanes, HEADS // 2, patches, 2 * lanes), jnp.float32),
@@ -280,18 +285,18 @@
     sems,
 ):
     users, events, _ = history_ref.shape
-    chunk = math.gcd(events, 1024)
+    chunk = math.gcd(events, 2048)
     copies = [
         pltpu.make_async_copy(history_hbm.at[user], history_ref.at[user], sems.at[user])
         for user in range(users)
     ]
     copies.append(pltpu.make_async_copy(mlp_hbm, mlp_ref, sems.at[users]))
-    for copy in copies[:2]:
-        copy.start()
+    copies[0].start()
     slots = slots_ref[...]
     half, key_width = near_ref.shape
     places = lax.broadcasted_iota(jnp.int32, (slots.shape[0], half), 1)
     queries = dot((slots == places).astype(jnp.bfloat16), near_ref[...])
+    copies[1].start()
     queries += dot((slots == places + half).astype(jnp.bfloat16), far_ref[...])
     queries_ref[...] = queries.astype(jnp.bfloat16)
     per_user = slots.shape[0] // users
@@ -413,7 +418,7 @@
 def attend_back_kernel(first, grad_att_ref, direct_ref, slope_ref, history_ref, grad_rows_ref):
     users, events, key_width = history_ref.shape
     per_user = grad_att_ref.shape[0] // users
-    chunk = math.gcd(events, 1024)
+    chunk = math.gcd(events, 2048)
     for user in range(grad_rows_ref.shape[0] // per_user):
         rows = slice((first + user) * per_user, (first + user + 1) * per_user)
         back = jnp.zeros((per_user, key_width), jnp.float32)

time: 81.6 us -> 81.7 us (level)
  no operation moved by 1% of the time
where the time goes in v9:
time: 81.7 us; the launch traced here: 81.5 us
  Pallas kernels  36.8 us (45%)
  starting transfers between devices  24.3 us (30%)
  waiting for transfers between devices  17 us (21%)
  other arithmetic  1.75 us (2%)
  between operations  1.02 us (1%)
    ppermute x22, starting transfers between devices, exchange(): lax.ppermute(values, axis_name, [(i, i ^ distance) for i in range(size)])  24.3 us
    ppermute x22, waiting for transfers between devices, exchange(): lax.ppermute(values, axis_name, [(i, i ^ distance) for i in range(size)])  17 us
    pallas_call x1, Pallas kernels, encode_block(): pl.pallas_call(functools.partial(encode_kernel, tokens), in_specs=[pl.Blo...  14.7 us
    pallas_call x1, Pallas kernels, attend(): pl.pallas_call(attend_kernel, in_specs=[pl.BlockSpec(memory_space=pltpu.S...  7.63 us
    pallas_call x1, Pallas kernels, score(): pl.pallas_call(score_kernel, in_specs=[pl.BlockSpec(memory_space=pltpu.SM...  6.88 us
    pallas_call x2, Pallas kernels, attend_back(): pl.pallas_call(functools.partial(attend_back_kernel, first), in_specs=[wh...  4.89 us
    pallas_call x1, Pallas kernels, chip_terms(): pl.pallas_call(functools.partial(terms_kernel, origins), in_specs=[pl.Blo...  1.73 us
  transfers between devices with their start and end apart: 22, of which 10 were waited for; matrix products, arithmetic and copies ran while one was open for 2% of the time, Pallas kernels for 25%

profile of v9, /device:TPU:0, one launch (start us, length us, event | category | flops | bytes accessed | tf_op | source)
XLA Modules:
  0.0 81.5 jit_solution(13716972789074937765)
XLA Ops:
  0.7 14.7 %encode.1 = (bf16[32,512]{1,0:T(8,128)(2,1)S(1)}, bf16[32,512]{1,0:T(8,128)(2,1)S(1)}, bf16[32,512]{1,0:T(8,128)(2,1)S(1)}) custom-call(s32[1]{0:T(128)} %bitcast.1.core_ref, bf16[1536,1024]{1,0:T(8,128)(2,1)} %bitcast.5, bf16[1024,3072]{1,0:T(8,128)(2,1)} %qkv_hbm.1, bf16[1024,1024]{1,0:T(8,128)(2,1)} %out_hbm.1, bf16[1024,512]{1,0:T(8,128)(2,1)} %proj_hbm.1), custom_call_target="tpu_custom_call" | custom-call | flops 8053063680 | bytes 16777216 | tf_op jit(solution)/shard_map/encode/pallas_call | solution.py:242
  15.4 5.1 %collective-permute-start = (bf16[32,512]{1,0:T(8,128)(2,1)S(1)}, bf16[32,512]{1,0:T(8,128)(2,1)S(1)}, u32[]{:S(2)}, u32[]{:S(2)}) collective-permute-start(bf16[32,512]{1,0:T(8,128)(2,1)S(1)} %get-tuple-element.31), channel_id=1, source_target_pairs={{0,12},{1,13},{2,14},{3,15},{4,8},{5,9},{6,10},{7,11},{8,4},{9,5},... | collective-permute-start | bytes 98312 | tf_op jit(solution)/shard_map/ppermute | solution.py:560
  22.4 2.9 %collective-permute-done.1 = bf16[32,512]{1,0:T(8,128)(2,1)S(1)} collective-permute-done((bf16[32,512]{1,0:T(8,128)(2,1)S(1)}, bf16[32,512]{1,0:T(8,128)(2,1)S(1)}, u32[]{:S(2)}, u32[]{:S(2)}) %collective-permute-start.1) | collective-permute-done | bytes 32800 | tf_op jit(solution)/shard_map/ppermute | solution.py:560
  25.3 2.5 %collective-permute-start.5 = (bf16[128,512]{1,0:T(8,128)(2,1)S(1)}, bf16[128,512]{1,0:T(8,128)(2,1)S(1)}, u32[]{:S(2)}, u32[]{:S(2)}) collective-permute-start(bf16[128,512]{1,0:T(8,128)(2,1)S(1)} %get-tuple-element.73), channel_id=1, source_target_pairs={{0,3},{1,2},{2,1},{3,0},{4,7},{5,6},{6,5},{7,4},{8,11},{9,10},{10,... | collective-permute-start | bytes 393224 | tf_op jit(solution)/shard_map/ppermute | solution.py:560
  29.0 4.3 %collective-permute-done.8 = bf16[64,512]{1,0:T(8,128)(2,1)S(1)} collective-permute-done((bf16[64,512]{1,0:T(8,128)(2,1)S(1)}, bf16[64,512]{1,0:T(8,128)(2,1)S(1)}, u32[]{:S(2)}, u32[]{:S(2)}) %collective-permute-start.8) | collective-permute-done | bytes 65568 | tf_op jit(solution)/shard_map/ppermute | solution.py:560
  34.4 2.1 %collective-permute-start.9 = (bf16[128,512]{1,0:T(8,128)(2,1)S(1)}, bf16[128,512]{1,0:T(8,128)(2,1)S(1)}, u32[]{:S(2)}, u32[]{:S(2)}) collective-permute-start(bf16[128,512]{1,0:T(8,128)(2,1)S(1)} %pad_maximum_fusion), channel_id=1, source_target_pairs={{0,8},{1,9},{2,10},{3,11},{4,12},{5,13},{6,14},{7,15},{8,0},{9,1},... | collective-permute-start | bytes 393224 | tf_op jit(solution)/shard_map/ppermute | solution.py:560
  36.5 7.6 %attend.1 = (bf16[768,512]{1,0:T(8,128)(2,1)S(1)}, f32[768,512]{1,0:T(8,128)S(1)}, bf16[768,2048]{1,0:T(8,128)(2,1)S(1)}, bf16[1536,1024]{1,0:T(8,128)(2,1)S(1)}) custom-call(f32[4]{0:T(128)S(1)} %rsqrt.3.inv_ref, s32[768,1]{1,0:T(8,128)S(1)} %reshape.68.slots_ref, bf16[512,512]{1,0:T(8,128)(2,1)S(1)} %constant_dynamic-update-slice_fusion.4.near_ref, ...), custom_call_target="tpu_custom_call" | custom-call | flops 3221225472 | bytes 16777216 | tf_op jit(solution)/shard_map/attend/pallas_call | solution.py:325
  44.2 2.3 %collective-permute-start.11 = (bf16[256,512]{1,0:T(8,128)(2,1)S(1)}, bf16[256,512]{1,0:T(8,128)(2,1)S(1)}, u32[]{:S(2)}, u32[]{:S(2)}) collective-permute-start(bf16[256,512]{1,0:T(8,128)(2,1)S(1)} %get-tuple-element.69), channel_id=1, source_target_pairs={{0,3},{1,2},{2,1},{3,0},{4,7},{5,6},{6,5},{7,4},{8,11},{9,10},{10,... | collective-permute-start | bytes 786440 | tf_op jit(solution)/shard_map/ppermute | solution.py:560
  47.0 0.7 collective-permute-start.13
  47.8 6.9 %score.1 = (f32[768,1]{1,0:T(8,128)S(1)}, bf16[768,512]{1,0:T(8,128)(2,1)S(1)}, f32[768,512]{1,0:T(8,128)S(1)}) custom-call(f32[4]{0:T(128)S(1)} %rsqrt.3.inv_ref, bf16[768,512]{1,0:T(8,128)(2,1)S(1)} %get-tuple-element.46.queries_ref, f32[768,512]{1,0:T(8,128)S(1)} %get-tuple-element.43.attended_ref, s32[768,1]{1,0:T(8,128)S(1)} %reshape.69.labels_ref, ...), custom_call_target="tpu_custom_call" | custom-call | flops 4831838208 | bytes 8388608 | tf_op jit(solution)/shard_map/score/pallas_call | solution.py:398
  54.7 3.4 %attend_back.2.first_ref = bf16[576,512]{1,0:T(8,128)(2,1)S(1)} custom-call(bf16[768,512]{1,0:T(8,128)(2,1)S(1)} %get-tuple-element.52.grad_att_ref, f32[768,512]{1,0:T(8,128)S(1)} %get-tuple-element.49.direct_ref, bf16[768,2048]{1,0:T(8,128)(2,1)S(1)} %get-tuple-element.50.slope_ref, bf16[4,2048,512]{2,1,0:T(8,128)(2,1)S(1)} %bitcast.4), custom_call_target="tpu_custom_call" | custom-call | flops 2415919104 | bytes 8388608 | tf_op jit(solution)/shard_map/attend_back/pallas_call | solution.py:438
  58.1 1.1 %collective-permute-done.12 = bf16[256,512]{1,0:T(8,128)(2,1)S(1)} collective-permute-done((bf16[256,512]{1,0:T(8,128)(2,1)S(1)}, bf16[256,512]{1,0:T(8,128)(2,1)S(1)}, u32[]{:S(2)}, u32[]{:S(2)}) %collective-permute-start.12) | collective-permute-done | bytes 262176 | tf_op jit(solution)/shard_map/ppermute | solution.py:560
  59.3 1.5 %attend_back.3.second_ref = bf16[192,512]{1,0:T(8,128)(2,1)S(1)} custom-call(bf16[768,512]{1,0:T(8,128)(2,1)S(1)} %get-tuple-element.52.grad_att_ref, f32[768,512]{1,0:T(8,128)S(1)} %get-tuple-element.49.direct_ref, bf16[768,2048]{1,0:T(8,128)(2,1)S(1)} %get-tuple-element.50.slope_ref, bf16[4,2048,512]{2,1,0:T(8,128)(2,1)S(1)} %bitcast.4), custom_call_target="tpu_custom_call" | custom-call | flops 805306368 | bytes 8388608 | tf_op jit(solution)/shard_map/attend_back/pallas_call | solution.py:438
  61.3 1.0 %own_cand_grad.1.cand_grad_ref = f32[1024,512]{1,0:T(8,128)S(1)} custom-call(s32[1,768]{1,0:T(1,128)S(1)} %reshape.59.slots_ref, bf16[576,512]{1,0:T(8,128)(2,1)S(1)} %attend_back.2.first_ref, bf16[192,512]{1,0:T(8,128)(2,1)S(1)} %attend_back.3.second_ref), custom_call_target="tpu_custom_call" | custom-call | flops 805306368 | bytes 4194304 | tf_op jit(solution)/shard_map/own_cand_grad/pallas_call | solution.py:476
  62.4 1.7 %chip_terms.1 = bf16[512,512]{1,0:T(8,128)(2,1)S(1)} custom-call(s32[1]{0:T(128)} %bitcast.wide_ref, f32[1024,512]{1,0:T(8,128)S(1)} %own_cand_grad.1.cand_grad_ref, s32[1,768]{1,0:T(1,128)S(1)} %reshape.66.slots_ref, bf16[576,512]{1,0:T(8,128)(2,1)S(1)} %collective-permute-done.14.first_ref, bf16[192,512]{1,0:T(8,128)(2,1)S(1)} %collective-permute-done.15.second_ref, ...), custom_call_target="tpu_custom_call" | custom-call | flops 1342177280 | bytes 4194304 | tf_op jit(solution)/shard_map/chip_terms/pallas_call | solution.py:530
  64.2 1.8 %collective-permute-start.16 = (bf16[128,512]{1,0:T(8,128)(2,1)S(1)}, bf16[128,512]{1,0:T(8,128)(2,1)S(1)}, u32[]{:S(2)}, u32[]{:S(2)}) collective-permute-start(bf16[128,512]{1,0:T(8,128)(2,1)S(1)} %get-tuple-element.62), channel_id=1, source_target_pairs={{0,3},{1,2},{2,1},{3,0},{4,7},{5,6},{6,5},{7,4},{8,11},{9,10},{10,... | collective-permute-start | bytes 393224 | tf_op jit(solution)/shard_map/ppermute | solution.py:560
  66.0 1.1 %collective-permute-start.17 = (bf16[128,512]{1,0:T(8,128)(2,1)S(1)}, bf16[128,512]{1,0:T(8,128)(2,1)S(1)}, u32[]{:S(2)}, u32[]{:S(2)}) collective-permute-start(bf16[128,512]{1,0:T(8,128)(2,1)S(1)} %get-tuple-element.64), channel_id=1, source_target_pairs={{0,2},{1,3},{2,0},{3,1},{4,6},{5,7},{6,4},{7,5},{8,10},{9,11},{10,... | collective-permute-start | bytes 393224 | tf_op jit(solution)/shard_map/ppermute | solution.py:560
  67.7 0.8 reduce.1
  68.5 3.0 %collective-permute-done.16 = bf16[128,512]{1,0:T(8,128)(2,1)S(1)} collective-permute-done((bf16[128,512]{1,0:T(8,128)(2,1)S(1)}, bf16[128,512]{1,0:T(8,128)(2,1)S(1)}, u32[]{:S(2)}, u32[]{:S(2)}) %collective-permute-start.16) | collective-permute-done | bytes 131104 | tf_op jit(solution)/shard_map/ppermute | solution.py:560
  71.5 2.2 %collective-permute-done.17 = bf16[128,512]{1,0:T(8,128)(2,1)S(1)} collective-permute-done((bf16[128,512]{1,0:T(8,128)(2,1)S(1)}, bf16[128,512]{1,0:T(8,128)(2,1)S(1)}, u32[]{:S(2)}, u32[]{:S(2)}) %collective-permute-start.17) | collective-permute-done | bytes 131104 | tf_op jit(solution)/shard_map/ppermute | solution.py:560
  73.8 2.1 %collective-permute-start.19 = (bf16[32,512]{1,0:T(8,128)(2,1)S(1)}, bf16[32,512]{1,0:T(8,128)(2,1)S(1)}, u32[]{:S(2)}, u32[]{:S(2)}) collective-permute-start(bf16[32,512]{1,0:T(8,128)(2,1)S(1)} %get-tuple-element.65), channel_id=1, source_target_pairs={{0,12},{1,13},{2,14},{3,15},{4,8},{5,9},{6,10},{7,11},{8,4},{9,5},... | collective-permute-start | bytes 98312 | tf_op jit(solution)/shard_map/ppermute | solution.py:560
  76.4 1.8 %collective-permute-start.21 = (bf16[32,512]{1,0:T(8,128)(2,1)S(1)}, bf16[32,512]{1,0:T(8,128)(2,1)S(1)}, u32[]{:S(2)}, u32[]{:S(2)}) collective-permute-start(bf16[32,512]{1,0:T(8,128)(2,1)S(1)} %get-tuple-element.67), channel_id=1, source_target_pairs={{0,4},{1,5},{2,6},{3,7},{4,0},{5,1},{6,2},{7,3},{8,12},{9,13},{10,... | collective-permute-start | bytes 98312 | tf_op jit(solution)/shard_map/ppermute | solution.py:560
  78.2 1.3 %collective-permute-done.19 = bf16[32,512]{1,0:T(8,128)(2,1)S(1)} collective-permute-done((bf16[32,512]{1,0:T(8,128)(2,1)S(1)}, bf16[32,512]{1,0:T(8,128)(2,1)S(1)}, u32[]{:S(2)}, u32[]{:S(2)}) %collective-permute-start.19) | collective-permute-done | bytes 32800 | tf_op jit(solution)/shard_map/ppermute | solution.py:560
  79.6 1.2 %collective-permute-done.20 = bf16[32,512]{1,0:T(8,128)(2,1)S(1)} collective-permute-done((bf16[32,512]{1,0:T(8,128)(2,1)S(1)}, bf16[32,512]{1,0:T(8,128)(2,1)S(1)}, u32[]{:S(2)}, u32[]{:S(2)}) %collective-permute-start.20) | collective-permute-done | bytes 32800 | tf_op jit(solution)/shard_map/ppermute | solution.py:560
  (74 shorter events, 7.4 us)
Async XLA Ops:
  0.7 33.3 %copy-start.1 = (s32[768]{0:T(1024)S(1)}, s32[768]{0:T(1024)}, u32[]{:S(2)}) copy-start(s32[768]{0:T(1024)} %param.23) | copy-start | bytes 9220
  0.7 33.7 %copy-start.4 = (bf16[1024]{0:T(1024)(128)(2,1)S(1)}, bf16[1024]{0:T(1024)(128)(2,1)}, u32[]{:S(2)}) copy-start(bf16[1024]{0:T(1024)(128)(2,1)} %param.17) | copy-start | bytes 6148
  15.4 7.0 %collective-permute-start = (bf16[32,512]{1,0:T(8,128)(2,1)S(1)}, bf16[32,512]{1,0:T(8,128)(2,1)S(1)}, u32[]{:S(2)}, u32[]{:S(2)}) collective-permute-start(bf16[32,512]{1,0:T(8,128)(2,1)S(1)} %get-tuple-element.31), channel_id=1, source_target_pairs={{0,12},{1,13},{2,14},{3,15},{4,8},{5,9},{6,10},{7,11},{8,4},{9,5},... | collective-permute-start | bytes 98312 | tf_op jit(solution)/shard_map/ppermute | solution.py:560
  20.5 4.8 %collective-permute-start.1 = (bf16[32,512]{1,0:T(8,128)(2,1)S(1)}, bf16[32,512]{1,0:T(8,128)(2,1)S(1)}, u32[]{:S(2)}, u32[]{:S(2)}) collective-permute-start(bf16[32,512]{1,0:T(8,128)(2,1)S(1)} %get-tuple-element.31), channel_id=1, source_target_pairs={{0,8},{1,9},{2,10},{3,11},{4,12},{5,13},{6,14},{7,15},{8,0},{9,1},... | collective-permute-start | bytes 98312 | tf_op jit(solution)/shard_map/ppermute | solution.py:560
  20.5 4.8 %collective-permute-start.2 = (bf16[32,512]{1,0:T(8,128)(2,1)S(1)}, bf16[32,512]{1,0:T(8,128)(2,1)S(1)}, u32[]{:S(2)}, u32[]{:S(2)}) collective-permute-start(bf16[32,512]{1,0:T(8,128)(2,1)S(1)} %get-tuple-element.31), channel_id=1, source_target_pairs={{0,4},{1,5},{2,6},{3,7},{4,0},{5,1},{6,2},{7,3},{8,12},{9,13},{10,... | collective-permute-start | bytes 98312 | tf_op jit(solution)/shard_map/ppermute | solution.py:560
  21.2 1.2 %collective-permute-start.4 = (s32[768]{0:T(1024)S(1)}, s32[768]{0:T(1024)S(1)}, u32[]{:S(2)}, u32[]{:S(2)}) collective-permute-start(s32[768]{0:T(1024)S(1)} %get-tuple-element.81), channel_id=1, source_target_pairs={{0,16},{16,0},{1,17},{17,1},{2,18},{18,2},{3,19},{19,3},{4,20},{20... | collective-permute-start | bytes 9224 | tf_op jit(solution)/shard_map/ppermute | solution.py:560
  21.3 4.0 %collective-permute-start.3 = (bf16[32,512]{1,0:T(8,128)(2,1)S(1)}, bf16[32,512]{1,0:T(8,128)(2,1)S(1)}, u32[]{:S(2)}, u32[]{:S(2)}) collective-permute-start(bf16[32,512]{1,0:T(8,128)(2,1)S(1)} %get-tuple-element.33), channel_id=1, source_target_pairs={{0,16},{16,0},{1,17},{17,1},{2,18},{18,2},{3,19},{19,3},{4,20},{20... | collective-permute-start | bytes 98312 | tf_op jit(solution)/shard_map/ppermute | solution.py:560
  25.3 7.9 %collective-permute-start.5 = (bf16[128,512]{1,0:T(8,128)(2,1)S(1)}, bf16[128,512]{1,0:T(8,128)(2,1)S(1)}, u32[]{:S(2)}, u32[]{:S(2)}) collective-permute-start(bf16[128,512]{1,0:T(8,128)(2,1)S(1)} %get-tuple-element.73), channel_id=1, source_target_pairs={{0,3},{1,2},{2,1},{3,0},{4,7},{5,6},{6,5},{7,4},{8,11},{9,10},{10,... | collective-permute-start | bytes 393224 | tf_op jit(solution)/shard_map/ppermute | solution.py:560
  27.9 5.6 %collective-permute-start.6 = (bf16[128,512]{1,0:T(8,128)(2,1)S(1)}, bf16[128,512]{1,0:T(8,128)(2,1)S(1)}, u32[]{:S(2)}, u32[]{:S(2)}) collective-permute-start(bf16[128,512]{1,0:T(8,128)(2,1)S(1)} %get-tuple-element.73), channel_id=1, source_target_pairs={{0,2},{1,3},{2,0},{3,1},{4,6},{5,7},{6,4},{7,5},{8,10},{9,11},{10,... | collective-permute-start | bytes 393224 | tf_op jit(solution)/shard_map/ppermute | solution.py:560
  28.4 5.1 %collective-permute-start.7 = (bf16[128,512]{1,0:T(8,128)(2,1)S(1)}, bf16[128,512]{1,0:T(8,128)(2,1)S(1)}, u32[]{:S(2)}, u32[]{:S(2)}) collective-permute-start(bf16[128,512]{1,0:T(8,128)(2,1)S(1)} %get-tuple-element.73), channel_id=1, source_target_pairs={{0,1},{1,0},{2,3},{3,2},{4,5},{5,4},{6,7},{7,6},{8,9},{9,8},{10,11... | collective-permute-start | bytes 393224 | tf_op jit(solution)/shard_map/ppermute | solution.py:560
  28.9 4.3 %collective-permute-start.8 = (bf16[64,512]{1,0:T(8,128)(2,1)S(1)}, bf16[64,512]{1,0:T(8,128)(2,1)S(1)}, u32[]{:S(2)}, u32[]{:S(2)}) collective-permute-start(bf16[64,512]{1,0:T(8,128)(2,1)S(1)} %maximum_select_fusion), channel_id=1, source_target_pairs={{0,4},{1,5},{2,6},{3,7},{4,0},{5,1},{6,2},{7,3},{8,12},{9,13},{10,... | collective-permute-start | bytes 196616 | tf_op jit(solution)/shard_map/ppermute | solution.py:560
  33.5 3.0 %collective-permute-start.10 = (bf16[512,512]{1,0:T(8,128)(2,1)S(1)}, bf16[512,512]{1,0:T(8,128)(2,1)S(1)}, u32[]{:S(2)}, u32[]{:S(2)}) collective-permute-start(bf16[512,512]{1,0:T(8,128)(2,1)S(1)} %constant_dynamic-update-slice_fusion.4.near_ref), channel_id=1, source_target_pairs={{0,16},{16,0},{1,17},{17,1},{2,18},{18,2},{3,19},{19,3},{4,20},{20... | collective-permute-start | bytes 1572872 | tf_op jit(solution)/shard_map/ppermute | solution.py:560
  34.4 9.7 %collective-permute-start.9 = (bf16[128,512]{1,0:T(8,128)(2,1)S(1)}, bf16[128,512]{1,0:T(8,128)(2,1)S(1)}, u32[]{:S(2)}, u32[]{:S(2)}) collective-permute-start(bf16[128,512]{1,0:T(8,128)(2,1)S(1)} %pad_maximum_fusion), channel_id=1, source_target_pairs={{0,8},{1,9},{2,10},{3,11},{4,12},{5,13},{6,14},{7,15},{8,0},{9,1},... | collective-permute-start | bytes 393224 | tf_op jit(solution)/shard_map/ppermute | solution.py:560
  44.2 13.9 %collective-permute-start.11 = (bf16[256,512]{1,0:T(8,128)(2,1)S(1)}, bf16[256,512]{1,0:T(8,128)(2,1)S(1)}, u32[]{:S(2)}, u32[]{:S(2)}) collective-permute-start(bf16[256,512]{1,0:T(8,128)(2,1)S(1)} %get-tuple-element.69), channel_id=1, source_target_pairs={{0,3},{1,2},{2,1},{3,0},{4,7},{5,6},{6,5},{7,4},{8,11},{9,10},{10,... | collective-permute-start | bytes 786440 | tf_op jit(solution)/shard_map/ppermute | solution.py:560
  46.5 12.7 %collective-permute-start.12 = (bf16[256,512]{1,0:T(8,128)(2,1)S(1)}, bf16[256,512]{1,0:T(8,128)(2,1)S(1)}, u32[]{:S(2)}, u32[]{:S(2)}) collective-permute-start(bf16[256,512]{1,0:T(8,128)(2,1)S(1)} %get-tuple-element.69), channel_id=1, source_target_pairs={{0,2},{1,3},{2,0},{3,1},{4,6},{5,7},{6,4},{7,5},{8,10},{9,11},{10,... | collective-permute-start | bytes 786440 | tf_op jit(solution)/shard_map/ppermute | solution.py:560
  47.0 12.2 %collective-permute-start.13 = (bf16[256,512]{1,0:T(8,128)(2,1)S(1)}, bf16[256,512]{1,0:T(8,128)(2,1)S(1)}, u32[]{:S(2)}, u32[]{:S(2)}) collective-permute-start(bf16[256,512]{1,0:T(8,128)(2,1)S(1)} %get-tuple-element.69), channel_id=1, source_target_pairs={{0,1},{1,0},{2,3},{3,2},{4,5},{5,4},{6,7},{7,6},{8,9},{9,8},{10,11... | collective-permute-start | bytes 786440 | tf_op jit(solution)/shard_map/ppermute | solution.py:560
  59.2 3.1 %collective-permute-start.14 = (bf16[576,512]{1,0:T(8,128)(2,1)S(1)}, bf16[576,512]{1,0:T(8,128)(2,1)S(1)}, u32[]{:S(2)}, u32[]{:S(2)}) collective-permute-start(bf16[576,512]{1,0:T(8,128)(2,1)S(1)} %attend_back.2.first_ref), channel_id=1, source_target_pairs={{0,16},{16,0},{1,17},{17,1},{2,18},{18,2},{3,19},{19,3},{4,20},{20... | collective-permute-start | bytes 1769480 | tf_op jit(solution)/shard_map/ppermute | solution.py:560
  60.7 1.6 %collective-permute-start.15 = (bf16[192,512]{1,0:T(8,128)(2,1)S(1)}, bf16[192,512]{1,0:T(8,128)(2,1)S(1)}, u32[]{:S(2)}, u32[]{:S(2)}) collective-permute-start(bf16[192,512]{1,0:T(8,128)(2,1)S(1)} %attend_back.3.second_ref), channel_id=1, source_target_pairs={{0,16},{16,0},{1,17},{17,1},{2,18},{18,2},{3,19},{19,3},{4,20},{20... | collective-permute-start | bytes 589832 | tf_op jit(solution)/shard_map/ppermute | solution.py:560
  64.2 7.3 %collective-permute-start.16 = (bf16[128,512]{1,0:T(8,128)(2,1)S(1)}, bf16[128,512]{1,0:T(8,128)(2,1)S(1)}, u32[]{:S(2)}, u32[]{:S(2)}) collective-permute-start(bf16[128,512]{1,0:T(8,128)(2,1)S(1)} %get-tuple-element.62), channel_id=1, source_target_pairs={{0,3},{1,2},{2,1},{3,0},{4,7},{5,6},{6,5},{7,4},{8,11},{9,10},{10,... | collective-permute-start | bytes 393224 | tf_op jit(solution)/shard_map/ppermute | solution.py:560
  66.0 7.7 %collective-permute-start.17 = (bf16[128,512]{1,0:T(8,128)(2,1)S(1)}, bf16[128,512]{1,0:T(8,128)(2,1)S(1)}, u32[]{:S(2)}, u32[]{:S(2)}) collective-permute-start(bf16[128,512]{1,0:T(8,128)(2,1)S(1)} %get-tuple-element.64), channel_id=1, source_target_pairs={{0,2},{1,3},{2,0},{3,1},{4,6},{5,7},{6,4},{7,5},{8,10},{9,11},{10,... | collective-permute-start | bytes 393224 | tf_op jit(solution)/shard_map/ppermute | solution.py:560
  67.1 6.6 %collective-permute-start.18 = (bf16[128,512]{1,0:T(8,128)(2,1)S(1)}, bf16[128,512]{1,0:T(8,128)(2,1)S(1)}, u32[]{:S(2)}, u32[]{:S(2)}) collective-permute-start(bf16[128,512]{1,0:T(8,128)(2,1)S(1)} %get-tuple-element.63), channel_id=1, source_target_pairs={{0,1},{1,0},{2,3},{3,2},{4,5},{5,4},{6,7},{7,6},{8,9},{9,8},{10,11... | collective-permute-start | bytes 393224 | tf_op jit(solution)/shard_map/ppermute | solution.py:560
  73.8 5.8 %collective-permute-start.19 = (bf16[32,512]{1,0:T(8,128)(2,1)S(1)}, bf16[32,512]{1,0:T(8,128)(2,1)S(1)}, u32[]{:S(2)}, u32[]{:S(2)}) collective-permute-start(bf16[32,512]{1,0:T(8,128)(2,1)S(1)} %get-tuple-element.65), channel_id=1, source_target_pairs={{0,12},{1,13},{2,14},{3,15},{4,8},{5,9},{6,10},{7,11},{8,4},{9,5},... | collective-permute-start | bytes 98312 | tf_op jit(solution)/shard_map/ppermute | solution.py:560
  75.9 4.9 %collective-permute-start.20 = (bf16[32,512]{1,0:T(8,128)(2,1)S(1)}, bf16[32,512]{1,0:T(8,128)(2,1)S(1)}, u32[]{:S(2)}, u32[]{:S(2)}) collective-permute-start(bf16[32,512]{1,0:T(8,128)(2,1)S(1)} %get-tuple-element.66), channel_id=1, source_target_pairs={{0,8},{1,9},{2,10},{3,11},{4,12},{5,13},{6,14},{7,15},{8,0},{9,1},... | collective-permute-start | bytes 98312 | tf_op jit(solution)/shard_map/ppermute | solution.py:560
  76.4 4.5 %collective-permute-start.21 = (bf16[32,512]{1,0:T(8,128)(2,1)S(1)}, bf16[32,512]{1,0:T(8,128)(2,1)S(1)}, u32[]{:S(2)}, u32[]{:S(2)}) collective-permute-start(bf16[32,512]{1,0:T(8,128)(2,1)S(1)} %get-tuple-element.67), channel_id=1, source_target_pairs={{0,4},{1,5},{2,6},{3,7},{4,0},{5,1},{6,2},{7,3},{8,12},{9,13},{10,... | collective-permute-start | bytes 98312 | tf_op jit(solution)/shard_map/ppermute | solution.py:560
  (6 other events, 121.0 us)
